TPU v7x, 32 devices: a whole 2x2x4 slice. The times are simulated.
32 devices in a mesh: pa: 4 (over x, core), pb: 8 (over z, y).
Axes of the slice: x: 2, y: 2, z: 4, core: 2. Of those that a mesh axis runs over, the one named last changes fastest.
Arguments:
- queries: bfloat16 [1024, 768], replicated, may hold values from -500 to 500, as said below
- passages: bfloat16 [16384, 768], P(('pa', 'pb')), may hold values from -32 to 32
- noise: bfloat16 [1024, 16384], P(None, ('pa', 'pb')), may hold values from 0.0099487305 to 0.98828125
- mix_weight: bfloat16 [768, 1024], replicated, may hold values from -0.046875 to 0.046875
- answer_queries: bfloat16 [1024, 1024], P('pb'), may hold values from -150 to 150, as said below
- key_weight: bfloat16 [1024, 1024], replicated, may hold values from -1 to 1
- value_weight: bfloat16 [1024, 1024], replicated, may hold values from -0.1875 to 0.1875
- token_states: bfloat16 [256, 256, 1024], P(('pa', 'pb')), may hold values from -6 to 6, as said below
- block_owner: int32 [256], replicated, may hold values from 0 to 255, as said below
- listed: int32 [8, 64], P('pb', 'pa'), may hold values from 0 to 255, as said below
Outputs:
- attended: bfloat16 [1024, 1024], P('pb', 'pa')
Inputs may be any that keep to these rules, and one draw needn't show every extreme that they name: A permutation: block b lies in slot block_owner[b]; slots run through the devices in pa+pb order, 8 to a device, and the holding device's shelf is slot // 8. Entries p * 16 to (p + 1) * 16 - 1 of row g name blocks whose slots lie on devices with pa index p; they come in groups of exactly 2 from 8 different devices. No block appears twice in a row; a block may appear in several rows, and some devices hold blocks listed by many rows. `queries`: embedding values. `answer_queries`: query values. `token_states`: state values.
All inputs are finite; a program needn't handle non-finite values.
Results may differ from a plain program's by a relative error of at most 0.012.
The roundings to bfloat16 on the way count: a program that leaves them out, or rounds other values in their place, can miss the bound.
Values may be sent and summed in bfloat16 or wider, within the bound.
No kernel may reach another device: no remote copies, remote signals or barrier semaphores. Data moves between devices by JAX's collectives and lax.ppermute only.
A program may use at most 192 MiB of HBM per device.

v0:
```python
import jax
import jax.numpy as jnp
from jax import lax
from jax.sharding import PartitionSpec as P

HEADS = 16
CAP = 2


TEMPER = 0.5
FLOOR = -1e30


def merged(value, axis, join):
    pieces = jax.tree.map(lambda part: lax.all_gather(part, axis), value)
    head = jax.tree.map(lambda part: part[0], pieces)
    tail = jax.tree.map(lambda part: part[1:], pieces)
    total, _ = lax.scan(lambda total, slab: (join(total, slab), None), head, tail)
    return total


def softened(queries, passages, noise):
    logits = jnp.einsum("qd,pd->qp", queries, passages, preferred_element_type=jnp.float32)
    gumbel = -jnp.log(-jnp.log(noise.astype(jnp.float32)))
    return (logits * queries.shape[1] ** (-0.5) + gumbel) / TEMPER


def holders(block_owner, block_ids, readers, shelf_size):
    slot_ids = jnp.take(block_owner, block_ids, axis=0)
    column = slot_ids // shelf_size % readers
    inside = slot_ids % shelf_size
    shared = column[..., :, None] == column[..., None, :]
    length = block_ids.shape[-1]
    before = jnp.arange(length)[None, :] < jnp.arange(length)[:, None]
    position = jnp.sum((shared & before).astype(jnp.int32), -1)
    return (column, inside, position)


def join_partials(former, latter):
    highest = jnp.maximum(former[0], latter[0])
    leading = jnp.exp(former[0] - highest)
    trailing = jnp.exp(latter[0] - highest)
    return (
        highest,
        former[1] * leading + latter[1] * trailing,
        former[2] * leading[..., None] + latter[2] * trailing[..., None],
    )


def local(
    queries,
    passages,
    noise,
    mix_weight,
    answer_queries,
    key_weight,
    value_weight,
    token_states,
    block_owner,
    listed,
):
    readers = lax.axis_size("pb")
    group = lax.axis_index("pb")
    runner = lax.axis_index("pa")
    answer_count = answer_queries.shape[0]
    model_width = key_weight.shape[0]
    head_width = model_width // HEADS
    shelf_size = token_states.shape[0]
    tokens_each = token_states.shape[1]
    requests = lax.all_gather(listed, "pb", axis=0, tiled=True)
    scores = softened(queries, passages, noise)
    highest = lax.pmax(jnp.max(scores, 1), ("pa", "pb"))
    denominator = lax.psum(jnp.sum(jnp.exp(scores - highest[:, None]), 1), ("pa", "pb"))
    weights = (jnp.exp(scores - highest[:, None]) / denominator[:, None]).astype(jnp.bfloat16)
    partial_mix = jnp.dot(weights, passages, preferred_element_type=jnp.float32)
    blended_all = lax.psum(partial_mix, ("pa", "pb"))
    blended = lax.dynamic_slice_in_dim(blended_all, group * answer_count, answer_count, 0)
    conditioned = (
        answer_queries.astype(jnp.float32)
        + jnp.dot(blended.astype(jnp.bfloat16), mix_weight, preferred_element_type=jnp.float32)
    ).astype(jnp.bfloat16)
    column, inside, position = holders(block_owner, requests, readers, shelf_size)
    capacity_slots = jnp.arange(CAP, dtype=jnp.int32)
    matches = (column[:, None, :] == group) & (
        position[:, None, :] == capacity_slots[None, :, None]
    )
    chosen_slot = jnp.sum(jnp.where(matches, inside[:, None, :], 0), 2)
    filled = jnp.any(matches, 2)
    own_column, own_inside, own_position = holders(block_owner, listed[0], readers, shelf_size)
    outgoing = jnp.take(token_states, chosen_slot.reshape(-1), axis=0)
    outgoing = outgoing.reshape(readers, CAP, tokens_each, model_width) * filled[
        :, :, None, None
    ].astype(jnp.bfloat16)
    arrived = lax.all_to_all(outgoing, "pb", split_axis=0, concat_axis=0, tiled=True)
    picked = jnp.take(
        arrived.reshape(readers * CAP, tokens_each, model_width),
        own_column * CAP + own_position,
        axis=0,
    )
    flat_states = picked.reshape(-1, model_width)
    key_rows = jnp.dot(flat_states, key_weight, preferred_element_type=jnp.float32).astype(
        jnp.bfloat16
    )
    key_rows = key_rows.reshape(-1, tokens_each, HEADS, head_width)
    value_rows = jnp.dot(flat_states, value_weight, preferred_element_type=jnp.float32).astype(
        jnp.bfloat16
    )
    value_rows = value_rows.reshape(-1, tokens_each, HEADS, head_width)
    query_heads = conditioned.reshape(answer_count, HEADS, head_width)
    block_scores = jnp.einsum(
        "rhd,bthd->rhbt", query_heads, key_rows, preferred_element_type=jnp.float32
    )
    block_high = jnp.max(block_scores, 3)
    shared = own_column[:, None] == own_column[None, :]
    shelf_high = jnp.max(jnp.where(shared[None, None], block_high[:, :, None, :], FLOOR), 3)
    exponent = jnp.exp(block_scores - shelf_high[..., None])
    block_total = jnp.sum(exponent, 3)
    block_out = jnp.einsum(
        "rhbt,bthd->rhbd",
        exponent.astype(jnp.bfloat16),
        value_rows,
        preferred_element_type=jnp.float32,
    )
    run_high = jnp.max(shelf_high, 2)
    factor = jnp.exp(shelf_high - run_high[..., None])
    run_total = jnp.sum(factor * block_total, 2)
    run_out = jnp.sum(factor[..., None] * block_out, 2)
    merged_high, merged_total, merged_out = merged(
        (run_high, run_total, run_out), "pa", join_partials
    )
    normalized = (merged_out / merged_total[..., None]).reshape(answer_count, model_width)
    stride = model_width // lax.axis_size("pa")
    return lax.dynamic_slice_in_dim(normalized, runner * stride, stride, 1).astype(jnp.bfloat16)


def solution(mesh):
    return jax.shard_map(
        local,
        mesh=mesh,
        in_specs=(
            P(),
            P(("pa", "pb"), None),
            P(None, ("pa", "pb")),
            P(),
            P("pb", None),
            P(),
            P(),
            P(("pa", "pb"), None, None),
            P(),
            P("pb", "pa"),
        ),
        out_specs=P("pb", "pa"),
        check_vma=False,
    )
```

profile of v0, /device:TPU:0, one launch (start us, length us, event | category | flops | bytes accessed | tf_op | source)
XLA Modules:
  0.0 554.7 jit_solution(8204217291980997043)
XLA Ops:
  6.5 22.4 %all-gather.3 = s32[8,1,16]{2,1,0:T(1,128)S(1)} all-gather(s32[1,1,16]{2,1,0:T(1,128)} %bitcast.99), channel_id=1, replica_groups=mesh['pa'=4,'pb'=8] {'pb'}, dimensions={0}, use_global_device_ids=true | all-gather | bytes 576 | tf_op jit(solution)/shard_map/all_gather | solution.py:70
  29.1 1.6 gather_fusion.1
  31.8 6.9 %gather_fusion.2 = bf16[16,256,1024]{2,1,0:T(8,128)(2,1)} fusion(bf16[8,256,1024]{2,1,0:T(8,128)(2,1)} %param.19, s32[1024]{0:T(1024)S(1)} %pad_clamp_fusion.1), kind=kCustom, calls=%fused_computation.2 | custom fusion | bytes 16777280 | tf_op jit(solution)/shard_map/jit(_take)/gather | solution.py:90
  38.8 7.4 %select_multiply_fusion = bf16[8,2,256,1024]{3,2,1,0:T(8,128)(2,1)} fusion(bf16[8,2,256,1024]{3,2,1,0:T(8,128)(2,1)} %bitcast.90, pred[8,2]{1,0:T(8,128)(4,1)S(1)} %copy.66, bf16[8,2]{1,0:T(8,128)(2,1)S(1)} %copy.68), kind=kLoop, calls=%fused_computation.24 | loop fusion | flops 8388608 | bytes 16777264 | tf_op jit(solution)/shard_map/mul | solution.py:91
  46.2 5.1 all-to-all-start
  52.4 1.3 copy.70
  53.7 4.6 fusion.35
  58.3 192.7 %pmax.7 = f32[1024]{0:T(1024)S(1)} all-reduce(f32[1024]{0:T(1024)S(1)} %get-tuple-element.99), channel_id=1, replica_groups=mesh['pa'=4,'pb'=8] {'pa','pb'}, use_global_device_ids=true, to_apply=%region_5.6 | all-reduce | flops 1024 | bytes 8192 | tf_op jit(solution)/shard_map/pmax | solution.py:72
  251.0 1.9 fusion.15
  252.9 39.3 %psum.14 = f32[1024]{0:T(1024)S(1)} all-reduce(f32[1024]{0:T(1024)S(1)} %fusion.15), channel_id=1, replica_groups=mesh['pa'=4,'pb'=8] {'pa','pb'}, use_global_device_ids=true, to_apply=%region_7.8 | all-reduce | flops 1024 | bytes 8192 | tf_op jit(solution)/shard_map/psum | solution.py:73
  292.3 4.5 fusion.17
  296.8 77.5 %all-reduce.1 = bf16[1024,768]{1,0:T(8,128)(2,1)} all-reduce(f32[1024,768]{1,0:T(8,128)} %fusion.17), channel_id=1, replica_groups=mesh['pa'=4,'pb'=8] {'pa','pb'}, use_global_device_ids=true, to_apply=%region_8.9 | all-reduce | flops 786432 | bytes 4718592 | tf_op jit(solution)/shard_map/psum | solution.py:76
  374.3 1.9 fusion.16
  376.5 8.1 %gather_fusion.3 = bf16[16,256,1024]{2,1,0:T(8,128)(2,1)} fusion(bf16[16,256,1024]{2,1,0:T(8,128)(2,1)} %bitcast.12, s32[1024]{0:T(1024)S(1)} %pad_clamp_fusion), kind=kCustom, calls=%fused_computation.3 | custom fusion | bytes 16777280 | tf_op jit(solution)/shard_map/jit(_take)/gather | solution.py:95
  384.6 4.5 bitcast_select_fusion
  389.1 3.2 copy-done.3
  392.3 10.8 %convolution_convert_fusion.1 = bf16[4096,1024]{1,0:T(8,128)(2,1)} fusion(bf16[4096,1024]{1,0:T(8,128)(2,1)S(1)} %bitcast_select_fusion, bf16[1024,1024]{1,0:T(8,128)(2,1)S(1)} %copy-done), kind=kOutput, calls=%fused_computation.26 | convolution fusion | flops 8594128896 | bytes 18874368 | tf_op jit(solution)/shard_map/dot_general | solution.py:101
  403.1 22.2 %reshape.431 = bf16[16,256,16,64]{3,2,1,0:T(8,128)(2,1)} reshape(bf16[4096,1024]{1,0:T(8,128)(2,1)} %convolution_convert_fusion.1) | data formatting | bytes 16777216 | tf_op jit(solution)/shard_map/reshape | solution.py:104
  425.4 14.5 %convolution_convert_fusion = bf16[4096,1024]{1,0:T(8,128)(2,1)} fusion(bf16[4096,1024]{1,0:T(8,128)(2,1)} %copy-done.3, bf16[1024,1024]{1,0:T(8,128)(2,1)S(1)} %copy-done.7), kind=kOutput, calls=%fused_computation.25 | convolution fusion | flops 8594128896 | bytes 18874368 | tf_op jit(solution)/shard_map/dot_general | solution.py:105
  439.9 22.1 %reshape.432 = bf16[16,256,16,64]{3,2,1,0:T(8,128)(2,1)} reshape(bf16[4096,1024]{1,0:T(8,128)(2,1)} %convolution_convert_fusion) | data formatting | bytes 16777216 | tf_op jit(solution)/shard_map/reshape | solution.py:108
  462.0 16.7 %bitcast_reduce_fusion = (f32[128,16,16]{0,2,1:T(8,128)S(1)}, f32[16,16,256,128]{3,2,1,0:T(8,128)}) fusion(bf16[128,16,64,1]{0,2,3,1:T(8,128)(2,1)S(1)} %bitcast.92, bf16[16,256,16,64]{3,2,1,0:T(8,128)(2,1)} %reshape.431), kind=kOutput, calls=%fused_computation.12 | convolution fusion | flops 1082097664 | bytes 42336256 | tf_op jit(solution)/shard_map/rhd,bthd->rhbt/dot_general | solution.py:110
  479.5 13.4 %fusion.3 = f32[128,16,16]{0,2,1:T(8,128)S(1)} fusion(f32[16,16,256,128]{3,2,1,0:T(8,128)} %get-tuple-element.102, f32[128,16,16]{0,2,1:T(8,128)S(1)} %get-tuple-element.73), kind=kLoop, calls=%fused_computation.15 | loop fusion | flops 16744448 | bytes 33816576 | tf_op jit(solution)/shard_map/reduce_sum | solution.py:117
  492.9 19.1 %fusion.10 = f32[128,16,64]{0,2,1:T(8,128)} fusion(f32[128,16,16]{0,2,1:T(8,128)S(1)} %get-tuple-element.94, f32[16,16,256,128]{3,2,1,0:T(8,128)} %get-tuple-element.102, f32[128,16,16]{0,2,1:T(8,128)S(1)} %get-tuple-element.73, bf16[16,256,16,64]{3,2,1,0:T(8,128)(2,1)} %reshape.432), kind=kOutput, calls=%fused_computation.22 | convolution fusion | flops 1094582272 | bytes 42729472 | tf_op jit(solution)/shard_map/rhbt,bthd->rhbd/dot_general | solution.py:118
  512.1 5.2 all-gather.1
  517.3 5.2 all-gather
  522.5 11.3 %all-gather.6.cloned.1.call-done = f32[512,16,64]{0,2,1:T(8,128)} async-done(((f32[128,16,64]{0,2,1:T(8,128)}), f32[512,16,64]{0,2,1:T(8,128)}) %all-gather.6.cloned.1.call-update) | async-done | bytes 2097168 | tf_op jit(solution)/shard_map/all_gather | solution.py:15
  533.7 1.6 slice.43
  535.4 2.3 copy.88
  538.1 6.6 %while.14 = (s32[]{:T(128)}, f32[128,16]{0,1:T(8,128)S(1)}, f32[128,16]{0,1:T(8,128)S(1)}, f32[128,16,64]{2,1,0:T(8,128)S(1)}, f32[3,128,16]{1,0,2:T(4,128)S(1)}...) while((s32[]{:T(128)}, f32[128,16]{0,1:T(8,128)S(1)}, f32[128,16]{0,1:T(8,128)S(1)}, ...), condition=%wide.region_16.17_spmd, body=%wide.region_15.16_spmd.sunk | while | flops 405506 | bytes 1720413 | solution.py:18
  538.4 2.0 fusion.46
  540.7 1.9 fusion.46
  542.9 1.9 fusion.46
  (76 shorter events, 7.7 us)
Async XLA Ops:
  6.5 385.8 %copy-start = (bf16[1024,1024]{1,0:T(8,128)(2,1)S(1)}, bf16[1024,1024]{1,0:T(8,128)(2,1)}, u32[]{:S(2)}) copy-start(bf16[1024,1024]{1,0:T(8,128)(2,1)} %param.17) | copy-start | bytes 6291460
  46.2 5.2 copy-start.6
  46.2 5.2 copy-start.2
  46.2 6.2 %copy-start.4 = (bf16[1024,512]{1,0:T(8,128)(2,1)S(1)}, bf16[1024,512]{1,0:T(8,128)(2,1)}, u32[]{:S(2)}) copy-start(bf16[1024,512]{1,0:T(8,128)(2,1)} %param.14) | copy-start | bytes 3145732
  46.2 330.3 %all-to-all-start = ((bf16[8,2,256,1024]{3,2,1,0:T(8,128)(2,1)}), bf16[8,2,256,1024]{3,2,1,0:T(8,128)(2,1)}, u32[]{:S(2)}, u32[]{:S(2)}) async-start(bf16[8,2,256,1024]{3,2,1,0:T(8,128)(2,1)} %select_multiply_fusion), calls=%async_computation | async-start | bytes 16777216 | tf_op jit(solution)/shard_map/all_to_all | solution.py:94
  51.3 482.5 %all-gather.6.cloned.1.call-start = ((), (), s32[]{:S(2)}) async-start(), calls=%async_computation.1 | async-start | bytes 2621440 | tf_op jit(solution)/shard_map/all_gather | solution.py:15
  292.2 82.0 %copy-start.5 = (bf16[128,1024]{1,0:T(8,128)(2,1)S(1)}, bf16[128,1024]{1,0:T(8,128)(2,1)}, u32[]{:S(2)}) copy-start(bf16[128,1024]{1,0:T(8,128)(2,1)} %param.16) | copy-start | bytes 786436
  389.1 3.2 copy-start.3
  403.1 22.2 %copy-start.7 = (bf16[1024,1024]{1,0:T(8,128)(2,1)S(1)}, bf16[1024,1024]{1,0:T(8,128)(2,1)}, u32[]{:S(2)}) copy-start(bf16[1024,1024]{1,0:T(8,128)(2,1)} %param.18) | copy-start | bytes 6291460
  533.7 3.9 slice-start
  538.1 9.7 %copy-start.1 = (bf16[1024,1024]{1,0:T(8,128)(2,1)S(1)}, bf16[1024,1024]{1,0:T(8,128)(2,1)}, u32[]{:S(2)}) copy-start(bf16[1024,1024]{1,0:T(8,128)(2,1)} %param.17) | copy-start | bytes 6291460
Sparse Core Ops, SparseCore 0:
  512.2 21.5 all-gather.5
where the time goes:
time: 557 us; the launch traced here: 555 us
  blocking collectives  342 us (61%)
  local copies, waits for them, and re-layouts  74.1 us (13%)
  matrix products  72.1 us (13%)
  other arithmetic  36 us (6%)
  between operations  13.6 us (2%)
  waiting for transfers between devices  11.3 us (2%)
    pmax x1, blocking collectives, local(): highest = lax.pmax(jnp.max(scores, 1), ('pa', 'pb'))  193 us
    psum x1, blocking collectives, local(): blended_all = lax.psum(partial_mix, ('pa', 'pb'))  77.5 us
    psum x1, blocking collectives, local(): lax.psum(jnp.sum(jnp.exp(scores - highest[:, None]), 1), ('pa', 'pb'))  39.3 us
    all_gather x1, blocking collectives, local(): requests = lax.all_gather(listed, 'pb', axis=0, tiled=True)  22.4 us
    reshape x1, local copies, waits for them, and re-layouts, local(): key_rows = key_rows.reshape(-1, tokens_each, HEADS, head_width)  22.2 us
    reshape x1, local copies, waits for them, and re-layouts, local(): value_rows = value_rows.reshape(-1, tokens_each, HEADS, head_width)  22.1 us
    dot_general x1, matrix products, local(): jnp.einsum('rhbt,bthd->rhbd', exponent.astype(jnp.bfloat16), value_rows,...  19.1 us
    dot_general x1, matrix products, local(): jnp.einsum('rhd,bthd->rhbt', query_heads, key_rows, preferred_element_typ...  16.7 us
  transfers between devices with their start and end apart: 2, of which 1 were waited for; matrix products, arithmetic and copies ran while one was open for 3% of the time, Pallas kernels for 0%

commit v1 on v0

v1 whole, which is shorter than its diff:
```python
import functools

import jax
import jax.numpy as jnp
from jax import lax
from jax.experimental import pallas as pl
from jax.experimental.pallas import tpu as pltpu
from jax.sharding import PartitionSpec as P

HEADS = 16
PAIR = 2
TEMPER = 0.5
FLOOR = -1e30
LANES = 128
STAT_ROWS = 32
VMEM_BYTES = 40 * 1024 * 1024
F32 = jnp.float32
BF16 = jnp.bfloat16
NT = (((1,), (1,)), ((), ()))


def grant():
    return pltpu.CompilerParams(vmem_limit_bytes=VMEM_BYTES)


def thirds(value):
    first = value.astype(BF16).astype(F32)
    rest = value - first
    second = rest.astype(BF16).astype(F32)
    return first, second, rest - second


def pack_row(mixed, shift, total):
    lane = lax.broadcasted_iota(jnp.int32, (mixed.shape[0], LANES), 1)
    tail = jnp.zeros((mixed.shape[0], LANES), F32)
    for at, term in enumerate(thirds(shift) + thirds(total)):
        tail = jnp.where(lane == at, term, tail)
    return jnp.concatenate([mixed, tail], 1).astype(BF16)


def unpack_row(packed):
    width = packed.shape[1] - LANES
    tail = packed[:, width:].astype(F32)
    shift = tail[:, 0:1] + tail[:, 1:2] + tail[:, 2:3]
    total = tail[:, 3:4] + tail[:, 4:5] + tail[:, 5:6]
    return packed[:, :width].astype(F32), shift, total


def merge_rows(parts):
    shift = functools.reduce(jnp.maximum, [part[1] for part in parts])
    mixed, total = 0.0, 0.0
    for part in parts:
        factor = jnp.exp(part[1] - shift)
        mixed = mixed + part[0] * factor
        total = total + part[2] * factor
    return mixed, shift, total


def retrieval_kernel(place, queries, passages, noise, keep, send, rows_scratch, *, spread):
    core = place[0]
    logits = lax.dot_general(queries[...], passages[...], NT, preferred_element_type=F32)
    gumbel = -jnp.log(-jnp.log(noise[...].astype(F32)))
    scores = (logits * queries.shape[1] ** (-0.5) + gumbel) / TEMPER
    shift = jnp.max(scores, 1, keepdims=True)
    weight = jnp.exp(scores - shift)
    total = jnp.sum(weight, 1, keepdims=True)
    mixed = jnp.dot(weight.astype(BF16), passages[...], preferred_element_type=F32)
    rows_scratch[...] = pack_row(mixed, shift, total).astype(F32)
    part = keep.shape[2]
    for column in range(spread):
        mine = pl.multiple_of((column * PAIR + core) * part, part)
        other = pl.multiple_of((column * PAIR + 1 - core) * part, part)
        keep[column, 0] = rows_scratch[pl.ds(mine, part), :].astype(BF16)
        send[column, 0] = rows_scratch[pl.ds(other, part), :].astype(BF16)


def retrieve(place, queries, passages, noise, readers, spread):
    count, width = queries.shape
    group = count // readers
    part = group // (PAIR * spread)
    shape = jax.ShapeDtypeStruct((spread, readers, part, width + LANES), BF16)
    spec = pl.BlockSpec((spread, 1, part, width + LANES), lambda g, place: (0, g, 0, 0))
    return pl.pallas_call(
        functools.partial(retrieval_kernel, spread=spread),
        grid_spec=pltpu.PrefetchScalarGridSpec(
            num_scalar_prefetch=1,
            grid=(readers,),
            in_specs=[
                pl.BlockSpec((group, width), lambda g, place: (g, 0)),
                pl.BlockSpec(passages.shape, lambda g, place: (0, 0)),
                pl.BlockSpec((group, noise.shape[1]), lambda g, place: (g, 0)),
            ],
            out_specs=[spec, spec],
            scratch_shapes=[pltpu.VMEM((group, width + LANES), F32)],
        ),
        out_shape=[shape, shape],
        compiler_params=grant(),
        name="retrieve",
    )(place, queries, passages, noise)


def pair_kernel(place, keep, recv, out, *, spread):
    for offset in range(spread):
        column = lax.bitwise_xor(place[1], offset)
        merged = merge_rows([unpack_row(keep[column, 0]), unpack_row(recv[column, 0])])
        out[offset, 0] = pack_row(*merged)


def merge_pair(place, keep, recv, spread):
    spec = pl.BlockSpec((spread, 1) + keep.shape[2:], lambda g, place: (0, g, 0, 0))
    return pl.pallas_call(
        functools.partial(pair_kernel, spread=spread),
        grid_spec=pltpu.PrefetchScalarGridSpec(
            num_scalar_prefetch=1, grid=(keep.shape[1],), in_specs=[spec, spec], out_specs=spec
        ),
        out_shape=jax.ShapeDtypeStruct(keep.shape, BF16),
        compiler_params=grant(),
        name="merge_pair",
    )(place, keep, recv)


def column_kernel(*refs):
    *parts, out = refs
    out[0] = pack_row(*merge_rows([unpack_row(part[0]) for part in parts]))


def merge_columns(parts):
    spec = pl.BlockSpec((1,) + parts[0].shape[1:], lambda g: (g, 0, 0))
    return pl.pallas_call(
        column_kernel,
        grid=(parts[0].shape[0],),
        in_specs=[spec] * len(parts),
        out_specs=spec,
        out_shape=jax.ShapeDtypeStruct(parts[0].shape, BF16),
        compiler_params=grant(),
        name="merge_columns",
    )(*parts)


def condition_kernel(place, parts, mix_weight, answers, keep, send, rows_scratch, *, spread):
    mixed, _, total = merge_rows([unpack_row(parts[at]) for at in range(parts.shape[0])])
    blended_half = (mixed / total).astype(BF16)
    part = blended_half.shape[0]
    start = pl.multiple_of((place[1] * PAIR + place[0]) * part, part)
    answer = answers[pl.ds(start, part), :].astype(F32)
    rows_scratch[...] = answer + jnp.dot(blended_half, mix_weight[...], preferred_element_type=F32)
    stride = keep.shape[1] // spread
    for column in range(spread):
        mine = pl.multiple_of((column * PAIR + place[0]) * stride, stride)
        other = pl.multiple_of((column * PAIR + 1 - place[0]) * stride, stride)
        keep[:, column * stride : (column + 1) * stride] = rows_scratch[:, pl.ds(mine, stride)].astype(BF16)
        send[:, column * stride : (column + 1) * stride] = rows_scratch[:, pl.ds(other, stride)].astype(BF16)


def condition(place, parts, mix_weight, answers, spread):
    model_width = mix_weight.shape[1]
    shape = jax.ShapeDtypeStruct((parts.shape[1], model_width // PAIR), BF16)
    whole = pl.BlockSpec(memory_space=pltpu.VMEM)
    return pl.pallas_call(
        functools.partial(condition_kernel, spread=spread),
        in_specs=[pl.BlockSpec(memory_space=pltpu.SMEM), whole, whole, whole],
        out_specs=[whole, whole],
        out_shape=[shape, shape],
        scratch_shapes=[pltpu.VMEM((parts.shape[1], model_width), F32)],
        compiler_params=grant(),
        name="condition",
    )(place, parts, mix_weight, answers.astype(F32))


def attend_kernel(place, table, pieces, key_own, key_pair, value_own, value_pair, out, *, offset, rows, inner, head_width):
    z = pl.program_id(0)
    relative = lax.bitwise_xor(z, place[3])
    spread = pieces.shape[0]
    quarters = []
    for column in range(spread):
        for core in range(PAIR):
            quarters.append(
                pieces[lax.bitwise_xor(place[1], column), relative, lax.bitwise_xor(place[0], core)]
            )
    query = jnp.concatenate(quarters, 0)
    width = query.shape[1]
    count = width // head_width
    lane = lax.broadcasted_iota(jnp.int32, query.shape, 1) // head_width
    spaced = jnp.concatenate([jnp.where(lane == head, query, jnp.zeros_like(query)) for head in range(count)], 0)
    entry = relative * inner + offset
    tokens = key_own.shape[1]
    shelves = []
    for shelf, (keys, values) in enumerate(((key_own, value_own), (key_pair, value_pair))):
        scores, slots = [], []
        for at in range(2):
            slot = table[entry * 6 + shelf * 3 + at]
            slots.append(slot)
            scores.append(lax.dot_general(keys[slot], spaced, NT, preferred_element_type=F32))
        high = jnp.maximum(jnp.max(scores[0], 0, keepdims=True), jnp.max(scores[1], 0, keepdims=True))
        total, mixed = 0.0, 0.0
        for slot, score in zip(slots, scores):
            exponent = jnp.exp(score - high)
            total = total + jnp.sum(exponent, 0, keepdims=True)
            start = pl.multiple_of(slot * tokens, tokens)
            mixed = mixed + jnp.dot(
                values[:, pl.ds(start, tokens)], exponent.astype(BF16), preferred_element_type=F32
            )
        there = table[entry * 6 + shelf * 3 + 2] > 0
        shelves.append((jnp.where(there, high, FLOOR), jnp.where(there, total, 0.0), mixed, there))
    high = jnp.maximum(shelves[0][0], shelves[1][0])
    total, mixed = 0.0, 0.0
    for shelf_high, shelf_total, shelf_mixed, there in shelves:
        factor = jnp.where(there, jnp.exp(shelf_high - high), 0.0)
        total = total + shelf_total * factor
        mixed = mixed + shelf_mixed * factor
    for head in range(count):
        out[0, head * head_width : (head + 1) * head_width, :] = mixed[
            head * head_width : (head + 1) * head_width, head * rows : (head + 1) * rows
        ].astype(BF16)
    out[0, width:, :] = pack_stats(high, total, count, rows)


def pack_stats(high, total, count, rows):
    places = lax.broadcasted_iota(jnp.int32, (STAT_ROWS, rows), 0)
    packed = jnp.zeros((STAT_ROWS, rows), F32)
    for head in range(count):
        here = slice(head * rows, (head + 1) * rows)
        for at, term in enumerate(thirds(high[:, here]) + thirds(total[:, here])):
            packed = jnp.where(places == head * 6 + at, term, packed)
    return packed.astype(BF16)


def attend(place, table, pieces, keys, values, offset, column, inner, head_width):
    spread, outer, pair, part, half = pieces.shape
    width = half // spread
    rows = spread * pair * part
    slots, tokens = keys[0].shape[:2]

    def at_column(*lead):
        return lambda z, place, table: lead + (lax.bitwise_xor(place[1], column),)

    key_spec = pl.BlockSpec((slots, tokens, width), at_column(0, 0))
    value_spec = pl.BlockSpec(
        (width, slots * tokens), lambda z, place, table: (lax.bitwise_xor(place[1], column), 0)
    )
    return pl.pallas_call(
        functools.partial(attend_kernel, offset=offset, rows=rows, inner=inner, head_width=head_width),
        grid_spec=pltpu.PrefetchScalarGridSpec(
            num_scalar_prefetch=2,
            grid=(outer,),
            in_specs=[
                pl.BlockSpec((spread, outer, pair, part, width), at_column(0, 0, 0, 0)),
                key_spec,
                key_spec,
                value_spec,
                value_spec,
            ],
            out_specs=pl.BlockSpec((1, width + STAT_ROWS, rows), lambda z, place, table: (z, 0, 0)),
        ),
        out_shape=jax.ShapeDtypeStruct((outer, width + STAT_ROWS, rows), BF16),
        compiler_params=grant(),
        cost_estimate=pl.CostEstimate(
            flops=outer * 4 * 4 * rows * tokens * width * (width // head_width),
            bytes_accessed=4 * slots * tokens * width * 2,
            transcendentals=outer * 4 * rows * tokens * (width // head_width),
        ),
        name="attend",
    )(place, table, pieces, *keys, *values)


def unpack_stats(packed, width, count):
    tail = packed[width:, :].astype(F32)
    highs, totals = [], []
    for head in range(count):
        base = head * 6
        highs.append(tail[base : base + 1] + tail[base + 1 : base + 2] + tail[base + 2 : base + 3])
        totals.append(tail[base + 3 : base + 4] + tail[base + 4 : base + 5] + tail[base + 5 : base + 6])
    return highs, totals


def merge_heads(parts, width, head_width):
    count = width // head_width
    stats = [unpack_stats(part, width, count) for part in parts]
    mixes, highs, totals = [], [], []
    for head in range(count):
        high = functools.reduce(jnp.maximum, [stat[0][head] for stat in stats])
        mixed, total = 0.0, 0.0
        for part, stat in zip(parts, stats):
            factor = jnp.where(stat[1][head] > 0, jnp.exp(stat[0][head] - high), 0.0)
            total = total + stat[1][head] * factor
            mixed = mixed + part[head * head_width : (head + 1) * head_width, :].astype(F32) * factor
        mixes.append(mixed)
        highs.append(high)
        totals.append(total)
    return mixes, highs, totals


def gather_kernel(place, *refs, inner, spread, head_width):
    *parts, out = refs
    width = out.shape[2] - STAT_ROWS
    rows = out.shape[3]
    count = width // head_width
    for offset in range(inner):
        taken = [parts[offset * spread + column][0] for column in range(spread)]
        mixes, highs, totals = merge_heads(taken, width, head_width)
        target = lax.bitwise_xor(place[2], offset)
        for head in range(count):
            out[0, target, head * head_width : (head + 1) * head_width, :] = mixes[head].astype(BF16)
        out[0, target, width:, :] = pack_stats(
            jnp.concatenate(highs, 1), jnp.concatenate(totals, 1), count, rows
        )


def merge_lots(place, parts, inner, spread, head_width):
    outer, height, rows = parts[0].shape
    spec = pl.BlockSpec((1, height, rows), lambda z, place: (z, 0, 0))
    return pl.pallas_call(
        functools.partial(gather_kernel, inner=inner, spread=spread, head_width=head_width),
        grid_spec=pltpu.PrefetchScalarGridSpec(
            num_scalar_prefetch=1,
            grid=(outer,),
            in_specs=[spec] * len(parts),
            out_specs=pl.BlockSpec((1, inner, height, rows), lambda z, place: (z, 0, 0, 0)),
        ),
        out_shape=jax.ShapeDtypeStruct((outer, inner, height, rows), BF16),
        compiler_params=grant(),
        name="merge_lots",
    )(place, *parts)


def finish_kernel(parts, out, *, head_width):
    width = parts.shape[1] - STAT_ROWS
    mixes, _, totals = merge_heads([parts[at] for at in range(parts.shape[0])], width, head_width)
    done = jnp.concatenate([mixed / total for mixed, total in zip(mixes, totals)], 0)
    out[...] = done.T.astype(BF16)


def finish(parts, head_width):
    whole = pl.BlockSpec(memory_space=pltpu.VMEM)
    return pl.pallas_call(
        functools.partial(finish_kernel, head_width=head_width),
        in_specs=[whole],
        out_specs=whole,
        out_shape=jax.ShapeDtypeStruct((parts.shape[2], parts.shape[1] - STAT_ROWS), BF16),
        compiler_params=grant(),
        name="finish",
    )(parts)


def local(
    queries,
    passages,
    noise,
    mix_weight,
    answer_queries,
    key_weight,
    value_weight,
    token_states,
    block_owner,
    listed,
):
    readers = lax.axis_size("pb")
    runners = lax.axis_size("pa")
    group = lax.axis_index("pb")
    runner = lax.axis_index("pa")
    spread = runners // PAIR
    inner = 1
    while (2 * inner) * (2 * inner) <= readers:
        inner *= 2
    outer = readers // inner
    model_width = key_weight.shape[0]
    head_width = model_width // HEADS
    slots, tokens = token_states.shape[:2]
    place = jnp.stack([runner % PAIR, runner // PAIR, group % inner, group // inner]).astype(jnp.int32)

    def swap(value, axis, bits):
        size = lax.axis_size(axis)
        return lax.ppermute(value, axis, [(at, at ^ bits) for at in range(size)])

    entries = listed
    step = 1
    while step < readers:
        entries = jnp.concatenate([entries, swap(entries, "pb", step)], 0)
        step *= 2
    slot_ids = jnp.take(block_owner, entries, axis=0)
    held = slot_ids // slots == runner * readers + group
    inside = slot_ids % slots
    chosen = jnp.stack(
        [
            jnp.min(jnp.where(held, inside, slots - 1), 1),
            jnp.max(jnp.where(held, inside, 0), 1),
            jnp.any(held, 1).astype(jnp.int32),
        ],
        1,
    )
    table = jnp.concatenate([chosen, swap(chosen, "pa", 1)], 1).reshape(-1)

    states = token_states.reshape(slots * tokens, model_width)
    pair_states = swap(states, "pa", 1)

    def core_columns(weight):
        split = weight.reshape(model_width, spread, PAIR, model_width // runners)
        return lax.dynamic_index_in_dim(split, runner % PAIR, 2, keepdims=False).reshape(model_width, -1)

    own_key, own_value = core_columns(key_weight), core_columns(value_weight)
    keys, values = [], []
    for rows in (states, pair_states):
        keys.append(
            jnp.dot(rows, own_key, preferred_element_type=F32).astype(BF16).reshape(slots, tokens, -1)
        )
        values.append(
            lax.dot_general(own_value, rows, (((0,), (1,)), ((), ())), preferred_element_type=F32).astype(BF16)
        )

    keep, send = retrieve(place, queries, passages, noise, readers, spread)
    by_column = merge_pair(place, keep, swap(send, "pa", 1), spread)
    parts = [by_column[0]] + [swap(by_column[at], "pa", at * PAIR) for at in range(1, spread)]
    by_group = merge_columns(parts)
    mine = lax.all_to_all(by_group, "pb", split_axis=0, concat_axis=0, tiled=True)
    kept, sent = condition(place, mine, mix_weight, answer_queries, spread)

    pieces = jnp.stack([kept, swap(sent, "pa", 1)])[None]
    step = inner
    while step < readers:
        pieces = jnp.concatenate([pieces, swap(pieces, "pb", step)], 0)
        step *= 2
    pieces = jnp.stack([pieces] + [swap(pieces, "pa", at * PAIR) for at in range(1, spread)])
    lots = []
    for offset in range(inner):
        query = pieces if offset == 0 else swap(pieces, "pb", offset)
        own = []
        for column in reversed(range(spread)):
            lot = attend(place, table, query, keys, values, offset, column, inner, head_width)
            own.append(lot if column == 0 else swap(lot, "pa", column * PAIR))
        lots += own[::-1]
    merged = merge_lots(place, lots, inner, spread, head_width)
    merged = merged.reshape((readers,) + merged.shape[2:])
    return finish(lax.all_to_all(merged, "pb", split_axis=0, concat_axis=0, tiled=True), head_width)


def solution(mesh):
    return jax.shard_map(
        local,
        mesh=mesh,
        in_specs=(
            P(),
            P(("pa", "pb"), None),
            P(None, ("pa", "pb")),
            P(),
            P("pb", None),
            P(),
            P(),
            P(("pa", "pb"), None, None),
            P(),
            P("pb", "pa"),
        ),
        out_specs=P("pb", "pa"),
        check_vma=False,
    )
```

time: 557 us -> 148 us (0.27)
  blocking collectives: 342 us -> 17.1 us
  local copies, waits for them, and re-layouts: 74.1 us -> 23 us
  matrix products: 72.1 us -> 21.1 us
  Pallas kernels: 0 us -> 41.6 us
  other arithmetic: 36 us -> 0.58 us
  starting transfers between devices: 5.13 us -> 24 us
  between operations: 13.6 us -> 0.27 us
  waiting for transfers between devices: 11.3 us -> 19.3 us
    pmax x1 -> x0, blocking collectives: 193 us -> none  [local(): highest = lax.pmax(jnp.max(scores, 1), ('pa', 'pb'))]
    psum x2 -> x0, blocking collectives: 117 us -> none  [the longest x1 77.5 us: local(): blended_all = lax.psum(partial_mix, ('pa', 'pb'))]
    dot_general x7 -> x4, matrix products: 72.1 us -> 21.1 us  [the longest x2 11.1 us: local(): lax.dot_general(own_value, rows, (((0,), (1,)), ((), ())), preferred_elem...]
    reshape x3 -> x1, local copies, waits for them, and re-layouts: 44.4 us -> 0.08 us  [local(): table = jnp.concatenate([chosen, swap(chosen, 'pa', 1)], 1).reshape(-1)]
    pallas_call x0 -> x10, Pallas kernels: none -> 41.6 us  [the longest x4 25 us: attend(): pl.pallas_call(functools.partial(attend_kernel, offset=offset, rows=rows,...]
    all_gather x3 -> x0, blocking collectives: 32.8 us -> none  [the longest x1 22.4 us: local(): requests = lax.all_gather(listed, 'pb', axis=0, tiled=True)]
    ppermute x0 -> x14, waiting for transfers between devices: none -> 19.3 us  [swap(): return lax.ppermute(value, axis, [(at, at ^ bits) for at in range(size)])]
    ppermute x0 -> x14, starting transfers between devices: none -> 19.2 us  [swap(): return lax.ppermute(value, axis, [(at, at ^ bits) for at in range(size)])]
  transfers between devices with their start and end apart: 2 -> 15, of which waited for: 1 -> 7; matrix products, arithmetic and copies ran while one was open for 3% -> 28% of each run, Pallas kernels for 0% -> 23%
where the time goes in v1:
time: 148 us; the launch traced here: 147 us
  Pallas kernels  41.6 us (28%)
  starting transfers between devices  24 us (16%)
  local copies, waits for them, and re-layouts  23 us (16%)
  matrix products  21.1 us (14%)
  waiting for transfers between devices  19.3 us (13%)
  blocking collectives  17.1 us (12%)
    pallas_call x4, Pallas kernels, attend(): pl.pallas_call(functools.partial(attend_kernel, offset=offset, rows=rows,...  25 us
    ppermute x14, waiting for transfers between devices, swap(): return lax.ppermute(value, axis, [(at, at ^ bits) for at in range(size)])  19.3 us
    ppermute x14, starting transfers between devices, swap(): return lax.ppermute(value, axis, [(at, at ^ bits) for at in range(size)])  19.2 us
    all_to_all x1, blocking collectives, local(): lax.all_to_all(merged, 'pb', split_axis=0, concat_axis=0, tiled=True)  17.1 us
    unnamed x26, local copies, waits for them, and re-layouts  11.7 us
    dot_general x2, matrix products, local(): lax.dot_general(own_value, rows, (((0,), (1,)), ((), ())), preferred_elem...  11.1 us
    dot_general x2, matrix products, local(): jnp.dot(rows, own_key, preferred_element_type=F32).astype(BF16)  9.98 us
    convert_element_type x2, local copies, waits for them, and re-layouts, local(): jnp.dot(rows, own_key, preferred_element_type=F32).astype(BF16)  6.79 us
  transfers between devices with their start and end apart: 15, of which 7 were waited for; matrix products, arithmetic and copies ran while one was open for 28% of the time, Pallas kernels for 23%

profile of v1, /device:TPU:0, one launch (start us, length us, event | category | flops | bytes accessed | tf_op | source)
XLA Modules:
  0.0 146.9 jit_solution(13593368411745146562)
XLA Ops:
  4.3 6.7 %retrieve.1 = (bf16[2,8,32,896]{3,2,1,0:T(8,128)(2,1)S(1)}, bf16[2,8,32,896]{3,2,1,0:T(8,128)(2,1)S(1)}) custom-call(s32[4]{0:T(128)S(1)} %pad_add_fusion.4.place, bf16[1024,768]{1,0:T(8,128)(2,1)S(1)} %copy-done.3, bf16[512,768]{1,0:T(8,128)(2,1)S(1)} %copy-done.6, bf16[1024,512]{1,0:T(8,128)(2,1)S(1)} %copy-done.5), custom_call_target="tpu_custom_call" | custom-call | tf_op jit(solution)/shard_map/retrieve/pallas_call | solution.py:83
  11.1 3.0 %collective-permute-start = (s32[1,16]{1,0:T(1,128)}, s32[1,16]{1,0:T(1,128)S(1)}, u32[]{:S(2)}, u32[]{:S(2)}) collective-permute-start(s32[1,16]{1,0:T(1,128)} %param.19), channel_id=1, source_target_pairs={{0,1},{1,0},{2,3},{3,2},{4,5},{5,4},{6,7},{7,6},{8,9},{9,8},{10,11... | collective-permute-start | bytes 200 | tf_op jit(solution)/shard_map/ppermute | solution.py:373
  14.1 3.9 %copy.24 = bf16[1024,1024]{0,1:T(8,128)(2,1)} copy(bf16[1024,1024]{1,0:T(8,128)(2,1)} %param.15) | data formatting | bytes 4194304 | tf_op args[5]
  18.0 3.9 %copy.27 = bf16[1024,1024]{0,1:T(8,128)(2,1)} copy(bf16[1024,1024]{1,0:T(8,128)(2,1)} %param.16) | data formatting | bytes 4194304 | tf_op args[6]
  22.0 2.9 %constant_dynamic-slice_fusion = (bf16[1024,2,1,256]{0,3,2,1:T(8,128)(2,1)}, bf16[1024,2,1,256]{0,3,2,1:T(8,128)(2,1)S(1)}) fusion(bf16[1024,2,2,256]{0,3,2,1:T(8,128)(2,1)} %bitcast.60, s32[]{:T(128)S(6)} %select_n.75, bf16[1024,2,2,256]{0,3,2,1:T(8,128)(2,1)} %bitcast.59), kind=kLoop, calls=%fused_computation.34 | loop fusion | bytes 4194308 | tf_op jit(solution)/shard_map/jit(dynamic_index_in_dim)/dynamic_slice | solution.py:398
  24.8 3.1 %merge_pair.1 = bf16[2,8,32,896]{3,2,1,0:T(8,128)(2,1)S(1)} custom-call(s32[4]{0:T(128)S(1)} %pad_add_fusion.4.place, bf16[2,8,32,896]{3,2,1,0:T(8,128)(2,1)S(1)} %get-tuple-element.9.keep, bf16[2,8,32,896]{3,2,1,0:T(8,128)(2,1)S(1)} %collective-permute-done.4.recv), custom_call_target="tpu_custom_call" | custom-call | tf_op jit(solution)/shard_map/merge_pair/pallas_call | solution.py:111
  28.0 1.6 %collective-permute-start.5 = (bf16[8,32,896]{2,1,0:T(8,128)(2,1)S(1)}, bf16[8,32,896]{2,1,0:T(8,128)(2,1)S(1)}, u32[]{:S(2)}, u32[]{:S(2)}) collective-permute-start(bf16[8,32,896]{2,1,0:T(8,128)(2,1)S(1)} %get-tuple-element.16), channel_id=1, source_target_pairs={{0,16},{8,24},{16,0},{24,8},{1,17},{9,25},{17,1},{25,9},{2,18},{10... | collective-permute-start | bytes 1376264 | tf_op jit(solution)/shard_map/ppermute | solution.py:373
  29.6 3.8 %fusion = bf16[2048,512]{0,1:T(8,128)(2,1)} fusion(bf16[1024,512]{0,1:T(8,128)(2,1)S(1)} %bitcast.63, bf16[2048,1024]{1,0:T(8,128)(2,1)S(1)} %bitcast.77), kind=kOutput, calls=%fused_computation.5 | convolution fusion | flops 2148532224 | bytes 7340032 | tf_op jit(solution)/shard_map/dot_general | solution.py:404
  33.4 6.9 %collective-permute-done.5.refs_1_ = bf16[8,32,896]{2,1,0:T(8,128)(2,1)S(1)} collective-permute-done((bf16[8,32,896]{2,1,0:T(8,128)(2,1)S(1)}, bf16[8,32,896]{2,1,0:T(8,128)(2,1)S(1)}, u32[]{:S(2)}, u32[]{:S(2)}) %collective-permute-start.5) | collective-permute-done | bytes 458784 | tf_op jit(solution)/shard_map/ppermute | solution.py:373
  40.3 3.7 %merge_columns.1 = bf16[8,32,896]{2,1,0:T(8,128)(2,1)} custom-call(bf16[8,32,896]{2,1,0:T(8,128)(2,1)S(1)} %get-tuple-element.17.refs_0_, bf16[8,32,896]{2,1,0:T(8,128)(2,1)S(1)} %collective-permute-done.5.refs_1_), custom_call_target="tpu_custom_call" | custom-call | tf_op jit(solution)/shard_map/merge_columns/pallas_call | solution.py:129
  44.0 4.9 %all-to-all-start = ((bf16[8,32,896]{2,1,0:T(8,128)(2,1)}), bf16[8,32,896]{2,1,0:T(8,128)(2,1)S(1)}, u32[]{:S(2)}, u32[]{:S(2)}) async-start(bf16[8,32,896]{2,1,0:T(8,128)(2,1)} %merge_columns.1), calls=%async_computation | async-start | bytes 917504 | tf_op jit(solution)/shard_map/all_to_all | solution.py:414
  48.9 6.1 %convolution_convert_fusion.1.value_own = bf16[512,2048]{1,0:T(8,128)(2,1)} fusion(bf16[1024,512]{0,1:T(8,128)(2,1)S(1)} %bitcast.62, bf16[2048,1024]{1,0:T(8,128)(2,1)} %bitcast.76), kind=kOutput, calls=%fused_computation.2 | convolution fusion | flops 2148532224 | bytes 7340032 | tf_op jit(solution)/shard_map/dot_general | solution.py:407
  55.1 2.1 %collective-permute-start.1 = (s32[2,16]{1,0:T(2,128)S(1)}, s32[2,16]{1,0:T(2,128)S(1)}, u32[]{:S(2)}, u32[]{:S(2)}) collective-permute-start(s32[2,16]{1,0:T(2,128)S(1)} %pad_add_fusion.3), channel_id=1, source_target_pairs={{0,2},{1,3},{2,0},{3,1},{4,6},{5,7},{6,4},{7,5},{8,10},{9,11},{10,... | collective-permute-start | bytes 392 | tf_op jit(solution)/shard_map/ppermute | solution.py:373
  57.2 1.6 %collective-permute-done.1 = s32[2,16]{1,0:T(2,128)S(1)} collective-permute-done((s32[2,16]{1,0:T(2,128)S(1)}, s32[2,16]{1,0:T(2,128)S(1)}, u32[]{:S(2)}, u32[]{:S(2)}) %collective-permute-start.1) | collective-permute-done | bytes 160 | tf_op jit(solution)/shard_map/ppermute | solution.py:373
  58.7 3.0 %collective-permute-start.2 = (s32[4,16]{1,0:T(4,128)S(1)}, s32[4,16]{1,0:T(4,128)S(1)}, u32[]{:S(2)}, u32[]{:S(2)}) collective-permute-start(s32[4,16]{1,0:T(4,128)S(1)} %pad_add_fusion.1), channel_id=1, source_target_pairs={{0,4},{1,5},{2,6},{3,7},{4,0},{5,1},{6,2},{7,3},{8,12},{9,13},{10,... | collective-permute-start | bytes 776 | tf_op jit(solution)/shard_map/ppermute | solution.py:373
  64.2 1.5 %collective-permute-start.7 = (bf16[1,2,32,512]{3,2,1,0:T(8,128)(2,1)S(1)}, bf16[1,2,32,512]{3,2,1,0:T(8,128)(2,1)S(1)}, u32[]{:S(2)}, u32[]{:S(2)}) collective-permute-start(bf16[1,2,32,512]{3,2,1,0:T(8,128)(2,1)S(1)} %maximum_bitcast_fusion), channel_id=1, source_target_pairs={{0,2},{1,3},{2,0},{3,1},{4,6},{5,7},{6,4},{7,5},{8,10},{9,11},{10,... | collective-permute-start | bytes 196616 | tf_op jit(solution)/shard_map/ppermute | solution.py:373
  67.1 1.4 collective-permute-done.7
  68.5 2.2 %collective-permute-start.8 = (bf16[2,2,32,512]{3,2,1,0:T(8,128)(2,1)S(1)}, bf16[2,2,32,512]{3,2,1,0:T(8,128)(2,1)S(1)}, u32[]{:S(2)}, u32[]{:S(2)}) collective-permute-start(bf16[2,2,32,512]{3,2,1,0:T(8,128)(2,1)S(1)} %pad_maximum_fusion.2), channel_id=1, source_target_pairs={{0,4},{1,5},{2,6},{3,7},{4,0},{5,1},{6,2},{7,3},{8,12},{9,13},{10,... | collective-permute-start | bytes 393224 | tf_op jit(solution)/shard_map/ppermute | solution.py:373
  71.0 5.6 %collective-permute-done.8 = bf16[2,2,32,512]{3,2,1,0:T(8,128)(2,1)S(1)} collective-permute-done((bf16[2,2,32,512]{3,2,1,0:T(8,128)(2,1)S(1)}, bf16[2,2,32,512]{3,2,1,0:T(8,128)(2,1)S(1)}, u32[]{:S(2)}, u32[]{:S(2)}) %collective-permute-start.8) | collective-permute-done | bytes 131104 | tf_op jit(solution)/shard_map/ppermute | solution.py:373
  76.7 1.6 %collective-permute-start.9 = (bf16[4,2,32,512]{3,2,1,0:T(8,128)(2,1)S(1)}, bf16[4,2,32,512]{3,2,1,0:T(8,128)(2,1)S(1)}, u32[]{:S(2)}, u32[]{:S(2)}) collective-permute-start(bf16[4,2,32,512]{3,2,1,0:T(8,128)(2,1)S(1)} %get-tuple-element.19), channel_id=1, source_target_pairs={{0,16},{8,24},{16,0},{24,8},{1,17},{9,25},{17,1},{25,9},{2,18},{10... | collective-permute-start | bytes 786440 | tf_op jit(solution)/shard_map/ppermute | solution.py:373
  78.3 2.9 %copy.25 = bf16[2048,512]{1,0:T(8,128)(2,1)S(1)} copy(bf16[2048,512]{0,1:T(8,128)(2,1)} %fusion) | data formatting | bytes 4194304 | tf_op jit(solution)/shard_map/convert_element_type | solution.py:404
  81.4 2.6 %collective-permute-done.9 = bf16[4,2,32,512]{3,2,1,0:T(8,128)(2,1)S(1)} collective-permute-done((bf16[4,2,32,512]{3,2,1,0:T(8,128)(2,1)S(1)}, bf16[4,2,32,512]{3,2,1,0:T(8,128)(2,1)S(1)}, u32[]{:S(2)}, u32[]{:S(2)}) %collective-permute-start.9) | collective-permute-done | bytes 262176 | tf_op jit(solution)/shard_map/ppermute | solution.py:373
  84.1 1.5 %collective-permute-start.12 = (bf16[2,4,2,32,512]{4,3,2,1,0:T(8,128)(2,1)S(1)}, bf16[2,4,2,32,512]{4,3,2,1,0:T(8,128)(2,1)S(1)}, u32[]{:S(2)}, u32[]{:S(2)}) collective-permute-start(bf16[2,4,2,32,512]{4,3,2,1,0:T(8,128)(2,1)S(1)} %pad_maximum_fusion.pieces), channel_id=1, source_target_pairs={{0,1},{1,0},{2,3},{3,2},{4,5},{5,4},{6,7},{7,6},{8,9},{9,8},{10,11... | collective-permute-start | bytes 1572872 | tf_op jit(solution)/shard_map/ppermute | solution.py:373
  85.6 6.2 %fusion.1 = bf16[2048,512]{0,1:T(8,128)(2,1)} fusion(bf16[1024,512]{0,1:T(8,128)(2,1)} %bitcast.64, bf16[2048,1024]{1,0:T(8,128)(2,1)} %collective-permute-done.10), kind=kOutput, calls=%fused_computation.6 | convolution fusion | flops 2148532224 | bytes 7340032 | tf_op jit(solution)/shard_map/dot_general | solution.py:404
  91.8 3.9 %copy.26 = bf16[2048,512]{1,0:T(8,128)(2,1)} copy(bf16[2048,512]{0,1:T(8,128)(2,1)} %fusion.1) | data formatting | bytes 4194304 | tf_op jit(solution)/shard_map/convert_element_type | solution.py:404
  95.7 5.0 %convolution_convert_fusion.value_pair = bf16[512,2048]{1,0:T(8,128)(2,1)S(1)} fusion(bf16[1024,512]{0,1:T(8,128)(2,1)} %bitcast.61, bf16[2048,1024]{1,0:T(8,128)(2,1)} %collective-permute-done.10), kind=kOutput, calls=%fused_computation.1 | convolution fusion | flops 2148532224 | bytes 7340032 | tf_op jit(solution)/shard_map/dot_general | solution.py:407
  100.7 6.2 %attend.5 = bf16[4,288,128]{2,1,0:T(8,128)(2,1)S(1)} custom-call(s32[4]{0:T(128)S(1)} %pad_add_fusion.4.place, s32[48]{0:T(128)S(1)} %reshape.211.table, bf16[2,4,2,32,512]{4,3,2,1,0:T(8,128)(2,1)S(1)} %pad_maximum_fusion.pieces, bf16[8,256,512]{2,1,0:T(8,128)(2,1)S(1)} %bitcast.49, bf16[8,256,512]{2,1,0:T(8,128)(2,1)S(1)} %bitcast.53, ...), custom_call_target="tpu_custom_call" | custom-call | flops 2147483648 | bytes 4194304 | tf_op jit(solution)/shard_map/attend/pallas_call | solution.py:241
  106.9 6.2 %attend.7 = bf16[4,288,128]{2,1,0:T(8,128)(2,1)S(1)} custom-call(s32[4]{0:T(128)S(1)} %pad_add_fusion.4.place, s32[48]{0:T(128)S(1)} %reshape.211.table, bf16[2,4,2,32,512]{4,3,2,1,0:T(8,128)(2,1)S(1)} %collective-permute-done.12.pieces, bf16[8,256,512]{2,1,0:T(8,128)(2,1)S(1)} %bitcast.50, bf16[8,256,512]{2,1,0:T(8,128)(2,1)S(1)} %bitcast.54, ...), custom_call_target="tpu_custom_call" | custom-call | flops 2147483648 | bytes 4194304 | tf_op jit(solution)/shard_map/attend/pallas_call | solution.py:241
  113.1 1.6 %collective-permute-start.13 = (bf16[4,288,128]{2,1,0:T(8,128)(2,1)S(1)}, bf16[4,288,128]{2,1,0:T(8,128)(2,1)S(1)}, u32[]{:S(2)}, u32[]{:S(2)}) collective-permute-start(bf16[4,288,128]{2,1,0:T(8,128)(2,1)S(1)} %attend.7), channel_id=1, source_target_pairs={{0,16},{8,24},{16,0},{24,8},{1,17},{9,25},{17,1},{25,9},{2,18},{10... | collective-permute-start | bytes 884744 | tf_op jit(solution)/shard_map/ppermute | solution.py:373
  115.2 6.4 %attend.4.refs_0_ = bf16[4,288,128]{2,1,0:T(8,128)(2,1)S(1)} custom-call(s32[4]{0:T(128)S(1)} %pad_add_fusion.4.place, s32[48]{0:T(128)S(1)} %reshape.211.table, bf16[2,4,2,32,512]{4,3,2,1,0:T(8,128)(2,1)S(1)} %pad_maximum_fusion.pieces, bf16[8,256,512]{2,1,0:T(8,128)(2,1)S(1)} %bitcast.51, bf16[8,256,512]{2,1,0:T(8,128)(2,1)S(1)} %bitcast.55, ...), custom_call_target="tpu_custom_call" | custom-call | flops 2147483648 | bytes 4194304 | tf_op jit(solution)/shard_map/attend/pallas_call | solution.py:241
  121.6 6.2 %attend.6.refs_2_ = bf16[4,288,128]{2,1,0:T(8,128)(2,1)S(1)} custom-call(s32[4]{0:T(128)S(1)} %pad_add_fusion.4.place, s32[48]{0:T(128)S(1)} %reshape.211.table, bf16[2,4,2,32,512]{4,3,2,1,0:T(8,128)(2,1)S(1)} %collective-permute-done.12.pieces, bf16[8,256,512]{2,1,0:T(8,128)(2,1)S(1)} %bitcast.52, bf16[8,256,512]{2,1,0:T(8,128)(2,1)S(1)} %bitcast.56, ...), custom_call_target="tpu_custom_call" | custom-call | flops 2147483648 | bytes 4194304 | tf_op jit(solution)/shard_map/attend/pallas_call | solution.py:241
  129.0 17.1 %all_to_all.10.parts = bf16[8,288,128]{2,1,0:T(8,128)(2,1)S(1)} all-to-all(bf16[8,288,128]{2,1,0:T(8,128)(2,1)S(1)} %bitcast.57), channel_id=1, replica_groups=mesh['pa'=4,'pb'=8] {'pb'}, dimensions={0} | all-to-all | bytes 1179648 | tf_op jit(solution)/shard_map/all_to_all | solution.py:433
  (63 shorter events, 11.5 us)
Async XLA Ops:
  0.0 65.7 %copy-start = (s32[256]{0:T(256)S(1)}, s32[256]{0:T(256)}, u32[]{:S(2)}) copy-start(s32[256]{0:T(256)} %param.18) | copy-start | bytes 3076
  0.0 85.6 %collective-permute-start.10 = (bf16[2048,1024]{1,0:T(8,128)(2,1)}, bf16[2048,1024]{1,0:T(8,128)(2,1)}, u32[]{:S(2)}, u32[]{:S(2)}) collective-permute-start(bf16[2048,1024]{1,0:T(8,128)(2,1)} %bitcast.75), channel_id=1, source_target_pairs={{0,8},{8,0},{16,24},{24,16},{1,9},{9,1},{17,25},{25,17},{2,10},{10... | collective-permute-start | bytes 12582920 | tf_op jit(solution)/shard_map/ppermute | solution.py:373
  0.5 1.4 copy-start.3
  1.9 1.2 copy-start.5
  3.2 1.1 copy-start.6
  11.0 13.8 %collective-permute-start.4 = (bf16[2,8,32,896]{3,2,1,0:T(8,128)(2,1)S(1)}, bf16[2,8,32,896]{3,2,1,0:T(8,128)(2,1)S(1)}, u32[]{:S(2)}, u32[]{:S(2)}) collective-permute-start(bf16[2,8,32,896]{3,2,1,0:T(8,128)(2,1)S(1)} %get-tuple-element.10), channel_id=1, source_target_pairs={{0,8},{8,0},{16,24},{24,16},{1,9},{9,1},{17,25},{25,17},{2,10},{10... | collective-permute-start | bytes 2752520 | tf_op jit(solution)/shard_map/ppermute | solution.py:373
  11.1 43.9 %collective-permute-start = (s32[1,16]{1,0:T(1,128)}, s32[1,16]{1,0:T(1,128)S(1)}, u32[]{:S(2)}, u32[]{:S(2)}) collective-permute-start(s32[1,16]{1,0:T(1,128)} %param.19), channel_id=1, source_target_pairs={{0,1},{1,0},{2,3},{3,2},{4,5},{5,4},{6,7},{7,6},{8,9},{9,8},{10,11... | collective-permute-start | bytes 200 | tf_op jit(solution)/shard_map/ppermute | solution.py:373
  22.0 7.6 %copy-start.11 = (bf16[8,256,1024]{2,1,0:T(8,128)(2,1)S(1)}, bf16[8,256,1024]{2,1,0:T(8,128)(2,1)}, u32[]{:S(2)}) copy-start(bf16[8,256,1024]{2,1,0:T(8,128)(2,1)} %param.17) | copy-start | bytes 12582916
  24.8 8.5 %copy-start.8 = (bf16[1024,2,1,256]{0,3,2,1:T(8,128)(2,1)}, bf16[1024,2,1,256]{0,3,2,1:T(8,128)(2,1)S(1)}, u32[]{:S(2)}) copy-start(bf16[1024,2,1,256]{0,3,2,1:T(8,128)(2,1)S(1)} %get-tuple-element.21) | copy-start | bytes 3145732
  28.0 12.3 %collective-permute-start.5 = (bf16[8,32,896]{2,1,0:T(8,128)(2,1)S(1)}, bf16[8,32,896]{2,1,0:T(8,128)(2,1)S(1)}, u32[]{:S(2)}, u32[]{:S(2)}) collective-permute-start(bf16[8,32,896]{2,1,0:T(8,128)(2,1)S(1)} %get-tuple-element.16), channel_id=1, source_target_pairs={{0,16},{8,24},{16,0},{24,8},{1,17},{9,25},{17,1},{25,9},{2,18},{10... | collective-permute-start | bytes 1376264 | tf_op jit(solution)/shard_map/ppermute | solution.py:373
  29.6 19.3 %copy-start.7 = (bf16[1024,2,1,256]{0,3,2,1:T(8,128)(2,1)S(1)}, bf16[1024,2,1,256]{0,3,2,1:T(8,128)(2,1)}, u32[]{:S(2)}) copy-start(bf16[1024,2,1,256]{0,3,2,1:T(8,128)(2,1)} %get-tuple-element.20) | copy-start | bytes 3145732
  44.0 17.7 %all-to-all-start = ((bf16[8,32,896]{2,1,0:T(8,128)(2,1)}), bf16[8,32,896]{2,1,0:T(8,128)(2,1)S(1)}, u32[]{:S(2)}, u32[]{:S(2)}) async-start(bf16[8,32,896]{2,1,0:T(8,128)(2,1)} %merge_columns.1), calls=%async_computation | async-start | bytes 917504 | tf_op jit(solution)/shard_map/all_to_all | solution.py:414
  48.9 6.1 %copy-start.9 = (bf16[128,1024]{1,0:T(8,128)(2,1)S(1)}, bf16[128,1024]{1,0:T(8,128)(2,1)}, u32[]{:S(2)}) copy-start(bf16[128,1024]{1,0:T(8,128)(2,1)} %param.14) | copy-start | bytes 786436
  48.9 6.2 %copy-start.10 = (s32[1,16]{1,0:T(1,128)S(1)}, s32[1,16]{1,0:T(1,128)}, u32[]{:S(2)}) copy-start(s32[1,16]{1,0:T(1,128)} %param.19) | copy-start | bytes 196
  48.9 12.8 %copy-start.4 = (bf16[768,1024]{1,0:T(8,128)(2,1)S(1)}, bf16[768,1024]{1,0:T(8,128)(2,1)}, u32[]{:S(2)}) copy-start(bf16[768,1024]{1,0:T(8,128)(2,1)} %mix_weight.1) | copy-start | bytes 4718596
  55.1 3.6 %collective-permute-start.1 = (s32[2,16]{1,0:T(2,128)S(1)}, s32[2,16]{1,0:T(2,128)S(1)}, u32[]{:S(2)}, u32[]{:S(2)}) collective-permute-start(s32[2,16]{1,0:T(2,128)S(1)} %pad_add_fusion.3), channel_id=1, source_target_pairs={{0,2},{1,3},{2,0},{3,1},{4,6},{5,7},{6,4},{7,5},{8,10},{9,11},{10,... | collective-permute-start | bytes 392 | tf_op jit(solution)/shard_map/ppermute | solution.py:373
  58.7 4.5 %collective-permute-start.2 = (s32[4,16]{1,0:T(4,128)S(1)}, s32[4,16]{1,0:T(4,128)S(1)}, u32[]{:S(2)}, u32[]{:S(2)}) collective-permute-start(s32[4,16]{1,0:T(4,128)S(1)} %pad_add_fusion.1), channel_id=1, source_target_pairs={{0,4},{1,5},{2,6},{3,7},{4,0},{5,1},{6,2},{7,3},{8,12},{9,13},{10,... | collective-permute-start | bytes 776 | tf_op jit(solution)/shard_map/ppermute | solution.py:373
  62.9 1.3 collective-permute-start.6
  64.2 4.3 %collective-permute-start.7 = (bf16[1,2,32,512]{3,2,1,0:T(8,128)(2,1)S(1)}, bf16[1,2,32,512]{3,2,1,0:T(8,128)(2,1)S(1)}, u32[]{:S(2)}, u32[]{:S(2)}) collective-permute-start(bf16[1,2,32,512]{3,2,1,0:T(8,128)(2,1)S(1)} %maximum_bitcast_fusion), channel_id=1, source_target_pairs={{0,2},{1,3},{2,0},{3,1},{4,6},{5,7},{6,4},{7,5},{8,10},{9,11},{10,... | collective-permute-start | bytes 196616 | tf_op jit(solution)/shard_map/ppermute | solution.py:373
  68.5 8.1 %collective-permute-start.8 = (bf16[2,2,32,512]{3,2,1,0:T(8,128)(2,1)S(1)}, bf16[2,2,32,512]{3,2,1,0:T(8,128)(2,1)S(1)}, u32[]{:S(2)}, u32[]{:S(2)}) collective-permute-start(bf16[2,2,32,512]{3,2,1,0:T(8,128)(2,1)S(1)} %pad_maximum_fusion.2), channel_id=1, source_target_pairs={{0,4},{1,5},{2,6},{3,7},{4,0},{5,1},{6,2},{7,3},{8,12},{9,13},{10,... | collective-permute-start | bytes 393224 | tf_op jit(solution)/shard_map/ppermute | solution.py:373
  76.7 7.3 %collective-permute-start.9 = (bf16[4,2,32,512]{3,2,1,0:T(8,128)(2,1)S(1)}, bf16[4,2,32,512]{3,2,1,0:T(8,128)(2,1)S(1)}, u32[]{:S(2)}, u32[]{:S(2)}) collective-permute-start(bf16[4,2,32,512]{3,2,1,0:T(8,128)(2,1)S(1)} %get-tuple-element.19), channel_id=1, source_target_pairs={{0,16},{8,24},{16,0},{24,8},{1,17},{9,25},{17,1},{25,9},{2,18},{10... | collective-permute-start | bytes 786440 | tf_op jit(solution)/shard_map/ppermute | solution.py:373
  78.3 3.0 %collective-permute-start.3 = (s32[8,3]{0,1:T(4,128)S(1)}, s32[8,3]{0,1:T(4,128)S(1)}, u32[]{:S(2)}, u32[]{:S(2)}) collective-permute-start(s32[8,3]{0,1:T(4,128)S(1)} %pad_add_fusion.2), channel_id=1, source_target_pairs={{0,8},{8,0},{16,24},{24,16},{1,9},{9,1},{17,25},{25,17},{2,10},{10... | collective-permute-start | bytes 296 | tf_op jit(solution)/shard_map/ppermute | solution.py:373
  84.1 22.9 %collective-permute-start.12 = (bf16[2,4,2,32,512]{4,3,2,1,0:T(8,128)(2,1)S(1)}, bf16[2,4,2,32,512]{4,3,2,1,0:T(8,128)(2,1)S(1)}, u32[]{:S(2)}, u32[]{:S(2)}) collective-permute-start(bf16[2,4,2,32,512]{4,3,2,1,0:T(8,128)(2,1)S(1)} %pad_maximum_fusion.pieces), channel_id=1, source_target_pairs={{0,1},{1,0},{2,3},{3,2},{4,5},{5,4},{6,7},{7,6},{8,9},{9,8},{10,11... | collective-permute-start | bytes 1572872 | tf_op jit(solution)/shard_map/ppermute | solution.py:373
  95.7 5.0 %copy-start.1 = (bf16[2048,512]{1,0:T(8,128)(2,1)S(1)}, bf16[2048,512]{1,0:T(8,128)(2,1)}, u32[]{:S(2)}) copy-start(bf16[2048,512]{1,0:T(8,128)(2,1)} %copy.26) | copy-start | bytes 6291460
  95.7 5.0 %copy-start.2 = (bf16[512,2048]{1,0:T(8,128)(2,1)S(1)}, bf16[512,2048]{1,0:T(8,128)(2,1)}, u32[]{:S(2)}) copy-start(bf16[512,2048]{1,0:T(8,128)(2,1)} %convolution_convert_fusion.1.value_own) | copy-start | bytes 6291460
  113.1 14.7 %collective-permute-start.13 = (bf16[4,288,128]{2,1,0:T(8,128)(2,1)S(1)}, bf16[4,288,128]{2,1,0:T(8,128)(2,1)S(1)}, u32[]{:S(2)}, u32[]{:S(2)}) collective-permute-start(bf16[4,288,128]{2,1,0:T(8,128)(2,1)S(1)} %attend.7), channel_id=1, source_target_pairs={{0,16},{8,24},{16,0},{24,8},{1,17},{9,25},{17,1},{25,9},{2,18},{10... | collective-permute-start | bytes 884744 | tf_op jit(solution)/shard_map/ppermute | solution.py:373
  114.7 13.1 %collective-permute-start.11 = (bf16[4,288,128]{2,1,0:T(8,128)(2,1)S(1)}, bf16[4,288,128]{2,1,0:T(8,128)(2,1)S(1)}, u32[]{:S(2)}, u32[]{:S(2)}) collective-permute-start(bf16[4,288,128]{2,1,0:T(8,128)(2,1)S(1)} %attend.5), channel_id=1, source_target_pairs={{0,16},{8,24},{16,0},{24,8},{1,17},{9,25},{17,1},{25,9},{2,18},{10... | collective-permute-start | bytes 884744 | tf_op jit(solution)/shard_map/ppermute | solution.py:373

commit v2 on v1

v2 whole, which is shorter than its diff:
```python
import functools

import jax
import jax.numpy as jnp
from jax import lax
from jax.experimental import pallas as pl
from jax.experimental.pallas import tpu as pltpu
from jax.sharding import PartitionSpec as P

HEADS = 16
PAIR = 2
TEMPER = 0.5
FLOOR = -1e30
LANES = 128
STAT_ROWS = 32
NOTE_AT = 6
STEP_GROUPS = 2
PROJECT_STEPS = 4
VMEM_BYTES = 40 * 1024 * 1024
WIDE_BYTES = 60 * 1024 * 1024
F32 = jnp.float32
BF16 = jnp.bfloat16
NT = (((1,), (1,)), ((), ()))


def grant():
    return pltpu.CompilerParams(vmem_limit_bytes=VMEM_BYTES)


def thirds(value):
    first = value.astype(BF16).astype(F32)
    rest = value - first
    second = rest.astype(BF16).astype(F32)
    return first, second, rest - second


def pack_tail(shift, total):
    lane = lax.broadcasted_iota(jnp.int32, (shift.shape[0], LANES), 1)
    tail = jnp.zeros((shift.shape[0], LANES), F32)
    for at, term in enumerate(thirds(shift) + thirds(total)):
        tail = jnp.where(lane == at, term, tail)
    return tail


def unpack_tail(tail):
    term = lax.broadcasted_iota(jnp.int32, (LANES, 2 * LANES), 0)
    half = lax.broadcasted_iota(jnp.int32, (LANES, 2 * LANES), 1) // LANES
    pick = jnp.where(term // 3 == half, 1.0, 0.0).astype(BF16)
    both = jnp.dot(tail, pick, preferred_element_type=F32)
    return both[:, :LANES], both[:, LANES:]


def merge_rows(parts):
    width = parts[0].shape[1] - LANES
    stats = [unpack_tail(part[:, width:]) for part in parts]
    shift = functools.reduce(jnp.maximum, [stat[0] for stat in stats])
    factors = [jnp.exp(stat[0] - shift) for stat in stats]
    total = sum(stat[1] * factor for stat, factor in zip(stats, factors))
    tiles = [
        sum(part[:, at : at + LANES].astype(F32) * factor for part, factor in zip(parts, factors))
        for at in range(0, width, LANES)
    ]
    return tiles, shift, total


def flat(value):
    return value.reshape((-1, value.shape[-1]))


def retrieval_kernel(place, queries, passages, noise, keep, send, rows_scratch, *, spread):
    core = place[0]
    groups, part = keep.shape[1:3]
    width = queries.shape[1]
    logits = lax.dot_general(queries[...], passages[...], NT, preferred_element_type=F32)
    gumbel = -jnp.log(-jnp.log(noise[...].astype(F32)))
    scores = (logits * width ** (-0.5) + gumbel) / TEMPER
    shift = jnp.max(scores, 1, keepdims=True)
    weight = jnp.exp(scores - shift)
    total = jnp.sum(weight, 1, keepdims=True)
    rows_scratch[:, :width] = jnp.dot(weight.astype(BF16), passages[...], preferred_element_type=F32)
    rows_scratch[:, width:] = pack_tail(shift, total)
    for at in range(groups):
        for column in range(spread):
            base = (at * spread + column) * PAIR
            mine = pl.multiple_of((base + core) * part, part)
            other = pl.multiple_of((base + 1 - core) * part, part)
            keep[column, at] = rows_scratch[pl.ds(mine, part), :].astype(BF16)
            send[column, at] = rows_scratch[pl.ds(other, part), :].astype(BF16)


def retrieve(place, queries, passages, noise, readers, spread):
    count, width = queries.shape
    group = count // readers
    part = group // (PAIR * spread)
    shape = jax.ShapeDtypeStruct((spread, readers, part, width + LANES), BF16)
    spec = pl.BlockSpec((spread, STEP_GROUPS, part, width + LANES), lambda g, place: (0, g, 0, 0))
    rows = group * STEP_GROUPS
    return pl.pallas_call(
        functools.partial(retrieval_kernel, spread=spread),
        grid_spec=pltpu.PrefetchScalarGridSpec(
            num_scalar_prefetch=1,
            grid=(readers // STEP_GROUPS,),
            in_specs=[
                pl.BlockSpec((rows, width), lambda g, place: (g, 0)),
                pl.BlockSpec(passages.shape, lambda g, place: (0, 0)),
                pl.BlockSpec((rows, noise.shape[1]), lambda g, place: (g, 0)),
            ],
            out_specs=[spec, spec],
            scratch_shapes=[pltpu.VMEM((rows, width + LANES), F32)],
        ),
        out_shape=[shape, shape],
        compiler_params=pltpu.CompilerParams(vmem_limit_bytes=WIDE_BYTES),
        cost_estimate=pl.CostEstimate(
            flops=4 * count * width * passages.shape[0],
            bytes_accessed=2 * (2 * count * width + passages.size + noise.size),
            transcendentals=3 * noise.size,
        ),
        name="retrieve",
    )(place, queries, passages, noise)


def store_rows(out, tiles, shift, total, note=None):
    for at, tile in enumerate(tiles):
        out[..., at * LANES : (at + 1) * LANES] = tile.astype(BF16).reshape(out.shape[:-1] + (LANES,))
    tail = pack_tail(shift, total)
    if note is not None:
        tail = tail + note
    out[..., len(tiles) * LANES :] = tail.astype(BF16).reshape(out.shape[:-1] + (LANES,))


def pair_kernel(place, keep, recv, *outs):
    for offset, out in enumerate(outs):
        column = lax.bitwise_xor(place[1], offset)
        store_rows(out, *merge_rows([flat(keep[column]), flat(recv[column])]))


def merge_pair(place, keep, recv, spread):
    readers = keep.shape[1]
    spec = pl.BlockSpec((spread, readers // 2) + keep.shape[2:], lambda g, place: (0, g, 0, 0))
    out = pl.BlockSpec((readers // 2,) + keep.shape[2:], lambda g, place: (g, 0, 0))
    return pl.pallas_call(
        pair_kernel,
        grid_spec=pltpu.PrefetchScalarGridSpec(
            num_scalar_prefetch=1, grid=(2,), in_specs=[spec, spec], out_specs=[out] * spread
        ),
        out_shape=[jax.ShapeDtypeStruct(keep.shape[1:], BF16)] * spread,
        compiler_params=grant(),
        name="merge_pair",
    )(place, keep, recv)


def column_kernel(note, *refs):
    *parts, out = refs
    store_rows(out, *merge_rows([flat(part[...]) for part in parts]), note[...])


def merge_columns(note, parts):
    readers = parts[0].shape[0]
    spec = pl.BlockSpec((readers // 2,) + parts[0].shape[1:], lambda g: (g, 0, 0))
    return pl.pallas_call(
        column_kernel,
        grid=(2,),
        in_specs=[pl.BlockSpec(note.shape, lambda g: (0, 0))] + [spec] * len(parts),
        out_specs=spec,
        out_shape=jax.ShapeDtypeStruct(parts[0].shape, BF16),
        compiler_params=grant(),
        name="merge_columns",
    )(note, *parts)


def condition_kernel(place, parts, mix_weight, answers, keep, send, rows_scratch, *, spread):
    tiles, _, total = merge_rows([parts[at] for at in range(parts.shape[0])])
    blended_half = jnp.concatenate([(tile / total).astype(BF16) for tile in tiles], 1)
    part = blended_half.shape[0]
    start = pl.multiple_of((place[1] * PAIR + place[0]) * part, part)
    answer = answers[pl.ds(start, part), :].astype(F32)
    rows_scratch[...] = answer + jnp.dot(blended_half, mix_weight[...], preferred_element_type=F32)
    stride = keep.shape[1] // spread
    for column in range(spread):
        mine = pl.multiple_of((column * PAIR + place[0]) * stride, stride)
        other = pl.multiple_of((column * PAIR + 1 - place[0]) * stride, stride)
        keep[:, column * stride : (column + 1) * stride] = rows_scratch[:, pl.ds(mine, stride)].astype(BF16)
        send[:, column * stride : (column + 1) * stride] = rows_scratch[:, pl.ds(other, stride)].astype(BF16)


def condition(place, parts, mix_weight, answers, spread):
    model_width = mix_weight.shape[1]
    shape = jax.ShapeDtypeStruct((parts.shape[1], model_width // PAIR), BF16)
    whole = pl.BlockSpec(memory_space=pltpu.VMEM)
    return pl.pallas_call(
        functools.partial(condition_kernel, spread=spread),
        in_specs=[pl.BlockSpec(memory_space=pltpu.SMEM), whole, whole, whole],
        out_specs=[whole, whole],
        out_shape=[shape, shape],
        scratch_shapes=[pltpu.VMEM((parts.shape[1], model_width), F32)],
        compiler_params=grant(),
        name="condition",
    )(place, parts, mix_weight, answers)


def project_kernel(place, states, *refs):
    spread = len(refs) // 2 - 1
    keys, values = refs[-2:]
    width = keys.shape[1] // spread
    for column in range(spread):
        key = jnp.dot(states[...], refs[column][...], preferred_element_type=F32)
        keys[:, column * width : (column + 1) * width] = key.astype(BF16)
        value = jnp.dot(states[...], refs[spread + column][...], preferred_element_type=F32)
        values[column * width : (column + 1) * width, :] = value.astype(BF16).T


def project(place, states, key_weight, value_weight, spread):
    rows, model_width = states.shape
    width = model_width // (PAIR * spread)
    chunk = rows // PROJECT_STEPS

    def weight_spec(column):
        return pl.BlockSpec((model_width, width), lambda t, place: (0, column * PAIR + place[0]))

    specs = [weight_spec(column) for column in range(spread)]
    return pl.pallas_call(
        project_kernel,
        grid_spec=pltpu.PrefetchScalarGridSpec(
            num_scalar_prefetch=1,
            grid=(PROJECT_STEPS,),
            in_specs=[pl.BlockSpec((chunk, model_width), lambda t, place: (t, 0))] + specs + specs,
            out_specs=[
                pl.BlockSpec((chunk, spread * width), lambda t, place: (t, 0)),
                pl.BlockSpec((spread * width, chunk), lambda t, place: (0, t)),
            ],
        ),
        out_shape=[
            jax.ShapeDtypeStruct((rows, spread * width), BF16),
            jax.ShapeDtypeStruct((spread * width, rows), BF16),
        ],
        compiler_params=grant(),
        cost_estimate=pl.CostEstimate(
            flops=4 * rows * model_width * spread * width,
            bytes_accessed=2 * (2 * model_width * spread * width + 2 * rows * model_width),
            transcendentals=0,
        ),
        name="project",
    )(place, states, *([key_weight] * spread), *([value_weight] * spread))


def attend_kernel(
    place, table, pieces, key_own, key_pair, value_own, value_pair, out, *, offset, column, inner, tokens, head_width
):
    z = pl.program_id(0)
    relative = lax.bitwise_xor(z, place[3])
    spread, rows = pieces.shape[0], out.shape[2]
    width = out.shape[1] - STAT_ROWS
    count = width // head_width
    left = pl.multiple_of(lax.bitwise_xor(place[1], column) * width, width)
    quarters = []
    for lane in range(spread):
        for core in range(PAIR):
            lead = (lax.bitwise_xor(place[1], lane), relative, lax.bitwise_xor(place[0], core))
            quarters.append(pieces[lead + (slice(None), pl.ds(left, width))])
    query = jnp.concatenate(quarters, 0).T
    head_at = lax.broadcasted_iota(jnp.int32, query.shape, 0) // head_width
    spaced = jnp.concatenate([jnp.where(head_at == head, query, jnp.zeros_like(query)) for head in range(count)], 1)
    entry = z * inner + lax.bitwise_xor(place[2], offset)
    shelves = []
    for shelf, (keys, values) in enumerate(((key_own, value_own), (key_pair, value_pair))):
        scores, starts = [], []
        for at in range(2):
            start = pl.multiple_of(table[entry * 6 + shelf * 3 + at] * tokens, tokens)
            starts.append(start)
            key = keys[pl.ds(start, tokens), pl.ds(left, width)]
            scores.append(jnp.dot(key, spaced, preferred_element_type=F32))
        high = jnp.maximum(jnp.max(scores[0], 0, keepdims=True), jnp.max(scores[1], 0, keepdims=True))
        total, mixed = 0.0, 0.0
        for start, score in zip(starts, scores):
            exponent = jnp.exp(score - high)
            total = total + jnp.sum(exponent, 0, keepdims=True)
            value = values[pl.ds(left, width), pl.ds(start, tokens)]
            mixed = mixed + jnp.dot(value, exponent.astype(BF16), preferred_element_type=F32)
        there = table[entry * 6 + shelf * 3 + 2] > 0
        blocks = [
            mixed[head * head_width : (head + 1) * head_width, head * rows : (head + 1) * rows]
            for head in range(count)
        ]
        shelves.append((jnp.where(there, high, FLOOR), jnp.where(there, total, 0.0), blocks, there))
    high = jnp.maximum(shelves[0][0], shelves[1][0])
    factors = [jnp.where(there, jnp.exp(shelf_high - high), 0.0) for shelf_high, _, _, there in shelves]
    total = shelves[0][1] * factors[0] + shelves[1][1] * factors[1]
    for head in range(count):
        here = slice(head * rows, (head + 1) * rows)
        joined = shelves[0][2][head] * factors[0][:, here] + shelves[1][2][head] * factors[1][:, here]
        out[0, head * head_width : (head + 1) * head_width, :] = joined.astype(BF16)
    out[0, width:, :] = pack_stats(high, total, count, rows)


def pack_stats(high, total, count, rows):
    places = lax.broadcasted_iota(jnp.int32, (STAT_ROWS, rows), 0)
    packed = jnp.zeros((STAT_ROWS, rows), F32)
    for head in range(count):
        here = slice(head * rows, (head + 1) * rows)
        for at, term in enumerate(thirds(high[:, here]) + thirds(total[:, here])):
            packed = jnp.where(places == head * 6 + at, term, packed)
    return packed.astype(BF16)


def attend(place, table, pieces, keys, values, offset, column, inner, tokens, head_width):
    spread, outer, pair, part, half = pieces.shape
    width = half // spread
    rows = spread * pair * part
    whole = pl.BlockSpec(memory_space=pltpu.VMEM)
    return pl.pallas_call(
        functools.partial(
            attend_kernel, offset=offset, column=column, inner=inner, tokens=tokens, head_width=head_width
        ),
        grid_spec=pltpu.PrefetchScalarGridSpec(
            num_scalar_prefetch=2,
            grid=(outer,),
            in_specs=[whole] * 5,
            out_specs=pl.BlockSpec((1, width + STAT_ROWS, rows), lambda z, place, table: (z, 0, 0)),
        ),
        out_shape=jax.ShapeDtypeStruct((outer, width + STAT_ROWS, rows), BF16),
        compiler_params=grant(),
        cost_estimate=pl.CostEstimate(
            flops=outer * 4 * 4 * rows * tokens * width * (width // head_width),
            bytes_accessed=outer * 2 * (width + STAT_ROWS) * rows,
            transcendentals=outer * 4 * rows * tokens * (width // head_width),
        ),
        name="attend",
    )(place, table, pieces, *keys, *values)


def unpack_stats(packed, width, count):
    tail = packed[width:, :].astype(F32)
    highs, totals = [], []
    for head in range(count):
        base = head * 6
        highs.append(tail[base : base + 1] + tail[base + 1 : base + 2] + tail[base + 2 : base + 3])
        totals.append(tail[base + 3 : base + 4] + tail[base + 4 : base + 5] + tail[base + 5 : base + 6])
    return highs, totals


def merge_heads(parts, width, head_width):
    count = width // head_width
    stats = [unpack_stats(part, width, count) for part in parts]
    mixes, highs, totals = [], [], []
    for head in range(count):
        high = functools.reduce(jnp.maximum, [stat[0][head] for stat in stats])
        mixed, total = 0.0, 0.0
        for part, stat in zip(parts, stats):
            factor = jnp.where(stat[1][head] > 0, jnp.exp(stat[0][head] - high), 0.0)
            total = total + stat[1][head] * factor
            mixed = mixed + part[head * head_width : (head + 1) * head_width, :].astype(F32) * factor
        mixes.append(mixed)
        highs.append(high)
        totals.append(total)
    return mixes, highs, totals


def gather_kernel(place, *refs, inner, spread, head_width):
    *parts, out = refs
    width = out.shape[2] - STAT_ROWS
    rows = out.shape[3]
    count = width // head_width
    for offset in range(inner):
        taken = [parts[offset * spread + column][0] for column in range(spread)]
        mixes, highs, totals = merge_heads(taken, width, head_width)
        target = lax.bitwise_xor(place[2], offset)
        for head in range(count):
            out[0, target, head * head_width : (head + 1) * head_width, :] = mixes[head].astype(BF16)
        out[0, target, width:, :] = pack_stats(
            jnp.concatenate(highs, 1), jnp.concatenate(totals, 1), count, rows
        )


def merge_lots(place, parts, inner, spread, head_width):
    outer, height, rows = parts[0].shape
    spec = pl.BlockSpec((1, height, rows), lambda z, place: (z, 0, 0))
    return pl.pallas_call(
        functools.partial(gather_kernel, inner=inner, spread=spread, head_width=head_width),
        grid_spec=pltpu.PrefetchScalarGridSpec(
            num_scalar_prefetch=1,
            grid=(outer,),
            in_specs=[spec] * len(parts),
            out_specs=pl.BlockSpec((1, inner, height, rows), lambda z, place: (z, 0, 0, 0)),
        ),
        out_shape=jax.ShapeDtypeStruct((outer, inner, height, rows), BF16),
        compiler_params=grant(),
        name="merge_lots",
    )(place, *parts)


def finish_kernel(parts, out, *, head_width):
    width = parts.shape[1] - STAT_ROWS
    mixes, _, totals = merge_heads([parts[at] for at in range(parts.shape[0])], width, head_width)
    done = jnp.concatenate([mixed / total for mixed, total in zip(mixes, totals)], 0)
    out[...] = done.T.astype(BF16)


def finish(parts, head_width):
    whole = pl.BlockSpec(memory_space=pltpu.VMEM)
    return pl.pallas_call(
        functools.partial(finish_kernel, head_width=head_width),
        in_specs=[whole],
        out_specs=whole,
        out_shape=jax.ShapeDtypeStruct((parts.shape[2], parts.shape[1] - STAT_ROWS), BF16),
        compiler_params=grant(),
        name="finish",
    )(parts)


def local(
    queries,
    passages,
    noise,
    mix_weight,
    answer_queries,
    key_weight,
    value_weight,
    token_states,
    block_owner,
    listed,
):
    readers = lax.axis_size("pb")
    runners = lax.axis_size("pa")
    group = lax.axis_index("pb")
    runner = lax.axis_index("pa")
    spread = runners // PAIR
    inner = 1
    while (2 * inner) * (2 * inner) <= readers:
        inner *= 2
    outer = readers // inner
    model_width = key_weight.shape[0]
    head_width = model_width // HEADS
    slots, tokens = token_states.shape[:2]
    place = jnp.stack([runner % PAIR, runner // PAIR, group % inner, group // inner]).astype(jnp.int32)

    def swap(value, axis, bits):
        size = lax.axis_size(axis)
        return lax.ppermute(value, axis, [(at, at ^ bits) for at in range(size)])

    states = token_states.reshape(slots * tokens, model_width)
    pair_states = swap(states, "pa", 1)

    keep, send = retrieve(place, queries, passages, noise, readers, spread)
    wanted = jnp.take(block_owner, listed[0], axis=0)
    digits = jnp.concatenate([wanted // LANES, wanted % LANES]).astype(F32)
    note = jnp.pad(digits[None], ((0, 0), (NOTE_AT, LANES - NOTE_AT - digits.shape[0])))
    by_column = merge_pair(place, keep, swap(send, "pa", 1), spread)
    own_key, own_value = project(place, states, key_weight, value_weight, spread)
    parts = [by_column[0]] + [swap(by_column[at], "pa", at * PAIR) for at in range(1, spread)]
    by_group = merge_columns(note, parts)
    mine = lax.all_to_all(by_group, "pb", split_axis=0, concat_axis=0, tiled=True)
    pair_key, pair_value = project(place, pair_states, key_weight, value_weight, spread)
    keys, values = (own_key, pair_key), (own_value, pair_value)
    kept, sent = condition(place, mine, mix_weight, answer_queries, spread)

    digits = mine[:, 0, queries.shape[1] + NOTE_AT :][:, : digits.shape[0]].astype(jnp.int32)
    slot_ids = digits[:, : wanted.shape[0]] * LANES + digits[:, wanted.shape[0] :]
    held = slot_ids // slots == runner * readers + group
    inside = slot_ids % slots
    chosen = jnp.stack(
        [
            jnp.min(jnp.where(held, inside, slots - 1), 1),
            jnp.max(jnp.where(held, inside, 0), 1),
            jnp.any(held, 1).astype(jnp.int32),
        ],
        1,
    )
    table = jnp.concatenate([chosen, swap(chosen, "pa", 1)], 1).reshape(-1)

    pieces = jnp.stack([kept, swap(sent, "pa", 1)])[None]
    step = inner
    while step < readers:
        pieces = jnp.concatenate([pieces, swap(pieces, "pb", step)], 0)
        step *= 2
    pieces = jnp.stack([pieces] + [swap(pieces, "pa", at * PAIR) for at in range(1, spread)])
    lots = []
    for offset in range(inner):
        query = pieces if offset == 0 else swap(pieces, "pb", offset)
        own = []
        for column in reversed(range(spread)):
            lot = attend(place, table, query, keys, values, offset, column, inner, tokens, head_width)
            own.append(lot if column == 0 else swap(lot, "pa", column * PAIR))
        lots += own[::-1]
    merged = merge_lots(place, lots, inner, spread, head_width)
    merged = merged.reshape((readers,) + merged.shape[2:])
    return finish(lax.all_to_all(merged, "pb", split_axis=0, concat_axis=0, tiled=True), head_width)


def solution(mesh):
    return jax.shard_map(
        local,
        mesh=mesh,
        in_specs=(
            P(),
            P(("pa", "pb"), None),
            P(None, ("pa", "pb")),
            P(),
            P("pb", None),
            P(),
            P(),
            P(("pa", "pb"), None, None),
            P(),
            P("pb", "pa"),
        ),
        out_specs=P("pb", "pa"),
        check_vma=False,
    )
```

time: 148 us -> 137 us (0.926)
  matrix products: 21.1 us -> 0 us
  waiting for transfers between devices: 19.3 us -> 37.3 us
  local copies, waits for them, and re-layouts: 23 us -> 12.1 us
  Pallas kernels: 41.6 us -> 51.6 us
  starting transfers between devices: 24 us -> 16.2 us
    dot_general x4 -> x0, matrix products: 21.1 us -> none  [the longest x2 11.1 us: local(): lax.dot_general(own_value, rows, (((0,), (1,)), ((), ())), preferred_elem...]
    all_to_all x1, waiting for transfers between devices: 0.01 us -> 12.8 us  [local(): lax.all_to_all(by_group, 'pb', split_axis=0, concat_axis=0, tiled=True)]
    pallas_call x6 -> x8, Pallas kernels: 31.7 us -> 41 us  [the longest x4 24.5 us: attend(): pl.pallas_call(functools.partial(attend_kernel, offset=offset, column=col...]
    ppermute x14 -> x11, starting transfers between devices: 19.2 us -> 10.1 us  [swap(): return lax.ppermute(value, axis, [(at, at ^ bits) for at in range(size)])]
    convert_element_type x2 -> x0, local copies, waits for them, and re-layouts: 6.79 us -> none  [local(): jnp.dot(rows, own_key, preferred_element_type=F32).astype(BF16)]
    ppermute x14 -> x11, waiting for transfers between devices: 19.3 us -> 24.5 us  [swap(): return lax.ppermute(value, axis, [(at, at ^ bits) for at in range(size)])]
    dynamic_slice x1 -> x0, local copies, waits for them, and re-layouts: 2.87 us -> none  [core_columns(): lax.dynamic_index_in_dim(split, runner % PAIR, 2, keepdims=False)]
    unnamed x26 -> x27, local copies, waits for them, and re-layouts: 11.7 us -> 11.1 us
  transfers between devices with their start and end apart: 15 -> 12, of which waited for: 7 -> 7; matrix products, arithmetic and copies ran while one was open for 28% -> 2% of each run, Pallas kernels for 23% -> 32%
where the time goes in v2:
time: 137 us; the launch traced here: 136 us
  Pallas kernels  51.6 us (38%)
  waiting for transfers between devices  37.3 us (27%)
  blocking collectives  17.9 us (13%)
  starting transfers between devices  16.2 us (12%)
  local copies, waits for them, and re-layouts  12.1 us (9%)
    pallas_call x4, Pallas kernels, attend(): pl.pallas_call(functools.partial(attend_kernel, offset=offset, column=col...  24.5 us
    ppermute x11, waiting for transfers between devices, swap(): return lax.ppermute(value, axis, [(at, at ^ bits) for at in range(size)])  24.5 us
    all_to_all x1, blocking collectives, local(): lax.all_to_all(merged, 'pb', split_axis=0, concat_axis=0, tiled=True)  17.9 us
    pallas_call x2, Pallas kernels, project(): pl.pallas_call(project_kernel, grid_spec=pltpu.PrefetchScalarGridSpec(num...  13.6 us
    all_to_all x1, waiting for transfers between devices, local(): lax.all_to_all(by_group, 'pb', split_axis=0, concat_axis=0, tiled=True)  12.8 us
    unnamed x27, local copies, waits for them, and re-layouts  11.1 us
    ppermute x11, starting transfers between devices, swap(): return lax.ppermute(value, axis, [(at, at ^ bits) for at in range(size)])  10.1 us
    pallas_call x1, Pallas kernels, retrieve(): pl.pallas_call(functools.partial(retrieval_kernel, spread=spread), grid_s...  7.42 us
  transfers between devices with their start and end apart: 12, of which 7 were waited for; matrix products, arithmetic and copies ran while one was open for 2% of the time, Pallas kernels for 32%

profile of v2, /device:TPU:0, one launch (start us, length us, event | category | flops | bytes accessed | tf_op | source)
XLA Modules:
  0.0 136.5 jit_solution(12293737214057177073)
XLA Ops:
  1.1 7.4 %retrieve.1 = (bf16[2,8,32,896]{3,2,1,0:T(8,128)(2,1)}, bf16[2,8,32,896]{3,2,1,0:T(8,128)(2,1)}) custom-call(s32[4]{0:T(128)} %pad_add_fusion.2.place, bf16[1024,768]{1,0:T(8,128)(2,1)} %queries.1, bf16[512,768]{1,0:T(8,128)(2,1)} %passages.1, bf16[1024,512]{1,0:T(8,128)(2,1)} %noise.1), custom_call_target="tpu_custom_call" | custom-call | flops 1610612736 | bytes 4980736 | tf_op jit(solution)/shard_map/retrieve/pallas_call | solution.py:98
  9.3 1.9 %collective-permute-done.recv = bf16[2,8,32,896]{3,2,1,0:T(8,128)(2,1)S(1)} collective-permute-done((bf16[2,8,32,896]{3,2,1,0:T(8,128)(2,1)}, bf16[2,8,32,896]{3,2,1,0:T(8,128)(2,1)S(1)}, u32[]{:S(2)}, u32[]{:S(2)}) %collective-permute-start) | collective-permute-done | bytes 917536 | tf_op jit(solution)/shard_map/ppermute | solution.py:438
  11.2 1.2 copy-done.4
  12.4 1.6 %merge_pair.1 = (bf16[8,32,896]{2,1,0:T(8,128)(2,1)S(1)}, bf16[8,32,896]{2,1,0:T(8,128)(2,1)S(1)}) custom-call(s32[4]{0:T(128)S(1)} %copy-done.6, bf16[2,8,32,896]{3,2,1,0:T(8,128)(2,1)S(1)} %copy-done.4, bf16[2,8,32,896]{3,2,1,0:T(8,128)(2,1)S(1)} %collective-permute-done.recv), custom_call_target="tpu_custom_call" | custom-call | tf_op jit(solution)/shard_map/merge_pair/pallas_call | solution.py:141
  14.0 2.7 %collective-permute-start.1 = (bf16[8,32,896]{2,1,0:T(8,128)(2,1)S(1)}, bf16[8,32,896]{2,1,0:T(8,128)(2,1)S(1)}, u32[]{:S(2)}, u32[]{:S(2)}) collective-permute-start(bf16[8,32,896]{2,1,0:T(8,128)(2,1)S(1)} %get-tuple-element.18), channel_id=1, source_target_pairs={{0,16},{8,24},{16,0},{24,8},{1,17},{9,25},{17,1},{25,9},{2,18},{10... | collective-permute-start | bytes 1376264 | tf_op jit(solution)/shard_map/ppermute | solution.py:438
  16.9 10.9 %collective-permute-done.1.refs_1_ = bf16[8,32,896]{2,1,0:T(8,128)(2,1)S(1)} collective-permute-done((bf16[8,32,896]{2,1,0:T(8,128)(2,1)S(1)}, bf16[8,32,896]{2,1,0:T(8,128)(2,1)S(1)}, u32[]{:S(2)}, u32[]{:S(2)}) %collective-permute-start.1) | collective-permute-done | bytes 458784 | tf_op jit(solution)/shard_map/ppermute | solution.py:438
  27.7 1.3 merge_columns.1
  29.0 6.1 %all-to-all-start = ((bf16[8,32,896]{2,1,0:T(8,128)(2,1)}), bf16[8,32,896]{2,1,0:T(8,128)(2,1)S(1)}, u32[]{:S(2)}, u32[]{:S(2)}) async-start(bf16[8,32,896]{2,1,0:T(8,128)(2,1)} %merge_columns.1), calls=%async_computation | async-start | bytes 917504 | tf_op jit(solution)/shard_map/all_to_all | solution.py:451
  35.1 12.8 %all-to-all-done.parts = bf16[8,32,896]{2,1,0:T(8,128)(2,1)S(1)} async-done(((bf16[8,32,896]{2,1,0:T(8,128)(2,1)}), bf16[8,32,896]{2,1,0:T(8,128)(2,1)S(1)}, u32[]{:S(2)}, u32[]{:S(2)}) %all-to-all-start) | async-done | bytes 458784 | tf_op jit(solution)/shard_map/all_to_all | solution.py:451
  48.0 1.2 condition.1
  49.3 1.1 collective-permute-done.3
  50.4 0.9 collective-permute-start.4
  51.6 3.1 %collective-permute-done.4 = bf16[1,2,32,512]{3,2,1,0:T(8,128)(2,1)S(1)} collective-permute-done((bf16[1,2,32,512]{3,2,1,0:T(8,128)(2,1)S(1)}, bf16[1,2,32,512]{3,2,1,0:T(8,128)(2,1)S(1)}, u32[]{:S(2)}, u32[]{:S(2)}) %collective-permute-start.4) | collective-permute-done | bytes 65568 | tf_op jit(solution)/shard_map/ppermute | solution.py:438
  55.6 7.3 %collective-permute-done.5 = bf16[2,2,32,512]{3,2,1,0:T(8,128)(2,1)S(1)} collective-permute-done((bf16[2,2,32,512]{3,2,1,0:T(8,128)(2,1)S(1)}, bf16[2,2,32,512]{3,2,1,0:T(8,128)(2,1)S(1)}, u32[]{:S(2)}, u32[]{:S(2)}) %collective-permute-start.5) | collective-permute-done | bytes 131104 | tf_op jit(solution)/shard_map/ppermute | solution.py:438
  63.0 1.6 %collective-permute-start.6 = (bf16[4,2,32,512]{3,2,1,0:T(8,128)(2,1)S(1)}, bf16[4,2,32,512]{3,2,1,0:T(8,128)(2,1)S(1)}, u32[]{:S(2)}, u32[]{:S(2)}) collective-permute-start(bf16[4,2,32,512]{3,2,1,0:T(8,128)(2,1)S(1)} %get-tuple-element.31), channel_id=1, source_target_pairs={{0,16},{8,24},{16,0},{24,8},{1,17},{9,25},{17,1},{25,9},{2,18},{10... | collective-permute-start | bytes 786440 | tf_op jit(solution)/shard_map/ppermute | solution.py:438
  64.5 2.2 %copy-done.7 = bf16[8,256,1024]{2,1,0:T(8,128)(2,1)S(1)} copy-done((bf16[8,256,1024]{2,1,0:T(8,128)(2,1)S(1)}, bf16[8,256,1024]{2,1,0:T(8,128)(2,1)}, u32[]{:S(2)}) %copy-start.7) | copy-done | bytes 4194328
  66.7 1.6 %copy-done.8 = bf16[1024,1024]{1,0:T(8,128)(2,1)S(1)} copy-done((bf16[1024,1024]{1,0:T(8,128)(2,1)S(1)}, bf16[1024,1024]{1,0:T(8,128)(2,1)}, u32[]{:S(2)}) %copy-start.8) | copy-done | bytes 2097176
  68.3 1.6 %copy-done.10 = bf16[1024,1024]{1,0:T(8,128)(2,1)S(1)} copy-done((bf16[1024,1024]{1,0:T(8,128)(2,1)S(1)}, bf16[1024,1024]{1,0:T(8,128)(2,1)}, u32[]{:S(2)}) %copy-start.10) | copy-done | bytes 2097176
  69.9 6.3 %project.2 = (bf16[2048,512]{1,0:T(8,128)(2,1)S(1)}, bf16[512,2048]{1,0:T(8,128)(2,1)S(1)}) custom-call(s32[4]{0:T(128)S(1)} %copy-done.6, bf16[2048,1024]{1,0:T(8,128)(2,1)S(1)} %bitcast.30, bf16[1024,1024]{1,0:T(8,128)(2,1)S(1)} %copy-done.8, bf16[1024,1024]{1,0:T(8,128)(2,1)S(1)} %copy-done.8, bf16[1024,1024]{1,0:T(8,128)(2,1)S(1)} %copy-done.10, ...), custom_call_target="tpu_custom_call" | custom-call | flops 4294967296 | bytes 10485760 | tf_op jit(solution)/shard_map/project/pallas_call | solution.py:221
  76.2 1.3 copy-done.1
  77.8 1.5 %collective-permute-start.9 = (bf16[2,4,2,32,512]{4,3,2,1,0:T(8,128)(2,1)S(1)}, bf16[2,4,2,32,512]{4,3,2,1,0:T(8,128)(2,1)S(1)}, u32[]{:S(2)}, u32[]{:S(2)}) collective-permute-start(bf16[2,4,2,32,512]{4,3,2,1,0:T(8,128)(2,1)S(1)} %pad_maximum_fusion.pieces), channel_id=1, source_target_pairs={{0,1},{1,0},{2,3},{3,2},{4,5},{5,4},{6,7},{7,6},{8,9},{9,8},{10,11... | collective-permute-start | bytes 1572872 | tf_op jit(solution)/shard_map/ppermute | solution.py:438
  79.3 1.6 %copy-done.9 = bf16[1024,1024]{1,0:T(8,128)(2,1)S(1)} copy-done((bf16[1024,1024]{1,0:T(8,128)(2,1)S(1)}, bf16[1024,1024]{1,0:T(8,128)(2,1)}, u32[]{:S(2)}) %copy-start.9) | copy-done | bytes 2097176
  80.9 1.6 %copy-done.11 = bf16[1024,1024]{1,0:T(8,128)(2,1)S(1)} copy-done((bf16[1024,1024]{1,0:T(8,128)(2,1)S(1)}, bf16[1024,1024]{1,0:T(8,128)(2,1)}, u32[]{:S(2)}) %copy-start.11) | copy-done | bytes 2097176
  82.5 7.3 %project.3 = (bf16[2048,512]{1,0:T(8,128)(2,1)S(1)}, bf16[512,2048]{1,0:T(8,128)(2,1)S(1)}) custom-call(s32[4]{0:T(128)S(1)} %copy-done.6, bf16[2048,1024]{1,0:T(8,128)(2,1)} %collective-permute-done.7.states, bf16[1024,1024]{1,0:T(8,128)(2,1)S(1)} %copy-done.9, bf16[1024,1024]{1,0:T(8,128)(2,1)S(1)} %copy-done.9, bf16[1024,1024]{1,0:T(8,128)(2,1)S(1)} %copy-done.11, ...), custom_call_target="tpu_custom_call" | custom-call | flops 4294967296 | bytes 10485760 | tf_op jit(solution)/shard_map/project/pallas_call | solution.py:221
  89.8 6.1 %attend.5 = bf16[4,288,128]{2,1,0:T(8,128)(2,1)S(1)} custom-call(s32[4]{0:T(128)S(1)} %copy-done.6, s32[48]{0:T(128)S(1)} %reshape.77.table, bf16[2,4,2,32,512]{4,3,2,1,0:T(8,128)(2,1)S(1)} %pad_maximum_fusion.pieces, bf16[2048,512]{1,0:T(8,128)(2,1)S(1)} %get-tuple-element.21.key_own, bf16[2048,512]{1,0:T(8,128)(2,1)S(1)} %get-tuple-element.22.key_pair, ...), custom_call_target="tpu_custom_call" | custom-call | flops 2147483648 | bytes 294912 | tf_op jit(solution)/shard_map/attend/pallas_call | solution.py:310
  95.9 6.1 %attend.7 = bf16[4,288,128]{2,1,0:T(8,128)(2,1)S(1)} custom-call(s32[4]{0:T(128)S(1)} %copy-done.6, s32[48]{0:T(128)S(1)} %reshape.77.table, bf16[2,4,2,32,512]{4,3,2,1,0:T(8,128)(2,1)S(1)} %collective-permute-done.9.pieces, bf16[2048,512]{1,0:T(8,128)(2,1)S(1)} %get-tuple-element.21.key_own, bf16[2048,512]{1,0:T(8,128)(2,1)S(1)} %get-tuple-element.22.key_pair, ...), custom_call_target="tpu_custom_call" | custom-call | flops 2147483648 | bytes 294912 | tf_op jit(solution)/shard_map/attend/pallas_call | solution.py:310
  102.7 1.5 %collective-permute-start.8 = (bf16[4,288,128]{2,1,0:T(8,128)(2,1)S(1)}, bf16[4,288,128]{2,1,0:T(8,128)(2,1)S(1)}, u32[]{:S(2)}, u32[]{:S(2)}) collective-permute-start(bf16[4,288,128]{2,1,0:T(8,128)(2,1)S(1)} %attend.5), channel_id=1, source_target_pairs={{0,16},{8,24},{16,0},{24,8},{1,17},{9,25},{17,1},{25,9},{2,18},{10... | collective-permute-start | bytes 884744 | tf_op jit(solution)/shard_map/ppermute | solution.py:438
  104.2 6.1 %attend.4.refs_0_ = bf16[4,288,128]{2,1,0:T(8,128)(2,1)S(1)} custom-call(s32[4]{0:T(128)S(1)} %copy-done.6, s32[48]{0:T(128)S(1)} %reshape.77.table, bf16[2,4,2,32,512]{4,3,2,1,0:T(8,128)(2,1)S(1)} %pad_maximum_fusion.pieces, bf16[2048,512]{1,0:T(8,128)(2,1)S(1)} %get-tuple-element.21.key_own, bf16[2048,512]{1,0:T(8,128)(2,1)S(1)} %get-tuple-element.22.key_pair, ...), custom_call_target="tpu_custom_call" | custom-call | flops 2147483648 | bytes 294912 | tf_op jit(solution)/shard_map/attend/pallas_call | solution.py:310
  110.3 6.1 %attend.6.refs_2_ = bf16[4,288,128]{2,1,0:T(8,128)(2,1)S(1)} custom-call(s32[4]{0:T(128)S(1)} %copy-done.6, s32[48]{0:T(128)S(1)} %reshape.77.table, bf16[2,4,2,32,512]{4,3,2,1,0:T(8,128)(2,1)S(1)} %collective-permute-done.9.pieces, bf16[2048,512]{1,0:T(8,128)(2,1)S(1)} %get-tuple-element.21.key_own, bf16[2048,512]{1,0:T(8,128)(2,1)S(1)} %get-tuple-element.22.key_pair, ...), custom_call_target="tpu_custom_call" | custom-call | flops 2147483648 | bytes 294912 | tf_op jit(solution)/shard_map/attend/pallas_call | solution.py:310
  116.6 1.1 merge_lots.1
  117.7 17.9 %all_to_all.10.parts = bf16[8,288,128]{2,1,0:T(8,128)(2,1)S(1)} all-to-all(bf16[8,288,128]{2,1,0:T(8,128)(2,1)S(1)} %bitcast.27), channel_id=1, replica_groups=mesh['pa'=4,'pb'=8] {'pb'}, dimensions={0} | all-to-all | bytes 1179648 | tf_op jit(solution)/shard_map/all_to_all | solution.py:486
  135.6 0.9 finish.1
  (53 shorter events, 4.4 us)
Async XLA Ops:
  0.0 8.6 %copy-start = (s32[256]{0:T(256)S(1)}, s32[256]{0:T(256)}, u32[]{:S(2)}) copy-start(s32[256]{0:T(256)} %param.18) | copy-start | bytes 3076
  0.0 79.3 %collective-permute-start.7 = (bf16[2048,1024]{1,0:T(8,128)(2,1)}, bf16[2048,1024]{1,0:T(8,128)(2,1)}, u32[]{:S(2)}, u32[]{:S(2)}) collective-permute-start(bf16[2048,1024]{1,0:T(8,128)(2,1)} %bitcast.29), channel_id=1, source_target_pairs={{0,8},{8,0},{16,24},{24,16},{1,9},{9,1},{17,25},{25,17},{2,10},{10... | collective-permute-start | bytes 12582920 | tf_op jit(solution)/shard_map/ppermute | solution.py:438
  1.1 7.5 %copy-start.12 = (s32[1,16]{1,0:T(1,128)S(1)}, s32[1,16]{1,0:T(1,128)}, u32[]{:S(2)}) copy-start(s32[1,16]{1,0:T(1,128)} %param.19) | copy-start | bytes 196
  1.1 10.1 %copy-start.6 = (s32[4]{0:T(128)S(1)}, s32[4]{0:T(128)}, u32[]{:S(2)}) copy-start(s32[4]{0:T(128)} %pad_add_fusion.2.place) | copy-start | bytes 52
  8.5 2.7 %collective-permute-start = (bf16[2,8,32,896]{3,2,1,0:T(8,128)(2,1)}, bf16[2,8,32,896]{3,2,1,0:T(8,128)(2,1)S(1)}, u32[]{:S(2)}, u32[]{:S(2)}) collective-permute-start(bf16[2,8,32,896]{3,2,1,0:T(8,128)(2,1)} %get-tuple-element.16), channel_id=1, source_target_pairs={{0,8},{8,0},{16,24},{24,16},{1,9},{9,1},{17,25},{25,17},{2,10},{10... | collective-permute-start | bytes 2752520 | tf_op jit(solution)/shard_map/ppermute | solution.py:438
  8.6 39.4 %copy-start.5 = (bf16[128,1024]{1,0:T(8,128)(2,1)S(1)}, bf16[128,1024]{1,0:T(8,128)(2,1)}, u32[]{:S(2)}) copy-start(bf16[128,1024]{1,0:T(8,128)(2,1)} %answers.1) | copy-start | bytes 786436
  9.3 38.7 %copy-start.3 = (bf16[768,1024]{1,0:T(8,128)(2,1)S(1)}, bf16[768,1024]{1,0:T(8,128)(2,1)}, u32[]{:S(2)}) copy-start(bf16[768,1024]{1,0:T(8,128)(2,1)} %mix_weight.1) | copy-start | bytes 4718596
  11.2 1.2 copy-start.4
  14.0 13.7 %collective-permute-start.1 = (bf16[8,32,896]{2,1,0:T(8,128)(2,1)S(1)}, bf16[8,32,896]{2,1,0:T(8,128)(2,1)S(1)}, u32[]{:S(2)}, u32[]{:S(2)}) collective-permute-start(bf16[8,32,896]{2,1,0:T(8,128)(2,1)S(1)} %get-tuple-element.18), channel_id=1, source_target_pairs={{0,16},{8,24},{16,0},{24,8},{1,17},{9,25},{17,1},{25,9},{2,18},{10... | collective-permute-start | bytes 1376264 | tf_op jit(solution)/shard_map/ppermute | solution.py:438
  29.0 18.9 %all-to-all-start = ((bf16[8,32,896]{2,1,0:T(8,128)(2,1)}), bf16[8,32,896]{2,1,0:T(8,128)(2,1)S(1)}, u32[]{:S(2)}, u32[]{:S(2)}) async-start(bf16[8,32,896]{2,1,0:T(8,128)(2,1)} %merge_columns.1), calls=%async_computation | async-start | bytes 917504 | tf_op jit(solution)/shard_map/all_to_all | solution.py:451
  49.1 1.3 collective-permute-start.3
  50.4 4.3 %collective-permute-start.4 = (bf16[1,2,32,512]{3,2,1,0:T(8,128)(2,1)S(1)}, bf16[1,2,32,512]{3,2,1,0:T(8,128)(2,1)S(1)}, u32[]{:S(2)}, u32[]{:S(2)}) collective-permute-start(bf16[1,2,32,512]{3,2,1,0:T(8,128)(2,1)S(1)} %maximum_bitcast_fusion), channel_id=1, source_target_pairs={{0,2},{1,3},{2,0},{3,1},{4,6},{5,7},{6,4},{7,5},{8,10},{9,11},{10,... | collective-permute-start | bytes 196616 | tf_op jit(solution)/shard_map/ppermute | solution.py:438
  54.8 8.1 %collective-permute-start.5 = (bf16[2,2,32,512]{3,2,1,0:T(8,128)(2,1)S(1)}, bf16[2,2,32,512]{3,2,1,0:T(8,128)(2,1)S(1)}, u32[]{:S(2)}, u32[]{:S(2)}) collective-permute-start(bf16[2,2,32,512]{3,2,1,0:T(8,128)(2,1)S(1)} %pad_maximum_fusion.2), channel_id=1, source_target_pairs={{0,4},{1,5},{2,6},{3,7},{4,0},{5,1},{6,2},{7,3},{8,12},{9,13},{10,... | collective-permute-start | bytes 393224 | tf_op jit(solution)/shard_map/ppermute | solution.py:438
  55.6 22.0 %collective-permute-start.2 = (s32[8,3]{0,1:T(4,128)S(1)}, s32[8,3]{0,1:T(4,128)S(1)}, u32[]{:S(2)}, u32[]{:S(2)}) collective-permute-start(s32[8,3]{0,1:T(4,128)S(1)} %pad_add_fusion.1), channel_id=1, source_target_pairs={{0,8},{8,0},{16,24},{24,16},{1,9},{9,1},{17,25},{25,17},{2,10},{10... | collective-permute-start | bytes 296 | tf_op jit(solution)/shard_map/ppermute | solution.py:438
  63.0 14.8 %collective-permute-start.6 = (bf16[4,2,32,512]{3,2,1,0:T(8,128)(2,1)S(1)}, bf16[4,2,32,512]{3,2,1,0:T(8,128)(2,1)S(1)}, u32[]{:S(2)}, u32[]{:S(2)}) collective-permute-start(bf16[4,2,32,512]{3,2,1,0:T(8,128)(2,1)S(1)} %get-tuple-element.31), channel_id=1, source_target_pairs={{0,16},{8,24},{16,0},{24,8},{1,17},{9,25},{17,1},{25,9},{2,18},{10... | collective-permute-start | bytes 786440 | tf_op jit(solution)/shard_map/ppermute | solution.py:438
  64.5 2.2 %copy-start.7 = (bf16[8,256,1024]{2,1,0:T(8,128)(2,1)S(1)}, bf16[8,256,1024]{2,1,0:T(8,128)(2,1)}, u32[]{:S(2)}) copy-start(bf16[8,256,1024]{2,1,0:T(8,128)(2,1)} %param.17) | copy-start | bytes 12582916
  66.7 1.6 %copy-start.8 = (bf16[1024,1024]{1,0:T(8,128)(2,1)S(1)}, bf16[1024,1024]{1,0:T(8,128)(2,1)}, u32[]{:S(2)}) copy-start(bf16[1024,1024]{1,0:T(8,128)(2,1)} %refs_1_.3) | copy-start | bytes 6291460
  68.3 1.6 %copy-start.10 = (bf16[1024,1024]{1,0:T(8,128)(2,1)S(1)}, bf16[1024,1024]{1,0:T(8,128)(2,1)}, u32[]{:S(2)}) copy-start(bf16[1024,1024]{1,0:T(8,128)(2,1)} %refs_3_.3) | copy-start | bytes 6291460
  76.2 1.3 copy-start.1
  77.8 12.0 %copy-start.2 = (bf16[512,2048]{1,0:T(8,128)(2,1)S(1)}, bf16[512,2048]{1,0:T(8,128)(2,1)}, u32[]{:S(2)}) copy-start(bf16[512,2048]{1,0:T(8,128)(2,1)} %copy-done.1) | copy-start | bytes 6291460
  77.8 18.1 %collective-permute-start.9 = (bf16[2,4,2,32,512]{4,3,2,1,0:T(8,128)(2,1)S(1)}, bf16[2,4,2,32,512]{4,3,2,1,0:T(8,128)(2,1)S(1)}, u32[]{:S(2)}, u32[]{:S(2)}) collective-permute-start(bf16[2,4,2,32,512]{4,3,2,1,0:T(8,128)(2,1)S(1)} %pad_maximum_fusion.pieces), channel_id=1, source_target_pairs={{0,1},{1,0},{2,3},{3,2},{4,5},{5,4},{6,7},{7,6},{8,9},{9,8},{10,11... | collective-permute-start | bytes 1572872 | tf_op jit(solution)/shard_map/ppermute | solution.py:438
  79.3 1.6 %copy-start.9 = (bf16[1024,1024]{1,0:T(8,128)(2,1)S(1)}, bf16[1024,1024]{1,0:T(8,128)(2,1)}, u32[]{:S(2)}) copy-start(bf16[1024,1024]{1,0:T(8,128)(2,1)} %refs_1_.3) | copy-start | bytes 6291460
  80.9 1.6 %copy-start.11 = (bf16[1024,1024]{1,0:T(8,128)(2,1)S(1)}, bf16[1024,1024]{1,0:T(8,128)(2,1)}, u32[]{:S(2)}) copy-start(bf16[1024,1024]{1,0:T(8,128)(2,1)} %refs_3_.3) | copy-start | bytes 6291460
  102.1 14.4 %collective-permute-start.10 = (bf16[4,288,128]{2,1,0:T(8,128)(2,1)S(1)}, bf16[4,288,128]{2,1,0:T(8,128)(2,1)S(1)}, u32[]{:S(2)}, u32[]{:S(2)}) collective-permute-start(bf16[4,288,128]{2,1,0:T(8,128)(2,1)S(1)} %attend.7), channel_id=1, source_target_pairs={{0,16},{8,24},{16,0},{24,8},{1,17},{9,25},{17,1},{25,9},{2,18},{10... | collective-permute-start | bytes 884744 | tf_op jit(solution)/shard_map/ppermute | solution.py:438
  102.7 13.9 %collective-permute-start.8 = (bf16[4,288,128]{2,1,0:T(8,128)(2,1)S(1)}, bf16[4,288,128]{2,1,0:T(8,128)(2,1)S(1)}, u32[]{:S(2)}, u32[]{:S(2)}) collective-permute-start(bf16[4,288,128]{2,1,0:T(8,128)(2,1)S(1)} %attend.5), channel_id=1, source_target_pairs={{0,16},{8,24},{16,0},{24,8},{1,17},{9,25},{17,1},{25,9},{2,18},{10... | collective-permute-start | bytes 884744 | tf_op jit(solution)/shard_map/ppermute | solution.py:438

commit v3 on v2

--- a/solution.py
+++ b/solution.py
@@ -15,7 +15,9 @@
 STAT_ROWS = 32
 NOTE_AT = 6
 STEP_GROUPS = 2
-PROJECT_STEPS = 4
+PROJECT_STEPS = 2
+ATTEND_GROUPS = 4
+HEAD_BUNDLE = 2
 VMEM_BYTES = 40 * 1024 * 1024
 WIDE_BYTES = 60 * 1024 * 1024
 F32 = jnp.float32
@@ -243,10 +245,7 @@
     )(place, states, *([key_weight] * spread), *([value_weight] * spread))
 
 
-def attend_kernel(
-    place, table, pieces, key_own, key_pair, value_own, value_pair, out, *, offset, column, inner, tokens, head_width
-):
-    z = pl.program_id(0)
+def attend_group(z, place, table, pieces, keys, values, out, row, offset, column, inner, tokens, head_width):
     relative = lax.bitwise_xor(z, place[3])
     spread, rows = pieces.shape[0], out.shape[2]
     width = out.shape[1] - STAT_ROWS
@@ -261,35 +260,48 @@
     head_at = lax.broadcasted_iota(jnp.int32, query.shape, 0) // head_width
     spaced = jnp.concatenate([jnp.where(head_at == head, query, jnp.zeros_like(query)) for head in range(count)], 1)
     entry = z * inner + lax.bitwise_xor(place[2], offset)
+    bundle = min(HEAD_BUNDLE, count)
     shelves = []
-    for shelf, (keys, values) in enumerate(((key_own, value_own), (key_pair, value_pair))):
-        scores, starts = [], []
-        for at in range(2):
-            start = pl.multiple_of(table[entry * 6 + shelf * 3 + at] * tokens, tokens)
-            starts.append(start)
-            key = keys[pl.ds(start, tokens), pl.ds(left, width)]
-            scores.append(jnp.dot(key, spaced, preferred_element_type=F32))
-        high = jnp.maximum(jnp.max(scores[0], 0, keepdims=True), jnp.max(scores[1], 0, keepdims=True))
-        total, mixed = 0.0, 0.0
-        for start, score in zip(starts, scores):
-            exponent = jnp.exp(score - high)
-            total = total + jnp.sum(exponent, 0, keepdims=True)
-            value = values[pl.ds(left, width), pl.ds(start, tokens)]
-            mixed = mixed + jnp.dot(value, exponent.astype(BF16), preferred_element_type=F32)
+    for shelf in range(PAIR):
+        starts = [
+            pl.multiple_of(table[entry * 6 + shelf * 3 + at] * tokens, tokens) for at in range(2)
+        ]
+        scores = [
+            jnp.dot(keys[shelf][pl.ds(start, tokens), pl.ds(left, width)], spaced, preferred_element_type=F32)
+            for start in starts
+        ]
+        high = functools.reduce(jnp.maximum, [jnp.max(score, 0, keepdims=True) for score in scores])
+        exponents = [jnp.exp(score - high) for score in scores]
+        total = sum(jnp.sum(exponent, 0, keepdims=True) for exponent in exponents)
+        probs = jnp.concatenate([exponent.astype(BF16) for exponent in exponents], 0)
         there = table[entry * 6 + shelf * 3 + 2] > 0
-        blocks = [
-            mixed[head * head_width : (head + 1) * head_width, head * rows : (head + 1) * rows]
-            for head in range(count)
-        ]
+        blocks = []
+        for first in range(0, count, bundle):
+            top = pl.multiple_of(left + first * head_width, bundle * head_width)
+            value = jnp.concatenate(
+                [values[shelf][pl.ds(top, bundle * head_width), pl.ds(start, tokens)] for start in starts], 1
+            )
+            mixed = jnp.dot(value, probs[:, first * rows : (first + bundle) * rows], preferred_element_type=F32)
+            for head in range(bundle):
+                blocks.append(
+                    mixed[head * head_width : (head + 1) * head_width, head * rows : (head + 1) * rows]
+                )
         shelves.append((jnp.where(there, high, FLOOR), jnp.where(there, total, 0.0), blocks, there))
-    high = jnp.maximum(shelves[0][0], shelves[1][0])
+    high = functools.reduce(jnp.maximum, [shelf[0] for shelf in shelves])
     factors = [jnp.where(there, jnp.exp(shelf_high - high), 0.0) for shelf_high, _, _, there in shelves]
-    total = shelves[0][1] * factors[0] + shelves[1][1] * factors[1]
+    total = sum(shelf[1] * factor for shelf, factor in zip(shelves, factors))
     for head in range(count):
         here = slice(head * rows, (head + 1) * rows)
-        joined = shelves[0][2][head] * factors[0][:, here] + shelves[1][2][head] * factors[1][:, here]
-        out[0, head * head_width : (head + 1) * head_width, :] = joined.astype(BF16)
-    out[0, width:, :] = pack_stats(high, total, count, rows)
+        joined = sum(shelf[2][head] * factor[:, here] for shelf, factor in zip(shelves, factors))
+        out[row, head * head_width : (head + 1) * head_width, :] = joined.astype(BF16)
+    out[row, width:, :] = pack_stats(high, total, count, rows)
+
+
+def attend_kernel(place, table, pieces, key_own, key_pair, value_own, value_pair, out, **fixed):
+    step = out.shape[0]
+    for row in range(step):
+        z = pl.program_id(0) * step + row
+        attend_group(z, place, table, pieces, (key_own, key_pair), (value_own, value_pair), out, row, **fixed)
 
 
 def pack_stats(high, total, count, rows):
@@ -306,6 +318,7 @@
     spread, outer, pair, part, half = pieces.shape
     width = half // spread
     rows = spread * pair * part
+    at_once = min(ATTEND_GROUPS, outer)
     whole = pl.BlockSpec(memory_space=pltpu.VMEM)
     return pl.pallas_call(
         functools.partial(
@@ -313,9 +326,9 @@
         ),
         grid_spec=pltpu.PrefetchScalarGridSpec(
             num_scalar_prefetch=2,
-            grid=(outer,),
+            grid=(outer // at_once,),
             in_specs=[whole] * 5,
-            out_specs=pl.BlockSpec((1, width + STAT_ROWS, rows), lambda z, place, table: (z, 0, 0)),
+            out_specs=pl.BlockSpec((at_once, width + STAT_ROWS, rows), lambda z, place, table: (z, 0, 0)),
         ),
         out_shape=jax.ShapeDtypeStruct((outer, width + STAT_ROWS, rows), BF16),
         compiler_params=grant(),
@@ -445,11 +458,15 @@
     digits = jnp.concatenate([wanted // LANES, wanted % LANES]).astype(F32)
     note = jnp.pad(digits[None], ((0, 0), (NOTE_AT, LANES - NOTE_AT - digits.shape[0])))
     by_column = merge_pair(place, keep, swap(send, "pa", 1), spread)
+    *by_column, states = lax.optimization_barrier((*by_column, states))
+    parts = [by_column[0]] + [swap(by_column[at], "pa", at * PAIR) for at in range(1, spread)]
     own_key, own_value = project(place, states, key_weight, value_weight, spread)
-    parts = [by_column[0]] + [swap(by_column[at], "pa", at * PAIR) for at in range(1, spread)]
+    *parts, own_key, own_value = lax.optimization_barrier((*parts, own_key, own_value))
     by_group = merge_columns(note, parts)
+    by_group, pair_states = lax.optimization_barrier((by_group, pair_states))
     mine = lax.all_to_all(by_group, "pb", split_axis=0, concat_axis=0, tiled=True)
     pair_key, pair_value = project(place, pair_states, key_weight, value_weight, spread)
+    mine, pair_key, pair_value = lax.optimization_barrier((mine, pair_key, pair_value))
     keys, values = (own_key, pair_key), (own_value, pair_value)
     kept, sent = condition(place, mine, mix_weight, answer_queries, spread)
 

time: 137 us -> 128 us (0.934)
  waiting for transfers between devices: 37.3 us -> 17.7 us
  local copies, waits for them, and re-layouts: 12.1 us -> 20.9 us
  Pallas kernels: 51.6 us -> 46.4 us
  blocking collectives: 17.9 us -> 21.1 us
  starting transfers between devices: 16.2 us -> 19.3 us
    all_to_all x1, waiting for transfers between devices: 12.8 us -> 0.19 us  [local(): lax.all_to_all(by_group, 'pb', split_axis=0, concat_axis=0, tiled=True)]
    unnamed x27 -> x35, local copies, waits for them, and re-layouts: 11.1 us -> 19.9 us
    ppermute x11, waiting for transfers between devices: 24.5 us -> 17.5 us  [swap(): return lax.ppermute(value, axis, [(at, at ^ bits) for at in range(size)])]
    pallas_call x4, Pallas kernels: 24.5 us -> 19.9 us  [attend(): pl.pallas_call(functools.partial(attend_kernel, offset=offset, column=col...]
    ppermute x11, starting transfers between devices: 10.1 us -> 13.5 us  [swap(): return lax.ppermute(value, axis, [(at, at ^ bits) for at in range(size)])]
    all_to_all x1, blocking collectives: 17.9 us -> 21.1 us  [local(): lax.all_to_all(merged, 'pb', split_axis=0, concat_axis=0, tiled=True)]
  transfers between devices with their start and end apart: 12 -> 12, of which waited for: 7 -> 7; matrix products, arithmetic and copies ran while one was open for 2% -> 2% of each run, Pallas kernels for 32% -> 34%
where the time goes in v3:
time: 128 us; the launch traced here: 127 us
  Pallas kernels  46.4 us (36%)
  blocking collectives  21.1 us (16%)
  local copies, waits for them, and re-layouts  20.9 us (16%)
  starting transfers between devices  19.3 us (15%)
  waiting for transfers between devices  17.7 us (14%)
    all_to_all x1, blocking collectives, local(): lax.all_to_all(merged, 'pb', split_axis=0, concat_axis=0, tiled=True)  21.1 us
    unnamed x35, local copies, waits for them, and re-layouts  19.9 us
    pallas_call x4, Pallas kernels, attend(): pl.pallas_call(functools.partial(attend_kernel, offset=offset, column=col...  19.9 us
    ppermute x11, waiting for transfers between devices, swap(): return lax.ppermute(value, axis, [(at, at ^ bits) for at in range(size)])  17.5 us
    ppermute x11, starting transfers between devices, swap(): return lax.ppermute(value, axis, [(at, at ^ bits) for at in range(size)])  13.5 us
    pallas_call x2, Pallas kernels, project(): pl.pallas_call(project_kernel, grid_spec=pltpu.PrefetchScalarGridSpec(num...  13.1 us
    pallas_call x1, Pallas kernels, retrieve(): pl.pallas_call(functools.partial(retrieval_kernel, spread=spread), grid_s...  7.44 us
    all_to_all x1, starting transfers between devices, local(): lax.all_to_all(by_group, 'pb', split_axis=0, concat_axis=0, tiled=True)  5.84 us
  transfers between devices with their start and end apart: 12, of which 7 were waited for; matrix products, arithmetic and copies ran while one was open for 2% of the time, Pallas kernels for 34%

profile of v3, /device:TPU:0, one launch (start us, length us, event | category | flops | bytes accessed | tf_op | source)
XLA Modules:
  0.0 126.9 jit_solution(10933736622243712870)
XLA Ops:
  1.1 7.4 %retrieve.1 = (bf16[2,8,32,896]{3,2,1,0:T(8,128)(2,1)}, bf16[2,8,32,896]{3,2,1,0:T(8,128)(2,1)}) custom-call(s32[4]{0:T(128)} %pad_add_fusion.2.place, bf16[1024,768]{1,0:T(8,128)(2,1)} %queries.1, bf16[512,768]{1,0:T(8,128)(2,1)} %passages.1, bf16[1024,512]{1,0:T(8,128)(2,1)} %noise.1), custom_call_target="tpu_custom_call" | custom-call | flops 1610612736 | bytes 4980736 | tf_op jit(solution)/shard_map/retrieve/pallas_call | solution.py:100
  9.3 1.9 %collective-permute-done.recv = bf16[2,8,32,896]{3,2,1,0:T(8,128)(2,1)S(1)} collective-permute-done((bf16[2,8,32,896]{3,2,1,0:T(8,128)(2,1)}, bf16[2,8,32,896]{3,2,1,0:T(8,128)(2,1)S(1)}, u32[]{:S(2)}, u32[]{:S(2)}) %collective-permute-start) | collective-permute-done | bytes 917536 | tf_op jit(solution)/shard_map/ppermute | solution.py:451
  12.4 1.6 %merge_pair.1 = (bf16[8,32,896]{2,1,0:T(8,128)(2,1)S(1)}, bf16[8,32,896]{2,1,0:T(8,128)(2,1)S(1)}) custom-call(s32[4]{0:T(128)S(1)} %copy-done.10, bf16[2,8,32,896]{3,2,1,0:T(8,128)(2,1)S(1)} %copy-done.8, bf16[2,8,32,896]{3,2,1,0:T(8,128)(2,1)S(1)} %collective-permute-done.recv), custom_call_target="tpu_custom_call" | custom-call | tf_op jit(solution)/shard_map/merge_pair/pallas_call | solution.py:143
  14.0 2.7 %collective-permute-start.1 = (bf16[8,32,896]{2,1,0:T(8,128)(2,1)S(1)}, bf16[8,32,896]{2,1,0:T(8,128)(2,1)S(1)}, u32[]{:S(2)}, u32[]{:S(2)}) collective-permute-start(bf16[8,32,896]{2,1,0:T(8,128)(2,1)S(1)} %get-tuple-element.32), channel_id=1, source_target_pairs={{0,16},{8,24},{16,0},{24,8},{1,17},{9,25},{17,1},{25,9},{2,18},{10... | collective-permute-start | bytes 1376264 | tf_op jit(solution)/shard_map/ppermute | solution.py:451
  16.9 2.2 %copy-done.11 = bf16[8,256,1024]{2,1,0:T(8,128)(2,1)S(1)} copy-done((bf16[8,256,1024]{2,1,0:T(8,128)(2,1)S(1)}, bf16[8,256,1024]{2,1,0:T(8,128)(2,1)}, u32[]{:S(2)}) %copy-start.11) | copy-done | bytes 4194328
  19.1 1.6 %copy-done.12 = bf16[1024,1024]{1,0:T(8,128)(2,1)S(1)} copy-done((bf16[1024,1024]{1,0:T(8,128)(2,1)S(1)}, bf16[1024,1024]{1,0:T(8,128)(2,1)}, u32[]{:S(2)}) %copy-start.12) | copy-done | bytes 2097176
  20.7 1.6 %copy-done.14 = bf16[1024,1024]{1,0:T(8,128)(2,1)S(1)} copy-done((bf16[1024,1024]{1,0:T(8,128)(2,1)S(1)}, bf16[1024,1024]{1,0:T(8,128)(2,1)}, u32[]{:S(2)}) %copy-start.14) | copy-done | bytes 2097176
  22.3 5.8 %project.2 = (bf16[2048,512]{1,0:T(8,128)(2,1)S(1)}, bf16[512,2048]{1,0:T(8,128)(2,1)S(1)}) custom-call(s32[4]{0:T(128)S(1)} %copy-done.10, bf16[2048,1024]{1,0:T(8,128)(2,1)S(1)} %bitcast.30, bf16[1024,1024]{1,0:T(8,128)(2,1)S(1)} %copy-done.12, bf16[1024,1024]{1,0:T(8,128)(2,1)S(1)} %copy-done.12, bf16[1024,1024]{1,0:T(8,128)(2,1)S(1)} %copy-done.14, ...), custom_call_target="tpu_custom_call" | custom-call | flops 4294967296 | bytes 10485760 | tf_op jit(solution)/shard_map/project/pallas_call | solution.py:223
  28.1 1.4 %copy-done.1 = bf16[512,2048]{1,0:T(8,128)(2,1)} copy-done((bf16[512,2048]{1,0:T(8,128)(2,1)}, bf16[512,2048]{1,0:T(8,128)(2,1)S(1)}, u32[]{:S(2)}) %copy-start.1) | copy-done | bytes 2097176
  29.5 1.3 %merge_columns.1 = bf16[8,32,896]{2,1,0:T(8,128)(2,1)} custom-call(f32[1,128]{1,0:T(1,128)S(1)} %pad.4.note, bf16[8,32,896]{2,1,0:T(8,128)(2,1)S(1)} %get-tuple-element.36.refs_0_, bf16[8,32,896]{2,1,0:T(8,128)(2,1)S(1)} %collective-permute-done.1.refs_1_), custom_call_target="tpu_custom_call" | custom-call | tf_op jit(solution)/shard_map/merge_columns/pallas_call | solution.py:162
  30.8 5.8 %all-to-all-start = ((bf16[8,32,896]{2,1,0:T(8,128)(2,1)}), bf16[8,32,896]{2,1,0:T(8,128)(2,1)S(1)}, u32[]{:S(2)}, u32[]{:S(2)}) async-start(bf16[8,32,896]{2,1,0:T(8,128)(2,1)} %merge_columns.1), calls=%async_computation | async-start | bytes 917504 | tf_op jit(solution)/shard_map/all_to_all | solution.py:467
  36.6 1.6 %copy-done.13 = bf16[1024,1024]{1,0:T(8,128)(2,1)S(1)} copy-done((bf16[1024,1024]{1,0:T(8,128)(2,1)S(1)}, bf16[1024,1024]{1,0:T(8,128)(2,1)}, u32[]{:S(2)}) %copy-start.13) | copy-done | bytes 2097176
  38.2 1.6 %copy-done.15 = bf16[1024,1024]{1,0:T(8,128)(2,1)S(1)} copy-done((bf16[1024,1024]{1,0:T(8,128)(2,1)S(1)}, bf16[1024,1024]{1,0:T(8,128)(2,1)}, u32[]{:S(2)}) %copy-start.15) | copy-done | bytes 2097176
  39.8 7.3 %project.3 = (bf16[2048,512]{1,0:T(8,128)(2,1)S(1)}, bf16[512,2048]{1,0:T(8,128)(2,1)S(1)}) custom-call(s32[4]{0:T(128)S(1)} %copy-done.10, bf16[2048,1024]{1,0:T(8,128)(2,1)} %collective-permute-done.2.states, bf16[1024,1024]{1,0:T(8,128)(2,1)S(1)} %copy-done.13, bf16[1024,1024]{1,0:T(8,128)(2,1)S(1)} %copy-done.13, bf16[1024,1024]{1,0:T(8,128)(2,1)S(1)} %copy-done.15, ...), custom_call_target="tpu_custom_call" | custom-call | flops 4294967296 | bytes 10485760 | tf_op jit(solution)/shard_map/project/pallas_call | solution.py:223
  47.1 1.3 %copy-done.3 = bf16[2048,512]{1,0:T(8,128)(2,1)} copy-done((bf16[2048,512]{1,0:T(8,128)(2,1)}, bf16[2048,512]{1,0:T(8,128)(2,1)S(1)}, u32[]{:S(2)}) %copy-start.3) | copy-done | bytes 2097176
  48.4 1.3 %copy-done.5 = bf16[512,2048]{1,0:T(8,128)(2,1)} copy-done((bf16[512,2048]{1,0:T(8,128)(2,1)}, bf16[512,2048]{1,0:T(8,128)(2,1)S(1)}, u32[]{:S(2)}) %copy-start.5) | copy-done | bytes 2097176
  49.9 1.4 %copy-done.7 = bf16[768,1024]{1,0:T(8,128)(2,1)S(1)} copy-done((bf16[768,1024]{1,0:T(8,128)(2,1)S(1)}, bf16[768,1024]{1,0:T(8,128)(2,1)}, u32[]{:S(2)}) %copy-start.7) | copy-done | bytes 1572888
  53.8 1.9 %collective-permute-start.5 = (bf16[1,2,32,512]{3,2,1,0:T(8,128)(2,1)S(1)}, bf16[1,2,32,512]{3,2,1,0:T(8,128)(2,1)S(1)}, u32[]{:S(2)}, u32[]{:S(2)}) collective-permute-start(bf16[1,2,32,512]{3,2,1,0:T(8,128)(2,1)S(1)} %maximum_bitcast_fusion), channel_id=1, source_target_pairs={{0,2},{1,3},{2,0},{3,1},{4,6},{5,7},{6,4},{7,5},{8,10},{9,11},{10,... | collective-permute-start | bytes 196616 | tf_op jit(solution)/shard_map/ppermute | solution.py:451
  55.7 2.4 %collective-permute-done.5 = bf16[1,2,32,512]{3,2,1,0:T(8,128)(2,1)S(1)} collective-permute-done((bf16[1,2,32,512]{3,2,1,0:T(8,128)(2,1)S(1)}, bf16[1,2,32,512]{3,2,1,0:T(8,128)(2,1)S(1)}, u32[]{:S(2)}, u32[]{:S(2)}) %collective-permute-start.5) | collective-permute-done | bytes 65568 | tf_op jit(solution)/shard_map/ppermute | solution.py:451
  58.1 2.8 %collective-permute-start.6 = (bf16[2,2,32,512]{3,2,1,0:T(8,128)(2,1)S(1)}, bf16[2,2,32,512]{3,2,1,0:T(8,128)(2,1)S(1)}, u32[]{:S(2)}, u32[]{:S(2)}) collective-permute-start(bf16[2,2,32,512]{3,2,1,0:T(8,128)(2,1)S(1)} %pad_maximum_fusion.2), channel_id=1, source_target_pairs={{0,4},{1,5},{2,6},{3,7},{4,0},{5,1},{6,2},{7,3},{8,12},{9,13},{10,... | collective-permute-start | bytes 393224 | tf_op jit(solution)/shard_map/ppermute | solution.py:451
  61.0 5.4 %collective-permute-done.6 = bf16[2,2,32,512]{3,2,1,0:T(8,128)(2,1)S(1)} collective-permute-done((bf16[2,2,32,512]{3,2,1,0:T(8,128)(2,1)S(1)}, bf16[2,2,32,512]{3,2,1,0:T(8,128)(2,1)S(1)}, u32[]{:S(2)}, u32[]{:S(2)}) %collective-permute-start.6) | collective-permute-done | bytes 131104 | tf_op jit(solution)/shard_map/ppermute | solution.py:451
  67.4 5.5 %collective-permute-done.7 = bf16[4,2,32,512]{3,2,1,0:T(8,128)(2,1)S(1)} collective-permute-done((bf16[4,2,32,512]{3,2,1,0:T(8,128)(2,1)S(1)}, bf16[4,2,32,512]{3,2,1,0:T(8,128)(2,1)S(1)}, u32[]{:S(2)}, u32[]{:S(2)}) %collective-permute-start.7) | collective-permute-done | bytes 262176 | tf_op jit(solution)/shard_map/ppermute | solution.py:451
  72.9 2.7 %collective-permute-start.9 = (bf16[2,4,2,32,512]{4,3,2,1,0:T(8,128)(2,1)S(1)}, bf16[2,4,2,32,512]{4,3,2,1,0:T(8,128)(2,1)S(1)}, u32[]{:S(2)}, u32[]{:S(2)}) collective-permute-start(bf16[2,4,2,32,512]{4,3,2,1,0:T(8,128)(2,1)S(1)} %pad_maximum_fusion.pieces), channel_id=1, source_target_pairs={{0,1},{1,0},{2,3},{3,2},{4,5},{5,4},{6,7},{7,6},{8,9},{9,8},{10,11... | collective-permute-start | bytes 1572872 | tf_op jit(solution)/shard_map/ppermute | solution.py:451
  77.0 1.6 %copy-done.2 = bf16[512,2048]{1,0:T(8,128)(2,1)S(1)} copy-done((bf16[512,2048]{1,0:T(8,128)(2,1)S(1)}, bf16[512,2048]{1,0:T(8,128)(2,1)}, u32[]{:S(2)}) %copy-start.2) | copy-done | bytes 2097176
  78.6 1.6 %copy-done.4 = bf16[2048,512]{1,0:T(8,128)(2,1)S(1)} copy-done((bf16[2048,512]{1,0:T(8,128)(2,1)S(1)}, bf16[2048,512]{1,0:T(8,128)(2,1)}, u32[]{:S(2)}) %copy-start.4) | copy-done | bytes 2097176
  80.2 1.6 %copy-done.6 = bf16[512,2048]{1,0:T(8,128)(2,1)S(1)} copy-done((bf16[512,2048]{1,0:T(8,128)(2,1)S(1)}, bf16[512,2048]{1,0:T(8,128)(2,1)}, u32[]{:S(2)}) %copy-start.6) | copy-done | bytes 2097176
  81.8 4.9 %attend.5 = bf16[4,288,128]{2,1,0:T(8,128)(2,1)S(1)} custom-call(s32[4]{0:T(128)S(1)} %copy-done.10, s32[48]{0:T(128)S(1)} %reshape.78.table, bf16[2,4,2,32,512]{4,3,2,1,0:T(8,128)(2,1)S(1)} %pad_maximum_fusion.pieces, bf16[2048,512]{1,0:T(8,128)(2,1)S(1)} %get-tuple-element.45.key_own, bf16[2048,512]{1,0:T(8,128)(2,1)S(1)} %copy-done.4, ...), custom_call_target="tpu_custom_call" | custom-call | flops 2147483648 | bytes 294912 | tf_op jit(solution)/shard_map/attend/pallas_call | solution.py:323
  87.3 4.9 %attend.7 = bf16[4,288,128]{2,1,0:T(8,128)(2,1)S(1)} custom-call(s32[4]{0:T(128)S(1)} %copy-done.10, s32[48]{0:T(128)S(1)} %reshape.78.table, bf16[2,4,2,32,512]{4,3,2,1,0:T(8,128)(2,1)S(1)} %collective-permute-done.9.pieces, bf16[2048,512]{1,0:T(8,128)(2,1)S(1)} %get-tuple-element.45.key_own, bf16[2048,512]{1,0:T(8,128)(2,1)S(1)} %copy-done.4, ...), custom_call_target="tpu_custom_call" | custom-call | flops 2147483648 | bytes 294912 | tf_op jit(solution)/shard_map/attend/pallas_call | solution.py:323
  92.2 1.6 %collective-permute-start.10 = (bf16[4,288,128]{2,1,0:T(8,128)(2,1)S(1)}, bf16[4,288,128]{2,1,0:T(8,128)(2,1)S(1)}, u32[]{:S(2)}, u32[]{:S(2)}) collective-permute-start(bf16[4,288,128]{2,1,0:T(8,128)(2,1)S(1)} %attend.7), channel_id=1, source_target_pairs={{0,16},{8,24},{16,0},{24,8},{1,17},{9,25},{17,1},{25,9},{2,18},{10... | collective-permute-start | bytes 884744 | tf_op jit(solution)/shard_map/ppermute | solution.py:451
  93.8 5.1 %attend.4.refs_0_ = bf16[4,288,128]{2,1,0:T(8,128)(2,1)S(1)} custom-call(s32[4]{0:T(128)S(1)} %copy-done.10, s32[48]{0:T(128)S(1)} %reshape.78.table, bf16[2,4,2,32,512]{4,3,2,1,0:T(8,128)(2,1)S(1)} %pad_maximum_fusion.pieces, bf16[2048,512]{1,0:T(8,128)(2,1)S(1)} %get-tuple-element.45.key_own, bf16[2048,512]{1,0:T(8,128)(2,1)S(1)} %copy-done.4, ...), custom_call_target="tpu_custom_call" | custom-call | flops 2147483648 | bytes 294912 | tf_op jit(solution)/shard_map/attend/pallas_call | solution.py:323
  98.9 4.9 %attend.6.refs_2_ = bf16[4,288,128]{2,1,0:T(8,128)(2,1)S(1)} custom-call(s32[4]{0:T(128)S(1)} %copy-done.10, s32[48]{0:T(128)S(1)} %reshape.78.table, bf16[2,4,2,32,512]{4,3,2,1,0:T(8,128)(2,1)S(1)} %collective-permute-done.9.pieces, bf16[2048,512]{1,0:T(8,128)(2,1)S(1)} %get-tuple-element.45.key_own, bf16[2048,512]{1,0:T(8,128)(2,1)S(1)} %copy-done.4, ...), custom_call_target="tpu_custom_call" | custom-call | flops 2147483648 | bytes 294912 | tf_op jit(solution)/shard_map/attend/pallas_call | solution.py:323
  105.0 21.1 %all_to_all.10.parts = bf16[8,288,128]{2,1,0:T(8,128)(2,1)S(1)} all-to-all(bf16[8,288,128]{2,1,0:T(8,128)(2,1)S(1)} %bitcast.27), channel_id=1, replica_groups=mesh['pa'=4,'pb'=8] {'pb'}, dimensions={0} | all-to-all | bytes 1179648 | tf_op jit(solution)/shard_map/all_to_all | solution.py:503
  (61 shorter events, 10.9 us)
Async XLA Ops:
  0.0 8.6 %copy-start = (s32[256]{0:T(256)S(1)}, s32[256]{0:T(256)}, u32[]{:S(2)}) copy-start(s32[256]{0:T(256)} %param.18) | copy-start | bytes 3076
  0.0 30.8 %collective-permute-start.2 = (bf16[2048,1024]{1,0:T(8,128)(2,1)}, bf16[2048,1024]{1,0:T(8,128)(2,1)}, u32[]{:S(2)}, u32[]{:S(2)}) collective-permute-start(bf16[2048,1024]{1,0:T(8,128)(2,1)} %bitcast.29), channel_id=1, source_target_pairs={{0,8},{8,0},{16,24},{24,16},{1,9},{9,1},{17,25},{25,17},{2,10},{10... | collective-permute-start | bytes 12582920 | tf_op jit(solution)/shard_map/ppermute | solution.py:451
  1.1 7.5 %copy-start.16 = (s32[1,16]{1,0:T(1,128)S(1)}, s32[1,16]{1,0:T(1,128)}, u32[]{:S(2)}) copy-start(s32[1,16]{1,0:T(1,128)} %param.19) | copy-start | bytes 196
  1.1 10.1 %copy-start.10 = (s32[4]{0:T(128)S(1)}, s32[4]{0:T(128)}, u32[]{:S(2)}) copy-start(s32[4]{0:T(128)} %pad_add_fusion.2.place) | copy-start | bytes 52
  8.6 2.7 %collective-permute-start = (bf16[2,8,32,896]{3,2,1,0:T(8,128)(2,1)}, bf16[2,8,32,896]{3,2,1,0:T(8,128)(2,1)S(1)}, u32[]{:S(2)}, u32[]{:S(2)}) collective-permute-start(bf16[2,8,32,896]{3,2,1,0:T(8,128)(2,1)} %get-tuple-element.28), channel_id=1, source_target_pairs={{0,8},{8,0},{16,24},{24,16},{1,9},{9,1},{17,25},{25,17},{2,10},{10... | collective-permute-start | bytes 2752520 | tf_op jit(solution)/shard_map/ppermute | solution.py:451
  11.3 1.2 copy-start.8
  14.0 15.4 %collective-permute-start.1 = (bf16[8,32,896]{2,1,0:T(8,128)(2,1)S(1)}, bf16[8,32,896]{2,1,0:T(8,128)(2,1)S(1)}, u32[]{:S(2)}, u32[]{:S(2)}) collective-permute-start(bf16[8,32,896]{2,1,0:T(8,128)(2,1)S(1)} %get-tuple-element.32), channel_id=1, source_target_pairs={{0,16},{8,24},{16,0},{24,8},{1,17},{9,25},{17,1},{25,9},{2,18},{10... | collective-permute-start | bytes 1376264 | tf_op jit(solution)/shard_map/ppermute | solution.py:451
  16.9 2.2 %copy-start.11 = (bf16[8,256,1024]{2,1,0:T(8,128)(2,1)S(1)}, bf16[8,256,1024]{2,1,0:T(8,128)(2,1)}, u32[]{:S(2)}) copy-start(bf16[8,256,1024]{2,1,0:T(8,128)(2,1)} %param.17) | copy-start | bytes 12582916
  19.1 1.6 %copy-start.12 = (bf16[1024,1024]{1,0:T(8,128)(2,1)S(1)}, bf16[1024,1024]{1,0:T(8,128)(2,1)}, u32[]{:S(2)}) copy-start(bf16[1024,1024]{1,0:T(8,128)(2,1)} %refs_1_.3) | copy-start | bytes 6291460
  20.7 1.6 %copy-start.14 = (bf16[1024,1024]{1,0:T(8,128)(2,1)S(1)}, bf16[1024,1024]{1,0:T(8,128)(2,1)}, u32[]{:S(2)}) copy-start(bf16[1024,1024]{1,0:T(8,128)(2,1)} %refs_3_.3) | copy-start | bytes 6291460
  28.1 1.4 %copy-start.1 = (bf16[512,2048]{1,0:T(8,128)(2,1)}, bf16[512,2048]{1,0:T(8,128)(2,1)S(1)}, u32[]{:S(2)}) copy-start(bf16[512,2048]{1,0:T(8,128)(2,1)S(1)} %get-tuple-element.47.value_own) | copy-start | bytes 6291460
  30.8 19.2 %all-to-all-start = ((bf16[8,32,896]{2,1,0:T(8,128)(2,1)}), bf16[8,32,896]{2,1,0:T(8,128)(2,1)S(1)}, u32[]{:S(2)}, u32[]{:S(2)}) async-start(bf16[8,32,896]{2,1,0:T(8,128)(2,1)} %merge_columns.1), calls=%async_computation | async-start | bytes 917504 | tf_op jit(solution)/shard_map/all_to_all | solution.py:467
  36.6 1.6 %copy-start.13 = (bf16[1024,1024]{1,0:T(8,128)(2,1)S(1)}, bf16[1024,1024]{1,0:T(8,128)(2,1)}, u32[]{:S(2)}) copy-start(bf16[1024,1024]{1,0:T(8,128)(2,1)} %refs_1_.3) | copy-start | bytes 6291460
  38.2 1.6 %copy-start.15 = (bf16[1024,1024]{1,0:T(8,128)(2,1)S(1)}, bf16[1024,1024]{1,0:T(8,128)(2,1)}, u32[]{:S(2)}) copy-start(bf16[1024,1024]{1,0:T(8,128)(2,1)} %refs_3_.3) | copy-start | bytes 6291460
  39.8 10.1 %copy-start.9 = (bf16[128,1024]{1,0:T(8,128)(2,1)S(1)}, bf16[128,1024]{1,0:T(8,128)(2,1)}, u32[]{:S(2)}) copy-start(bf16[128,1024]{1,0:T(8,128)(2,1)} %answers.1) | copy-start | bytes 786436
  47.1 1.3 %copy-start.3 = (bf16[2048,512]{1,0:T(8,128)(2,1)}, bf16[2048,512]{1,0:T(8,128)(2,1)S(1)}, u32[]{:S(2)}) copy-start(bf16[2048,512]{1,0:T(8,128)(2,1)S(1)} %get-tuple-element.46.key_pair) | copy-start | bytes 6291460
  48.4 1.3 %copy-start.5 = (bf16[512,2048]{1,0:T(8,128)(2,1)}, bf16[512,2048]{1,0:T(8,128)(2,1)S(1)}, u32[]{:S(2)}) copy-start(bf16[512,2048]{1,0:T(8,128)(2,1)S(1)} %get-tuple-element.48.value_pair) | copy-start | bytes 6291460
  49.9 1.4 %copy-start.7 = (bf16[768,1024]{1,0:T(8,128)(2,1)S(1)}, bf16[768,1024]{1,0:T(8,128)(2,1)}, u32[]{:S(2)}) copy-start(bf16[768,1024]{1,0:T(8,128)(2,1)} %mix_weight.1) | copy-start | bytes 4718596
  52.5 1.3 %collective-permute-start.4 = (bf16[32,512]{1,0:T(8,128)(2,1)S(1)}, bf16[32,512]{1,0:T(8,128)(2,1)S(1)}, u32[]{:S(2)}, u32[]{:S(2)}) collective-permute-start(bf16[32,512]{1,0:T(8,128)(2,1)S(1)} %get-tuple-element.44), channel_id=1, source_target_pairs={{0,8},{8,0},{16,24},{24,16},{1,9},{9,1},{17,25},{25,17},{2,10},{10... | collective-permute-start | bytes 98312 | tf_op jit(solution)/shard_map/ppermute | solution.py:451
  53.8 4.3 %collective-permute-start.5 = (bf16[1,2,32,512]{3,2,1,0:T(8,128)(2,1)S(1)}, bf16[1,2,32,512]{3,2,1,0:T(8,128)(2,1)S(1)}, u32[]{:S(2)}, u32[]{:S(2)}) collective-permute-start(bf16[1,2,32,512]{3,2,1,0:T(8,128)(2,1)S(1)} %maximum_bitcast_fusion), channel_id=1, source_target_pairs={{0,2},{1,3},{2,0},{3,1},{4,6},{5,7},{6,4},{7,5},{8,10},{9,11},{10,... | collective-permute-start | bytes 196616 | tf_op jit(solution)/shard_map/ppermute | solution.py:451
  58.1 8.2 %collective-permute-start.6 = (bf16[2,2,32,512]{3,2,1,0:T(8,128)(2,1)S(1)}, bf16[2,2,32,512]{3,2,1,0:T(8,128)(2,1)S(1)}, u32[]{:S(2)}, u32[]{:S(2)}) collective-permute-start(bf16[2,2,32,512]{3,2,1,0:T(8,128)(2,1)S(1)} %pad_maximum_fusion.2), channel_id=1, source_target_pairs={{0,4},{1,5},{2,6},{3,7},{4,0},{5,1},{6,2},{7,3},{8,12},{9,13},{10,... | collective-permute-start | bytes 393224 | tf_op jit(solution)/shard_map/ppermute | solution.py:451
  66.4 6.4 %collective-permute-start.7 = (bf16[4,2,32,512]{3,2,1,0:T(8,128)(2,1)S(1)}, bf16[4,2,32,512]{3,2,1,0:T(8,128)(2,1)S(1)}, u32[]{:S(2)}, u32[]{:S(2)}) collective-permute-start(bf16[4,2,32,512]{3,2,1,0:T(8,128)(2,1)S(1)} %get-tuple-element.55), channel_id=1, source_target_pairs={{0,16},{8,24},{16,0},{24,8},{1,17},{9,25},{17,1},{25,9},{2,18},{10... | collective-permute-start | bytes 786440 | tf_op jit(solution)/shard_map/ppermute | solution.py:451
  72.9 14.4 %collective-permute-start.9 = (bf16[2,4,2,32,512]{4,3,2,1,0:T(8,128)(2,1)S(1)}, bf16[2,4,2,32,512]{4,3,2,1,0:T(8,128)(2,1)S(1)}, u32[]{:S(2)}, u32[]{:S(2)}) collective-permute-start(bf16[2,4,2,32,512]{4,3,2,1,0:T(8,128)(2,1)S(1)} %pad_maximum_fusion.pieces), channel_id=1, source_target_pairs={{0,1},{1,0},{2,3},{3,2},{4,5},{5,4},{6,7},{7,6},{8,9},{9,8},{10,11... | collective-permute-start | bytes 1572872 | tf_op jit(solution)/shard_map/ppermute | solution.py:451
  75.6 1.2 collective-permute-start.3
  77.0 1.6 %copy-start.2 = (bf16[512,2048]{1,0:T(8,128)(2,1)S(1)}, bf16[512,2048]{1,0:T(8,128)(2,1)}, u32[]{:S(2)}) copy-start(bf16[512,2048]{1,0:T(8,128)(2,1)} %copy-done.1) | copy-start | bytes 6291460
  78.6 1.6 %copy-start.4 = (bf16[2048,512]{1,0:T(8,128)(2,1)S(1)}, bf16[2048,512]{1,0:T(8,128)(2,1)}, u32[]{:S(2)}) copy-start(bf16[2048,512]{1,0:T(8,128)(2,1)} %copy-done.3) | copy-start | bytes 6291460
  80.2 1.6 %copy-start.6 = (bf16[512,2048]{1,0:T(8,128)(2,1)S(1)}, bf16[512,2048]{1,0:T(8,128)(2,1)}, u32[]{:S(2)}) copy-start(bf16[512,2048]{1,0:T(8,128)(2,1)} %copy-done.5) | copy-start | bytes 6291460
  86.7 17.1 %collective-permute-start.8 = (bf16[4,288,128]{2,1,0:T(8,128)(2,1)S(1)}, bf16[4,288,128]{2,1,0:T(8,128)(2,1)S(1)}, u32[]{:S(2)}, u32[]{:S(2)}) collective-permute-start(bf16[4,288,128]{2,1,0:T(8,128)(2,1)S(1)} %attend.5), channel_id=1, source_target_pairs={{0,16},{8,24},{16,0},{24,8},{1,17},{9,25},{17,1},{25,9},{2,18},{10... | collective-permute-start | bytes 884744 | tf_op jit(solution)/shard_map/ppermute | solution.py:451
  92.2 11.6 %collective-permute-start.10 = (bf16[4,288,128]{2,1,0:T(8,128)(2,1)S(1)}, bf16[4,288,128]{2,1,0:T(8,128)(2,1)S(1)}, u32[]{:S(2)}, u32[]{:S(2)}) collective-permute-start(bf16[4,288,128]{2,1,0:T(8,128)(2,1)S(1)} %attend.7), channel_id=1, source_target_pairs={{0,16},{8,24},{16,0},{24,8},{1,17},{9,25},{17,1},{25,9},{2,18},{10... | collective-permute-start | bytes 884744 | tf_op jit(solution)/shard_map/ppermute | solution.py:451

commit v4 on v3

--- a/solution.py
+++ b/solution.py
@@ -15,14 +15,15 @@
 STAT_ROWS = 32
 NOTE_AT = 6
 STEP_GROUPS = 2
-PROJECT_STEPS = 2
+PROJECT_STEPS = 4
 ATTEND_GROUPS = 4
 HEAD_BUNDLE = 2
-VMEM_BYTES = 40 * 1024 * 1024
-WIDE_BYTES = 60 * 1024 * 1024
+VMEM_BYTES = 16 * 1024 * 1024
+WIDE_BYTES = 24 * 1024 * 1024
 F32 = jnp.float32
 BF16 = jnp.bfloat16
 NT = (((1,), (1,)), ((), ()))
+SCALARS = pl.BlockSpec(memory_space=pltpu.SMEM)
 
 
 def grant():
@@ -75,7 +76,7 @@
     width = queries.shape[1]
     logits = lax.dot_general(queries[...], passages[...], NT, preferred_element_type=F32)
     gumbel = -jnp.log(-jnp.log(noise[...].astype(F32)))
-    scores = (logits * width ** (-0.5) + gumbel) / TEMPER
+    scores = (logits * width ** (-0.5) + gumbel) * (1 / TEMPER)
     shift = jnp.max(scores, 1, keepdims=True)
     weight = jnp.exp(scores - shift)
     total = jnp.sum(weight, 1, keepdims=True)
@@ -130,7 +131,14 @@
     out[..., len(tiles) * LANES :] = tail.astype(BF16).reshape(out.shape[:-1] + (LANES,))
 
 
+def hand_on(place, out):
+    for at in range(out.shape[0]):
+        out[at] = place[at]
+
+
 def pair_kernel(place, keep, recv, *outs):
+    *outs, later = outs
+    hand_on(place, later)
     for offset, out in enumerate(outs):
         column = lax.bitwise_xor(place[1], offset)
         store_rows(out, *merge_rows([flat(keep[column]), flat(recv[column])]))
@@ -143,34 +151,46 @@
     return pl.pallas_call(
         pair_kernel,
         grid_spec=pltpu.PrefetchScalarGridSpec(
-            num_scalar_prefetch=1, grid=(2,), in_specs=[spec, spec], out_specs=[out] * spread
-        ),
-        out_shape=[jax.ShapeDtypeStruct(keep.shape[1:], BF16)] * spread,
+            num_scalar_prefetch=1, grid=(2,), in_specs=[spec, spec], out_specs=[out] * spread + [SCALARS]
+        ),
+        out_shape=[jax.ShapeDtypeStruct(keep.shape[1:], BF16)] * spread
+        + [jax.ShapeDtypeStruct(place.shape, place.dtype)],
         compiler_params=grant(),
         name="merge_pair",
     )(place, keep, recv)
 
 
-def column_kernel(note, *refs):
-    *parts, out = refs
-    store_rows(out, *merge_rows([flat(part[...]) for part in parts]), note[...])
-
-
-def merge_columns(note, parts):
+def column_kernel(place, note, done, *refs):
+    *parts, out, later = refs
+    hand_on(place, later)
+    store_rows(out, *merge_rows([flat(part[...]) for part in parts]), note[...] + done[0:1, :])
+
+
+def merge_columns(place, note, done, parts):
     readers = parts[0].shape[0]
-    spec = pl.BlockSpec((readers // 2,) + parts[0].shape[1:], lambda g: (g, 0, 0))
+    spec = pl.BlockSpec((readers // 2,) + parts[0].shape[1:], lambda g, place: (g, 0, 0))
     return pl.pallas_call(
         column_kernel,
-        grid=(2,),
-        in_specs=[pl.BlockSpec(note.shape, lambda g: (0, 0))] + [spec] * len(parts),
-        out_specs=spec,
-        out_shape=jax.ShapeDtypeStruct(parts[0].shape, BF16),
+        grid_spec=pltpu.PrefetchScalarGridSpec(
+            num_scalar_prefetch=1,
+            grid=(2,),
+            in_specs=[
+                pl.BlockSpec(note.shape, lambda g, place: (0, 0)),
+                pl.BlockSpec(done.shape, lambda g, place: (0, 0)),
+            ]
+            + [spec] * len(parts),
+            out_specs=[spec, SCALARS],
+        ),
+        out_shape=[
+            jax.ShapeDtypeStruct(parts[0].shape, BF16),
+            jax.ShapeDtypeStruct(place.shape, place.dtype),
+        ],
         compiler_params=grant(),
         name="merge_columns",
-    )(note, *parts)
-
-
-def condition_kernel(place, parts, mix_weight, answers, keep, send, rows_scratch, *, spread):
+    )(place, note, done, *parts)
+
+
+def condition_kernel(place, parts, mix_weight, answers, done, keep, send, rows_scratch, *, spread):
     tiles, _, total = merge_rows([parts[at] for at in range(parts.shape[0])])
     blended_half = jnp.concatenate([(tile / total).astype(BF16) for tile in tiles], 1)
     part = blended_half.shape[0]
@@ -185,24 +205,25 @@
         send[:, column * stride : (column + 1) * stride] = rows_scratch[:, pl.ds(other, stride)].astype(BF16)
 
 
-def condition(place, parts, mix_weight, answers, spread):
+def condition(place, parts, mix_weight, answers, done, spread):
     model_width = mix_weight.shape[1]
     shape = jax.ShapeDtypeStruct((parts.shape[1], model_width // PAIR), BF16)
     whole = pl.BlockSpec(memory_space=pltpu.VMEM)
     return pl.pallas_call(
         functools.partial(condition_kernel, spread=spread),
-        in_specs=[pl.BlockSpec(memory_space=pltpu.SMEM), whole, whole, whole],
+        in_specs=[SCALARS, whole, whole, whole, whole],
         out_specs=[whole, whole],
         out_shape=[shape, shape],
         scratch_shapes=[pltpu.VMEM((parts.shape[1], model_width), F32)],
         compiler_params=grant(),
         name="condition",
-    )(place, parts, mix_weight, answers)
+    )(place, parts, mix_weight, answers, done)
 
 
 def project_kernel(place, states, *refs):
-    spread = len(refs) // 2 - 1
-    keys, values = refs[-2:]
+    spread = (len(refs) - 3) // 2
+    keys, values, done = refs[-3:]
+    done[...] = jnp.zeros_like(done)
     width = keys.shape[1] // spread
     for column in range(spread):
         key = jnp.dot(states[...], refs[column][...], preferred_element_type=F32)
@@ -229,11 +250,13 @@
             out_specs=[
                 pl.BlockSpec((chunk, spread * width), lambda t, place: (t, 0)),
                 pl.BlockSpec((spread * width, chunk), lambda t, place: (0, t)),
+                pl.BlockSpec((8, LANES), lambda t, place: (0, 0)),
             ],
         ),
         out_shape=[
             jax.ShapeDtypeStruct((rows, spread * width), BF16),
             jax.ShapeDtypeStruct((spread * width, rows), BF16),
+            jax.ShapeDtypeStruct((8, LANES), F32),
         ],
         compiler_params=grant(),
         cost_estimate=pl.CostEstimate(
@@ -453,49 +476,51 @@
     states = token_states.reshape(slots * tokens, model_width)
     pair_states = swap(states, "pa", 1)
 
-    keep, send = retrieve(place, queries, passages, noise, readers, spread)
     wanted = jnp.take(block_owner, listed[0], axis=0)
+    wanted = jnp.concatenate([wanted, swap(wanted, "pa", 1)])
     digits = jnp.concatenate([wanted // LANES, wanted % LANES]).astype(F32)
     note = jnp.pad(digits[None], ((0, 0), (NOTE_AT, LANES - NOTE_AT - digits.shape[0])))
-    by_column = merge_pair(place, keep, swap(send, "pa", 1), spread)
-    *by_column, states = lax.optimization_barrier((*by_column, states))
+    keep, send = retrieve(place, queries, passages, noise, readers, spread)
+    *by_column, place_own = merge_pair(place, keep, swap(send, "pa", 1), spread)
     parts = [by_column[0]] + [swap(by_column[at], "pa", at * PAIR) for at in range(1, spread)]
-    own_key, own_value = project(place, states, key_weight, value_weight, spread)
-    *parts, own_key, own_value = lax.optimization_barrier((*parts, own_key, own_value))
-    by_group = merge_columns(note, parts)
-    by_group, pair_states = lax.optimization_barrier((by_group, pair_states))
+    own_key, own_value, own_done = project(place_own, states, key_weight, value_weight, spread)
+    by_group, place_pair = merge_columns(place, note, own_done, parts)
     mine = lax.all_to_all(by_group, "pb", split_axis=0, concat_axis=0, tiled=True)
-    pair_key, pair_value = project(place, pair_states, key_weight, value_weight, spread)
-    mine, pair_key, pair_value = lax.optimization_barrier((mine, pair_key, pair_value))
+    pair_key, pair_value, pair_done = project(place_pair, pair_states, key_weight, value_weight, spread)
     keys, values = (own_key, pair_key), (own_value, pair_value)
-    kept, sent = condition(place, mine, mix_weight, answer_queries, spread)
+    kept, sent = condition(place, mine, mix_weight, answer_queries, pair_done, spread)
 
     digits = mine[:, 0, queries.shape[1] + NOTE_AT :][:, : digits.shape[0]].astype(jnp.int32)
     slot_ids = digits[:, : wanted.shape[0]] * LANES + digits[:, wanted.shape[0] :]
-    held = slot_ids // slots == runner * readers + group
+    slot_ids = slot_ids.reshape(readers, PAIR, -1)
+    holder = (runner ^ jnp.arange(PAIR, dtype=jnp.int32)) * readers + group
+    held = slot_ids // slots == holder[None, :, None]
     inside = slot_ids % slots
-    chosen = jnp.stack(
+    table = jnp.stack(
         [
-            jnp.min(jnp.where(held, inside, slots - 1), 1),
-            jnp.max(jnp.where(held, inside, 0), 1),
-            jnp.any(held, 1).astype(jnp.int32),
+            jnp.min(jnp.where(held, inside, slots - 1), 2),
+            jnp.max(jnp.where(held, inside, 0), 2),
+            jnp.any(held, 2).astype(jnp.int32),
         ],
-        1,
-    )
-    table = jnp.concatenate([chosen, swap(chosen, "pa", 1)], 1).reshape(-1)
+        2,
+    ).reshape(-1)
 
     pieces = jnp.stack([kept, swap(sent, "pa", 1)])[None]
     step = inner
     while step < readers:
         pieces = jnp.concatenate([pieces, swap(pieces, "pb", step)], 0)
         step *= 2
+    own_pieces = pieces
     pieces = jnp.stack([pieces] + [swap(pieces, "pa", at * PAIR) for at in range(1, spread)])
+    far = [pieces]
+    for offset in range(1, inner):
+        near = swap(own_pieces, "pb", offset)[None]
+        far.append(jnp.concatenate([near, swap(pieces[1:], "pb", offset)], 0))
     lots = []
     for offset in range(inner):
-        query = pieces if offset == 0 else swap(pieces, "pb", offset)
         own = []
         for column in reversed(range(spread)):
-            lot = attend(place, table, query, keys, values, offset, column, inner, tokens, head_width)
+            lot = attend(place, table, far[offset], keys, values, offset, column, inner, tokens, head_width)
             own.append(lot if column == 0 else swap(lot, "pa", column * PAIR))
         lots += own[::-1]
     merged = merge_lots(place, lots, inner, spread, head_width)

time: 128 us -> 126 us (0.984)
  local copies, waits for them, and re-layouts: 20.9 us -> 23.9 us
  waiting for transfers between devices: 17.7 us -> 15.1 us
  blocking collectives: 21.1 us -> 19.1 us
    unnamed x35 -> x37, local copies, waits for them, and re-layouts: 19.9 us -> 22.5 us
    ppermute x11 -> x12, waiting for transfers between devices: 17.5 us -> 15.1 us  [swap(): return lax.ppermute(value, axis, [(at, at ^ bits) for at in range(size)])]
    pallas_call x1, Pallas kernels: 7.44 us -> 5.48 us  [retrieve(): pl.pallas_call(functools.partial(retrieval_kernel, spread=spread), grid_s...]
    all_to_all x1, blocking collectives: 21.1 us -> 19.1 us  [local(): lax.all_to_all(merged, 'pb', split_axis=0, concat_axis=0, tiled=True)]
    ppermute x11 -> x12, starting transfers between devices: 13.5 us -> 13.9 us  [swap(): return lax.ppermute(value, axis, [(at, at ^ bits) for at in range(size)])]
  transfers between devices with their start and end apart: 12 -> 13, of which waited for: 7 -> 6; matrix products, arithmetic and copies ran while one was open for 2% -> 2% of each run, Pallas kernels for 34% -> 34%
where the time goes in v4:
time: 126 us; the launch traced here: 125 us
  Pallas kernels  46.2 us (37%)
  local copies, waits for them, and re-layouts  23.9 us (19%)
  starting transfers between devices  19.7 us (16%)
  blocking collectives  19.1 us (15%)
  waiting for transfers between devices  15.1 us (12%)
    unnamed x37, local copies, waits for them, and re-layouts  22.5 us
    pallas_call x4, Pallas kernels, attend(): pl.pallas_call(functools.partial(attend_kernel, offset=offset, column=col...  19.9 us
    all_to_all x1, blocking collectives, local(): lax.all_to_all(merged, 'pb', split_axis=0, concat_axis=0, tiled=True)  19.1 us
    ppermute x12, waiting for transfers between devices, swap(): return lax.ppermute(value, axis, [(at, at ^ bits) for at in range(size)])  15.1 us
    ppermute x12, starting transfers between devices, swap(): return lax.ppermute(value, axis, [(at, at ^ bits) for at in range(size)])  13.9 us
    pallas_call x2, Pallas kernels, project(): pl.pallas_call(project_kernel, grid_spec=pltpu.PrefetchScalarGridSpec(num...  13.8 us
    all_to_all x1, starting transfers between devices, local(): lax.all_to_all(by_group, 'pb', split_axis=0, concat_axis=0, tiled=True)  5.84 us
    pallas_call x1, Pallas kernels, retrieve(): pl.pallas_call(functools.partial(retrieval_kernel, spread=spread), grid_s...  5.48 us
  transfers between devices with their start and end apart: 13, of which 6 were waited for; matrix products, arithmetic and copies ran while one was open for 2% of the time, Pallas kernels for 34%

profile of v4, /device:TPU:0, one launch (start us, length us, event | category | flops | bytes accessed | tf_op | source)
XLA Modules:
  0.0 125.4 jit_solution(7240945745237071214)
XLA Ops:
  0.5 1.4 %copy-done.14 = bf16[1024,768]{1,0:T(8,128)(2,1)S(1)} copy-done((bf16[1024,768]{1,0:T(8,128)(2,1)S(1)}, bf16[1024,768]{1,0:T(8,128)(2,1)}, u32[]{:S(2)}) %copy-start.14) | copy-done | bytes 1572888
  4.3 5.5 %retrieve.1 = (bf16[2,8,32,896]{3,2,1,0:T(8,128)(2,1)S(1)}, bf16[2,8,32,896]{3,2,1,0:T(8,128)(2,1)}) custom-call(s32[4]{0:T(128)S(1)} %pad_add_fusion.1.place, bf16[1024,768]{1,0:T(8,128)(2,1)S(1)} %copy-done.14, bf16[512,768]{1,0:T(8,128)(2,1)S(1)} %copy-done.16, bf16[1024,512]{1,0:T(8,128)(2,1)S(1)} %copy-done.15), custom_call_target="tpu_custom_call" | custom-call | flops 1610612736 | bytes 4980736 | tf_op jit(solution)/shard_map/retrieve/pallas_call | solution.py:101
  12.5 2.1 %merge_pair.1 = (bf16[8,32,896]{2,1,0:T(8,128)(2,1)S(1)}, bf16[8,32,896]{2,1,0:T(8,128)(2,1)S(1)}, s32[4]{0:T(128)S(1)}) custom-call(s32[4]{0:T(128)S(1)} %pad_add_fusion.1.place, bf16[2,8,32,896]{3,2,1,0:T(8,128)(2,1)S(1)} %get-tuple-element.20.keep, bf16[2,8,32,896]{3,2,1,0:T(8,128)(2,1)S(1)} %collective-permute-done.1.recv), custom_call_target="tpu_custom_call" | custom-call | tf_op jit(solution)/shard_map/merge_pair/pallas_call | solution.py:151
  14.5 2.7 %collective-permute-start.2 = (bf16[8,32,896]{2,1,0:T(8,128)(2,1)S(1)}, bf16[8,32,896]{2,1,0:T(8,128)(2,1)S(1)}, u32[]{:S(2)}, u32[]{:S(2)}) collective-permute-start(bf16[8,32,896]{2,1,0:T(8,128)(2,1)S(1)} %get-tuple-element.25), channel_id=1, source_target_pairs={{0,16},{8,24},{16,0},{24,8},{1,17},{9,25},{17,1},{25,9},{2,18},{10... | collective-permute-start | bytes 1376264 | tf_op jit(solution)/shard_map/ppermute | solution.py:474
  17.4 2.2 %copy-done.9 = bf16[8,256,1024]{2,1,0:T(8,128)(2,1)S(1)} copy-done((bf16[8,256,1024]{2,1,0:T(8,128)(2,1)S(1)}, bf16[8,256,1024]{2,1,0:T(8,128)(2,1)}, u32[]{:S(2)}) %copy-start.9) | copy-done | bytes 4194328
  19.6 1.6 %copy-done.10 = bf16[1024,1024]{1,0:T(8,128)(2,1)S(1)} copy-done((bf16[1024,1024]{1,0:T(8,128)(2,1)S(1)}, bf16[1024,1024]{1,0:T(8,128)(2,1)}, u32[]{:S(2)}) %copy-start.10) | copy-done | bytes 2097176
  21.2 1.6 %copy-done.12 = bf16[1024,1024]{1,0:T(8,128)(2,1)S(1)} copy-done((bf16[1024,1024]{1,0:T(8,128)(2,1)S(1)}, bf16[1024,1024]{1,0:T(8,128)(2,1)}, u32[]{:S(2)}) %copy-start.12) | copy-done | bytes 2097176
  22.8 6.4 %project.2 = (bf16[2048,512]{1,0:T(8,128)(2,1)S(1)}, bf16[512,2048]{1,0:T(8,128)(2,1)S(1)}, f32[8,128]{1,0:T(8,128)S(1)}) custom-call(s32[4]{0:T(128)S(1)} %get-tuple-element.22.place, bf16[2048,1024]{1,0:T(8,128)(2,1)S(1)} %bitcast.33, bf16[1024,1024]{1,0:T(8,128)(2,1)S(1)} %copy-done.10, bf16[1024,1024]{1,0:T(8,128)(2,1)S(1)} %copy-done.10, ...), custom_call_target="tpu_custom_call" | custom-call | flops 4294967296 | bytes 10485760 | tf_op jit(solution)/shard_map/project/pallas_call | solution.py:244
  29.1 1.4 %copy-done.1 = bf16[512,2048]{1,0:T(8,128)(2,1)} copy-done((bf16[512,2048]{1,0:T(8,128)(2,1)}, bf16[512,2048]{1,0:T(8,128)(2,1)S(1)}, u32[]{:S(2)}) %copy-start.1) | copy-done | bytes 2097176
  30.5 1.9 %merge_columns.1 = (bf16[8,32,896]{2,1,0:T(8,128)(2,1)}, s32[4]{0:T(128)S(1)}) custom-call(s32[4]{0:T(128)S(1)} %pad_add_fusion.1.place, f32[1,128]{1,0:T(1,128)S(1)} %pad.4.note, f32[8,128]{1,0:T(8,128)S(1)} %get-tuple-element.23.done, bf16[8,32,896]{2,1,0:T(8,128)(2,1)S(1)} %get-tuple-element.24.refs_0_, bf16[8,32,896]{2,1,0:T(8,128)(2,1)S(1)} %collective-permute-done.2.refs_1_), custom_call_target="tpu_custom_call" | custom-call | tf_op jit(solution)/shard_map/merge_columns/pallas_call | solution.py:172
  32.4 5.8 %all-to-all-start = ((bf16[8,32,896]{2,1,0:T(8,128)(2,1)}), bf16[8,32,896]{2,1,0:T(8,128)(2,1)S(1)}, u32[]{:S(2)}, u32[]{:S(2)}) async-start(bf16[8,32,896]{2,1,0:T(8,128)(2,1)} %get-tuple-element.26), calls=%async_computation | async-start | bytes 917504 | tf_op jit(solution)/shard_map/all_to_all | solution.py:488
  38.2 1.6 %copy-done.11 = bf16[1024,1024]{1,0:T(8,128)(2,1)S(1)} copy-done((bf16[1024,1024]{1,0:T(8,128)(2,1)S(1)}, bf16[1024,1024]{1,0:T(8,128)(2,1)}, u32[]{:S(2)}) %copy-start.11) | copy-done | bytes 2097176
  39.8 1.6 %copy-done.13 = bf16[1024,1024]{1,0:T(8,128)(2,1)S(1)} copy-done((bf16[1024,1024]{1,0:T(8,128)(2,1)S(1)}, bf16[1024,1024]{1,0:T(8,128)(2,1)}, u32[]{:S(2)}) %copy-start.13) | copy-done | bytes 2097176
  41.4 7.4 %project.3 = (bf16[2048,512]{1,0:T(8,128)(2,1)S(1)}, bf16[512,2048]{1,0:T(8,128)(2,1)S(1)}, f32[8,128]{1,0:T(8,128)S(1)}) custom-call(s32[4]{0:T(128)S(1)} %get-tuple-element.27.place, bf16[2048,1024]{1,0:T(8,128)(2,1)} %collective-permute-done.3.states, bf16[1024,1024]{1,0:T(8,128)(2,1)S(1)} %copy-done.11, bf16[1024,1024]{1,0:T(8,128)(2,1)S(1)} %copy-done.11, ...), custom_call_target="tpu_custom_call" | custom-call | flops 4294967296 | bytes 10485760 | tf_op jit(solution)/shard_map/project/pallas_call | solution.py:244
  48.9 1.4 %copy-done.3 = bf16[2048,512]{1,0:T(8,128)(2,1)} copy-done((bf16[2048,512]{1,0:T(8,128)(2,1)}, bf16[2048,512]{1,0:T(8,128)(2,1)S(1)}, u32[]{:S(2)}) %copy-start.3) | copy-done | bytes 2097176
  50.2 1.3 %copy-done.5 = bf16[512,2048]{1,0:T(8,128)(2,1)} copy-done((bf16[512,2048]{1,0:T(8,128)(2,1)}, bf16[512,2048]{1,0:T(8,128)(2,1)S(1)}, u32[]{:S(2)}) %copy-start.5) | copy-done | bytes 2097176
  51.5 1.4 %copy-done.7 = bf16[768,1024]{1,0:T(8,128)(2,1)S(1)} copy-done((bf16[768,1024]{1,0:T(8,128)(2,1)S(1)}, bf16[768,1024]{1,0:T(8,128)(2,1)}, u32[]{:S(2)}) %copy-start.7) | copy-done | bytes 1572888
  55.4 2.1 %collective-permute-start.5 = (bf16[1,2,32,512]{3,2,1,0:T(8,128)(2,1)S(1)}, bf16[1,2,32,512]{3,2,1,0:T(8,128)(2,1)S(1)}, u32[]{:S(2)}, u32[]{:S(2)}) collective-permute-start(bf16[1,2,32,512]{3,2,1,0:T(8,128)(2,1)S(1)} %maximum_bitcast_fusion), channel_id=1, source_target_pairs={{0,2},{1,3},{2,0},{3,1},{4,6},{5,7},{6,4},{7,5},{8,10},{9,11},{10,... | collective-permute-start | bytes 196616 | tf_op jit(solution)/shard_map/ppermute | solution.py:474
  57.5 2.4 %collective-permute-done.5 = bf16[1,2,32,512]{3,2,1,0:T(8,128)(2,1)S(1)} collective-permute-done((bf16[1,2,32,512]{3,2,1,0:T(8,128)(2,1)S(1)}, bf16[1,2,32,512]{3,2,1,0:T(8,128)(2,1)S(1)}, u32[]{:S(2)}, u32[]{:S(2)}) %collective-permute-start.5) | collective-permute-done | bytes 65568 | tf_op jit(solution)/shard_map/ppermute | solution.py:474
  59.9 2.9 %collective-permute-start.6 = (bf16[2,2,32,512]{3,2,1,0:T(8,128)(2,1)S(1)}, bf16[2,2,32,512]{3,2,1,0:T(8,128)(2,1)S(1)}, u32[]{:S(2)}, u32[]{:S(2)}) collective-permute-start(bf16[2,2,32,512]{3,2,1,0:T(8,128)(2,1)S(1)} %pad_maximum_fusion.3), channel_id=1, source_target_pairs={{0,4},{1,5},{2,6},{3,7},{4,0},{5,1},{6,2},{7,3},{8,12},{9,13},{10,... | collective-permute-start | bytes 393224 | tf_op jit(solution)/shard_map/ppermute | solution.py:474
  62.9 5.8 %collective-permute-done.6 = bf16[2,2,32,512]{3,2,1,0:T(8,128)(2,1)S(1)} collective-permute-done((bf16[2,2,32,512]{3,2,1,0:T(8,128)(2,1)S(1)}, bf16[2,2,32,512]{3,2,1,0:T(8,128)(2,1)S(1)}, u32[]{:S(2)}, u32[]{:S(2)}) %collective-permute-start.6) | collective-permute-done | bytes 131104 | tf_op jit(solution)/shard_map/ppermute | solution.py:474
  70.4 1.3 %collective-permute-start.9 = (bf16[4,2,32,512]{3,2,1,0:T(8,128)(2,1)S(1)}, bf16[4,2,32,512]{3,2,1,0:T(8,128)(2,1)S(1)}, u32[]{:S(2)}, u32[]{:S(2)}) collective-permute-start(bf16[4,2,32,512]{3,2,1,0:T(8,128)(2,1)S(1)} %get-tuple-element.41), channel_id=1, source_target_pairs={{0,1},{1,0},{2,3},{3,2},{4,5},{5,4},{6,7},{7,6},{8,9},{9,8},{10,11... | collective-permute-start | bytes 786440 | tf_op jit(solution)/shard_map/ppermute | solution.py:474
  71.7 4.5 %collective-permute-done.7 = bf16[4,2,32,512]{3,2,1,0:T(8,128)(2,1)S(1)} collective-permute-done((bf16[4,2,32,512]{3,2,1,0:T(8,128)(2,1)S(1)}, bf16[4,2,32,512]{3,2,1,0:T(8,128)(2,1)S(1)}, u32[]{:S(2)}, u32[]{:S(2)}) %collective-permute-start.7) | collective-permute-done | bytes 262176 | tf_op jit(solution)/shard_map/ppermute | solution.py:474
  77.4 1.6 %copy-done.2 = bf16[512,2048]{1,0:T(8,128)(2,1)S(1)} copy-done((bf16[512,2048]{1,0:T(8,128)(2,1)S(1)}, bf16[512,2048]{1,0:T(8,128)(2,1)}, u32[]{:S(2)}) %copy-start.2) | copy-done | bytes 2097176
  78.9 1.6 %copy-done.4 = bf16[2048,512]{1,0:T(8,128)(2,1)S(1)} copy-done((bf16[2048,512]{1,0:T(8,128)(2,1)S(1)}, bf16[2048,512]{1,0:T(8,128)(2,1)}, u32[]{:S(2)}) %copy-start.4) | copy-done | bytes 2097176
  80.5 1.6 %copy-done.6 = bf16[512,2048]{1,0:T(8,128)(2,1)S(1)} copy-done((bf16[512,2048]{1,0:T(8,128)(2,1)S(1)}, bf16[512,2048]{1,0:T(8,128)(2,1)}, u32[]{:S(2)}) %copy-start.6) | copy-done | bytes 2097176
  82.1 4.9 %attend.5 = bf16[4,288,128]{2,1,0:T(8,128)(2,1)S(1)} custom-call(s32[4]{0:T(128)S(1)} %pad_add_fusion.1.place, s32[48]{0:T(128)S(1)} %reshape.116.table, bf16[2,4,2,32,512]{4,3,2,1,0:T(8,128)(2,1)S(1)} %pad_maximum_fusion.pieces, bf16[2048,512]{1,0:T(8,128)(2,1)S(1)} %get-tuple-element.31.key_own, bf16[2048,512]{1,0:T(8,128)(2,1)S(1)} %copy-done.4, ...), custom_call_target="tpu_custom_call" | custom-call | flops 2147483648 | bytes 294912 | tf_op jit(solution)/shard_map/attend/pallas_call | solution.py:346
  87.7 4.9 %attend.7 = bf16[4,288,128]{2,1,0:T(8,128)(2,1)S(1)} custom-call(s32[4]{0:T(128)S(1)} %pad_add_fusion.1.place, s32[48]{0:T(128)S(1)} %reshape.116.table, bf16[2,4,2,32,512]{4,3,2,1,0:T(8,128)(2,1)S(1)} %pad_maximum_fusion.1.pieces, bf16[2048,512]{1,0:T(8,128)(2,1)S(1)} %get-tuple-element.31.key_own, bf16[2048,512]{1,0:T(8,128)(2,1)S(1)} %copy-done.4, ...), custom_call_target="tpu_custom_call" | custom-call | flops 2147483648 | bytes 294912 | tf_op jit(solution)/shard_map/attend/pallas_call | solution.py:346
  92.6 1.5 %collective-permute-start.11 = (bf16[4,288,128]{2,1,0:T(8,128)(2,1)S(1)}, bf16[4,288,128]{2,1,0:T(8,128)(2,1)S(1)}, u32[]{:S(2)}, u32[]{:S(2)}) collective-permute-start(bf16[4,288,128]{2,1,0:T(8,128)(2,1)S(1)} %attend.7), channel_id=1, source_target_pairs={{0,16},{8,24},{16,0},{24,8},{1,17},{9,25},{17,1},{25,9},{2,18},{10... | collective-permute-start | bytes 884744 | tf_op jit(solution)/shard_map/ppermute | solution.py:474
  94.2 5.1 %attend.4.refs_0_ = bf16[4,288,128]{2,1,0:T(8,128)(2,1)S(1)} custom-call(s32[4]{0:T(128)S(1)} %pad_add_fusion.1.place, s32[48]{0:T(128)S(1)} %reshape.116.table, bf16[2,4,2,32,512]{4,3,2,1,0:T(8,128)(2,1)S(1)} %pad_maximum_fusion.pieces, bf16[2048,512]{1,0:T(8,128)(2,1)S(1)} %get-tuple-element.31.key_own, bf16[2048,512]{1,0:T(8,128)(2,1)S(1)} %copy-done.4, ...), custom_call_target="tpu_custom_call" | custom-call | flops 2147483648 | bytes 294912 | tf_op jit(solution)/shard_map/attend/pallas_call | solution.py:346
  99.3 4.9 %attend.6.refs_2_ = bf16[4,288,128]{2,1,0:T(8,128)(2,1)S(1)} custom-call(s32[4]{0:T(128)S(1)} %pad_add_fusion.1.place, s32[48]{0:T(128)S(1)} %reshape.116.table, bf16[2,4,2,32,512]{4,3,2,1,0:T(8,128)(2,1)S(1)} %pad_maximum_fusion.1.pieces, bf16[2048,512]{1,0:T(8,128)(2,1)S(1)} %get-tuple-element.31.key_own, bf16[2048,512]{1,0:T(8,128)(2,1)S(1)} %copy-done.4, ...), custom_call_target="tpu_custom_call" | custom-call | flops 2147483648 | bytes 294912 | tf_op jit(solution)/shard_map/attend/pallas_call | solution.py:346
  105.4 19.1 %all_to_all.10.parts = bf16[8,288,128]{2,1,0:T(8,128)(2,1)S(1)} all-to-all(bf16[8,288,128]{2,1,0:T(8,128)(2,1)S(1)} %bitcast.30), channel_id=1, replica_groups=mesh['pa'=4,'pb'=8] {'pb'}, dimensions={0} | all-to-all | bytes 1179648 | tf_op jit(solution)/shard_map/all_to_all | solution.py:528
  (72 shorter events, 13.8 us)
Async XLA Ops:
  0.0 9.9 %copy-start = (s32[256]{0:T(256)S(1)}, s32[256]{0:T(256)}, u32[]{:S(2)}) copy-start(s32[256]{0:T(256)} %param.18) | copy-start | bytes 3076
  0.0 38.2 %collective-permute-start.3 = (bf16[2048,1024]{1,0:T(8,128)(2,1)}, bf16[2048,1024]{1,0:T(8,128)(2,1)}, u32[]{:S(2)}, u32[]{:S(2)}) collective-permute-start(bf16[2048,1024]{1,0:T(8,128)(2,1)} %bitcast.32), channel_id=1, source_target_pairs={{0,8},{8,0},{16,24},{24,16},{1,9},{9,1},{17,25},{25,17},{2,10},{10... | collective-permute-start | bytes 12582920 | tf_op jit(solution)/shard_map/ppermute | solution.py:474
  0.5 1.4 %copy-start.14 = (bf16[1024,768]{1,0:T(8,128)(2,1)S(1)}, bf16[1024,768]{1,0:T(8,128)(2,1)}, u32[]{:S(2)}) copy-start(bf16[1024,768]{1,0:T(8,128)(2,1)} %queries.1) | copy-start | bytes 4718596
  1.9 1.2 copy-start.15
  3.2 1.1 copy-start.16
  4.3 5.5 %copy-start.17 = (s32[1,16]{1,0:T(1,128)S(1)}, s32[1,16]{1,0:T(1,128)}, u32[]{:S(2)}) copy-start(s32[1,16]{1,0:T(1,128)} %param.19) | copy-start | bytes 196
  9.8 2.7 %collective-permute-start.1 = (bf16[2,8,32,896]{3,2,1,0:T(8,128)(2,1)}, bf16[2,8,32,896]{3,2,1,0:T(8,128)(2,1)S(1)}, u32[]{:S(2)}, u32[]{:S(2)}) collective-permute-start(bf16[2,8,32,896]{3,2,1,0:T(8,128)(2,1)} %get-tuple-element.21), channel_id=1, source_target_pairs={{0,8},{8,0},{16,24},{24,16},{1,9},{9,1},{17,25},{25,17},{2,10},{10... | collective-permute-start | bytes 2752520 | tf_op jit(solution)/shard_map/ppermute | solution.py:474
  10.5 1.7 %collective-permute-start = (s32[16]{0:T(128)S(1)}, s32[16]{0:T(128)S(1)}, u32[]{:S(2)}, u32[]{:S(2)}) collective-permute-start(s32[16]{0:T(128)S(1)} %and_select_fusion.4), channel_id=1, source_target_pairs={{0,8},{8,0},{16,24},{24,16},{1,9},{9,1},{17,25},{25,17},{2,10},{10... | collective-permute-start | bytes 200 | tf_op jit(solution)/shard_map/ppermute | solution.py:474
  14.5 16.0 %collective-permute-start.2 = (bf16[8,32,896]{2,1,0:T(8,128)(2,1)S(1)}, bf16[8,32,896]{2,1,0:T(8,128)(2,1)S(1)}, u32[]{:S(2)}, u32[]{:S(2)}) collective-permute-start(bf16[8,32,896]{2,1,0:T(8,128)(2,1)S(1)} %get-tuple-element.25), channel_id=1, source_target_pairs={{0,16},{8,24},{16,0},{24,8},{1,17},{9,25},{17,1},{25,9},{2,18},{10... | collective-permute-start | bytes 1376264 | tf_op jit(solution)/shard_map/ppermute | solution.py:474
  17.4 2.2 %copy-start.9 = (bf16[8,256,1024]{2,1,0:T(8,128)(2,1)S(1)}, bf16[8,256,1024]{2,1,0:T(8,128)(2,1)}, u32[]{:S(2)}) copy-start(bf16[8,256,1024]{2,1,0:T(8,128)(2,1)} %param.17) | copy-start | bytes 12582916
  19.6 1.6 %copy-start.10 = (bf16[1024,1024]{1,0:T(8,128)(2,1)S(1)}, bf16[1024,1024]{1,0:T(8,128)(2,1)}, u32[]{:S(2)}) copy-start(bf16[1024,1024]{1,0:T(8,128)(2,1)} %refs_1_.3) | copy-start | bytes 6291460
  21.2 1.6 %copy-start.12 = (bf16[1024,1024]{1,0:T(8,128)(2,1)S(1)}, bf16[1024,1024]{1,0:T(8,128)(2,1)}, u32[]{:S(2)}) copy-start(bf16[1024,1024]{1,0:T(8,128)(2,1)} %refs_3_.3) | copy-start | bytes 6291460
  29.1 1.4 %copy-start.1 = (bf16[512,2048]{1,0:T(8,128)(2,1)}, bf16[512,2048]{1,0:T(8,128)(2,1)S(1)}, u32[]{:S(2)}) copy-start(bf16[512,2048]{1,0:T(8,128)(2,1)S(1)} %get-tuple-element.33.value_own) | copy-start | bytes 6291460
  32.4 19.2 %all-to-all-start = ((bf16[8,32,896]{2,1,0:T(8,128)(2,1)}), bf16[8,32,896]{2,1,0:T(8,128)(2,1)S(1)}, u32[]{:S(2)}, u32[]{:S(2)}) async-start(bf16[8,32,896]{2,1,0:T(8,128)(2,1)} %get-tuple-element.26), calls=%async_computation | async-start | bytes 917504 | tf_op jit(solution)/shard_map/all_to_all | solution.py:488
  38.2 1.6 %copy-start.11 = (bf16[1024,1024]{1,0:T(8,128)(2,1)S(1)}, bf16[1024,1024]{1,0:T(8,128)(2,1)}, u32[]{:S(2)}) copy-start(bf16[1024,1024]{1,0:T(8,128)(2,1)} %refs_1_.3) | copy-start | bytes 6291460
  39.8 1.6 %copy-start.13 = (bf16[1024,1024]{1,0:T(8,128)(2,1)S(1)}, bf16[1024,1024]{1,0:T(8,128)(2,1)}, u32[]{:S(2)}) copy-start(bf16[1024,1024]{1,0:T(8,128)(2,1)} %refs_3_.3) | copy-start | bytes 6291460
  41.4 10.2 %copy-start.8 = (bf16[128,1024]{1,0:T(8,128)(2,1)S(1)}, bf16[128,1024]{1,0:T(8,128)(2,1)}, u32[]{:S(2)}) copy-start(bf16[128,1024]{1,0:T(8,128)(2,1)} %answers.1) | copy-start | bytes 786436
  48.9 1.4 %copy-start.3 = (bf16[2048,512]{1,0:T(8,128)(2,1)}, bf16[2048,512]{1,0:T(8,128)(2,1)S(1)}, u32[]{:S(2)}) copy-start(bf16[2048,512]{1,0:T(8,128)(2,1)S(1)} %get-tuple-element.32.key_pair) | copy-start | bytes 6291460
  50.2 1.3 %copy-start.5 = (bf16[512,2048]{1,0:T(8,128)(2,1)}, bf16[512,2048]{1,0:T(8,128)(2,1)S(1)}, u32[]{:S(2)}) copy-start(bf16[512,2048]{1,0:T(8,128)(2,1)S(1)} %get-tuple-element.34.value_pair) | copy-start | bytes 6291460
  51.5 1.4 %copy-start.7 = (bf16[768,1024]{1,0:T(8,128)(2,1)S(1)}, bf16[768,1024]{1,0:T(8,128)(2,1)}, u32[]{:S(2)}) copy-start(bf16[768,1024]{1,0:T(8,128)(2,1)} %mix_weight.1) | copy-start | bytes 4718596
  54.1 1.3 %collective-permute-start.4 = (bf16[32,512]{1,0:T(8,128)(2,1)S(1)}, bf16[32,512]{1,0:T(8,128)(2,1)S(1)}, u32[]{:S(2)}, u32[]{:S(2)}) collective-permute-start(bf16[32,512]{1,0:T(8,128)(2,1)S(1)} %get-tuple-element.30), channel_id=1, source_target_pairs={{0,8},{8,0},{16,24},{24,16},{1,9},{9,1},{17,25},{25,17},{2,10},{10... | collective-permute-start | bytes 98312 | tf_op jit(solution)/shard_map/ppermute | solution.py:474
  55.4 4.5 %collective-permute-start.5 = (bf16[1,2,32,512]{3,2,1,0:T(8,128)(2,1)S(1)}, bf16[1,2,32,512]{3,2,1,0:T(8,128)(2,1)S(1)}, u32[]{:S(2)}, u32[]{:S(2)}) collective-permute-start(bf16[1,2,32,512]{3,2,1,0:T(8,128)(2,1)S(1)} %maximum_bitcast_fusion), channel_id=1, source_target_pairs={{0,2},{1,3},{2,0},{3,1},{4,6},{5,7},{6,4},{7,5},{8,10},{9,11},{10,... | collective-permute-start | bytes 196616 | tf_op jit(solution)/shard_map/ppermute | solution.py:474
  59.9 8.8 %collective-permute-start.6 = (bf16[2,2,32,512]{3,2,1,0:T(8,128)(2,1)S(1)}, bf16[2,2,32,512]{3,2,1,0:T(8,128)(2,1)S(1)}, u32[]{:S(2)}, u32[]{:S(2)}) collective-permute-start(bf16[2,2,32,512]{3,2,1,0:T(8,128)(2,1)S(1)} %pad_maximum_fusion.3), channel_id=1, source_target_pairs={{0,4},{1,5},{2,6},{3,7},{4,0},{5,1},{6,2},{7,3},{8,12},{9,13},{10,... | collective-permute-start | bytes 393224 | tf_op jit(solution)/shard_map/ppermute | solution.py:474
  68.7 7.5 %collective-permute-start.7 = (bf16[4,2,32,512]{3,2,1,0:T(8,128)(2,1)S(1)}, bf16[4,2,32,512]{3,2,1,0:T(8,128)(2,1)S(1)}, u32[]{:S(2)}, u32[]{:S(2)}) collective-permute-start(bf16[4,2,32,512]{3,2,1,0:T(8,128)(2,1)S(1)} %get-tuple-element.41), channel_id=1, source_target_pairs={{0,16},{8,24},{16,0},{24,8},{1,17},{9,25},{17,1},{25,9},{2,18},{10... | collective-permute-start | bytes 786440 | tf_op jit(solution)/shard_map/ppermute | solution.py:474
  70.4 17.3 %collective-permute-start.9 = (bf16[4,2,32,512]{3,2,1,0:T(8,128)(2,1)S(1)}, bf16[4,2,32,512]{3,2,1,0:T(8,128)(2,1)S(1)}, u32[]{:S(2)}, u32[]{:S(2)}) collective-permute-start(bf16[4,2,32,512]{3,2,1,0:T(8,128)(2,1)S(1)} %get-tuple-element.41), channel_id=1, source_target_pairs={{0,1},{1,0},{2,3},{3,2},{4,5},{5,4},{6,7},{7,6},{8,9},{9,8},{10,11... | collective-permute-start | bytes 786440 | tf_op jit(solution)/shard_map/ppermute | solution.py:474
  76.2 11.4 %collective-permute-start.10 = (bf16[1,4,2,32,512]{4,3,2,1,0:T(8,128)(2,1)S(1)}, bf16[1,4,2,32,512]{4,3,2,1,0:T(8,128)(2,1)S(1)}, u32[]{:S(2)}, u32[]{:S(2)}) collective-permute-start(bf16[1,4,2,32,512]{4,3,2,1,0:T(8,128)(2,1)S(1)} %bitcast.34), channel_id=1, source_target_pairs={{0,1},{1,0},{2,3},{3,2},{4,5},{5,4},{6,7},{7,6},{8,9},{9,8},{10,11... | collective-permute-start | bytes 786440 | tf_op jit(solution)/shard_map/ppermute | solution.py:474
  77.4 1.6 %copy-start.2 = (bf16[512,2048]{1,0:T(8,128)(2,1)S(1)}, bf16[512,2048]{1,0:T(8,128)(2,1)}, u32[]{:S(2)}) copy-start(bf16[512,2048]{1,0:T(8,128)(2,1)} %copy-done.1) | copy-start | bytes 6291460
  78.9 1.6 %copy-start.4 = (bf16[2048,512]{1,0:T(8,128)(2,1)S(1)}, bf16[2048,512]{1,0:T(8,128)(2,1)}, u32[]{:S(2)}) copy-start(bf16[2048,512]{1,0:T(8,128)(2,1)} %copy-done.3) | copy-start | bytes 6291460
  80.5 1.6 %copy-start.6 = (bf16[512,2048]{1,0:T(8,128)(2,1)S(1)}, bf16[512,2048]{1,0:T(8,128)(2,1)}, u32[]{:S(2)}) copy-start(bf16[512,2048]{1,0:T(8,128)(2,1)} %copy-done.5) | copy-start | bytes 6291460
  87.0 17.2 %collective-permute-start.8 = (bf16[4,288,128]{2,1,0:T(8,128)(2,1)S(1)}, bf16[4,288,128]{2,1,0:T(8,128)(2,1)S(1)}, u32[]{:S(2)}, u32[]{:S(2)}) collective-permute-start(bf16[4,288,128]{2,1,0:T(8,128)(2,1)S(1)} %attend.5), channel_id=1, source_target_pairs={{0,16},{8,24},{16,0},{24,8},{1,17},{9,25},{17,1},{25,9},{2,18},{10... | collective-permute-start | bytes 884744 | tf_op jit(solution)/shard_map/ppermute | solution.py:474
  92.6 11.6 %collective-permute-start.11 = (bf16[4,288,128]{2,1,0:T(8,128)(2,1)S(1)}, bf16[4,288,128]{2,1,0:T(8,128)(2,1)S(1)}, u32[]{:S(2)}, u32[]{:S(2)}) collective-permute-start(bf16[4,288,128]{2,1,0:T(8,128)(2,1)S(1)} %attend.7), channel_id=1, source_target_pairs={{0,16},{8,24},{16,0},{24,8},{1,17},{9,25},{17,1},{25,9},{2,18},{10... | collective-permute-start | bytes 884744 | tf_op jit(solution)/shard_map/ppermute | solution.py:474

commit v5 on v4

--- a/solution.py
+++ b/solution.py
@@ -9,6 +9,7 @@
 
 HEADS = 16
 PAIR = 2
+CAP = 2
 TEMPER = 0.5
 FLOOR = -1e30
 LANES = 128
@@ -16,10 +17,9 @@
 NOTE_AT = 6
 STEP_GROUPS = 2
 PROJECT_STEPS = 4
-ATTEND_GROUPS = 4
 HEAD_BUNDLE = 2
 VMEM_BYTES = 16 * 1024 * 1024
-WIDE_BYTES = 24 * 1024 * 1024
+WIDE_BYTES = 60 * 1024 * 1024
 F32 = jnp.float32
 BF16 = jnp.bfloat16
 NT = (((1,), (1,)), ((), ()))
@@ -258,7 +258,7 @@
             jax.ShapeDtypeStruct((spread * width, rows), BF16),
             jax.ShapeDtypeStruct((8, LANES), F32),
         ],
-        compiler_params=grant(),
+        compiler_params=pltpu.CompilerParams(vmem_limit_bytes=WIDE_BYTES),
         cost_estimate=pl.CostEstimate(
             flops=4 * rows * model_width * spread * width,
             bytes_accessed=2 * (2 * model_width * spread * width + 2 * rows * model_width),
@@ -268,7 +268,7 @@
     )(place, states, *([key_weight] * spread), *([value_weight] * spread))
 
 
-def attend_group(z, place, table, pieces, keys, values, out, row, offset, column, inner, tokens, head_width):
+def attend_group(z, place, table, pieces, blocks_in, out, offset, column, inner, head_width):
     relative = lax.bitwise_xor(z, place[3])
     spread, rows = pieces.shape[0], out.shape[2]
     width = out.shape[1] - STAT_ROWS
@@ -286,12 +286,8 @@
     bundle = min(HEAD_BUNDLE, count)
     shelves = []
     for shelf in range(PAIR):
-        starts = [
-            pl.multiple_of(table[entry * 6 + shelf * 3 + at] * tokens, tokens) for at in range(2)
-        ]
         scores = [
-            jnp.dot(keys[shelf][pl.ds(start, tokens), pl.ds(left, width)], spaced, preferred_element_type=F32)
-            for start in starts
+            jnp.dot(blocks_in[shelf][at][0][...], spaced, preferred_element_type=F32) for at in range(CAP)
         ]
         high = functools.reduce(jnp.maximum, [jnp.max(score, 0, keepdims=True) for score in scores])
         exponents = [jnp.exp(score - high) for score in scores]
@@ -300,10 +296,8 @@
         there = table[entry * 6 + shelf * 3 + 2] > 0
         blocks = []
         for first in range(0, count, bundle):
-            top = pl.multiple_of(left + first * head_width, bundle * head_width)
-            value = jnp.concatenate(
-                [values[shelf][pl.ds(top, bundle * head_width), pl.ds(start, tokens)] for start in starts], 1
-            )
+            here = slice(first * head_width, (first + bundle) * head_width)
+            value = jnp.concatenate([blocks_in[shelf][at][1][here, :] for at in range(CAP)], 1)
             mixed = jnp.dot(value, probs[:, first * rows : (first + bundle) * rows], preferred_element_type=F32)
             for head in range(bundle):
                 blocks.append(
@@ -316,15 +310,35 @@
     for head in range(count):
         here = slice(head * rows, (head + 1) * rows)
         joined = sum(shelf[2][head] * factor[:, here] for shelf, factor in zip(shelves, factors))
-        out[row, head * head_width : (head + 1) * head_width, :] = joined.astype(BF16)
-    out[row, width:, :] = pack_stats(high, total, count, rows)
-
-
-def attend_kernel(place, table, pieces, key_own, key_pair, value_own, value_pair, out, **fixed):
-    step = out.shape[0]
-    for row in range(step):
-        z = pl.program_id(0) * step + row
-        attend_group(z, place, table, pieces, (key_own, key_pair), (value_own, value_pair), out, row, **fixed)
+        out[z, head * head_width : (head + 1) * head_width, :] = joined.astype(BF16)
+    out[z, width:, :] = pack_stats(high, total, count, rows)
+
+
+def attend_kernel(
+    place, table, pieces, key_own, key_pair, value_own, value_pair, out, held, turned, arrived, *, offset, column, inner, head_width
+):
+    outer = out.shape[0]
+    tokens, width = held.shape[3:]
+    left = pl.multiple_of(lax.bitwise_xor(place[1], column) * width, width)
+    copies = []
+    for z in range(outer):
+        entry = z * inner + lax.bitwise_xor(place[2], offset)
+        for shelf, (keys, values) in enumerate(((key_own, value_own), (key_pair, value_pair))):
+            for at in range(CAP):
+                start = pl.multiple_of(table[entry * 6 + shelf * 3 + at] * tokens, tokens)
+                source = keys.at[pl.ds(start, tokens), pl.ds(left, width)]
+                lead = (z, shelf, at)
+                copies.append(pltpu.make_async_copy(source, held.at[lead], arrived.at[lead + (0,)]))
+                source = values.at[pl.ds(left, width), pl.ds(start, tokens)]
+                copies.append(pltpu.make_async_copy(source, turned.at[lead], arrived.at[lead + (1,)]))
+    for copy in copies:
+        copy.start()
+    each = len(copies) // outer
+    for z in range(outer):
+        for copy in copies[z * each : (z + 1) * each]:
+            copy.wait()
+        blocks_in = [[(held.at[z, shelf, at], turned.at[z, shelf, at]) for at in range(CAP)] for shelf in range(PAIR)]
+        attend_group(z, place, table, pieces, blocks_in, out, offset, column, inner, head_width)
 
 
 def pack_stats(high, total, count, rows):
@@ -341,20 +355,20 @@
     spread, outer, pair, part, half = pieces.shape
     width = half // spread
     rows = spread * pair * part
-    at_once = min(ATTEND_GROUPS, outer)
     whole = pl.BlockSpec(memory_space=pltpu.VMEM)
-    return pl.pallas_call(
-        functools.partial(
-            attend_kernel, offset=offset, column=column, inner=inner, tokens=tokens, head_width=head_width
-        ),
-        grid_spec=pltpu.PrefetchScalarGridSpec(
-            num_scalar_prefetch=2,
-            grid=(outer // at_once,),
-            in_specs=[whole] * 5,
-            out_specs=pl.BlockSpec((at_once, width + STAT_ROWS, rows), lambda z, place, table: (z, 0, 0)),
-        ),
+    scalars = pl.BlockSpec(memory_space=pltpu.SMEM)
+    apart = pl.BlockSpec(memory_space=pl.ANY)
+    return pl.pallas_call(
+        functools.partial(attend_kernel, offset=offset, column=column, inner=inner, head_width=head_width),
+        in_specs=[scalars, scalars, whole] + [apart] * 4,
+        out_specs=whole,
+        scratch_shapes=[
+            pltpu.VMEM((outer, PAIR, CAP, tokens, width), BF16),
+            pltpu.VMEM((outer, PAIR, CAP, width, tokens), BF16),
+            pltpu.SemaphoreType.DMA((outer, PAIR, CAP, 2)),
+        ],
         out_shape=jax.ShapeDtypeStruct((outer, width + STAT_ROWS, rows), BF16),
-        compiler_params=grant(),
+        compiler_params=pltpu.CompilerParams(vmem_limit_bytes=WIDE_BYTES),
         cost_estimate=pl.CostEstimate(
             flops=outer * 4 * 4 * rows * tokens * width * (width // head_width),
             bytes_accessed=outer * 2 * (width + STAT_ROWS) * rows,
@@ -419,7 +433,7 @@
             out_specs=pl.BlockSpec((1, inner, height, rows), lambda z, place: (z, 0, 0, 0)),
         ),
         out_shape=jax.ShapeDtypeStruct((outer, inner, height, rows), BF16),
-        compiler_params=grant(),
+        compiler_params=pltpu.CompilerParams(vmem_limit_bytes=WIDE_BYTES),
         name="merge_lots",
     )(place, *parts)
 

time: 126 us -> 139 us (1.10)
  Pallas kernels: 46.2 us -> 69.7 us
  local copies, waits for them, and re-layouts: 23.9 us -> 6.5 us
  waiting for transfers between devices: 15.1 us -> 21.6 us
  other arithmetic: 1.14 us -> 3.24 us
    unnamed x37 -> x25, local copies, waits for them, and re-layouts: 22.5 us -> 4.64 us
    pallas_call x4, Pallas kernels: 19.9 us -> 33.7 us  [attend(): pl.pallas_call(functools.partial(attend_kernel, offset=offset, column=col...]
    pallas_call x2, Pallas kernels: 13.8 us -> 18.3 us  [project(): pl.pallas_call(project_kernel, grid_spec=pltpu.PrefetchScalarGridSpec(num...]
    all_to_all x1, waiting for transfers between devices: 0.01 us -> 3.61 us  [local(): lax.all_to_all(by_group, 'pb', split_axis=0, concat_axis=0, tiled=True)]
    pallas_call x1, Pallas kernels: 1.1 us -> 4.26 us  [merge_lots(): pl.pallas_call(functools.partial(gather_kernel, inner=inner, spread=sprea...]
    ppermute x12, waiting for transfers between devices: 15.1 us -> 18 us  [swap(): return lax.ppermute(value, axis, [(at, at ^ bits) for at in range(size)])]
    pallas_call x1, Pallas kernels: 5.48 us -> 7.44 us  [retrieve(): pl.pallas_call(functools.partial(retrieval_kernel, spread=spread), grid_s...]
    ppermute x12, starting transfers between devices: 13.9 us -> 12.4 us  [swap(): return lax.ppermute(value, axis, [(at, at ^ bits) for at in range(size)])]
  transfers between devices with their start and end apart: 13 -> 13, of which waited for: 6 -> 8; matrix products, arithmetic and copies ran while one was open for 2% -> 4% of each run, Pallas kernels for 34% -> 46%
where the time goes in v5:
time: 139 us; the launch traced here: 138 us
  Pallas kernels  69.7 us (50%)
  waiting for transfers between devices  21.6 us (16%)
  blocking collectives  18.5 us (13%)
  starting transfers between devices  18.4 us (13%)
  local copies, waits for them, and re-layouts  6.5 us (5%)
  other arithmetic  3.24 us (2%)
    pallas_call x4, Pallas kernels, attend(): pl.pallas_call(functools.partial(attend_kernel, offset=offset, column=col...  33.7 us
    all_to_all x1, blocking collectives, local(): lax.all_to_all(merged, 'pb', split_axis=0, concat_axis=0, tiled=True)  18.5 us
    pallas_call x2, Pallas kernels, project(): pl.pallas_call(project_kernel, grid_spec=pltpu.PrefetchScalarGridSpec(num...  18.3 us
    ppermute x12, waiting for transfers between devices, swap(): return lax.ppermute(value, axis, [(at, at ^ bits) for at in range(size)])  18 us
    ppermute x12, starting transfers between devices, swap(): return lax.ppermute(value, axis, [(at, at ^ bits) for at in range(size)])  12.4 us
    pallas_call x1, Pallas kernels, retrieve(): pl.pallas_call(functools.partial(retrieval_kernel, spread=spread), grid_s...  7.44 us
    all_to_all x1, starting transfers between devices, local(): lax.all_to_all(by_group, 'pb', split_axis=0, concat_axis=0, tiled=True)  6.08 us
    unnamed x25, local copies, waits for them, and re-layouts  4.64 us
  transfers between devices with their start and end apart: 13, of which 8 were waited for; matrix products, arithmetic and copies ran while one was open for 4% of the time, Pallas kernels for 46%

profile of v5, /device:TPU:0, one launch (start us, length us, event | category | flops | bytes accessed | tf_op | source)
XLA Modules:
  0.0 138.2 jit_solution(951956168669352318)
XLA Ops:
  1.0 7.4 %retrieve.1 = (bf16[2,8,32,896]{3,2,1,0:T(8,128)(2,1)}, bf16[2,8,32,896]{3,2,1,0:T(8,128)(2,1)}) custom-call(s32[4]{0:T(128)} %pad_add_fusion.1.place, bf16[1024,768]{1,0:T(8,128)(2,1)} %queries.1, bf16[512,768]{1,0:T(8,128)(2,1)} %passages.1, bf16[1024,512]{1,0:T(8,128)(2,1)} %noise.1), custom_call_target="tpu_custom_call" | custom-call | flops 1610612736 | bytes 4980736 | tf_op jit(solution)/shard_map/retrieve/pallas_call | solution.py:101
  9.8 1.2 collective-permute-done
  11.2 1.2 copy-done.2
  12.3 2.1 %merge_pair.1 = (bf16[8,32,896]{2,1,0:T(8,128)(2,1)S(1)}, bf16[8,32,896]{2,1,0:T(8,128)(2,1)S(1)}, s32[4]{0:T(128)S(1)}) custom-call(s32[4]{0:T(128)S(1)} %copy-done.4, bf16[2,8,32,896]{3,2,1,0:T(8,128)(2,1)S(1)} %copy-done.2, bf16[2,8,32,896]{3,2,1,0:T(8,128)(2,1)S(1)} %collective-permute-done.1.recv), custom_call_target="tpu_custom_call" | custom-call | tf_op jit(solution)/shard_map/merge_pair/pallas_call | solution.py:151
  14.4 2.7 %collective-permute-start.2 = (bf16[8,32,896]{2,1,0:T(8,128)(2,1)S(1)}, bf16[8,32,896]{2,1,0:T(8,128)(2,1)S(1)}, u32[]{:S(2)}, u32[]{:S(2)}) collective-permute-start(bf16[8,32,896]{2,1,0:T(8,128)(2,1)S(1)} %get-tuple-element.25), channel_id=1, source_target_pairs={{0,16},{8,24},{16,0},{24,8},{1,17},{9,25},{17,1},{25,9},{2,18},{10... | collective-permute-start | bytes 1376264 | tf_op jit(solution)/shard_map/ppermute | solution.py:488
  17.3 9.1 %project.2 = (bf16[2048,512]{1,0:T(8,128)(2,1)}, bf16[512,2048]{1,0:T(8,128)(2,1)}, f32[8,128]{1,0:T(8,128)}) custom-call(s32[4]{0:T(128)} %copy-done.7, bf16[2048,1024]{1,0:T(8,128)(2,1)} %bitcast.41, bf16[1024,1024]{1,0:T(8,128)(2,1)} %refs_1_.3, bf16[1024,1024]{1,0:T(8,128)(2,1)} %refs_1_.3, bf16[1024,1024]{1,0:T(8,128)(2,1)} %refs_3_.3, ...), custom_call_target="tpu_custom_call" | custom-call | flops 4294967296 | bytes 10485760 | tf_op jit(solution)/shard_map/project/pallas_call | solution.py:244
  26.4 1.8 %collective-permute-done.2.refs_1_ = bf16[8,32,896]{2,1,0:T(8,128)(2,1)S(1)} collective-permute-done((bf16[8,32,896]{2,1,0:T(8,128)(2,1)S(1)}, bf16[8,32,896]{2,1,0:T(8,128)(2,1)S(1)}, u32[]{:S(2)}, u32[]{:S(2)}) %collective-permute-start.2) | collective-permute-done | bytes 458784 | tf_op jit(solution)/shard_map/ppermute | solution.py:488
  28.9 1.9 %merge_columns.1 = (bf16[8,32,896]{2,1,0:T(8,128)(2,1)}, s32[4]{0:T(128)S(1)}) custom-call(s32[4]{0:T(128)S(1)} %copy-done.4, f32[1,128]{1,0:T(1,128)S(1)} %pad.4.note, f32[8,128]{1,0:T(8,128)S(1)} %copy-done.5, bf16[8,32,896]{2,1,0:T(8,128)(2,1)S(1)} %get-tuple-element.24.refs_0_, bf16[8,32,896]{2,1,0:T(8,128)(2,1)S(1)} %collective-permute-done.2.refs_1_), custom_call_target="tpu_custom_call" | custom-call | tf_op jit(solution)/shard_map/merge_columns/pallas_call | solution.py:172
  31.3 6.1 %all-to-all-start = ((bf16[8,32,896]{2,1,0:T(8,128)(2,1)}), bf16[8,32,896]{2,1,0:T(8,128)(2,1)S(1)}, u32[]{:S(2)}, u32[]{:S(2)}) async-start(bf16[8,32,896]{2,1,0:T(8,128)(2,1)} %get-tuple-element.26), calls=%async_computation | async-start | bytes 917504 | tf_op jit(solution)/shard_map/all_to_all | solution.py:502
  37.5 9.2 %project.3 = (bf16[2048,512]{1,0:T(8,128)(2,1)}, bf16[512,2048]{1,0:T(8,128)(2,1)}, f32[8,128]{1,0:T(8,128)}) custom-call(s32[4]{0:T(128)} %copy-done.8, bf16[2048,1024]{1,0:T(8,128)(2,1)} %collective-permute-done.3.states, bf16[1024,1024]{1,0:T(8,128)(2,1)} %refs_1_.3, bf16[1024,1024]{1,0:T(8,128)(2,1)} %refs_1_.3, bf16[1024,1024]{1,0:T(8,128)(2,1)} %refs_3_.3, ...), custom_call_target="tpu_custom_call" | custom-call | flops 4294967296 | bytes 10485760 | tf_op jit(solution)/shard_map/project/pallas_call | solution.py:244
  46.7 3.6 %all-to-all-done.parts = bf16[8,32,896]{2,1,0:T(8,128)(2,1)S(1)} async-done(((bf16[8,32,896]{2,1,0:T(8,128)(2,1)}), bf16[8,32,896]{2,1,0:T(8,128)(2,1)S(1)}, u32[]{:S(2)}, u32[]{:S(2)}) %all-to-all-start) | async-done | bytes 458784 | tf_op jit(solution)/shard_map/all_to_all | solution.py:502
  51.0 1.2 condition.1
  52.3 1.1 collective-permute-done.4
  53.4 0.9 collective-permute-start.5
  54.3 3.5 %collective-permute-done.5 = bf16[1,2,32,512]{3,2,1,0:T(8,128)(2,1)S(1)} collective-permute-done((bf16[1,2,32,512]{3,2,1,0:T(8,128)(2,1)S(1)}, bf16[1,2,32,512]{3,2,1,0:T(8,128)(2,1)S(1)}, u32[]{:S(2)}, u32[]{:S(2)}) %collective-permute-start.5) | collective-permute-done | bytes 65568 | tf_op jit(solution)/shard_map/ppermute | solution.py:488
  57.8 0.8 collective-permute-start.6
  58.7 7.2 %collective-permute-done.6 = bf16[2,2,32,512]{3,2,1,0:T(8,128)(2,1)S(1)} collective-permute-done((bf16[2,2,32,512]{3,2,1,0:T(8,128)(2,1)S(1)}, bf16[2,2,32,512]{3,2,1,0:T(8,128)(2,1)S(1)}, u32[]{:S(2)}, u32[]{:S(2)}) %collective-permute-start.6) | collective-permute-done | bytes 131104 | tf_op jit(solution)/shard_map/ppermute | solution.py:488
  66.0 1.6 %collective-permute-start.7 = (bf16[4,2,32,512]{3,2,1,0:T(8,128)(2,1)S(1)}, bf16[4,2,32,512]{3,2,1,0:T(8,128)(2,1)S(1)}, u32[]{:S(2)}, u32[]{:S(2)}) collective-permute-start(bf16[4,2,32,512]{3,2,1,0:T(8,128)(2,1)S(1)} %get-tuple-element.41), channel_id=1, source_target_pairs={{0,16},{8,24},{16,0},{24,8},{1,17},{9,25},{17,1},{25,9},{2,18},{10... | collective-permute-start | bytes 786440 | tf_op jit(solution)/shard_map/ppermute | solution.py:488
  69.1 1.4 %collective-permute-start.9 = (bf16[4,2,32,512]{3,2,1,0:T(8,128)(2,1)S(1)}, bf16[4,2,32,512]{3,2,1,0:T(8,128)(2,1)S(1)}, u32[]{:S(2)}, u32[]{:S(2)}) collective-permute-start(bf16[4,2,32,512]{3,2,1,0:T(8,128)(2,1)S(1)} %get-tuple-element.41), channel_id=1, source_target_pairs={{0,1},{1,0},{2,3},{3,2},{4,5},{5,4},{6,7},{7,6},{8,9},{9,8},{10,11... | collective-permute-start | bytes 786440 | tf_op jit(solution)/shard_map/ppermute | solution.py:488
  70.5 3.1 %collective-permute-done.7 = bf16[4,2,32,512]{3,2,1,0:T(8,128)(2,1)S(1)} collective-permute-done((bf16[4,2,32,512]{3,2,1,0:T(8,128)(2,1)S(1)}, bf16[4,2,32,512]{3,2,1,0:T(8,128)(2,1)S(1)}, u32[]{:S(2)}, u32[]{:S(2)}) %collective-permute-start.7) | collective-permute-done | bytes 262176 | tf_op jit(solution)/shard_map/ppermute | solution.py:488
  73.7 1.8 %collective-permute-start.10 = (bf16[1,4,2,32,512]{4,3,2,1,0:T(8,128)(2,1)S(1)}, bf16[1,4,2,32,512]{4,3,2,1,0:T(8,128)(2,1)S(1)}, u32[]{:S(2)}, u32[]{:S(2)}) collective-permute-start(bf16[1,4,2,32,512]{4,3,2,1,0:T(8,128)(2,1)S(1)} %bitcast.32), channel_id=1, source_target_pairs={{0,1},{1,0},{2,3},{3,2},{4,5},{5,4},{6,7},{7,6},{8,9},{9,8},{10,11... | collective-permute-start | bytes 786440 | tf_op jit(solution)/shard_map/ppermute | solution.py:488
  75.5 0.9 pad_maximum_fusion.pieces
  76.3 8.4 %attend.5 = bf16[4,288,128]{2,1,0:T(8,128)(2,1)} custom-call(s32[4]{0:T(128)} %pad_add_fusion.1.place, s32[48]{0:T(128)} %reshape.116.table, bf16[2,4,2,32,512]{4,3,2,1,0:T(8,128)(2,1)} %pad_maximum_fusion.pieces, bf16[2048,512]{1,0:T(8,128)(2,1)} %get-tuple-element.31.key_own, bf16[2048,512]{1,0:T(8,128)(2,1)} %get-tuple-element.32.key_pair, ...), custom_call_target="tpu_custom_call" | custom-call | flops 2147483648 | bytes 294912 | tf_op jit(solution)/shard_map/attend/pallas_call | solution.py:361
  84.7 1.6 %collective-permute-start.8 = (bf16[4,288,128]{2,1,0:T(8,128)(2,1)}, bf16[4,288,128]{2,1,0:T(8,128)(2,1)S(1)}, u32[]{:S(2)}, u32[]{:S(2)}) collective-permute-start(bf16[4,288,128]{2,1,0:T(8,128)(2,1)} %attend.5), channel_id=1, source_target_pairs={{0,16},{8,24},{16,0},{24,8},{1,17},{9,25},{17,1},{25,9},{2,18},{10... | collective-permute-start | bytes 884744 | tf_op jit(solution)/shard_map/ppermute | solution.py:488
  86.3 0.8 pad_maximum_fusion.1.pieces
  87.1 8.4 %attend.7 = bf16[4,288,128]{2,1,0:T(8,128)(2,1)} custom-call(s32[4]{0:T(128)} %pad_add_fusion.1.place, s32[48]{0:T(128)} %reshape.116.table, bf16[2,4,2,32,512]{4,3,2,1,0:T(8,128)(2,1)} %pad_maximum_fusion.1.pieces, bf16[2048,512]{1,0:T(8,128)(2,1)} %get-tuple-element.31.key_own, bf16[2048,512]{1,0:T(8,128)(2,1)} %get-tuple-element.32.key_pair, ...), custom_call_target="tpu_custom_call" | custom-call | flops 2147483648 | bytes 294912 | tf_op jit(solution)/shard_map/attend/pallas_call | solution.py:361
  96.1 8.6 %attend.4.refs_0_ = bf16[4,288,128]{2,1,0:T(8,128)(2,1)} custom-call(s32[4]{0:T(128)} %pad_add_fusion.1.place, s32[48]{0:T(128)} %reshape.116.table, bf16[2,4,2,32,512]{4,3,2,1,0:T(8,128)(2,1)} %pad_maximum_fusion.pieces, bf16[2048,512]{1,0:T(8,128)(2,1)} %get-tuple-element.31.key_own, bf16[2048,512]{1,0:T(8,128)(2,1)} %get-tuple-element.32.key_pair, ...), custom_call_target="tpu_custom_call" | custom-call | flops 2147483648 | bytes 294912 | tf_op jit(solution)/shard_map/attend/pallas_call | solution.py:361
  104.7 8.3 %attend.6.refs_2_ = bf16[4,288,128]{2,1,0:T(8,128)(2,1)} custom-call(s32[4]{0:T(128)} %pad_add_fusion.1.place, s32[48]{0:T(128)} %reshape.116.table, bf16[2,4,2,32,512]{4,3,2,1,0:T(8,128)(2,1)} %pad_maximum_fusion.1.pieces, bf16[2048,512]{1,0:T(8,128)(2,1)} %get-tuple-element.31.key_own, bf16[2048,512]{1,0:T(8,128)(2,1)} %get-tuple-element.32.key_pair, ...), custom_call_target="tpu_custom_call" | custom-call | flops 2147483648 | bytes 294912 | tf_op jit(solution)/shard_map/attend/pallas_call | solution.py:361
  113.8 0.8 copy-done.10
  114.5 4.3 %merge_lots.1 = bf16[4,2,288,128]{3,2,1,0:T(8,128)(2,1)} custom-call(s32[4]{0:T(128)} %pad_add_fusion.1.place, bf16[4,288,128]{2,1,0:T(8,128)(2,1)} %attend.4.refs_0_, bf16[4,288,128]{2,1,0:T(8,128)(2,1)} %copy-done.9, bf16[4,288,128]{2,1,0:T(8,128)(2,1)} %attend.6.refs_2_, bf16[4,288,128]{2,1,0:T(8,128)(2,1)} %copy-done.10), custom_call_target="tpu_custom_call" | custom-call | tf_op jit(solution)/shard_map/merge_lots/pallas_call | solution.py:427
  118.8 18.5 %all_to_all.10.parts = bf16[8,288,128]{2,1,0:T(8,128)(2,1)S(1)} all-to-all(bf16[8,288,128]{2,1,0:T(8,128)(2,1)} %bitcast.31), channel_id=1, replica_groups=mesh['pa'=4,'pb'=8] {'pb'}, dimensions={0} | all-to-all | bytes 1179648 | tf_op jit(solution)/shard_map/all_to_all | solution.py:542
  137.3 0.9 finish.1
  (60 shorter events, 8.0 us)
Async XLA Ops:
  0.0 8.6 %copy-start = (s32[256]{0:T(256)S(1)}, s32[256]{0:T(256)}, u32[]{:S(2)}) copy-start(s32[256]{0:T(256)} %param.18) | copy-start | bytes 3076
  0.0 37.4 %collective-permute-start.3 = (bf16[2048,1024]{1,0:T(8,128)(2,1)}, bf16[2048,1024]{1,0:T(8,128)(2,1)}, u32[]{:S(2)}, u32[]{:S(2)}) collective-permute-start(bf16[2048,1024]{1,0:T(8,128)(2,1)} %bitcast.40), channel_id=1, source_target_pairs={{0,8},{8,0},{16,24},{24,16},{1,9},{9,1},{17,25},{25,17},{2,10},{10... | collective-permute-start | bytes 12582920 | tf_op jit(solution)/shard_map/ppermute | solution.py:488
  1.0 7.5 %copy-start.11 = (s32[1,16]{1,0:T(1,128)S(1)}, s32[1,16]{1,0:T(1,128)}, u32[]{:S(2)}) copy-start(s32[1,16]{1,0:T(1,128)} %param.19) | copy-start | bytes 196
  1.0 10.1 %copy-start.4 = (s32[4]{0:T(128)S(1)}, s32[4]{0:T(128)}, u32[]{:S(2)}) copy-start(s32[4]{0:T(128)} %pad_add_fusion.1.place) | copy-start | bytes 52
  8.5 2.7 %collective-permute-start.1 = (bf16[2,8,32,896]{3,2,1,0:T(8,128)(2,1)}, bf16[2,8,32,896]{3,2,1,0:T(8,128)(2,1)S(1)}, u32[]{:S(2)}, u32[]{:S(2)}) collective-permute-start(bf16[2,8,32,896]{3,2,1,0:T(8,128)(2,1)} %get-tuple-element.21), channel_id=1, source_target_pairs={{0,8},{8,0},{16,24},{24,16},{1,9},{9,1},{17,25},{25,17},{2,10},{10... | collective-permute-start | bytes 2752520 | tf_op jit(solution)/shard_map/ppermute | solution.py:488
  9.2 1.7 %collective-permute-start = (s32[16]{0:T(128)S(1)}, s32[16]{0:T(128)S(1)}, u32[]{:S(2)}, u32[]{:S(2)}) collective-permute-start(s32[16]{0:T(128)S(1)} %and_select_fusion.4), channel_id=1, source_target_pairs={{0,8},{8,0},{16,24},{24,16},{1,9},{9,1},{17,25},{25,17},{2,10},{10... | collective-permute-start | bytes 200 | tf_op jit(solution)/shard_map/ppermute | solution.py:488
  11.2 1.2 copy-start.2
  14.4 2.7 %copy-start.7 = (s32[4]{0:T(128)}, s32[4]{0:T(128)S(1)}, u32[]{:S(2)}) copy-start(s32[4]{0:T(128)S(1)} %get-tuple-element.22.place) | copy-start | bytes 52
  14.4 13.7 %collective-permute-start.2 = (bf16[8,32,896]{2,1,0:T(8,128)(2,1)S(1)}, bf16[8,32,896]{2,1,0:T(8,128)(2,1)S(1)}, u32[]{:S(2)}, u32[]{:S(2)}) collective-permute-start(bf16[8,32,896]{2,1,0:T(8,128)(2,1)S(1)} %get-tuple-element.25), channel_id=1, source_target_pairs={{0,16},{8,24},{16,0},{24,8},{1,17},{9,25},{17,1},{25,9},{2,18},{10... | collective-permute-start | bytes 1376264 | tf_op jit(solution)/shard_map/ppermute | solution.py:488
  28.2 0.7 copy-start.5
  30.8 0.6 copy-start.8
  31.3 18.9 %all-to-all-start = ((bf16[8,32,896]{2,1,0:T(8,128)(2,1)}), bf16[8,32,896]{2,1,0:T(8,128)(2,1)S(1)}, u32[]{:S(2)}, u32[]{:S(2)}) async-start(bf16[8,32,896]{2,1,0:T(8,128)(2,1)} %get-tuple-element.26), calls=%async_computation | async-start | bytes 917504 | tf_op jit(solution)/shard_map/all_to_all | solution.py:502
  37.4 12.8 %copy-start.1 = (bf16[768,1024]{1,0:T(8,128)(2,1)S(1)}, bf16[768,1024]{1,0:T(8,128)(2,1)}, u32[]{:S(2)}) copy-start(bf16[768,1024]{1,0:T(8,128)(2,1)} %mix_weight.1) | copy-start | bytes 4718596
  37.4 12.8 %copy-start.3 = (bf16[128,1024]{1,0:T(8,128)(2,1)S(1)}, bf16[128,1024]{1,0:T(8,128)(2,1)}, u32[]{:S(2)}) copy-start(bf16[128,1024]{1,0:T(8,128)(2,1)} %answers.1) | copy-start | bytes 786436
  50.3 0.7 copy-start.6
  52.1 1.3 collective-permute-start.4
  53.4 4.3 %collective-permute-start.5 = (bf16[1,2,32,512]{3,2,1,0:T(8,128)(2,1)S(1)}, bf16[1,2,32,512]{3,2,1,0:T(8,128)(2,1)S(1)}, u32[]{:S(2)}, u32[]{:S(2)}) collective-permute-start(bf16[1,2,32,512]{3,2,1,0:T(8,128)(2,1)S(1)} %maximum_bitcast_fusion), channel_id=1, source_target_pairs={{0,2},{1,3},{2,0},{3,1},{4,6},{5,7},{6,4},{7,5},{8,10},{9,11},{10,... | collective-permute-start | bytes 196616 | tf_op jit(solution)/shard_map/ppermute | solution.py:488
  57.8 8.1 %collective-permute-start.6 = (bf16[2,2,32,512]{3,2,1,0:T(8,128)(2,1)S(1)}, bf16[2,2,32,512]{3,2,1,0:T(8,128)(2,1)S(1)}, u32[]{:S(2)}, u32[]{:S(2)}) collective-permute-start(bf16[2,2,32,512]{3,2,1,0:T(8,128)(2,1)S(1)} %pad_maximum_fusion.3), channel_id=1, source_target_pairs={{0,4},{1,5},{2,6},{3,7},{4,0},{5,1},{6,2},{7,3},{8,12},{9,13},{10,... | collective-permute-start | bytes 393224 | tf_op jit(solution)/shard_map/ppermute | solution.py:488
  66.0 7.7 %collective-permute-start.7 = (bf16[4,2,32,512]{3,2,1,0:T(8,128)(2,1)S(1)}, bf16[4,2,32,512]{3,2,1,0:T(8,128)(2,1)S(1)}, u32[]{:S(2)}, u32[]{:S(2)}) collective-permute-start(bf16[4,2,32,512]{3,2,1,0:T(8,128)(2,1)S(1)} %get-tuple-element.41), channel_id=1, source_target_pairs={{0,16},{8,24},{16,0},{24,8},{1,17},{9,25},{17,1},{25,9},{2,18},{10... | collective-permute-start | bytes 786440 | tf_op jit(solution)/shard_map/ppermute | solution.py:488
  69.1 17.1 %collective-permute-start.9 = (bf16[4,2,32,512]{3,2,1,0:T(8,128)(2,1)S(1)}, bf16[4,2,32,512]{3,2,1,0:T(8,128)(2,1)S(1)}, u32[]{:S(2)}, u32[]{:S(2)}) collective-permute-start(bf16[4,2,32,512]{3,2,1,0:T(8,128)(2,1)S(1)} %get-tuple-element.41), channel_id=1, source_target_pairs={{0,1},{1,0},{2,3},{3,2},{4,5},{5,4},{6,7},{7,6},{8,9},{9,8},{10,11... | collective-permute-start | bytes 786440 | tf_op jit(solution)/shard_map/ppermute | solution.py:488
  73.7 12.6 %collective-permute-start.10 = (bf16[1,4,2,32,512]{4,3,2,1,0:T(8,128)(2,1)S(1)}, bf16[1,4,2,32,512]{4,3,2,1,0:T(8,128)(2,1)S(1)}, u32[]{:S(2)}, u32[]{:S(2)}) collective-permute-start(bf16[1,4,2,32,512]{4,3,2,1,0:T(8,128)(2,1)S(1)} %bitcast.32), channel_id=1, source_target_pairs={{0,1},{1,0},{2,3},{3,2},{4,5},{5,4},{6,7},{7,6},{8,9},{9,8},{10,11... | collective-permute-start | bytes 786440 | tf_op jit(solution)/shard_map/ppermute | solution.py:488
  84.7 28.3 %collective-permute-start.8 = (bf16[4,288,128]{2,1,0:T(8,128)(2,1)}, bf16[4,288,128]{2,1,0:T(8,128)(2,1)S(1)}, u32[]{:S(2)}, u32[]{:S(2)}) collective-permute-start(bf16[4,288,128]{2,1,0:T(8,128)(2,1)} %attend.5), channel_id=1, source_target_pairs={{0,16},{8,24},{16,0},{24,8},{1,17},{9,25},{17,1},{25,9},{2,18},{10... | collective-permute-start | bytes 884744 | tf_op jit(solution)/shard_map/ppermute | solution.py:488
  95.5 17.6 %collective-permute-start.11 = (bf16[4,288,128]{2,1,0:T(8,128)(2,1)}, bf16[4,288,128]{2,1,0:T(8,128)(2,1)S(1)}, u32[]{:S(2)}, u32[]{:S(2)}) collective-permute-start(bf16[4,288,128]{2,1,0:T(8,128)(2,1)} %attend.7), channel_id=1, source_target_pairs={{0,16},{8,24},{16,0},{24,8},{1,17},{9,25},{17,1},{25,9},{2,18},{10... | collective-permute-start | bytes 884744 | tf_op jit(solution)/shard_map/ppermute | solution.py:488
  113.0 0.7 copy-start.9
  113.8 0.8 copy-start.10

commit v6 on v5

--- a/solution.py
+++ b/solution.py
@@ -224,18 +224,19 @@
     spread = (len(refs) - 3) // 2
     keys, values, done = refs[-3:]
     done[...] = jnp.zeros_like(done)
-    width = keys.shape[1] // spread
+    tokens = values.shape[3]
     for column in range(spread):
-        key = jnp.dot(states[...], refs[column][...], preferred_element_type=F32)
-        keys[:, column * width : (column + 1) * width] = key.astype(BF16)
-        value = jnp.dot(states[...], refs[spread + column][...], preferred_element_type=F32)
-        values[column * width : (column + 1) * width, :] = value.astype(BF16).T
-
-
-def project(place, states, key_weight, value_weight, spread):
+        keys[column] = jnp.dot(states[...], refs[column][...], preferred_element_type=F32).astype(BF16)
+        value = jnp.dot(states[...], refs[spread + column][...], preferred_element_type=F32).astype(BF16)
+        for block in range(values.shape[1]):
+            values[column, block] = value[block * tokens : (block + 1) * tokens].T
+
+
+def project(place, states, key_weight, value_weight, spread, tokens):
     rows, model_width = states.shape
     width = model_width // (PAIR * spread)
     chunk = rows // PROJECT_STEPS
+    blocks = chunk // tokens
 
     def weight_spec(column):
         return pl.BlockSpec((model_width, width), lambda t, place: (0, column * PAIR + place[0]))
@@ -248,14 +249,14 @@
             grid=(PROJECT_STEPS,),
             in_specs=[pl.BlockSpec((chunk, model_width), lambda t, place: (t, 0))] + specs + specs,
             out_specs=[
-                pl.BlockSpec((chunk, spread * width), lambda t, place: (t, 0)),
-                pl.BlockSpec((spread * width, chunk), lambda t, place: (0, t)),
+                pl.BlockSpec((spread, chunk, width), lambda t, place: (0, t, 0)),
+                pl.BlockSpec((spread, blocks, width, tokens), lambda t, place: (0, t, 0, 0)),
                 pl.BlockSpec((8, LANES), lambda t, place: (0, 0)),
             ],
         ),
         out_shape=[
-            jax.ShapeDtypeStruct((rows, spread * width), BF16),
-            jax.ShapeDtypeStruct((spread * width, rows), BF16),
+            jax.ShapeDtypeStruct((spread, rows, width), BF16),
+            jax.ShapeDtypeStruct((spread, rows // tokens, width, tokens), BF16),
             jax.ShapeDtypeStruct((8, LANES), F32),
         ],
         compiler_params=pltpu.CompilerParams(vmem_limit_bytes=WIDE_BYTES),
@@ -319,18 +320,17 @@
 ):
     outer = out.shape[0]
     tokens, width = held.shape[3:]
-    left = pl.multiple_of(lax.bitwise_xor(place[1], column) * width, width)
+    side = lax.bitwise_xor(place[1], column)
     copies = []
     for z in range(outer):
         entry = z * inner + lax.bitwise_xor(place[2], offset)
         for shelf, (keys, values) in enumerate(((key_own, value_own), (key_pair, value_pair))):
             for at in range(CAP):
-                start = pl.multiple_of(table[entry * 6 + shelf * 3 + at] * tokens, tokens)
-                source = keys.at[pl.ds(start, tokens), pl.ds(left, width)]
+                slot = table[entry * 6 + shelf * 3 + at]
                 lead = (z, shelf, at)
+                source = keys.at[side, pl.ds(pl.multiple_of(slot * tokens, tokens), tokens), :]
                 copies.append(pltpu.make_async_copy(source, held.at[lead], arrived.at[lead + (0,)]))
-                source = values.at[pl.ds(left, width), pl.ds(start, tokens)]
-                copies.append(pltpu.make_async_copy(source, turned.at[lead], arrived.at[lead + (1,)]))
+                copies.append(pltpu.make_async_copy(values.at[side, slot], turned.at[lead], arrived.at[lead + (1,)]))
     for copy in copies:
         copy.start()
     each = len(copies) // outer
@@ -405,42 +405,36 @@
     return mixes, highs, totals
 
 
-def gather_kernel(place, *refs, inner, spread, head_width):
-    *parts, out = refs
-    width = out.shape[2] - STAT_ROWS
-    rows = out.shape[3]
+def gather_kernel(place, *refs, outer, head_width):
+    parts, outs = refs[:-outer], refs[-outer:]
+    rows = outs[0].shape[1]
+    width = outs[0].shape[0] - STAT_ROWS
     count = width // head_width
-    for offset in range(inner):
-        taken = [parts[offset * spread + column][0] for column in range(spread)]
-        mixes, highs, totals = merge_heads(taken, width, head_width)
-        target = lax.bitwise_xor(place[2], offset)
+    for step, out in enumerate(outs):
+        z = lax.bitwise_xor(place[3], step)
+        mixes, highs, totals = merge_heads([part[z] for part in parts], width, head_width)
         for head in range(count):
-            out[0, target, head * head_width : (head + 1) * head_width, :] = mixes[head].astype(BF16)
-        out[0, target, width:, :] = pack_stats(
-            jnp.concatenate(highs, 1), jnp.concatenate(totals, 1), count, rows
-        )
-
-
-def merge_lots(place, parts, inner, spread, head_width):
+            out[head * head_width : (head + 1) * head_width, :] = mixes[head].astype(BF16)
+        out[width:, :] = pack_stats(jnp.concatenate(highs, 1), jnp.concatenate(totals, 1), count, rows)
+
+
+def merge_lots(place, parts, head_width):
     outer, height, rows = parts[0].shape
-    spec = pl.BlockSpec((1, height, rows), lambda z, place: (z, 0, 0))
-    return pl.pallas_call(
-        functools.partial(gather_kernel, inner=inner, spread=spread, head_width=head_width),
-        grid_spec=pltpu.PrefetchScalarGridSpec(
-            num_scalar_prefetch=1,
-            grid=(outer,),
-            in_specs=[spec] * len(parts),
-            out_specs=pl.BlockSpec((1, inner, height, rows), lambda z, place: (z, 0, 0, 0)),
-        ),
-        out_shape=jax.ShapeDtypeStruct((outer, inner, height, rows), BF16),
-        compiler_params=pltpu.CompilerParams(vmem_limit_bytes=WIDE_BYTES),
+    whole = pl.BlockSpec(memory_space=pltpu.VMEM)
+    return pl.pallas_call(
+        functools.partial(gather_kernel, outer=outer, head_width=head_width),
+        in_specs=[SCALARS] + [whole] * len(parts),
+        out_specs=[whole] * outer,
+        out_shape=[jax.ShapeDtypeStruct((height, rows), BF16)] * outer,
+        compiler_params=grant(),
         name="merge_lots",
     )(place, *parts)
 
 
-def finish_kernel(parts, out, *, head_width):
-    width = parts.shape[1] - STAT_ROWS
-    mixes, _, totals = merge_heads([parts[at] for at in range(parts.shape[0])], width, head_width)
+def finish_kernel(*refs, head_width):
+    *parts, out = refs
+    width = out.shape[1]
+    mixes, _, totals = merge_heads([part[...] for part in parts], width, head_width)
     done = jnp.concatenate([mixed / total for mixed, total in zip(mixes, totals)], 0)
     out[...] = done.T.astype(BF16)
 
@@ -449,12 +443,12 @@
     whole = pl.BlockSpec(memory_space=pltpu.VMEM)
     return pl.pallas_call(
         functools.partial(finish_kernel, head_width=head_width),
-        in_specs=[whole],
+        in_specs=[whole] * len(parts),
         out_specs=whole,
-        out_shape=jax.ShapeDtypeStruct((parts.shape[2], parts.shape[1] - STAT_ROWS), BF16),
+        out_shape=jax.ShapeDtypeStruct((parts[0].shape[1], parts[0].shape[0] - STAT_ROWS), BF16),
         compiler_params=grant(),
         name="finish",
-    )(parts)
+    )(*parts)
 
 
 def local(
@@ -497,10 +491,10 @@
     keep, send = retrieve(place, queries, passages, noise, readers, spread)
     *by_column, place_own = merge_pair(place, keep, swap(send, "pa", 1), spread)
     parts = [by_column[0]] + [swap(by_column[at], "pa", at * PAIR) for at in range(1, spread)]
-    own_key, own_value, own_done = project(place_own, states, key_weight, value_weight, spread)
+    own_key, own_value, own_done = project(place_own, states, key_weight, value_weight, spread, tokens)
     by_group, place_pair = merge_columns(place, note, own_done, parts)
     mine = lax.all_to_all(by_group, "pb", split_axis=0, concat_axis=0, tiled=True)
-    pair_key, pair_value, pair_done = project(place_pair, pair_states, key_weight, value_weight, spread)
+    pair_key, pair_value, pair_done = project(place_pair, pair_states, key_weight, value_weight, spread, tokens)
     keys, values = (own_key, pair_key), (own_value, pair_value)
     kept, sent = condition(place, mine, mix_weight, answer_queries, pair_done, spread)
 
@@ -531,15 +525,15 @@
         near = swap(own_pieces, "pb", offset)[None]
         far.append(jnp.concatenate([near, swap(pieces[1:], "pb", offset)], 0))
     lots = []
-    for offset in range(inner):
-        own = []
-        for column in reversed(range(spread)):
-            lot = attend(place, table, far[offset], keys, values, offset, column, inner, tokens, head_width)
-            own.append(lot if column == 0 else swap(lot, "pa", column * PAIR))
-        lots += own[::-1]
-    merged = merge_lots(place, lots, inner, spread, head_width)
-    merged = merged.reshape((readers,) + merged.shape[2:])
-    return finish(lax.all_to_all(merged, "pb", split_axis=0, concat_axis=0, tiled=True), head_width)
+    for offset, column in [(o, c) for o in range(inner) for c in range(spread)][1:] + [(0, 0)]:
+        lot = attend(place, table, far[offset], keys, values, offset, column, inner, tokens, head_width)
+        bits = column * PAIR * readers + offset
+        if bits:
+            lot = lax.ppermute(lot, ("pa", "pb"), [(at, at ^ bits) for at in range(runners * readers)])
+        lots.append(lot)
+    kept, *away = merge_lots(place, lots, head_width)
+    back = [swap(part, "pb", (step + 1) * inner) for step, part in enumerate(away)]
+    return finish([kept] + back, head_width)
 
 
 def solution(mesh):

time: 139 us -> 130 us (0.935)
  blocking collectives: 18.5 us -> 0 us
  waiting for transfers between devices: 21.6 us -> 28.8 us
  starting transfers between devices: 18.4 us -> 24.3 us
  Pallas kernels: 69.7 us -> 66.6 us
    all_to_all x1 -> x0, blocking collectives: 18.5 us -> none  [local(): lax.all_to_all(merged, 'pb', split_axis=0, concat_axis=0, tiled=True)]
    ppermute x12 -> x13, waiting for transfers between devices: 18 us -> 21.9 us  [swap(): return lax.ppermute(value, axis, [(at, at ^ bits) for at in range(size)])]
    ppermute x0 -> x3, starting transfers between devices: none -> 3.51 us  [local(): lax.ppermute(lot, ('pa', 'pb'), [(at, at ^ bits) for at in range(runners...]
    ppermute x0 -> x3, waiting for transfers between devices: none -> 3.45 us  [local(): lax.ppermute(lot, ('pa', 'pb'), [(at, at ^ bits) for at in range(runners...]
    pallas_call x1, Pallas kernels: 4.26 us -> 0.97 us  [merge_lots(): pl.pallas_call(functools.partial(gather_kernel, outer=outer, head_width=h...]
    ppermute x12 -> x13, starting transfers between devices: 12.4 us -> 14.7 us  [swap(): return lax.ppermute(value, axis, [(at, at ^ bits) for at in range(size)])]
    unnamed x25 -> x27, local copies, waits for them, and re-layouts: 4.64 us -> 4.08 us
  transfers between devices with their start and end apart: 13 -> 17, of which waited for: 8 -> 11; matrix products, arithmetic and copies ran while one was open for 4% -> 4% of each run, Pallas kernels for 46% -> 49%
where the time goes in v6:
time: 130 us; the launch traced here: 129 us
  Pallas kernels  66.6 us (51%)
  waiting for transfers between devices  28.8 us (22%)
  starting transfers between devices  24.3 us (19%)
  local copies, waits for them, and re-layouts  5.93 us (5%)
  other arithmetic  3.29 us (3%)
    pallas_call x4, Pallas kernels, attend(): pl.pallas_call(functools.partial(attend_kernel, offset=offset, column=col...  33.7 us
    ppermute x13, waiting for transfers between devices, swap(): return lax.ppermute(value, axis, [(at, at ^ bits) for at in range(size)])  21.9 us
    pallas_call x2, Pallas kernels, project(): pl.pallas_call(project_kernel, grid_spec=pltpu.PrefetchScalarGridSpec(num...  18.5 us
    ppermute x13, starting transfers between devices, swap(): return lax.ppermute(value, axis, [(at, at ^ bits) for at in range(size)])  14.7 us
    pallas_call x1, Pallas kernels, retrieve(): pl.pallas_call(functools.partial(retrieval_kernel, spread=spread), grid_s...  7.48 us
    all_to_all x1, starting transfers between devices, local(): lax.all_to_all(by_group, 'pb', split_axis=0, concat_axis=0, tiled=True)  6.08 us
    unnamed x27, local copies, waits for them, and re-layouts  4.08 us
    ppermute x3, starting transfers between devices, local(): lax.ppermute(lot, ('pa', 'pb'), [(at, at ^ bits) for at in range(runners...  3.51 us
  transfers between devices with their start and end apart: 17, of which 11 were waited for; matrix products, arithmetic and copies ran while one was open for 4% of the time, Pallas kernels for 49%

profile of v6, /device:TPU:0, one launch (start us, length us, event | category | flops | bytes accessed | tf_op | source)
XLA Modules:
  0.0 129.1 jit_solution(1458156894503308708)
XLA Ops:
  1.1 7.5 %retrieve.1 = (bf16[2,8,32,896]{3,2,1,0:T(8,128)(2,1)}, bf16[2,8,32,896]{3,2,1,0:T(8,128)(2,1)}) custom-call(s32[4]{0:T(128)} %pad_add_fusion.1.place, bf16[1024,768]{1,0:T(8,128)(2,1)} %queries.1, bf16[512,768]{1,0:T(8,128)(2,1)} %passages.1, bf16[1024,512]{1,0:T(8,128)(2,1)} %noise.1), custom_call_target="tpu_custom_call" | custom-call | flops 1610612736 | bytes 4980736 | tf_op jit(solution)/shard_map/retrieve/pallas_call | solution.py:101
  9.8 1.2 collective-permute-done
  11.2 1.2 copy-done.3
  12.4 2.1 %merge_pair.1 = (bf16[8,32,896]{2,1,0:T(8,128)(2,1)S(1)}, bf16[8,32,896]{2,1,0:T(8,128)(2,1)S(1)}, s32[4]{0:T(128)S(1)}) custom-call(s32[4]{0:T(128)S(1)} %copy-done.5, bf16[2,8,32,896]{3,2,1,0:T(8,128)(2,1)S(1)} %copy-done.3, bf16[2,8,32,896]{3,2,1,0:T(8,128)(2,1)S(1)} %collective-permute-done.1.recv), custom_call_target="tpu_custom_call" | custom-call | tf_op jit(solution)/shard_map/merge_pair/pallas_call | solution.py:151
  14.5 2.7 %collective-permute-start.2 = (bf16[8,32,896]{2,1,0:T(8,128)(2,1)S(1)}, bf16[8,32,896]{2,1,0:T(8,128)(2,1)S(1)}, u32[]{:S(2)}, u32[]{:S(2)}) collective-permute-start(bf16[8,32,896]{2,1,0:T(8,128)(2,1)S(1)} %get-tuple-element.29), channel_id=1, source_target_pairs={{0,16},{8,24},{16,0},{24,8},{1,17},{9,25},{17,1},{25,9},{2,18},{10... | collective-permute-start | bytes 1376264 | tf_op jit(solution)/shard_map/ppermute | solution.py:482
  17.4 9.2 %project.2 = (bf16[2,2048,256]{2,1,0:T(8,128)(2,1)}, bf16[2,8,256,256]{3,2,1,0:T(8,128)(2,1)}, f32[8,128]{1,0:T(8,128)}) custom-call(s32[4]{0:T(128)} %copy-done.9, bf16[2048,1024]{1,0:T(8,128)(2,1)} %bitcast.39, bf16[1024,1024]{1,0:T(8,128)(2,1)} %refs_1_.3, bf16[1024,1024]{1,0:T(8,128)(2,1)} %refs_1_.3, bf16[1024,1024]{1,0:T(8,128)(2,1)} %refs_3_.3, ...), custom_call_target="tpu_custom_call" | custom-call | flops 4294967296 | bytes 10485760 | tf_op jit(solution)/shard_map/project/pallas_call | solution.py:245
  26.5 1.7 %collective-permute-done.2.refs_1_ = bf16[8,32,896]{2,1,0:T(8,128)(2,1)S(1)} collective-permute-done((bf16[8,32,896]{2,1,0:T(8,128)(2,1)S(1)}, bf16[8,32,896]{2,1,0:T(8,128)(2,1)S(1)}, u32[]{:S(2)}, u32[]{:S(2)}) %collective-permute-start.2) | collective-permute-done | bytes 458784 | tf_op jit(solution)/shard_map/ppermute | solution.py:482
  28.9 1.9 %merge_columns.1 = (bf16[8,32,896]{2,1,0:T(8,128)(2,1)}, s32[4]{0:T(128)S(1)}) custom-call(s32[4]{0:T(128)S(1)} %copy-done.5, f32[1,128]{1,0:T(1,128)S(1)} %pad.4.note, f32[8,128]{1,0:T(8,128)S(1)} %copy-done.7, bf16[8,32,896]{2,1,0:T(8,128)(2,1)S(1)} %get-tuple-element.28.refs_0_, bf16[8,32,896]{2,1,0:T(8,128)(2,1)S(1)} %collective-permute-done.2.refs_1_), custom_call_target="tpu_custom_call" | custom-call | tf_op jit(solution)/shard_map/merge_columns/pallas_call | solution.py:172
  31.3 6.1 %all-to-all-start = ((bf16[8,32,896]{2,1,0:T(8,128)(2,1)}), bf16[8,32,896]{2,1,0:T(8,128)(2,1)S(1)}, u32[]{:S(2)}, u32[]{:S(2)}) async-start(bf16[8,32,896]{2,1,0:T(8,128)(2,1)} %get-tuple-element.30), calls=%async_computation | async-start | bytes 917504 | tf_op jit(solution)/shard_map/all_to_all | solution.py:496
  37.5 9.4 %project.3 = (bf16[2,2048,256]{2,1,0:T(8,128)(2,1)}, bf16[2,8,256,256]{3,2,1,0:T(8,128)(2,1)}, f32[8,128]{1,0:T(8,128)}) custom-call(s32[4]{0:T(128)} %copy-done.10, bf16[2048,1024]{1,0:T(8,128)(2,1)} %collective-permute-done.3.states, bf16[1024,1024]{1,0:T(8,128)(2,1)} %refs_1_.3, bf16[1024,1024]{1,0:T(8,128)(2,1)} %refs_1_.3, bf16[1024,1024]{1,0:T(8,128)(2,1)} %refs_3_.3, ...), custom_call_target="tpu_custom_call" | custom-call | flops 4294967296 | bytes 10485760 | tf_op jit(solution)/shard_map/project/pallas_call | solution.py:245
  46.8 3.5 %all-to-all-done.parts = bf16[8,32,896]{2,1,0:T(8,128)(2,1)S(1)} async-done(((bf16[8,32,896]{2,1,0:T(8,128)(2,1)}), bf16[8,32,896]{2,1,0:T(8,128)(2,1)S(1)}, u32[]{:S(2)}, u32[]{:S(2)}) %all-to-all-start) | async-done | bytes 458784 | tf_op jit(solution)/shard_map/all_to_all | solution.py:496
  51.0 1.2 condition.1
  52.3 1.1 collective-permute-done.4
  53.4 0.9 collective-permute-start.5
  54.3 3.5 %collective-permute-done.5 = bf16[1,2,32,512]{3,2,1,0:T(8,128)(2,1)S(1)} collective-permute-done((bf16[1,2,32,512]{3,2,1,0:T(8,128)(2,1)S(1)}, bf16[1,2,32,512]{3,2,1,0:T(8,128)(2,1)S(1)}, u32[]{:S(2)}, u32[]{:S(2)}) %collective-permute-start.5) | collective-permute-done | bytes 65568 | tf_op jit(solution)/shard_map/ppermute | solution.py:482
  58.7 7.2 %collective-permute-done.6 = bf16[2,2,32,512]{3,2,1,0:T(8,128)(2,1)S(1)} collective-permute-done((bf16[2,2,32,512]{3,2,1,0:T(8,128)(2,1)S(1)}, bf16[2,2,32,512]{3,2,1,0:T(8,128)(2,1)S(1)}, u32[]{:S(2)}, u32[]{:S(2)}) %collective-permute-start.6) | collective-permute-done | bytes 131104 | tf_op jit(solution)/shard_map/ppermute | solution.py:482
  66.0 1.6 %collective-permute-start.7 = (bf16[4,2,32,512]{3,2,1,0:T(8,128)(2,1)S(1)}, bf16[4,2,32,512]{3,2,1,0:T(8,128)(2,1)S(1)}, u32[]{:S(2)}, u32[]{:S(2)}) collective-permute-start(bf16[4,2,32,512]{3,2,1,0:T(8,128)(2,1)S(1)} %get-tuple-element.49), channel_id=1, source_target_pairs={{0,16},{8,24},{16,0},{24,8},{1,17},{9,25},{17,1},{25,9},{2,18},{10... | collective-permute-start | bytes 786440 | tf_op jit(solution)/shard_map/ppermute | solution.py:482
  69.1 1.4 %collective-permute-start.9 = (bf16[4,2,32,512]{3,2,1,0:T(8,128)(2,1)S(1)}, bf16[4,2,32,512]{3,2,1,0:T(8,128)(2,1)S(1)}, u32[]{:S(2)}, u32[]{:S(2)}) collective-permute-start(bf16[4,2,32,512]{3,2,1,0:T(8,128)(2,1)S(1)} %get-tuple-element.49), channel_id=1, source_target_pairs={{0,1},{1,0},{2,3},{3,2},{4,5},{5,4},{6,7},{7,6},{8,9},{9,8},{10,11... | collective-permute-start | bytes 786440 | tf_op jit(solution)/shard_map/ppermute | solution.py:482
  70.5 3.1 %collective-permute-done.7 = bf16[4,2,32,512]{3,2,1,0:T(8,128)(2,1)S(1)} collective-permute-done((bf16[4,2,32,512]{3,2,1,0:T(8,128)(2,1)S(1)}, bf16[4,2,32,512]{3,2,1,0:T(8,128)(2,1)S(1)}, u32[]{:S(2)}, u32[]{:S(2)}) %collective-permute-start.7) | collective-permute-done | bytes 262176 | tf_op jit(solution)/shard_map/ppermute | solution.py:482
  73.7 1.8 %collective-permute-start.10 = (bf16[1,4,2,32,512]{4,3,2,1,0:T(8,128)(2,1)S(1)}, bf16[1,4,2,32,512]{4,3,2,1,0:T(8,128)(2,1)S(1)}, u32[]{:S(2)}, u32[]{:S(2)}) collective-permute-start(bf16[1,4,2,32,512]{4,3,2,1,0:T(8,128)(2,1)S(1)} %bitcast.30), channel_id=1, source_target_pairs={{0,1},{1,0},{2,3},{3,2},{4,5},{5,4},{6,7},{7,6},{8,9},{9,8},{10,11... | collective-permute-start | bytes 786440 | tf_op jit(solution)/shard_map/ppermute | solution.py:482
  76.3 8.3 %attend.4 = bf16[4,288,128]{2,1,0:T(8,128)(2,1)} custom-call(s32[4]{0:T(128)} %pad_add_fusion.1.place, s32[48]{0:T(128)} %reshape.113.table, bf16[2,4,2,32,512]{4,3,2,1,0:T(8,128)(2,1)} %pad_maximum_fusion.pieces, bf16[2,2048,256]{2,1,0:T(8,128)(2,1)} %get-tuple-element.35.key_own, bf16[2,2048,256]{2,1,0:T(8,128)(2,1)} %get-tuple-element.36.key_pair, ...), custom_call_target="tpu_custom_call" | custom-call | flops 2147483648 | bytes 294912 | tf_op jit(solution)/shard_map/attend/pallas_call | solution.py:361
  84.7 1.6 %collective-permute-start.8 = (bf16[4,288,128]{2,1,0:T(8,128)(2,1)}, bf16[4,288,128]{2,1,0:T(8,128)(2,1)S(1)}, u32[]{:S(2)}, u32[]{:S(2)}) collective-permute-start(bf16[4,288,128]{2,1,0:T(8,128)(2,1)} %attend.4), channel_id=1, source_target_pairs={{0,16},{1,17},{2,18},{3,19},{4,20},{5,21},{6,22},{7,23},{8,24},{9,... | collective-permute-start | bytes 884744 | tf_op jit(solution)/shard_map/ppermute | solution.py:532
  87.2 8.4 %attend.6 = bf16[4,288,128]{2,1,0:T(8,128)(2,1)} custom-call(s32[4]{0:T(128)} %pad_add_fusion.1.place, s32[48]{0:T(128)} %reshape.113.table, bf16[2,4,2,32,512]{4,3,2,1,0:T(8,128)(2,1)} %pad_maximum_fusion.1.pieces, bf16[2,2048,256]{2,1,0:T(8,128)(2,1)} %get-tuple-element.35.key_own, bf16[2,2048,256]{2,1,0:T(8,128)(2,1)} %get-tuple-element.36.key_pair, ...), custom_call_target="tpu_custom_call" | custom-call | flops 2147483648 | bytes 294912 | tf_op jit(solution)/shard_map/attend/pallas_call | solution.py:361
  95.6 8.6 %attend.5 = bf16[4,288,128]{2,1,0:T(8,128)(2,1)} custom-call(s32[4]{0:T(128)} %pad_add_fusion.1.place, s32[48]{0:T(128)} %reshape.113.table, bf16[2,4,2,32,512]{4,3,2,1,0:T(8,128)(2,1)} %pad_maximum_fusion.1.pieces, bf16[2,2048,256]{2,1,0:T(8,128)(2,1)} %get-tuple-element.35.key_own, bf16[2,2048,256]{2,1,0:T(8,128)(2,1)} %get-tuple-element.36.key_pair, ...), custom_call_target="tpu_custom_call" | custom-call | flops 2147483648 | bytes 294912 | tf_op jit(solution)/shard_map/attend/pallas_call | solution.py:361
  104.4 1.7 %collective-permute-start.12 = (bf16[4,288,128]{2,1,0:T(8,128)(2,1)S(1)}, bf16[4,288,128]{2,1,0:T(8,128)(2,1)S(1)}, u32[]{:S(2)}, u32[]{:S(2)}) collective-permute-start(bf16[4,288,128]{2,1,0:T(8,128)(2,1)S(1)} %copy-done.11), channel_id=1, source_target_pairs={{0,17},{1,16},{2,19},{3,18},{4,21},{5,20},{6,23},{7,22},{8,25},{9,... | collective-permute-start | bytes 884744 | tf_op jit(solution)/shard_map/ppermute | solution.py:532
  106.1 8.3 %attend.7.refs_3_ = bf16[4,288,128]{2,1,0:T(8,128)(2,1)} custom-call(s32[4]{0:T(128)} %pad_add_fusion.1.place, s32[48]{0:T(128)} %reshape.113.table, bf16[2,4,2,32,512]{4,3,2,1,0:T(8,128)(2,1)} %pad_maximum_fusion.pieces, bf16[2,2048,256]{2,1,0:T(8,128)(2,1)} %get-tuple-element.35.key_own, bf16[2,2048,256]{2,1,0:T(8,128)(2,1)} %get-tuple-element.36.key_pair, ...), custom_call_target="tpu_custom_call" | custom-call | flops 2147483648 | bytes 294912 | tf_op jit(solution)/shard_map/attend/pallas_call | solution.py:361
  114.5 3.4 %collective-permute-done.11.refs_1_ = bf16[4,288,128]{2,1,0:T(8,128)(2,1)S(1)} collective-permute-done((bf16[4,288,128]{2,1,0:T(8,128)(2,1)}, bf16[4,288,128]{2,1,0:T(8,128)(2,1)S(1)}, u32[]{:S(2)}, u32[]{:S(2)}) %collective-permute-start.11) | collective-permute-done | bytes 294944 | tf_op jit(solution)/shard_map/ppermute | solution.py:532
  117.9 1.0 copy-done.2
  118.9 1.0 merge_lots.1
  120.0 2.1 %collective-permute-start.14 = (bf16[288,128]{1,0:T(8,128)(2,1)S(1)}, bf16[288,128]{1,0:T(8,128)(2,1)S(1)}, u32[]{:S(2)}, u32[]{:S(2)}) collective-permute-start(bf16[288,128]{1,0:T(8,128)(2,1)S(1)} %get-tuple-element.41), channel_id=1, source_target_pairs={{0,4},{1,5},{2,6},{3,7},{4,0},{5,1},{6,2},{7,3},{8,12},{9,13},{10,... | collective-permute-start | bytes 221192 | tf_op jit(solution)/shard_map/ppermute | solution.py:482
  122.0 2.3 %collective-permute-start.15 = (bf16[288,128]{1,0:T(8,128)(2,1)S(1)}, bf16[288,128]{1,0:T(8,128)(2,1)S(1)}, u32[]{:S(2)}, u32[]{:S(2)}) collective-permute-start(bf16[288,128]{1,0:T(8,128)(2,1)S(1)} %get-tuple-element.42), channel_id=1, source_target_pairs={{0,6},{1,7},{2,4},{3,5},{4,2},{5,3},{6,0},{7,1},{8,14},{9,15},{10,... | collective-permute-start | bytes 221192 | tf_op jit(solution)/shard_map/ppermute | solution.py:482
  124.3 3.1 %collective-permute-done.14.refs_2_ = bf16[288,128]{1,0:T(8,128)(2,1)S(1)} collective-permute-done((bf16[288,128]{1,0:T(8,128)(2,1)S(1)}, bf16[288,128]{1,0:T(8,128)(2,1)S(1)}, u32[]{:S(2)}, u32[]{:S(2)}) %collective-permute-start.14) | collective-permute-done | bytes 73760 | tf_op jit(solution)/shard_map/ppermute | solution.py:482
  (69 shorter events, 11.0 us)
Async XLA Ops:
  0.0 8.6 %copy-start = (s32[256]{0:T(256)S(1)}, s32[256]{0:T(256)}, u32[]{:S(2)}) copy-start(s32[256]{0:T(256)} %param.18) | copy-start | bytes 3076
  0.0 37.4 %collective-permute-start.3 = (bf16[2048,1024]{1,0:T(8,128)(2,1)}, bf16[2048,1024]{1,0:T(8,128)(2,1)}, u32[]{:S(2)}, u32[]{:S(2)}) collective-permute-start(bf16[2048,1024]{1,0:T(8,128)(2,1)} %bitcast.38), channel_id=1, source_target_pairs={{0,8},{8,0},{16,24},{24,16},{1,9},{9,1},{17,25},{25,17},{2,10},{10... | collective-permute-start | bytes 12582920 | tf_op jit(solution)/shard_map/ppermute | solution.py:482
  1.1 7.5 %copy-start.12 = (s32[1,16]{1,0:T(1,128)S(1)}, s32[1,16]{1,0:T(1,128)}, u32[]{:S(2)}) copy-start(s32[1,16]{1,0:T(1,128)} %param.19) | copy-start | bytes 196
  1.1 10.2 %copy-start.5 = (s32[4]{0:T(128)S(1)}, s32[4]{0:T(128)}, u32[]{:S(2)}) copy-start(s32[4]{0:T(128)} %pad_add_fusion.1.place) | copy-start | bytes 52
  8.6 2.7 %collective-permute-start.1 = (bf16[2,8,32,896]{3,2,1,0:T(8,128)(2,1)}, bf16[2,8,32,896]{3,2,1,0:T(8,128)(2,1)S(1)}, u32[]{:S(2)}, u32[]{:S(2)}) collective-permute-start(bf16[2,8,32,896]{3,2,1,0:T(8,128)(2,1)} %get-tuple-element.25), channel_id=1, source_target_pairs={{0,8},{8,0},{16,24},{24,16},{1,9},{9,1},{17,25},{25,17},{2,10},{10... | collective-permute-start | bytes 2752520 | tf_op jit(solution)/shard_map/ppermute | solution.py:482
  9.3 1.7 %collective-permute-start = (s32[16]{0:T(128)S(1)}, s32[16]{0:T(128)S(1)}, u32[]{:S(2)}, u32[]{:S(2)}) collective-permute-start(s32[16]{0:T(128)S(1)} %and_select_fusion.4), channel_id=1, source_target_pairs={{0,8},{8,0},{16,24},{24,16},{1,9},{9,1},{17,25},{25,17},{2,10},{10... | collective-permute-start | bytes 200 | tf_op jit(solution)/shard_map/ppermute | solution.py:482
  11.2 1.2 copy-start.3
  14.5 2.7 %copy-start.9 = (s32[4]{0:T(128)}, s32[4]{0:T(128)S(1)}, u32[]{:S(2)}) copy-start(s32[4]{0:T(128)S(1)} %get-tuple-element.26.place) | copy-start | bytes 52
  14.5 13.7 %collective-permute-start.2 = (bf16[8,32,896]{2,1,0:T(8,128)(2,1)S(1)}, bf16[8,32,896]{2,1,0:T(8,128)(2,1)S(1)}, u32[]{:S(2)}, u32[]{:S(2)}) collective-permute-start(bf16[8,32,896]{2,1,0:T(8,128)(2,1)S(1)} %get-tuple-element.29), channel_id=1, source_target_pairs={{0,16},{8,24},{16,0},{24,8},{1,17},{9,25},{17,1},{25,9},{2,18},{10... | collective-permute-start | bytes 1376264 | tf_op jit(solution)/shard_map/ppermute | solution.py:482
  28.3 0.7 copy-start.7
  30.8 0.5 copy-start.10
  31.3 18.9 %all-to-all-start = ((bf16[8,32,896]{2,1,0:T(8,128)(2,1)}), bf16[8,32,896]{2,1,0:T(8,128)(2,1)S(1)}, u32[]{:S(2)}, u32[]{:S(2)}) async-start(bf16[8,32,896]{2,1,0:T(8,128)(2,1)} %get-tuple-element.30), calls=%async_computation | async-start | bytes 917504 | tf_op jit(solution)/shard_map/all_to_all | solution.py:496
  37.4 12.8 %copy-start.1 = (bf16[768,1024]{1,0:T(8,128)(2,1)S(1)}, bf16[768,1024]{1,0:T(8,128)(2,1)}, u32[]{:S(2)}) copy-start(bf16[768,1024]{1,0:T(8,128)(2,1)} %mix_weight.1) | copy-start | bytes 4718596
  37.4 12.8 %copy-start.4 = (bf16[128,1024]{1,0:T(8,128)(2,1)S(1)}, bf16[128,1024]{1,0:T(8,128)(2,1)}, u32[]{:S(2)}) copy-start(bf16[128,1024]{1,0:T(8,128)(2,1)} %answers.1) | copy-start | bytes 786436
  50.3 0.7 copy-start.8
  52.1 1.3 collective-permute-start.4
  53.4 4.3 %collective-permute-start.5 = (bf16[1,2,32,512]{3,2,1,0:T(8,128)(2,1)S(1)}, bf16[1,2,32,512]{3,2,1,0:T(8,128)(2,1)S(1)}, u32[]{:S(2)}, u32[]{:S(2)}) collective-permute-start(bf16[1,2,32,512]{3,2,1,0:T(8,128)(2,1)S(1)} %maximum_bitcast_fusion), channel_id=1, source_target_pairs={{0,2},{1,3},{2,0},{3,1},{4,6},{5,7},{6,4},{7,5},{8,10},{9,11},{10,... | collective-permute-start | bytes 196616 | tf_op jit(solution)/shard_map/ppermute | solution.py:482
  57.8 8.1 %collective-permute-start.6 = (bf16[2,2,32,512]{3,2,1,0:T(8,128)(2,1)S(1)}, bf16[2,2,32,512]{3,2,1,0:T(8,128)(2,1)S(1)}, u32[]{:S(2)}, u32[]{:S(2)}) collective-permute-start(bf16[2,2,32,512]{3,2,1,0:T(8,128)(2,1)S(1)} %pad_maximum_fusion.3), channel_id=1, source_target_pairs={{0,4},{1,5},{2,6},{3,7},{4,0},{5,1},{6,2},{7,3},{8,12},{9,13},{10,... | collective-permute-start | bytes 393224 | tf_op jit(solution)/shard_map/ppermute | solution.py:482
  66.0 7.7 %collective-permute-start.7 = (bf16[4,2,32,512]{3,2,1,0:T(8,128)(2,1)S(1)}, bf16[4,2,32,512]{3,2,1,0:T(8,128)(2,1)S(1)}, u32[]{:S(2)}, u32[]{:S(2)}) collective-permute-start(bf16[4,2,32,512]{3,2,1,0:T(8,128)(2,1)S(1)} %get-tuple-element.49), channel_id=1, source_target_pairs={{0,16},{8,24},{16,0},{24,8},{1,17},{9,25},{17,1},{25,9},{2,18},{10... | collective-permute-start | bytes 786440 | tf_op jit(solution)/shard_map/ppermute | solution.py:482
  69.1 17.2 %collective-permute-start.9 = (bf16[4,2,32,512]{3,2,1,0:T(8,128)(2,1)S(1)}, bf16[4,2,32,512]{3,2,1,0:T(8,128)(2,1)S(1)}, u32[]{:S(2)}, u32[]{:S(2)}) collective-permute-start(bf16[4,2,32,512]{3,2,1,0:T(8,128)(2,1)S(1)} %get-tuple-element.49), channel_id=1, source_target_pairs={{0,1},{1,0},{2,3},{3,2},{4,5},{5,4},{6,7},{7,6},{8,9},{9,8},{10,11... | collective-permute-start | bytes 786440 | tf_op jit(solution)/shard_map/ppermute | solution.py:482
  73.7 12.6 %collective-permute-start.10 = (bf16[1,4,2,32,512]{4,3,2,1,0:T(8,128)(2,1)S(1)}, bf16[1,4,2,32,512]{4,3,2,1,0:T(8,128)(2,1)S(1)}, u32[]{:S(2)}, u32[]{:S(2)}) collective-permute-start(bf16[1,4,2,32,512]{4,3,2,1,0:T(8,128)(2,1)S(1)} %bitcast.30), channel_id=1, source_target_pairs={{0,1},{1,0},{2,3},{3,2},{4,5},{5,4},{6,7},{7,6},{8,9},{9,8},{10,11... | collective-permute-start | bytes 786440 | tf_op jit(solution)/shard_map/ppermute | solution.py:482
  84.7 29.8 %collective-permute-start.8 = (bf16[4,288,128]{2,1,0:T(8,128)(2,1)}, bf16[4,288,128]{2,1,0:T(8,128)(2,1)S(1)}, u32[]{:S(2)}, u32[]{:S(2)}) collective-permute-start(bf16[4,288,128]{2,1,0:T(8,128)(2,1)} %attend.4), channel_id=1, source_target_pairs={{0,16},{1,17},{2,18},{3,19},{4,20},{5,21},{6,22},{7,23},{8,24},{9,... | collective-permute-start | bytes 884744 | tf_op jit(solution)/shard_map/ppermute | solution.py:532
  95.6 8.8 %copy-start.11 = (bf16[4,288,128]{2,1,0:T(8,128)(2,1)S(1)}, bf16[4,288,128]{2,1,0:T(8,128)(2,1)}, u32[]{:S(2)}) copy-start(bf16[4,288,128]{2,1,0:T(8,128)(2,1)} %attend.6) | copy-start | bytes 884740
  104.2 13.7 %copy-start.6 = (s32[4]{0:T(128)S(1)}, s32[4]{0:T(128)}, u32[]{:S(2)}) copy-start(s32[4]{0:T(128)} %pad_add_fusion.1.place) | copy-start | bytes 52
  104.2 13.7 %collective-permute-start.11 = (bf16[4,288,128]{2,1,0:T(8,128)(2,1)}, bf16[4,288,128]{2,1,0:T(8,128)(2,1)S(1)}, u32[]{:S(2)}, u32[]{:S(2)}) collective-permute-start(bf16[4,288,128]{2,1,0:T(8,128)(2,1)} %attend.5), channel_id=1, source_target_pairs={{0,1},{1,0},{2,3},{3,2},{4,5},{5,4},{6,7},{7,6},{8,9},{9,8},{10,11... | collective-permute-start | bytes 884744 | tf_op jit(solution)/shard_map/ppermute | solution.py:532
  104.4 13.6 %collective-permute-start.12 = (bf16[4,288,128]{2,1,0:T(8,128)(2,1)S(1)}, bf16[4,288,128]{2,1,0:T(8,128)(2,1)S(1)}, u32[]{:S(2)}, u32[]{:S(2)}) collective-permute-start(bf16[4,288,128]{2,1,0:T(8,128)(2,1)S(1)} %copy-done.11), channel_id=1, source_target_pairs={{0,17},{1,16},{2,19},{3,18},{4,21},{5,20},{6,23},{7,22},{8,25},{9,... | collective-permute-start | bytes 884744 | tf_op jit(solution)/shard_map/ppermute | solution.py:532
  117.9 1.0 copy-start.2
  119.9 4.5 %collective-permute-start.13 = (bf16[288,128]{1,0:T(8,128)(2,1)S(1)}, bf16[288,128]{1,0:T(8,128)(2,1)S(1)}, u32[]{:S(2)}, u32[]{:S(2)}) collective-permute-start(bf16[288,128]{1,0:T(8,128)(2,1)S(1)} %get-tuple-element.40), channel_id=1, source_target_pairs={{0,2},{1,3},{2,0},{3,1},{4,6},{5,7},{6,4},{7,5},{8,10},{9,11},{10,... | collective-permute-start | bytes 221192 | tf_op jit(solution)/shard_map/ppermute | solution.py:482
  120.0 7.5 %collective-permute-start.14 = (bf16[288,128]{1,0:T(8,128)(2,1)S(1)}, bf16[288,128]{1,0:T(8,128)(2,1)S(1)}, u32[]{:S(2)}, u32[]{:S(2)}) collective-permute-start(bf16[288,128]{1,0:T(8,128)(2,1)S(1)} %get-tuple-element.41), channel_id=1, source_target_pairs={{0,4},{1,5},{2,6},{3,7},{4,0},{5,1},{6,2},{7,3},{8,12},{9,13},{10,... | collective-permute-start | bytes 221192 | tf_op jit(solution)/shard_map/ppermute | solution.py:482
  122.0 6.3 %collective-permute-start.15 = (bf16[288,128]{1,0:T(8,128)(2,1)S(1)}, bf16[288,128]{1,0:T(8,128)(2,1)S(1)}, u32[]{:S(2)}, u32[]{:S(2)}) collective-permute-start(bf16[288,128]{1,0:T(8,128)(2,1)S(1)} %get-tuple-element.42), channel_id=1, source_target_pairs={{0,6},{1,7},{2,4},{3,5},{4,2},{5,3},{6,0},{7,1},{8,14},{9,15},{10,... | collective-permute-start | bytes 221192 | tf_op jit(solution)/shard_map/ppermute | solution.py:482

commit v7 on v6

--- a/solution.py
+++ b/solution.py
@@ -269,26 +269,34 @@
     )(place, states, *([key_weight] * spread), *([value_weight] * spread))
 
 
-def attend_group(z, place, table, pieces, blocks_in, out, offset, column, inner, head_width):
+def attend_group(z, place, table, pieces, keys, values, out, rows_scratch, offset, column, inner, head_width):
     relative = lax.bitwise_xor(z, place[3])
-    spread, rows = pieces.shape[0], out.shape[2]
+    part, rows = pieces[0].shape[2], out.shape[2]
     width = out.shape[1] - STAT_ROWS
     count = width // head_width
-    left = pl.multiple_of(lax.bitwise_xor(place[1], column) * width, width)
-    quarters = []
-    for lane in range(spread):
+    side = lax.bitwise_xor(place[1], column)
+    left = pl.multiple_of(side * width, width)
+    for step, piece in enumerate(pieces):
         for core in range(PAIR):
-            lead = (lax.bitwise_xor(place[1], lane), relative, lax.bitwise_xor(place[0], core))
-            quarters.append(pieces[lead + (slice(None), pl.ds(left, width))])
-    query = jnp.concatenate(quarters, 0).T
+            top = lax.bitwise_xor(place[1], step) * PAIR + lax.bitwise_xor(place[0], core)
+            top = pl.multiple_of(top * part, part)
+            rows_scratch[z, pl.ds(top, part), :] = piece[relative, core, :, pl.ds(left, width)]
+    query = rows_scratch[z].T
+    tokens = values[0].shape[3]
     head_at = lax.broadcasted_iota(jnp.int32, query.shape, 0) // head_width
     spaced = jnp.concatenate([jnp.where(head_at == head, query, jnp.zeros_like(query)) for head in range(count)], 1)
     entry = z * inner + lax.bitwise_xor(place[2], offset)
     bundle = min(HEAD_BUNDLE, count)
     shelves = []
     for shelf in range(PAIR):
+        chosen = [table[entry * 6 + shelf * 3 + at] for at in range(CAP)]
         scores = [
-            jnp.dot(blocks_in[shelf][at][0][...], spaced, preferred_element_type=F32) for at in range(CAP)
+            jnp.dot(
+                keys[shelf][side, pl.ds(pl.multiple_of(slot * tokens, tokens), tokens), :],
+                spaced,
+                preferred_element_type=F32,
+            )
+            for slot in chosen
         ]
         high = functools.reduce(jnp.maximum, [jnp.max(score, 0, keepdims=True) for score in scores])
         exponents = [jnp.exp(score - high) for score in scores]
@@ -298,7 +306,7 @@
         blocks = []
         for first in range(0, count, bundle):
             here = slice(first * head_width, (first + bundle) * head_width)
-            value = jnp.concatenate([blocks_in[shelf][at][1][here, :] for at in range(CAP)], 1)
+            value = jnp.concatenate([values[shelf][side, slot, here, :] for slot in chosen], 1)
             mixed = jnp.dot(value, probs[:, first * rows : (first + bundle) * rows], preferred_element_type=F32)
             for head in range(bundle):
                 blocks.append(
@@ -315,30 +323,11 @@
     out[z, width:, :] = pack_stats(high, total, count, rows)
 
 
-def attend_kernel(
-    place, table, pieces, key_own, key_pair, value_own, value_pair, out, held, turned, arrived, *, offset, column, inner, head_width
-):
-    outer = out.shape[0]
-    tokens, width = held.shape[3:]
-    side = lax.bitwise_xor(place[1], column)
-    copies = []
-    for z in range(outer):
-        entry = z * inner + lax.bitwise_xor(place[2], offset)
-        for shelf, (keys, values) in enumerate(((key_own, value_own), (key_pair, value_pair))):
-            for at in range(CAP):
-                slot = table[entry * 6 + shelf * 3 + at]
-                lead = (z, shelf, at)
-                source = keys.at[side, pl.ds(pl.multiple_of(slot * tokens, tokens), tokens), :]
-                copies.append(pltpu.make_async_copy(source, held.at[lead], arrived.at[lead + (0,)]))
-                copies.append(pltpu.make_async_copy(values.at[side, slot], turned.at[lead], arrived.at[lead + (1,)]))
-    for copy in copies:
-        copy.start()
-    each = len(copies) // outer
-    for z in range(outer):
-        for copy in copies[z * each : (z + 1) * each]:
-            copy.wait()
-        blocks_in = [[(held.at[z, shelf, at], turned.at[z, shelf, at]) for at in range(CAP)] for shelf in range(PAIR)]
-        attend_group(z, place, table, pieces, blocks_in, out, offset, column, inner, head_width)
+def attend_kernel(place, table, key_own, key_pair, value_own, value_pair, *refs, **fixed):
+    *pieces, out, rows_scratch = refs
+    for z in range(out.shape[0]):
+        keys, values = (key_own, key_pair), (value_own, value_pair)
+        attend_group(z, place, table, pieces, keys, values, out, rows_scratch, **fixed)
 
 
 def pack_stats(high, total, count, rows):
@@ -351,31 +340,61 @@
     return packed.astype(BF16)
 
 
-def attend(place, table, pieces, keys, values, offset, column, inner, tokens, head_width):
-    spread, outer, pair, part, half = pieces.shape
-    width = half // spread
-    rows = spread * pair * part
+def attend(place, table, pieces, keys, values, offset, column, inner, head_width):
+    outer, pair, part, half = pieces[0].shape
+    width = half // len(pieces)
+    rows = len(pieces) * pair * part
+    tokens = values[0].shape[3]
     whole = pl.BlockSpec(memory_space=pltpu.VMEM)
-    scalars = pl.BlockSpec(memory_space=pltpu.SMEM)
-    apart = pl.BlockSpec(memory_space=pl.ANY)
     return pl.pallas_call(
         functools.partial(attend_kernel, offset=offset, column=column, inner=inner, head_width=head_width),
-        in_specs=[scalars, scalars, whole] + [apart] * 4,
+        in_specs=[SCALARS, SCALARS] + [whole] * (4 + len(pieces)),
         out_specs=whole,
-        scratch_shapes=[
-            pltpu.VMEM((outer, PAIR, CAP, tokens, width), BF16),
-            pltpu.VMEM((outer, PAIR, CAP, width, tokens), BF16),
-            pltpu.SemaphoreType.DMA((outer, PAIR, CAP, 2)),
-        ],
+        scratch_shapes=[pltpu.VMEM((outer, rows, width), BF16)],
         out_shape=jax.ShapeDtypeStruct((outer, width + STAT_ROWS, rows), BF16),
-        compiler_params=pltpu.CompilerParams(vmem_limit_bytes=WIDE_BYTES),
+        compiler_params=grant(),
         cost_estimate=pl.CostEstimate(
             flops=outer * 4 * 4 * rows * tokens * width * (width // head_width),
             bytes_accessed=outer * 2 * (width + STAT_ROWS) * rows,
             transcendentals=outer * 4 * rows * tokens * (width // head_width),
         ),
         name="attend",
-    )(place, table, pieces, *keys, *values)
+    )(place, table, *keys, *values, *pieces)
+
+
+def stage_kernel(table, key_own, key_pair, value_own, value_pair, queries, out):
+    hand_on(table, out)
+
+
+def stage(table, keys, values, queries):
+    whole = pl.BlockSpec(memory_space=pltpu.VMEM)
+    return pl.pallas_call(
+        stage_kernel,
+        in_specs=[SCALARS] + [whole] * 4 + [pl.BlockSpec(memory_space=pl.ANY)],
+        out_specs=SCALARS,
+        out_shape=jax.ShapeDtypeStruct(table.shape, table.dtype),
+        compiler_params=grant(),
+        cost_estimate=pl.CostEstimate(flops=0, bytes_accessed=8 * 1024 * 1024, transcendentals=0),
+        name="stage",
+    )(table, *keys, *values, queries)
+
+
+def join_kernel(ready, first, second, out):
+    half = first.shape[0]
+    out[:half] = first[...]
+    out[half:] = second[...]
+
+
+def join(ready, first, second):
+    whole = pl.BlockSpec(memory_space=pltpu.VMEM)
+    return pl.pallas_call(
+        join_kernel,
+        in_specs=[SCALARS, whole, whole],
+        out_specs=whole,
+        out_shape=jax.ShapeDtypeStruct((2 * first.shape[0],) + first.shape[1:], first.dtype),
+        compiler_params=grant(),
+        name="join",
+    )(ready, first, second)
 
 
 def unpack_stats(packed, width, count):
@@ -515,18 +534,18 @@
 
     pieces = jnp.stack([kept, swap(sent, "pa", 1)])[None]
     step = inner
-    while step < readers:
+    while 2 * step < readers:
         pieces = jnp.concatenate([pieces, swap(pieces, "pb", step)], 0)
         step *= 2
-    own_pieces = pieces
-    pieces = jnp.stack([pieces] + [swap(pieces, "pa", at * PAIR) for at in range(1, spread)])
-    far = [pieces]
+    ready = stage(table, keys, values, pieces)
+    pieces = join(ready, pieces, swap(pieces, "pb", step))
+    near = [pieces] + [swap(pieces, "pa", at * PAIR) for at in range(1, spread)]
+    far = [near]
     for offset in range(1, inner):
-        near = swap(own_pieces, "pb", offset)[None]
-        far.append(jnp.concatenate([near, swap(pieces[1:], "pb", offset)], 0))
+        far.append([swap(piece, "pb", offset) for piece in near])
     lots = []
     for offset, column in [(o, c) for o in range(inner) for c in range(spread)][1:] + [(0, 0)]:
-        lot = attend(place, table, far[offset], keys, values, offset, column, inner, tokens, head_width)
+        lot = attend(place, ready, far[offset], keys, values, offset, column, inner, head_width)
         bits = column * PAIR * readers + offset
         if bits:
             lot = lax.ppermute(lot, ("pa", "pb"), [(at, at ^ bits) for at in range(runners * readers)])

time: 130 us -> 123 us (0.946)
  Pallas kernels: 66.6 us -> 54.4 us
  local copies, waits for them, and re-layouts: 5.93 us -> 10.8 us
  waiting for transfers between devices: 28.8 us -> 30.8 us
  other arithmetic: 3.29 us -> 1.51 us
    pallas_call x4, Pallas kernels: 33.7 us -> 19.8 us  [attend(): pl.pallas_call(functools.partial(attend_kernel, offset=offset, column=col...]
    all_to_all x1, waiting for transfers between devices: 3.45 us -> 12.8 us  [local(): lax.all_to_all(by_group, 'pb', split_axis=0, concat_axis=0, tiled=True)]
    ppermute x13, waiting for transfers between devices: 21.9 us -> 16.4 us  [swap(): return lax.ppermute(value, axis, [(at, at ^ bits) for at in range(size)])]
    unnamed x27 -> x31, local copies, waits for them, and re-layouts: 4.08 us -> 9.42 us
    ppermute x3, waiting for transfers between devices: 3.45 us -> 1.52 us  [local(): lax.ppermute(lot, ('pa', 'pb'), [(at, at ^ bits) for at in range(runners...]
    pallas_call x0 -> x2, Pallas kernels: none -> 1.72 us  [the longest x1 1.16 us: stage(): pl.pallas_call(stage_kernel, in_specs=[SCALARS] + [whole] * 4 + [pl.Block...]
  transfers between devices with their start and end apart: 17 -> 17, of which waited for: 11 -> 11; matrix products, arithmetic and copies ran while one was open for 4% -> 2% of each run, Pallas kernels for 49% -> 34%
where the time goes in v7:
time: 123 us; the launch traced here: 122 us
  Pallas kernels  54.4 us (44%)
  waiting for transfers between devices  30.8 us (25%)
  starting transfers between devices  24.4 us (20%)
  local copies, waits for them, and re-layouts  10.8 us (9%)
  other arithmetic  1.51 us (1%)
    pallas_call x4, Pallas kernels, attend(): pl.pallas_call(functools.partial(attend_kernel, offset=offset, column=col...  19.8 us
    pallas_call x2, Pallas kernels, project(): pl.pallas_call(project_kernel, grid_spec=pltpu.PrefetchScalarGridSpec(num...  18.5 us
    ppermute x13, waiting for transfers between devices, swap(): return lax.ppermute(value, axis, [(at, at ^ bits) for at in range(size)])  16.4 us
    ppermute x13, starting transfers between devices, swap(): return lax.ppermute(value, axis, [(at, at ^ bits) for at in range(size)])  14.6 us
    all_to_all x1, waiting for transfers between devices, local(): lax.all_to_all(by_group, 'pb', split_axis=0, concat_axis=0, tiled=True)  12.8 us
    unnamed x31, local copies, waits for them, and re-layouts  9.42 us
    pallas_call x1, Pallas kernels, retrieve(): pl.pallas_call(functools.partial(retrieval_kernel, spread=spread), grid_s...  7.46 us
    all_to_all x1, starting transfers between devices, local(): lax.all_to_all(by_group, 'pb', split_axis=0, concat_axis=0, tiled=True)  6.09 us
  transfers between devices with their start and end apart: 17, of which 11 were waited for; matrix products, arithmetic and copies ran while one was open for 2% of the time, Pallas kernels for 34%

profile of v7, /device:TPU:0, one launch (start us, length us, event | category | flops | bytes accessed | tf_op | source)
XLA Modules:
  0.0 122.1 jit_solution(4203524569894768049)
XLA Ops:
  1.1 7.5 %retrieve.1 = (bf16[2,8,32,896]{3,2,1,0:T(8,128)(2,1)}, bf16[2,8,32,896]{3,2,1,0:T(8,128)(2,1)}) custom-call(s32[4]{0:T(128)} %pad_add_fusion.1.place, bf16[1024,768]{1,0:T(8,128)(2,1)} %queries.1, bf16[512,768]{1,0:T(8,128)(2,1)} %passages.1, bf16[1024,512]{1,0:T(8,128)(2,1)} %noise.1), custom_call_target="tpu_custom_call" | custom-call | flops 1610612736 | bytes 4980736 | tf_op jit(solution)/shard_map/retrieve/pallas_call | solution.py:101
  9.8 1.2 collective-permute-done
  11.2 1.2 copy-done.7
  12.4 2.1 %merge_pair.1 = (bf16[8,32,896]{2,1,0:T(8,128)(2,1)S(1)}, bf16[8,32,896]{2,1,0:T(8,128)(2,1)S(1)}, s32[4]{0:T(128)S(1)}) custom-call(s32[4]{0:T(128)S(1)} %copy-done.9, bf16[2,8,32,896]{3,2,1,0:T(8,128)(2,1)S(1)} %copy-done.7, bf16[2,8,32,896]{3,2,1,0:T(8,128)(2,1)S(1)} %collective-permute-done.1.recv), custom_call_target="tpu_custom_call" | custom-call | tf_op jit(solution)/shard_map/merge_pair/pallas_call | solution.py:151
  14.5 2.7 %collective-permute-start.2 = (bf16[8,32,896]{2,1,0:T(8,128)(2,1)S(1)}, bf16[8,32,896]{2,1,0:T(8,128)(2,1)S(1)}, u32[]{:S(2)}, u32[]{:S(2)}) collective-permute-start(bf16[8,32,896]{2,1,0:T(8,128)(2,1)S(1)} %get-tuple-element.29), channel_id=1, source_target_pairs={{0,16},{8,24},{16,0},{24,8},{1,17},{9,25},{17,1},{25,9},{2,18},{10... | collective-permute-start | bytes 1376264 | tf_op jit(solution)/shard_map/ppermute | solution.py:501
  17.3 9.2 %project.2 = (bf16[2,2048,256]{2,1,0:T(8,128)(2,1)}, bf16[2,8,256,256]{3,2,1,0:T(8,128)(2,1)}, f32[8,128]{1,0:T(8,128)}) custom-call(s32[4]{0:T(128)} %copy-done.13, bf16[2048,1024]{1,0:T(8,128)(2,1)} %bitcast.32, bf16[1024,1024]{1,0:T(8,128)(2,1)} %refs_1_.3, bf16[1024,1024]{1,0:T(8,128)(2,1)} %refs_1_.3, bf16[1024,1024]{1,0:T(8,128)(2,1)} %refs_3_.3, ...), custom_call_target="tpu_custom_call" | custom-call | flops 4294967296 | bytes 10485760 | tf_op jit(solution)/shard_map/project/pallas_call | solution.py:245
  26.5 1.7 %collective-permute-done.2.refs_1_ = bf16[8,32,896]{2,1,0:T(8,128)(2,1)S(1)} collective-permute-done((bf16[8,32,896]{2,1,0:T(8,128)(2,1)S(1)}, bf16[8,32,896]{2,1,0:T(8,128)(2,1)S(1)}, u32[]{:S(2)}, u32[]{:S(2)}) %collective-permute-start.2) | collective-permute-done | bytes 458784 | tf_op jit(solution)/shard_map/ppermute | solution.py:501
  28.9 1.9 %merge_columns.1 = (bf16[8,32,896]{2,1,0:T(8,128)(2,1)}, s32[4]{0:T(128)S(1)}) custom-call(s32[4]{0:T(128)S(1)} %copy-done.9, f32[1,128]{1,0:T(1,128)S(1)} %pad.4.note, f32[8,128]{1,0:T(8,128)S(1)} %copy-done.10, bf16[8,32,896]{2,1,0:T(8,128)(2,1)S(1)} %get-tuple-element.28.refs_0_, bf16[8,32,896]{2,1,0:T(8,128)(2,1)S(1)} %collective-permute-done.2.refs_1_), custom_call_target="tpu_custom_call" | custom-call | tf_op jit(solution)/shard_map/merge_columns/pallas_call | solution.py:172
  31.3 6.1 %all-to-all-start = ((bf16[8,32,896]{2,1,0:T(8,128)(2,1)}), bf16[8,32,896]{2,1,0:T(8,128)(2,1)S(1)}, u32[]{:S(2)}, u32[]{:S(2)}) async-start(bf16[8,32,896]{2,1,0:T(8,128)(2,1)} %get-tuple-element.30), calls=%async_computation | async-start | bytes 917504 | tf_op jit(solution)/shard_map/all_to_all | solution.py:515
  37.4 12.8 %all-to-all-done.parts = bf16[8,32,896]{2,1,0:T(8,128)(2,1)S(1)} async-done(((bf16[8,32,896]{2,1,0:T(8,128)(2,1)}), bf16[8,32,896]{2,1,0:T(8,128)(2,1)S(1)}, u32[]{:S(2)}, u32[]{:S(2)}) %all-to-all-start) | async-done | bytes 458784 | tf_op jit(solution)/shard_map/all_to_all | solution.py:515
  50.3 9.4 %project.3 = (bf16[2,2048,256]{2,1,0:T(8,128)(2,1)}, bf16[2,8,256,256]{3,2,1,0:T(8,128)(2,1)}, f32[8,128]{1,0:T(8,128)}) custom-call(s32[4]{0:T(128)} %copy-done.12, bf16[2048,1024]{1,0:T(8,128)(2,1)} %collective-permute-done.3.states, bf16[1024,1024]{1,0:T(8,128)(2,1)} %refs_1_.3, bf16[1024,1024]{1,0:T(8,128)(2,1)} %refs_1_.3, bf16[1024,1024]{1,0:T(8,128)(2,1)} %refs_3_.3, ...), custom_call_target="tpu_custom_call" | custom-call | flops 4294967296 | bytes 10485760 | tf_op jit(solution)/shard_map/project/pallas_call | solution.py:245
  59.7 1.5 %copy-done.6 = bf16[768,1024]{1,0:T(8,128)(2,1)S(1)} copy-done((bf16[768,1024]{1,0:T(8,128)(2,1)S(1)}, bf16[768,1024]{1,0:T(8,128)(2,1)}, u32[]{:S(2)}) %copy-start.6) | copy-done | bytes 1572888
  62.0 1.2 condition.1
  63.2 1.2 collective-permute-done.4
  65.4 3.3 %collective-permute-done.5 = bf16[1,2,32,512]{3,2,1,0:T(8,128)(2,1)S(1)} collective-permute-done((bf16[1,2,32,512]{3,2,1,0:T(8,128)(2,1)S(1)}, bf16[1,2,32,512]{3,2,1,0:T(8,128)(2,1)S(1)}, u32[]{:S(2)}, u32[]{:S(2)}) %collective-permute-start.5) | collective-permute-done | bytes 65568 | tf_op jit(solution)/shard_map/ppermute | solution.py:501
  70.7 1.6 %copy-done.2 = bf16[2,8,256,256]{3,2,1,0:T(8,128)(2,1)S(1)} copy-done((bf16[2,8,256,256]{3,2,1,0:T(8,128)(2,1)S(1)}, bf16[2,8,256,256]{3,2,1,0:T(8,128)(2,1)}, u32[]{:S(2)}) %copy-start.2) | copy-done | bytes 2097176
  72.2 1.6 %copy-done.4 = bf16[2,2048,256]{2,1,0:T(8,128)(2,1)S(1)} copy-done((bf16[2,2048,256]{2,1,0:T(8,128)(2,1)S(1)}, bf16[2,2048,256]{2,1,0:T(8,128)(2,1)}, u32[]{:S(2)}) %copy-start.4) | copy-done | bytes 2097176
  73.8 1.6 %copy-done.5 = bf16[2,8,256,256]{3,2,1,0:T(8,128)(2,1)S(1)} copy-done((bf16[2,8,256,256]{3,2,1,0:T(8,128)(2,1)S(1)}, bf16[2,8,256,256]{3,2,1,0:T(8,128)(2,1)}, u32[]{:S(2)}) %copy-start.5) | copy-done | bytes 2097176
  77.5 1.6 %collective-permute-start.7 = (bf16[4,2,32,512]{3,2,1,0:T(8,128)(2,1)S(1)}, bf16[4,2,32,512]{3,2,1,0:T(8,128)(2,1)S(1)}, u32[]{:S(2)}, u32[]{:S(2)}) collective-permute-start(bf16[4,2,32,512]{3,2,1,0:T(8,128)(2,1)S(1)} %join.1.refs_0_), channel_id=1, source_target_pairs={{0,16},{8,24},{16,0},{24,8},{1,17},{9,25},{17,1},{25,9},{2,18},{10... | collective-permute-start | bytes 786440 | tf_op jit(solution)/shard_map/ppermute | solution.py:501
  79.0 1.4 %collective-permute-start.9 = (bf16[4,2,32,512]{3,2,1,0:T(8,128)(2,1)S(1)}, bf16[4,2,32,512]{3,2,1,0:T(8,128)(2,1)S(1)}, u32[]{:S(2)}, u32[]{:S(2)}) collective-permute-start(bf16[4,2,32,512]{3,2,1,0:T(8,128)(2,1)S(1)} %join.1.refs_0_), channel_id=1, source_target_pairs={{0,1},{1,0},{2,3},{3,2},{4,5},{5,4},{6,7},{7,6},{8,9},{9,8},{10,11... | collective-permute-start | bytes 786440 | tf_op jit(solution)/shard_map/ppermute | solution.py:501
  80.4 4.7 %collective-permute-done.7.refs_1_ = bf16[4,2,32,512]{3,2,1,0:T(8,128)(2,1)S(1)} collective-permute-done((bf16[4,2,32,512]{3,2,1,0:T(8,128)(2,1)S(1)}, bf16[4,2,32,512]{3,2,1,0:T(8,128)(2,1)S(1)}, u32[]{:S(2)}, u32[]{:S(2)}) %collective-permute-start.7) | collective-permute-done | bytes 262176 | tf_op jit(solution)/shard_map/ppermute | solution.py:501
  85.2 1.8 %collective-permute-start.10 = (bf16[4,2,32,512]{3,2,1,0:T(8,128)(2,1)S(1)}, bf16[4,2,32,512]{3,2,1,0:T(8,128)(2,1)S(1)}, u32[]{:S(2)}, u32[]{:S(2)}) collective-permute-start(bf16[4,2,32,512]{3,2,1,0:T(8,128)(2,1)S(1)} %collective-permute-done.7.refs_1_), channel_id=1, source_target_pairs={{0,1},{1,0},{2,3},{3,2},{4,5},{5,4},{6,7},{7,6},{8,9},{9,8},{10,11... | collective-permute-start | bytes 786440 | tf_op jit(solution)/shard_map/ppermute | solution.py:501
  87.0 4.9 %attend.4 = bf16[4,288,128]{2,1,0:T(8,128)(2,1)S(1)} custom-call(s32[4]{0:T(128)S(1)} %copy-done.9, s32[48]{0:T(128)S(1)} %stage.1.ready.table, bf16[2,2048,256]{2,1,0:T(8,128)(2,1)S(1)} %copy-done.1, bf16[2,2048,256]{2,1,0:T(8,128)(2,1)S(1)} %copy-done.4, bf16[2,8,256,256]{3,2,1,0:T(8,128)(2,1)S(1)} %copy-done.3, bf16[2,8,256,256]{3,2,1,0:T(8,128)(2,1)S(1)} %copy-done.5, ...), custom_call_target="tpu_custom_call" | custom-call | flops 2147483648 | bytes 294912 | tf_op jit(solution)/shard_map/attend/pallas_call | solution.py:349
  91.9 1.6 %collective-permute-start.8 = (bf16[4,288,128]{2,1,0:T(8,128)(2,1)S(1)}, bf16[4,288,128]{2,1,0:T(8,128)(2,1)S(1)}, u32[]{:S(2)}, u32[]{:S(2)}) collective-permute-start(bf16[4,288,128]{2,1,0:T(8,128)(2,1)S(1)} %attend.4), channel_id=1, source_target_pairs={{0,16},{1,17},{2,18},{3,19},{4,20},{5,21},{6,22},{7,23},{8,24},{9,... | collective-permute-start | bytes 884744 | tf_op jit(solution)/shard_map/ppermute | solution.py:551
  93.5 4.9 %attend.5 = bf16[4,288,128]{2,1,0:T(8,128)(2,1)S(1)} custom-call(s32[4]{0:T(128)S(1)} %copy-done.9, s32[48]{0:T(128)S(1)} %stage.1.ready.table, bf16[2,2048,256]{2,1,0:T(8,128)(2,1)S(1)} %copy-done.1, bf16[2,2048,256]{2,1,0:T(8,128)(2,1)S(1)} %copy-done.4, bf16[2,8,256,256]{3,2,1,0:T(8,128)(2,1)S(1)} %copy-done.3, bf16[2,8,256,256]{3,2,1,0:T(8,128)(2,1)S(1)} %copy-done.5, ...), custom_call_target="tpu_custom_call" | custom-call | flops 2147483648 | bytes 294912 | tf_op jit(solution)/shard_map/attend/pallas_call | solution.py:349
  99.1 5.1 %attend.6 = bf16[4,288,128]{2,1,0:T(8,128)(2,1)S(1)} custom-call(s32[4]{0:T(128)S(1)} %copy-done.9, s32[48]{0:T(128)S(1)} %stage.1.ready.table, bf16[2,2048,256]{2,1,0:T(8,128)(2,1)S(1)} %copy-done.1, bf16[2,2048,256]{2,1,0:T(8,128)(2,1)S(1)} %copy-done.4, bf16[2,8,256,256]{3,2,1,0:T(8,128)(2,1)S(1)} %copy-done.3, bf16[2,8,256,256]{3,2,1,0:T(8,128)(2,1)S(1)} %copy-done.5, ...), custom_call_target="tpu_custom_call" | custom-call | flops 2147483648 | bytes 294912 | tf_op jit(solution)/shard_map/attend/pallas_call | solution.py:349
  104.2 1.4 %collective-permute-start.12 = (bf16[4,288,128]{2,1,0:T(8,128)(2,1)S(1)}, bf16[4,288,128]{2,1,0:T(8,128)(2,1)S(1)}, u32[]{:S(2)}, u32[]{:S(2)}) collective-permute-start(bf16[4,288,128]{2,1,0:T(8,128)(2,1)S(1)} %attend.6), channel_id=1, source_target_pairs={{0,17},{1,16},{2,19},{3,18},{4,21},{5,20},{6,23},{7,22},{8,25},{9,... | collective-permute-start | bytes 884744 | tf_op jit(solution)/shard_map/ppermute | solution.py:551
  105.6 4.9 %attend.7.refs_3_ = bf16[4,288,128]{2,1,0:T(8,128)(2,1)S(1)} custom-call(s32[4]{0:T(128)S(1)} %copy-done.9, s32[48]{0:T(128)S(1)} %stage.1.ready.table, bf16[2,2048,256]{2,1,0:T(8,128)(2,1)S(1)} %copy-done.1, bf16[2,2048,256]{2,1,0:T(8,128)(2,1)S(1)} %copy-done.4, bf16[2,8,256,256]{3,2,1,0:T(8,128)(2,1)S(1)} %copy-done.3, ...), custom_call_target="tpu_custom_call" | custom-call | flops 2147483648 | bytes 294912 | tf_op jit(solution)/shard_map/attend/pallas_call | solution.py:349
  110.5 1.5 %collective-permute-done.11.refs_1_ = bf16[4,288,128]{2,1,0:T(8,128)(2,1)S(1)} collective-permute-done((bf16[4,288,128]{2,1,0:T(8,128)(2,1)S(1)}, bf16[4,288,128]{2,1,0:T(8,128)(2,1)S(1)}, u32[]{:S(2)}, u32[]{:S(2)}) %collective-permute-start.11) | collective-permute-done | bytes 294944 | tf_op jit(solution)/shard_map/ppermute | solution.py:551
  113.1 2.1 %collective-permute-start.14 = (bf16[288,128]{1,0:T(8,128)(2,1)S(1)}, bf16[288,128]{1,0:T(8,128)(2,1)S(1)}, u32[]{:S(2)}, u32[]{:S(2)}) collective-permute-start(bf16[288,128]{1,0:T(8,128)(2,1)S(1)} %get-tuple-element.41), channel_id=1, source_target_pairs={{0,4},{1,5},{2,6},{3,7},{4,0},{5,1},{6,2},{7,3},{8,12},{9,13},{10,... | collective-permute-start | bytes 221192 | tf_op jit(solution)/shard_map/ppermute | solution.py:501
  115.1 2.3 %collective-permute-start.15 = (bf16[288,128]{1,0:T(8,128)(2,1)S(1)}, bf16[288,128]{1,0:T(8,128)(2,1)S(1)}, u32[]{:S(2)}, u32[]{:S(2)}) collective-permute-start(bf16[288,128]{1,0:T(8,128)(2,1)S(1)} %get-tuple-element.42), channel_id=1, source_target_pairs={{0,6},{1,7},{2,4},{3,5},{4,2},{5,3},{6,0},{7,1},{8,14},{9,15},{10,... | collective-permute-start | bytes 221192 | tf_op jit(solution)/shard_map/ppermute | solution.py:501
  118.4 2.9 %collective-permute-done.15.refs_3_ = bf16[288,128]{1,0:T(8,128)(2,1)S(1)} collective-permute-done((bf16[288,128]{1,0:T(8,128)(2,1)S(1)}, bf16[288,128]{1,0:T(8,128)(2,1)S(1)}, u32[]{:S(2)}, u32[]{:S(2)}) %collective-permute-start.15) | collective-permute-done | bytes 73760 | tf_op jit(solution)/shard_map/ppermute | solution.py:501
  (72 shorter events, 13.3 us)
Async XLA Ops:
  0.0 8.6 %copy-start = (s32[256]{0:T(256)S(1)}, s32[256]{0:T(256)}, u32[]{:S(2)}) copy-start(s32[256]{0:T(256)} %param.18) | copy-start | bytes 3076
  0.0 50.3 %collective-permute-start.3 = (bf16[2048,1024]{1,0:T(8,128)(2,1)}, bf16[2048,1024]{1,0:T(8,128)(2,1)}, u32[]{:S(2)}, u32[]{:S(2)}) collective-permute-start(bf16[2048,1024]{1,0:T(8,128)(2,1)} %bitcast.31), channel_id=1, source_target_pairs={{0,8},{8,0},{16,24},{24,16},{1,9},{9,1},{17,25},{25,17},{2,10},{10... | collective-permute-start | bytes 12582920 | tf_op jit(solution)/shard_map/ppermute | solution.py:501
  1.1 7.5 %copy-start.14 = (s32[1,16]{1,0:T(1,128)S(1)}, s32[1,16]{1,0:T(1,128)}, u32[]{:S(2)}) copy-start(s32[1,16]{1,0:T(1,128)} %param.19) | copy-start | bytes 196
  1.1 10.2 %copy-start.9 = (s32[4]{0:T(128)S(1)}, s32[4]{0:T(128)}, u32[]{:S(2)}) copy-start(s32[4]{0:T(128)} %pad_add_fusion.1.place) | copy-start | bytes 52
  8.5 2.7 %collective-permute-start.1 = (bf16[2,8,32,896]{3,2,1,0:T(8,128)(2,1)}, bf16[2,8,32,896]{3,2,1,0:T(8,128)(2,1)S(1)}, u32[]{:S(2)}, u32[]{:S(2)}) collective-permute-start(bf16[2,8,32,896]{3,2,1,0:T(8,128)(2,1)} %get-tuple-element.25), channel_id=1, source_target_pairs={{0,8},{8,0},{16,24},{24,16},{1,9},{9,1},{17,25},{25,17},{2,10},{10... | collective-permute-start | bytes 2752520 | tf_op jit(solution)/shard_map/ppermute | solution.py:501
  9.3 1.7 %collective-permute-start = (s32[16]{0:T(128)S(1)}, s32[16]{0:T(128)S(1)}, u32[]{:S(2)}, u32[]{:S(2)}) collective-permute-start(s32[16]{0:T(128)S(1)} %and_select_fusion.4), channel_id=1, source_target_pairs={{0,8},{8,0},{16,24},{24,16},{1,9},{9,1},{17,25},{25,17},{2,10},{10... | collective-permute-start | bytes 200 | tf_op jit(solution)/shard_map/ppermute | solution.py:501
  11.2 1.2 copy-start.7
  14.5 2.7 %copy-start.13 = (s32[4]{0:T(128)}, s32[4]{0:T(128)S(1)}, u32[]{:S(2)}) copy-start(s32[4]{0:T(128)S(1)} %get-tuple-element.26.place) | copy-start | bytes 52
  14.5 13.7 %collective-permute-start.2 = (bf16[8,32,896]{2,1,0:T(8,128)(2,1)S(1)}, bf16[8,32,896]{2,1,0:T(8,128)(2,1)S(1)}, u32[]{:S(2)}, u32[]{:S(2)}) collective-permute-start(bf16[8,32,896]{2,1,0:T(8,128)(2,1)S(1)} %get-tuple-element.29), channel_id=1, source_target_pairs={{0,16},{8,24},{16,0},{24,8},{1,17},{9,25},{17,1},{25,9},{2,18},{10... | collective-permute-start | bytes 1376264 | tf_op jit(solution)/shard_map/ppermute | solution.py:501
  28.2 0.7 copy-start.10
  30.8 0.5 copy-start.12
  31.3 18.9 %all-to-all-start = ((bf16[8,32,896]{2,1,0:T(8,128)(2,1)}), bf16[8,32,896]{2,1,0:T(8,128)(2,1)S(1)}, u32[]{:S(2)}, u32[]{:S(2)}) async-start(bf16[8,32,896]{2,1,0:T(8,128)(2,1)} %get-tuple-element.30), calls=%async_computation | async-start | bytes 917504 | tf_op jit(solution)/shard_map/all_to_all | solution.py:515
  50.3 9.4 %copy-start.8 = (bf16[128,1024]{1,0:T(8,128)(2,1)S(1)}, bf16[128,1024]{1,0:T(8,128)(2,1)}, u32[]{:S(2)}) copy-start(bf16[128,1024]{1,0:T(8,128)(2,1)} %answers.1) | copy-start | bytes 786436
  59.7 10.9 %copy-start.1 = (bf16[2,2048,256]{2,1,0:T(8,128)(2,1)S(1)}, bf16[2,2048,256]{2,1,0:T(8,128)(2,1)}, u32[]{:S(2)}) copy-start(bf16[2,2048,256]{2,1,0:T(8,128)(2,1)} %get-tuple-element.31.key_own) | copy-start | bytes 6291460
  59.7 1.6 %copy-start.6 = (bf16[768,1024]{1,0:T(8,128)(2,1)S(1)}, bf16[768,1024]{1,0:T(8,128)(2,1)}, u32[]{:S(2)}) copy-start(bf16[768,1024]{1,0:T(8,128)(2,1)} %mix_weight.1) | copy-start | bytes 4718596
  61.3 0.7 copy-start.11
  63.1 1.3 %collective-permute-start.4 = (bf16[32,512]{1,0:T(8,128)(2,1)S(1)}, bf16[32,512]{1,0:T(8,128)(2,1)S(1)}, u32[]{:S(2)}, u32[]{:S(2)}) collective-permute-start(bf16[32,512]{1,0:T(8,128)(2,1)S(1)} %get-tuple-element.38), channel_id=1, source_target_pairs={{0,8},{8,0},{16,24},{24,16},{1,9},{9,1},{17,25},{25,17},{2,10},{10... | collective-permute-start | bytes 98312 | tf_op jit(solution)/shard_map/ppermute | solution.py:501
  64.4 4.3 %collective-permute-start.5 = (bf16[1,2,32,512]{3,2,1,0:T(8,128)(2,1)S(1)}, bf16[1,2,32,512]{3,2,1,0:T(8,128)(2,1)S(1)}, u32[]{:S(2)}, u32[]{:S(2)}) collective-permute-start(bf16[1,2,32,512]{3,2,1,0:T(8,128)(2,1)S(1)} %maximum_bitcast_fusion), channel_id=1, source_target_pairs={{0,2},{1,3},{2,0},{3,1},{4,6},{5,7},{6,4},{7,5},{8,10},{9,11},{10,... | collective-permute-start | bytes 196616 | tf_op jit(solution)/shard_map/ppermute | solution.py:501
  68.8 8.1 %collective-permute-start.6 = (bf16[2,2,32,512]{3,2,1,0:T(8,128)(2,1)S(1)}, bf16[2,2,32,512]{3,2,1,0:T(8,128)(2,1)S(1)}, u32[]{:S(2)}, u32[]{:S(2)}) collective-permute-start(bf16[2,2,32,512]{3,2,1,0:T(8,128)(2,1)S(1)} %pad_maximum_fusion.queries.first), channel_id=1, source_target_pairs={{0,4},{1,5},{2,6},{3,7},{4,0},{5,1},{6,2},{7,3},{8,12},{9,13},{10,... | collective-permute-start | bytes 393224 | tf_op jit(solution)/shard_map/ppermute | solution.py:501
  70.6 1.6 %copy-start.2 = (bf16[2,8,256,256]{3,2,1,0:T(8,128)(2,1)S(1)}, bf16[2,8,256,256]{3,2,1,0:T(8,128)(2,1)}, u32[]{:S(2)}) copy-start(bf16[2,8,256,256]{3,2,1,0:T(8,128)(2,1)} %get-tuple-element.34.value_own) | copy-start | bytes 6291460
  72.2 1.6 %copy-start.4 = (bf16[2,2048,256]{2,1,0:T(8,128)(2,1)S(1)}, bf16[2,2048,256]{2,1,0:T(8,128)(2,1)}, u32[]{:S(2)}) copy-start(bf16[2,2048,256]{2,1,0:T(8,128)(2,1)} %get-tuple-element.33.key_pair) | copy-start | bytes 6291460
  73.8 1.6 %copy-start.5 = (bf16[2,8,256,256]{3,2,1,0:T(8,128)(2,1)S(1)}, bf16[2,8,256,256]{3,2,1,0:T(8,128)(2,1)}, u32[]{:S(2)}) copy-start(bf16[2,8,256,256]{3,2,1,0:T(8,128)(2,1)} %get-tuple-element.35.value_pair) | copy-start | bytes 6291460
  75.4 11.6 %copy-start.3 = (bf16[2,8,256,256]{3,2,1,0:T(8,128)(2,1)S(1)}, bf16[2,8,256,256]{3,2,1,0:T(8,128)(2,1)}, u32[]{:S(2)}) copy-start(bf16[2,8,256,256]{3,2,1,0:T(8,128)(2,1)} %get-tuple-element.34.value_own) | copy-start | bytes 6291460
  77.5 7.7 %collective-permute-start.7 = (bf16[4,2,32,512]{3,2,1,0:T(8,128)(2,1)S(1)}, bf16[4,2,32,512]{3,2,1,0:T(8,128)(2,1)S(1)}, u32[]{:S(2)}, u32[]{:S(2)}) collective-permute-start(bf16[4,2,32,512]{3,2,1,0:T(8,128)(2,1)S(1)} %join.1.refs_0_), channel_id=1, source_target_pairs={{0,16},{8,24},{16,0},{24,8},{1,17},{9,25},{17,1},{25,9},{2,18},{10... | collective-permute-start | bytes 786440 | tf_op jit(solution)/shard_map/ppermute | solution.py:501
  79.0 14.4 %collective-permute-start.9 = (bf16[4,2,32,512]{3,2,1,0:T(8,128)(2,1)S(1)}, bf16[4,2,32,512]{3,2,1,0:T(8,128)(2,1)S(1)}, u32[]{:S(2)}, u32[]{:S(2)}) collective-permute-start(bf16[4,2,32,512]{3,2,1,0:T(8,128)(2,1)S(1)} %join.1.refs_0_), channel_id=1, source_target_pairs={{0,1},{1,0},{2,3},{3,2},{4,5},{5,4},{6,7},{7,6},{8,9},{9,8},{10,11... | collective-permute-start | bytes 786440 | tf_op jit(solution)/shard_map/ppermute | solution.py:501
  85.2 8.3 %collective-permute-start.10 = (bf16[4,2,32,512]{3,2,1,0:T(8,128)(2,1)S(1)}, bf16[4,2,32,512]{3,2,1,0:T(8,128)(2,1)S(1)}, u32[]{:S(2)}, u32[]{:S(2)}) collective-permute-start(bf16[4,2,32,512]{3,2,1,0:T(8,128)(2,1)S(1)} %collective-permute-done.7.refs_1_), channel_id=1, source_target_pairs={{0,1},{1,0},{2,3},{3,2},{4,5},{5,4},{6,7},{7,6},{8,9},{9,8},{10,11... | collective-permute-start | bytes 786440 | tf_op jit(solution)/shard_map/ppermute | solution.py:501
  91.9 18.6 %collective-permute-start.8 = (bf16[4,288,128]{2,1,0:T(8,128)(2,1)S(1)}, bf16[4,288,128]{2,1,0:T(8,128)(2,1)S(1)}, u32[]{:S(2)}, u32[]{:S(2)}) collective-permute-start(bf16[4,288,128]{2,1,0:T(8,128)(2,1)S(1)} %attend.4), channel_id=1, source_target_pairs={{0,16},{1,17},{2,18},{3,19},{4,20},{5,21},{6,22},{7,23},{8,24},{9,... | collective-permute-start | bytes 884744 | tf_op jit(solution)/shard_map/ppermute | solution.py:551
  98.3 13.7 %collective-permute-start.11 = (bf16[4,288,128]{2,1,0:T(8,128)(2,1)S(1)}, bf16[4,288,128]{2,1,0:T(8,128)(2,1)S(1)}, u32[]{:S(2)}, u32[]{:S(2)}) collective-permute-start(bf16[4,288,128]{2,1,0:T(8,128)(2,1)S(1)} %attend.5), channel_id=1, source_target_pairs={{0,1},{1,0},{2,3},{3,2},{4,5},{5,4},{6,7},{7,6},{8,9},{9,8},{10,11... | collective-permute-start | bytes 884744 | tf_op jit(solution)/shard_map/ppermute | solution.py:551
  104.2 7.8 %collective-permute-start.12 = (bf16[4,288,128]{2,1,0:T(8,128)(2,1)S(1)}, bf16[4,288,128]{2,1,0:T(8,128)(2,1)S(1)}, u32[]{:S(2)}, u32[]{:S(2)}) collective-permute-start(bf16[4,288,128]{2,1,0:T(8,128)(2,1)S(1)} %attend.6), channel_id=1, source_target_pairs={{0,17},{1,16},{2,19},{3,18},{4,21},{5,20},{6,23},{7,22},{8,25},{9,... | collective-permute-start | bytes 884744 | tf_op jit(solution)/shard_map/ppermute | solution.py:551
  113.0 4.5 %collective-permute-start.13 = (bf16[288,128]{1,0:T(8,128)(2,1)S(1)}, bf16[288,128]{1,0:T(8,128)(2,1)S(1)}, u32[]{:S(2)}, u32[]{:S(2)}) collective-permute-start(bf16[288,128]{1,0:T(8,128)(2,1)S(1)} %get-tuple-element.40), channel_id=1, source_target_pairs={{0,2},{1,3},{2,0},{3,1},{4,6},{5,7},{6,4},{7,5},{8,10},{9,11},{10,... | collective-permute-start | bytes 221192 | tf_op jit(solution)/shard_map/ppermute | solution.py:501
  113.1 5.3 %collective-permute-start.14 = (bf16[288,128]{1,0:T(8,128)(2,1)S(1)}, bf16[288,128]{1,0:T(8,128)(2,1)S(1)}, u32[]{:S(2)}, u32[]{:S(2)}) collective-permute-start(bf16[288,128]{1,0:T(8,128)(2,1)S(1)} %get-tuple-element.41), channel_id=1, source_target_pairs={{0,4},{1,5},{2,6},{3,7},{4,0},{5,1},{6,2},{7,3},{8,12},{9,13},{10,... | collective-permute-start | bytes 221192 | tf_op jit(solution)/shard_map/ppermute | solution.py:501
  115.1 6.2 %collective-permute-start.15 = (bf16[288,128]{1,0:T(8,128)(2,1)S(1)}, bf16[288,128]{1,0:T(8,128)(2,1)S(1)}, u32[]{:S(2)}, u32[]{:S(2)}) collective-permute-start(bf16[288,128]{1,0:T(8,128)(2,1)S(1)} %get-tuple-element.42), channel_id=1, source_target_pairs={{0,6},{1,7},{2,4},{3,5},{4,2},{5,3},{6,0},{7,1},{8,14},{9,15},{10,... | collective-permute-start | bytes 221192 | tf_op jit(solution)/shard_map/ppermute | solution.py:501

commit v8 on v7

--- a/solution.py
+++ b/solution.py
@@ -17,9 +17,10 @@
 NOTE_AT = 6
 STEP_GROUPS = 2
 PROJECT_STEPS = 4
+HINT = 16
 HEAD_BUNDLE = 2
 VMEM_BYTES = 16 * 1024 * 1024
-WIDE_BYTES = 60 * 1024 * 1024
+WIDE_BYTES = 62 * 1024 * 1024
 F32 = jnp.float32
 BF16 = jnp.bfloat16
 NT = (((1,), (1,)), ((), ()))
@@ -261,8 +262,8 @@
         ],
         compiler_params=pltpu.CompilerParams(vmem_limit_bytes=WIDE_BYTES),
         cost_estimate=pl.CostEstimate(
-            flops=4 * rows * model_width * spread * width,
-            bytes_accessed=2 * (2 * model_width * spread * width + 2 * rows * model_width),
+            flops=4 * rows * model_width * spread * width // HINT,
+            bytes_accessed=2 * (2 * model_width * spread * width + 2 * rows * model_width) // HINT,
             transcendentals=0,
         ),
         name="project",

time: 123 us -> 124 us (level)
  local copies, waits for them, and re-layouts: 10.8 us -> 12.7 us
    unnamed x31, local copies, waits for them, and re-layouts: 9.42 us -> 11.4 us
  transfers between devices with their start and end apart: 17 -> 17, of which waited for: 11 -> 10; matrix products, arithmetic and copies ran while one was open for 2% -> 2% of each run, Pallas kernels for 34% -> 34%
where the time goes in v8:
time: 124 us; the launch traced here: 123 us
  Pallas kernels  54.3 us (44%)
  waiting for transfers between devices  30.9 us (25%)
  starting transfers between devices  23.6 us (19%)
  local copies, waits for them, and re-layouts  12.7 us (10%)
  other arithmetic  1.52 us (1%)
    pallas_call x4, Pallas kernels, attend(): pl.pallas_call(functools.partial(attend_kernel, offset=offset, column=col...  19.7 us
    pallas_call x2, Pallas kernels, project(): pl.pallas_call(project_kernel, grid_spec=pltpu.PrefetchScalarGridSpec(num...  18.6 us
    ppermute x13, waiting for transfers between devices, swap(): return lax.ppermute(value, axis, [(at, at ^ bits) for at in range(size)])  16.8 us
    ppermute x13, starting transfers between devices, swap(): return lax.ppermute(value, axis, [(at, at ^ bits) for at in range(size)])  13.8 us
    all_to_all x1, waiting for transfers between devices, local(): lax.all_to_all(by_group, 'pb', split_axis=0, concat_axis=0, tiled=True)  12.8 us
    unnamed x31, local copies, waits for them, and re-layouts  11.4 us
    pallas_call x1, Pallas kernels, retrieve(): pl.pallas_call(functools.partial(retrieval_kernel, spread=spread), grid_s...  7.46 us
    all_to_all x1, starting transfers between devices, local(): lax.all_to_all(by_group, 'pb', split_axis=0, concat_axis=0, tiled=True)  6.08 us
  transfers between devices with their start and end apart: 17, of which 10 were waited for; matrix products, arithmetic and copies ran while one was open for 2% of the time, Pallas kernels for 34%

profile of v8, /device:TPU:0, one launch (start us, length us, event | category | flops | bytes accessed | tf_op | source)
XLA Modules:
  0.0 123.2 jit_solution(2434296514486062675)
XLA Ops:
  1.1 7.5 %retrieve.1 = (bf16[2,8,32,896]{3,2,1,0:T(8,128)(2,1)}, bf16[2,8,32,896]{3,2,1,0:T(8,128)(2,1)}) custom-call(s32[4]{0:T(128)} %pad_add_fusion.1.place, bf16[1024,768]{1,0:T(8,128)(2,1)} %queries.1, bf16[512,768]{1,0:T(8,128)(2,1)} %passages.1, bf16[1024,512]{1,0:T(8,128)(2,1)} %noise.1), custom_call_target="tpu_custom_call" | custom-call | flops 1610612736 | bytes 4980736 | tf_op jit(solution)/shard_map/retrieve/pallas_call | solution.py:102
  9.8 1.4 %collective-permute-done.1.recv = bf16[2,8,32,896]{3,2,1,0:T(8,128)(2,1)S(1)} collective-permute-done((bf16[2,8,32,896]{3,2,1,0:T(8,128)(2,1)}, bf16[2,8,32,896]{3,2,1,0:T(8,128)(2,1)S(1)}, u32[]{:S(2)}, u32[]{:S(2)}) %collective-permute-start.1) | collective-permute-done | bytes 917536 | tf_op jit(solution)/shard_map/ppermute | solution.py:502
  12.4 2.1 %merge_pair.1 = (bf16[8,32,896]{2,1,0:T(8,128)(2,1)S(1)}, bf16[8,32,896]{2,1,0:T(8,128)(2,1)S(1)}, s32[4]{0:T(128)S(1)}) custom-call(s32[4]{0:T(128)S(1)} %copy-done.9, bf16[2,8,32,896]{3,2,1,0:T(8,128)(2,1)S(1)} %copy-done.7, bf16[2,8,32,896]{3,2,1,0:T(8,128)(2,1)S(1)} %collective-permute-done.1.recv), custom_call_target="tpu_custom_call" | custom-call | tf_op jit(solution)/shard_map/merge_pair/pallas_call | solution.py:152
  15.0 2.6 %collective-permute-start.2 = (bf16[8,32,896]{2,1,0:T(8,128)(2,1)S(1)}, bf16[8,32,896]{2,1,0:T(8,128)(2,1)S(1)}, u32[]{:S(2)}, u32[]{:S(2)}) collective-permute-start(bf16[8,32,896]{2,1,0:T(8,128)(2,1)S(1)} %get-tuple-element.29), channel_id=1, source_target_pairs={{0,16},{8,24},{16,0},{24,8},{1,17},{9,25},{17,1},{25,9},{2,18},{10... | collective-permute-start | bytes 1376264 | tf_op jit(solution)/shard_map/ppermute | solution.py:502
  17.9 9.2 %project.2 = (bf16[2,2048,256]{2,1,0:T(8,128)(2,1)}, bf16[2,8,256,256]{3,2,1,0:T(8,128)(2,1)}, f32[8,128]{1,0:T(8,128)}) custom-call(s32[4]{0:T(128)} %copy-done.12, bf16[2048,1024]{1,0:T(8,128)(2,1)} %bitcast.27, bf16[1024,1024]{1,0:T(8,128)(2,1)} %refs_1_.3, bf16[1024,1024]{1,0:T(8,128)(2,1)} %refs_1_.3, bf16[1024,1024]{1,0:T(8,128)(2,1)} %refs_3_.3, ...), custom_call_target="tpu_custom_call" | custom-call | flops 268435456 | bytes 655360 | tf_op jit(solution)/shard_map/project/pallas_call | solution.py:246
  27.0 1.6 %collective-permute-done.2.refs_1_ = bf16[8,32,896]{2,1,0:T(8,128)(2,1)S(1)} collective-permute-done((bf16[8,32,896]{2,1,0:T(8,128)(2,1)S(1)}, bf16[8,32,896]{2,1,0:T(8,128)(2,1)S(1)}, u32[]{:S(2)}, u32[]{:S(2)}) %collective-permute-start.2) | collective-permute-done | bytes 458784 | tf_op jit(solution)/shard_map/ppermute | solution.py:502
  29.3 1.9 %merge_columns.1 = (bf16[8,32,896]{2,1,0:T(8,128)(2,1)}, s32[4]{0:T(128)S(1)}) custom-call(s32[4]{0:T(128)S(1)} %copy-done.9, f32[1,128]{1,0:T(1,128)S(1)} %pad.4.note, f32[8,128]{1,0:T(8,128)S(1)} %copy-done.10, bf16[8,32,896]{2,1,0:T(8,128)(2,1)S(1)} %get-tuple-element.28.refs_0_, bf16[8,32,896]{2,1,0:T(8,128)(2,1)S(1)} %collective-permute-done.2.refs_1_), custom_call_target="tpu_custom_call" | custom-call | tf_op jit(solution)/shard_map/merge_columns/pallas_call | solution.py:173
  31.7 6.1 %all-to-all-start = ((bf16[8,32,896]{2,1,0:T(8,128)(2,1)}), bf16[8,32,896]{2,1,0:T(8,128)(2,1)S(1)}, u32[]{:S(2)}, u32[]{:S(2)}) async-start(bf16[8,32,896]{2,1,0:T(8,128)(2,1)} %get-tuple-element.30), calls=%async_computation | async-start | bytes 917504 | tf_op jit(solution)/shard_map/all_to_all | solution.py:516
  37.8 12.8 %all-to-all-done.parts = bf16[8,32,896]{2,1,0:T(8,128)(2,1)S(1)} async-done(((bf16[8,32,896]{2,1,0:T(8,128)(2,1)}), bf16[8,32,896]{2,1,0:T(8,128)(2,1)S(1)}, u32[]{:S(2)}, u32[]{:S(2)}) %all-to-all-start) | async-done | bytes 458784 | tf_op jit(solution)/shard_map/all_to_all | solution.py:516
  50.8 9.4 %project.3 = (bf16[2,2048,256]{2,1,0:T(8,128)(2,1)}, bf16[2,8,256,256]{3,2,1,0:T(8,128)(2,1)}, f32[8,128]{1,0:T(8,128)}) custom-call(s32[4]{0:T(128)} %copy-done.13, bf16[2048,1024]{1,0:T(8,128)(2,1)} %collective-permute-done.3.states, bf16[1024,1024]{1,0:T(8,128)(2,1)} %refs_1_.3, bf16[1024,1024]{1,0:T(8,128)(2,1)} %refs_1_.3, bf16[1024,1024]{1,0:T(8,128)(2,1)} %refs_3_.3, ...), custom_call_target="tpu_custom_call" | custom-call | flops 268435456 | bytes 655360 | tf_op jit(solution)/shard_map/project/pallas_call | solution.py:246
  60.1 1.4 %copy-done.6 = bf16[768,1024]{1,0:T(8,128)(2,1)S(1)} copy-done((bf16[768,1024]{1,0:T(8,128)(2,1)S(1)}, bf16[768,1024]{1,0:T(8,128)(2,1)}, u32[]{:S(2)}) %copy-start.6) | copy-done | bytes 1572888
  63.5 1.2 collective-permute-done.4
  65.7 3.3 %collective-permute-done.5 = bf16[1,2,32,512]{3,2,1,0:T(8,128)(2,1)S(1)} collective-permute-done((bf16[1,2,32,512]{3,2,1,0:T(8,128)(2,1)S(1)}, bf16[1,2,32,512]{3,2,1,0:T(8,128)(2,1)S(1)}, u32[]{:S(2)}, u32[]{:S(2)}) %collective-permute-start.5) | collective-permute-done | bytes 65568 | tf_op jit(solution)/shard_map/ppermute | solution.py:502
  70.9 1.6 %copy-done.1 = bf16[2,2048,256]{2,1,0:T(8,128)(2,1)S(1)} copy-done((bf16[2,2048,256]{2,1,0:T(8,128)(2,1)S(1)}, bf16[2,2048,256]{2,1,0:T(8,128)(2,1)}, u32[]{:S(2)}) %copy-start.1) | copy-done | bytes 2097176
  72.5 1.6 %copy-done.3 = bf16[2,8,256,256]{3,2,1,0:T(8,128)(2,1)S(1)} copy-done((bf16[2,8,256,256]{3,2,1,0:T(8,128)(2,1)S(1)}, bf16[2,8,256,256]{3,2,1,0:T(8,128)(2,1)}, u32[]{:S(2)}) %copy-start.3) | copy-done | bytes 2097176
  74.1 1.6 %copy-done.4 = bf16[2,2048,256]{2,1,0:T(8,128)(2,1)S(1)} copy-done((bf16[2,2048,256]{2,1,0:T(8,128)(2,1)S(1)}, bf16[2,2048,256]{2,1,0:T(8,128)(2,1)}, u32[]{:S(2)}) %copy-start.4) | copy-done | bytes 2097176
  75.7 1.6 %copy-done.5 = bf16[2,8,256,256]{3,2,1,0:T(8,128)(2,1)S(1)} copy-done((bf16[2,8,256,256]{3,2,1,0:T(8,128)(2,1)S(1)}, bf16[2,8,256,256]{3,2,1,0:T(8,128)(2,1)}, u32[]{:S(2)}) %copy-start.5) | copy-done | bytes 2097176
  79.0 1.6 %collective-permute-start.7 = (bf16[4,2,32,512]{3,2,1,0:T(8,128)(2,1)S(1)}, bf16[4,2,32,512]{3,2,1,0:T(8,128)(2,1)S(1)}, u32[]{:S(2)}, u32[]{:S(2)}) collective-permute-start(bf16[4,2,32,512]{3,2,1,0:T(8,128)(2,1)S(1)} %join.1.refs_0_), channel_id=1, source_target_pairs={{0,16},{8,24},{16,0},{24,8},{1,17},{9,25},{17,1},{25,9},{2,18},{10... | collective-permute-start | bytes 786440 | tf_op jit(solution)/shard_map/ppermute | solution.py:502
  81.5 4.5 %collective-permute-done.7.refs_1_ = bf16[4,2,32,512]{3,2,1,0:T(8,128)(2,1)S(1)} collective-permute-done((bf16[4,2,32,512]{3,2,1,0:T(8,128)(2,1)S(1)}, bf16[4,2,32,512]{3,2,1,0:T(8,128)(2,1)S(1)}, u32[]{:S(2)}, u32[]{:S(2)}) %collective-permute-start.7) | collective-permute-done | bytes 262176 | tf_op jit(solution)/shard_map/ppermute | solution.py:502
  86.0 1.5 %collective-permute-start.10 = (bf16[4,2,32,512]{3,2,1,0:T(8,128)(2,1)S(1)}, bf16[4,2,32,512]{3,2,1,0:T(8,128)(2,1)S(1)}, u32[]{:S(2)}, u32[]{:S(2)}) collective-permute-start(bf16[4,2,32,512]{3,2,1,0:T(8,128)(2,1)S(1)} %collective-permute-done.7.refs_1_), channel_id=1, source_target_pairs={{0,1},{1,0},{2,3},{3,2},{4,5},{5,4},{6,7},{7,6},{8,9},{9,8},{10,11... | collective-permute-start | bytes 786440 | tf_op jit(solution)/shard_map/ppermute | solution.py:502
  87.5 4.9 %attend.4 = bf16[4,288,128]{2,1,0:T(8,128)(2,1)S(1)} custom-call(s32[4]{0:T(128)S(1)} %copy-done.9, s32[48]{0:T(128)S(1)} %stage.1.ready.table, bf16[2,2048,256]{2,1,0:T(8,128)(2,1)S(1)} %copy-done.2, bf16[2,2048,256]{2,1,0:T(8,128)(2,1)S(1)} %copy-done.4, bf16[2,8,256,256]{3,2,1,0:T(8,128)(2,1)S(1)} %copy-done.3, bf16[2,8,256,256]{3,2,1,0:T(8,128)(2,1)S(1)} %copy-done.5, ...), custom_call_target="tpu_custom_call" | custom-call | flops 2147483648 | bytes 294912 | tf_op jit(solution)/shard_map/attend/pallas_call | solution.py:350
  92.4 1.6 %collective-permute-start.8 = (bf16[4,288,128]{2,1,0:T(8,128)(2,1)S(1)}, bf16[4,288,128]{2,1,0:T(8,128)(2,1)S(1)}, u32[]{:S(2)}, u32[]{:S(2)}) collective-permute-start(bf16[4,288,128]{2,1,0:T(8,128)(2,1)S(1)} %attend.4), channel_id=1, source_target_pairs={{0,16},{1,17},{2,18},{3,19},{4,20},{5,21},{6,22},{7,23},{8,24},{9,... | collective-permute-start | bytes 884744 | tf_op jit(solution)/shard_map/ppermute | solution.py:552
  93.9 4.9 %attend.5 = bf16[4,288,128]{2,1,0:T(8,128)(2,1)S(1)} custom-call(s32[4]{0:T(128)S(1)} %copy-done.9, s32[48]{0:T(128)S(1)} %stage.1.ready.table, bf16[2,2048,256]{2,1,0:T(8,128)(2,1)S(1)} %copy-done.2, bf16[2,2048,256]{2,1,0:T(8,128)(2,1)S(1)} %copy-done.4, bf16[2,8,256,256]{3,2,1,0:T(8,128)(2,1)S(1)} %copy-done.3, bf16[2,8,256,256]{3,2,1,0:T(8,128)(2,1)S(1)} %copy-done.5, ...), custom_call_target="tpu_custom_call" | custom-call | flops 2147483648 | bytes 294912 | tf_op jit(solution)/shard_map/attend/pallas_call | solution.py:350
  99.4 5.1 %attend.6 = bf16[4,288,128]{2,1,0:T(8,128)(2,1)S(1)} custom-call(s32[4]{0:T(128)S(1)} %copy-done.9, s32[48]{0:T(128)S(1)} %stage.1.ready.table, bf16[2,2048,256]{2,1,0:T(8,128)(2,1)S(1)} %copy-done.2, bf16[2,2048,256]{2,1,0:T(8,128)(2,1)S(1)} %copy-done.4, bf16[2,8,256,256]{3,2,1,0:T(8,128)(2,1)S(1)} %copy-done.3, bf16[2,8,256,256]{3,2,1,0:T(8,128)(2,1)S(1)} %copy-done.5, ...), custom_call_target="tpu_custom_call" | custom-call | flops 2147483648 | bytes 294912 | tf_op jit(solution)/shard_map/attend/pallas_call | solution.py:350
  104.5 1.5 %collective-permute-start.12 = (bf16[4,288,128]{2,1,0:T(8,128)(2,1)S(1)}, bf16[4,288,128]{2,1,0:T(8,128)(2,1)S(1)}, u32[]{:S(2)}, u32[]{:S(2)}) collective-permute-start(bf16[4,288,128]{2,1,0:T(8,128)(2,1)S(1)} %attend.6), channel_id=1, source_target_pairs={{0,17},{1,16},{2,19},{3,18},{4,21},{5,20},{6,23},{7,22},{8,25},{9,... | collective-permute-start | bytes 884744 | tf_op jit(solution)/shard_map/ppermute | solution.py:552
  106.0 4.9 %attend.7.refs_3_ = bf16[4,288,128]{2,1,0:T(8,128)(2,1)S(1)} custom-call(s32[4]{0:T(128)S(1)} %copy-done.9, s32[48]{0:T(128)S(1)} %stage.1.ready.table, bf16[2,2048,256]{2,1,0:T(8,128)(2,1)S(1)} %copy-done.2, bf16[2,2048,256]{2,1,0:T(8,128)(2,1)S(1)} %copy-done.4, bf16[2,8,256,256]{3,2,1,0:T(8,128)(2,1)S(1)} %copy-done.3, ...), custom_call_target="tpu_custom_call" | custom-call | flops 2147483648 | bytes 294912 | tf_op jit(solution)/shard_map/attend/pallas_call | solution.py:350
  110.9 1.2 %collective-permute-done.12.refs_2_ = bf16[4,288,128]{2,1,0:T(8,128)(2,1)S(1)} collective-permute-done((bf16[4,288,128]{2,1,0:T(8,128)(2,1)S(1)}, bf16[4,288,128]{2,1,0:T(8,128)(2,1)S(1)}, u32[]{:S(2)}, u32[]{:S(2)}) %collective-permute-start.12) | collective-permute-done | bytes 294944 | tf_op jit(solution)/shard_map/ppermute | solution.py:552
  113.1 1.2 collective-permute-start.13
  114.3 1.9 %collective-permute-start.14 = (bf16[288,128]{1,0:T(8,128)(2,1)S(1)}, bf16[288,128]{1,0:T(8,128)(2,1)S(1)}, u32[]{:S(2)}, u32[]{:S(2)}) collective-permute-start(bf16[288,128]{1,0:T(8,128)(2,1)S(1)} %get-tuple-element.41), channel_id=1, source_target_pairs={{0,4},{1,5},{2,6},{3,7},{4,0},{5,1},{6,2},{7,3},{8,12},{9,13},{10,... | collective-permute-start | bytes 221192 | tf_op jit(solution)/shard_map/ppermute | solution.py:502
  116.2 1.4 %collective-permute-start.15 = (bf16[288,128]{1,0:T(8,128)(2,1)S(1)}, bf16[288,128]{1,0:T(8,128)(2,1)S(1)}, u32[]{:S(2)}, u32[]{:S(2)}) collective-permute-start(bf16[288,128]{1,0:T(8,128)(2,1)S(1)} %get-tuple-element.42), channel_id=1, source_target_pairs={{0,6},{1,7},{2,4},{3,5},{4,2},{5,3},{6,0},{7,1},{8,14},{9,15},{10,... | collective-permute-start | bytes 221192 | tf_op jit(solution)/shard_map/ppermute | solution.py:502
  117.9 2.5 %collective-permute-done.14.refs_2_ = bf16[288,128]{1,0:T(8,128)(2,1)S(1)} collective-permute-done((bf16[288,128]{1,0:T(8,128)(2,1)S(1)}, bf16[288,128]{1,0:T(8,128)(2,1)S(1)}, u32[]{:S(2)}, u32[]{:S(2)}) %collective-permute-start.14) | collective-permute-done | bytes 73760 | tf_op jit(solution)/shard_map/ppermute | solution.py:502
  120.4 2.0 %collective-permute-done.15.refs_3_ = bf16[288,128]{1,0:T(8,128)(2,1)S(1)} collective-permute-done((bf16[288,128]{1,0:T(8,128)(2,1)S(1)}, bf16[288,128]{1,0:T(8,128)(2,1)S(1)}, u32[]{:S(2)}, u32[]{:S(2)}) %collective-permute-start.15) | collective-permute-done | bytes 73760 | tf_op jit(solution)/shard_map/ppermute | solution.py:502
  (72 shorter events, 15.6 us)
Async XLA Ops:
  0.0 8.6 %copy-start = (s32[256]{0:T(256)S(1)}, s32[256]{0:T(256)}, u32[]{:S(2)}) copy-start(s32[256]{0:T(256)} %param.18) | copy-start | bytes 3076
  0.0 50.8 %collective-permute-start.3 = (bf16[2048,1024]{1,0:T(8,128)(2,1)}, bf16[2048,1024]{1,0:T(8,128)(2,1)}, u32[]{:S(2)}, u32[]{:S(2)}) collective-permute-start(bf16[2048,1024]{1,0:T(8,128)(2,1)} %bitcast.26), channel_id=1, source_target_pairs={{0,8},{8,0},{16,24},{24,16},{1,9},{9,1},{17,25},{25,17},{2,10},{10... | collective-permute-start | bytes 12582920 | tf_op jit(solution)/shard_map/ppermute | solution.py:502
  1.1 7.5 %copy-start.14 = (s32[1,16]{1,0:T(1,128)S(1)}, s32[1,16]{1,0:T(1,128)}, u32[]{:S(2)}) copy-start(s32[1,16]{1,0:T(1,128)} %param.19) | copy-start | bytes 196
  1.1 10.2 %copy-start.9 = (s32[4]{0:T(128)S(1)}, s32[4]{0:T(128)}, u32[]{:S(2)}) copy-start(s32[4]{0:T(128)} %pad_add_fusion.1.place) | copy-start | bytes 52
  8.5 2.7 %collective-permute-start.1 = (bf16[2,8,32,896]{3,2,1,0:T(8,128)(2,1)}, bf16[2,8,32,896]{3,2,1,0:T(8,128)(2,1)S(1)}, u32[]{:S(2)}, u32[]{:S(2)}) collective-permute-start(bf16[2,8,32,896]{3,2,1,0:T(8,128)(2,1)} %get-tuple-element.25), channel_id=1, source_target_pairs={{0,8},{8,0},{16,24},{24,16},{1,9},{9,1},{17,25},{25,17},{2,10},{10... | collective-permute-start | bytes 2752520 | tf_op jit(solution)/shard_map/ppermute | solution.py:502
  9.3 8.3 %collective-permute-start = (s32[16]{0:T(128)S(1)}, s32[16]{0:T(128)S(1)}, u32[]{:S(2)}, u32[]{:S(2)}) collective-permute-start(s32[16]{0:T(128)S(1)} %and_select_fusion.4), channel_id=1, source_target_pairs={{0,8},{8,0},{16,24},{24,16},{1,9},{9,1},{17,25},{25,17},{2,10},{10... | collective-permute-start | bytes 200 | tf_op jit(solution)/shard_map/ppermute | solution.py:502
  11.2 1.2 copy-start.7
  14.5 0.5 copy-start.12
  15.0 13.7 %collective-permute-start.2 = (bf16[8,32,896]{2,1,0:T(8,128)(2,1)S(1)}, bf16[8,32,896]{2,1,0:T(8,128)(2,1)S(1)}, u32[]{:S(2)}, u32[]{:S(2)}) collective-permute-start(bf16[8,32,896]{2,1,0:T(8,128)(2,1)S(1)} %get-tuple-element.29), channel_id=1, source_target_pairs={{0,16},{8,24},{16,0},{24,8},{1,17},{9,25},{17,1},{25,9},{2,18},{10... | collective-permute-start | bytes 1376264 | tf_op jit(solution)/shard_map/ppermute | solution.py:502
  28.6 0.7 copy-start.10
  31.2 0.5 copy-start.13
  31.7 18.9 %all-to-all-start = ((bf16[8,32,896]{2,1,0:T(8,128)(2,1)}), bf16[8,32,896]{2,1,0:T(8,128)(2,1)S(1)}, u32[]{:S(2)}, u32[]{:S(2)}) async-start(bf16[8,32,896]{2,1,0:T(8,128)(2,1)} %get-tuple-element.30), calls=%async_computation | async-start | bytes 917504 | tf_op jit(solution)/shard_map/all_to_all | solution.py:516
  50.8 9.4 %copy-start.8 = (bf16[128,1024]{1,0:T(8,128)(2,1)S(1)}, bf16[128,1024]{1,0:T(8,128)(2,1)}, u32[]{:S(2)}) copy-start(bf16[128,1024]{1,0:T(8,128)(2,1)} %answers.1) | copy-start | bytes 786436
  60.1 1.4 %copy-start.6 = (bf16[768,1024]{1,0:T(8,128)(2,1)S(1)}, bf16[768,1024]{1,0:T(8,128)(2,1)}, u32[]{:S(2)}) copy-start(bf16[768,1024]{1,0:T(8,128)(2,1)} %mix_weight.1) | copy-start | bytes 4718596
  61.5 0.7 copy-start.11
  63.4 1.3 %collective-permute-start.4 = (bf16[32,512]{1,0:T(8,128)(2,1)S(1)}, bf16[32,512]{1,0:T(8,128)(2,1)S(1)}, u32[]{:S(2)}, u32[]{:S(2)}) collective-permute-start(bf16[32,512]{1,0:T(8,128)(2,1)S(1)} %get-tuple-element.38), channel_id=1, source_target_pairs={{0,8},{8,0},{16,24},{24,16},{1,9},{9,1},{17,25},{25,17},{2,10},{10... | collective-permute-start | bytes 98312 | tf_op jit(solution)/shard_map/ppermute | solution.py:502
  64.7 4.3 %collective-permute-start.5 = (bf16[1,2,32,512]{3,2,1,0:T(8,128)(2,1)S(1)}, bf16[1,2,32,512]{3,2,1,0:T(8,128)(2,1)S(1)}, u32[]{:S(2)}, u32[]{:S(2)}) collective-permute-start(bf16[1,2,32,512]{3,2,1,0:T(8,128)(2,1)S(1)} %maximum_bitcast_fusion), channel_id=1, source_target_pairs={{0,2},{1,3},{2,0},{3,1},{4,6},{5,7},{6,4},{7,5},{8,10},{9,11},{10,... | collective-permute-start | bytes 196616 | tf_op jit(solution)/shard_map/ppermute | solution.py:502
  69.0 9.4 %collective-permute-start.6 = (bf16[2,2,32,512]{3,2,1,0:T(8,128)(2,1)S(1)}, bf16[2,2,32,512]{3,2,1,0:T(8,128)(2,1)S(1)}, u32[]{:S(2)}, u32[]{:S(2)}) collective-permute-start(bf16[2,2,32,512]{3,2,1,0:T(8,128)(2,1)S(1)} %pad_maximum_fusion.queries.first), channel_id=1, source_target_pairs={{0,4},{1,5},{2,6},{3,7},{4,0},{5,1},{6,2},{7,3},{8,12},{9,13},{10,... | collective-permute-start | bytes 393224 | tf_op jit(solution)/shard_map/ppermute | solution.py:502
  70.9 1.6 %copy-start.1 = (bf16[2,2048,256]{2,1,0:T(8,128)(2,1)S(1)}, bf16[2,2048,256]{2,1,0:T(8,128)(2,1)}, u32[]{:S(2)}) copy-start(bf16[2,2048,256]{2,1,0:T(8,128)(2,1)} %get-tuple-element.31.key_own) | copy-start | bytes 6291460
  72.5 1.6 %copy-start.3 = (bf16[2,8,256,256]{3,2,1,0:T(8,128)(2,1)S(1)}, bf16[2,8,256,256]{3,2,1,0:T(8,128)(2,1)}, u32[]{:S(2)}) copy-start(bf16[2,8,256,256]{3,2,1,0:T(8,128)(2,1)} %get-tuple-element.34.value_own) | copy-start | bytes 6291460
  74.1 1.6 %copy-start.4 = (bf16[2,2048,256]{2,1,0:T(8,128)(2,1)S(1)}, bf16[2,2048,256]{2,1,0:T(8,128)(2,1)}, u32[]{:S(2)}) copy-start(bf16[2,2048,256]{2,1,0:T(8,128)(2,1)} %get-tuple-element.33.key_pair) | copy-start | bytes 6291460
  75.7 1.6 %copy-start.5 = (bf16[2,8,256,256]{3,2,1,0:T(8,128)(2,1)S(1)}, bf16[2,8,256,256]{3,2,1,0:T(8,128)(2,1)}, u32[]{:S(2)}) copy-start(bf16[2,8,256,256]{3,2,1,0:T(8,128)(2,1)} %get-tuple-element.35.value_pair) | copy-start | bytes 6291460
  77.3 10.2 %copy-start.2 = (bf16[2,2048,256]{2,1,0:T(8,128)(2,1)S(1)}, bf16[2,2048,256]{2,1,0:T(8,128)(2,1)}, u32[]{:S(2)}) copy-start(bf16[2,2048,256]{2,1,0:T(8,128)(2,1)} %get-tuple-element.31.key_own) | copy-start | bytes 6291460
  79.0 7.0 %collective-permute-start.7 = (bf16[4,2,32,512]{3,2,1,0:T(8,128)(2,1)S(1)}, bf16[4,2,32,512]{3,2,1,0:T(8,128)(2,1)S(1)}, u32[]{:S(2)}, u32[]{:S(2)}) collective-permute-start(bf16[4,2,32,512]{3,2,1,0:T(8,128)(2,1)S(1)} %join.1.refs_0_), channel_id=1, source_target_pairs={{0,16},{8,24},{16,0},{24,8},{1,17},{9,25},{17,1},{25,9},{2,18},{10... | collective-permute-start | bytes 786440 | tf_op jit(solution)/shard_map/ppermute | solution.py:502
  80.6 13.4 %collective-permute-start.9 = (bf16[4,2,32,512]{3,2,1,0:T(8,128)(2,1)S(1)}, bf16[4,2,32,512]{3,2,1,0:T(8,128)(2,1)S(1)}, u32[]{:S(2)}, u32[]{:S(2)}) collective-permute-start(bf16[4,2,32,512]{3,2,1,0:T(8,128)(2,1)S(1)} %join.1.refs_0_), channel_id=1, source_target_pairs={{0,1},{1,0},{2,3},{3,2},{4,5},{5,4},{6,7},{7,6},{8,9},{9,8},{10,11... | collective-permute-start | bytes 786440 | tf_op jit(solution)/shard_map/ppermute | solution.py:502
  86.0 8.0 %collective-permute-start.10 = (bf16[4,2,32,512]{3,2,1,0:T(8,128)(2,1)S(1)}, bf16[4,2,32,512]{3,2,1,0:T(8,128)(2,1)S(1)}, u32[]{:S(2)}, u32[]{:S(2)}) collective-permute-start(bf16[4,2,32,512]{3,2,1,0:T(8,128)(2,1)S(1)} %collective-permute-done.7.refs_1_), channel_id=1, source_target_pairs={{0,1},{1,0},{2,3},{3,2},{4,5},{5,4},{6,7},{7,6},{8,9},{9,8},{10,11... | collective-permute-start | bytes 786440 | tf_op jit(solution)/shard_map/ppermute | solution.py:502
  92.4 18.5 %collective-permute-start.8 = (bf16[4,288,128]{2,1,0:T(8,128)(2,1)S(1)}, bf16[4,288,128]{2,1,0:T(8,128)(2,1)S(1)}, u32[]{:S(2)}, u32[]{:S(2)}) collective-permute-start(bf16[4,288,128]{2,1,0:T(8,128)(2,1)S(1)} %attend.4), channel_id=1, source_target_pairs={{0,16},{1,17},{2,18},{3,19},{4,20},{5,21},{6,22},{7,23},{8,24},{9,... | collective-permute-start | bytes 884744 | tf_op jit(solution)/shard_map/ppermute | solution.py:552
  98.8 12.1 %collective-permute-start.11 = (bf16[4,288,128]{2,1,0:T(8,128)(2,1)S(1)}, bf16[4,288,128]{2,1,0:T(8,128)(2,1)S(1)}, u32[]{:S(2)}, u32[]{:S(2)}) collective-permute-start(bf16[4,288,128]{2,1,0:T(8,128)(2,1)S(1)} %attend.5), channel_id=1, source_target_pairs={{0,1},{1,0},{2,3},{3,2},{4,5},{5,4},{6,7},{7,6},{8,9},{9,8},{10,11... | collective-permute-start | bytes 884744 | tf_op jit(solution)/shard_map/ppermute | solution.py:552
  104.5 7.7 %collective-permute-start.12 = (bf16[4,288,128]{2,1,0:T(8,128)(2,1)S(1)}, bf16[4,288,128]{2,1,0:T(8,128)(2,1)S(1)}, u32[]{:S(2)}, u32[]{:S(2)}) collective-permute-start(bf16[4,288,128]{2,1,0:T(8,128)(2,1)S(1)} %attend.6), channel_id=1, source_target_pairs={{0,17},{1,16},{2,19},{3,18},{4,21},{5,20},{6,23},{7,22},{8,25},{9,... | collective-permute-start | bytes 884744 | tf_op jit(solution)/shard_map/ppermute | solution.py:552
  113.1 4.7 %collective-permute-start.13 = (bf16[288,128]{1,0:T(8,128)(2,1)S(1)}, bf16[288,128]{1,0:T(8,128)(2,1)S(1)}, u32[]{:S(2)}, u32[]{:S(2)}) collective-permute-start(bf16[288,128]{1,0:T(8,128)(2,1)S(1)} %get-tuple-element.40), channel_id=1, source_target_pairs={{0,2},{1,3},{2,0},{3,1},{4,6},{5,7},{6,4},{7,5},{8,10},{9,11},{10,... | collective-permute-start | bytes 221192 | tf_op jit(solution)/shard_map/ppermute | solution.py:502
  114.3 6.0 %collective-permute-start.14 = (bf16[288,128]{1,0:T(8,128)(2,1)S(1)}, bf16[288,128]{1,0:T(8,128)(2,1)S(1)}, u32[]{:S(2)}, u32[]{:S(2)}) collective-permute-start(bf16[288,128]{1,0:T(8,128)(2,1)S(1)} %get-tuple-element.41), channel_id=1, source_target_pairs={{0,4},{1,5},{2,6},{3,7},{4,0},{5,1},{6,2},{7,3},{8,12},{9,13},{10,... | collective-permute-start | bytes 221192 | tf_op jit(solution)/shard_map/ppermute | solution.py:502
  116.2 6.2 %collective-permute-start.15 = (bf16[288,128]{1,0:T(8,128)(2,1)S(1)}, bf16[288,128]{1,0:T(8,128)(2,1)S(1)}, u32[]{:S(2)}, u32[]{:S(2)}) collective-permute-start(bf16[288,128]{1,0:T(8,128)(2,1)S(1)} %get-tuple-element.42), channel_id=1, source_target_pairs={{0,6},{1,7},{2,4},{3,5},{4,2},{5,3},{6,0},{7,1},{8,14},{9,15},{10,... | collective-permute-start | bytes 221192 | tf_op jit(solution)/shard_map/ppermute | solution.py:502

commit v9 on v8

--- a/solution.py
+++ b/solution.py
@@ -161,38 +161,61 @@
     )(place, keep, recv)
 
 
-def column_kernel(place, note, done, *refs):
-    *parts, out, later = refs
+def column_kernel(place, note, done, *refs, inner):
+    *refs, later = refs
+    parts, outs = refs[:-inner], refs[-inner:]
     hand_on(place, later)
-    store_rows(out, *merge_rows([flat(part[...]) for part in parts]), note[...] + done[0:1, :])
-
-
-def merge_columns(place, note, done, parts):
-    readers = parts[0].shape[0]
-    spec = pl.BlockSpec((readers // 2,) + parts[0].shape[1:], lambda g, place: (g, 0, 0))
-    return pl.pallas_call(
-        column_kernel,
-        grid_spec=pltpu.PrefetchScalarGridSpec(
-            num_scalar_prefetch=1,
-            grid=(2,),
-            in_specs=[
-                pl.BlockSpec(note.shape, lambda g, place: (0, 0)),
-                pl.BlockSpec(done.shape, lambda g, place: (0, 0)),
-            ]
-            + [spec] * len(parts),
-            out_specs=[spec, SCALARS],
-        ),
-        out_shape=[
-            jax.ShapeDtypeStruct(parts[0].shape, BF16),
-            jax.ShapeDtypeStruct(place.shape, place.dtype),
-        ],
+    row = lax.broadcasted_iota(jnp.int32, (outs[0].shape[1], LANES), 0)
+    first = jnp.where(row == 0, note[...] + done[0:1, :], 0.0)
+    for offset, out in enumerate(outs):
+        for z in range(out.shape[0]):
+            at = z * inner + lax.bitwise_xor(place[2], offset)
+            store_rows(out.at[z], *merge_rows([part[at] for part in parts]), first)
+
+
+def merge_columns(place, note, done, parts, inner):
+    readers, part, width = parts[0].shape
+    whole = pl.BlockSpec(memory_space=pltpu.VMEM)
+    return pl.pallas_call(
+        functools.partial(column_kernel, inner=inner),
+        in_specs=[SCALARS] + [whole] * (2 + len(parts)),
+        out_specs=[whole] * inner + [SCALARS],
+        out_shape=[jax.ShapeDtypeStruct((readers // inner, part, width), BF16)] * inner
+        + [jax.ShapeDtypeStruct(place.shape, place.dtype)],
         compiler_params=grant(),
         name="merge_columns",
     )(place, note, done, *parts)
 
 
-def condition_kernel(place, parts, mix_weight, answers, done, keep, send, rows_scratch, *, spread):
-    tiles, _, total = merge_rows([parts[at] for at in range(parts.shape[0])])
+def near_kernel(place, done, *refs, outer):
+    parts, outs = refs[:-outer], refs[-outer:]
+    shape = (outs[0].shape[0], LANES)
+    row, lane = (lax.broadcasted_iota(jnp.int32, shape, at) for at in range(2))
+    for step, out in enumerate(outs):
+        taken = [part[lax.bitwise_xor(place[3], step)] for part in parts]
+        notes = jnp.zeros(shape, F32) + done[0:1, :]
+        for offset, part in enumerate(taken):
+            carried = part[0:1, part.shape[1] - LANES :].astype(F32)
+            notes = jnp.where((row == offset) & (lane >= NOTE_AT), carried, notes)
+        store_rows(out, *merge_rows(taken), notes)
+
+
+def merge_near(place, done, parts):
+    outer, part, width = parts[0].shape
+    whole = pl.BlockSpec(memory_space=pltpu.VMEM)
+    return pl.pallas_call(
+        functools.partial(near_kernel, outer=outer),
+        in_specs=[SCALARS] + [whole] * (1 + len(parts)),
+        out_specs=[whole] * outer,
+        out_shape=[jax.ShapeDtypeStruct((part, width), BF16)] * outer,
+        compiler_params=grant(),
+        name="merge_near",
+    )(place, done, *parts)
+
+
+def condition_kernel(place, mix_weight, answers, *refs, spread):
+    *parts, keep, send, rows_scratch = refs
+    tiles, _, total = merge_rows([part[...] for part in parts])
     blended_half = jnp.concatenate([(tile / total).astype(BF16) for tile in tiles], 1)
     part = blended_half.shape[0]
     start = pl.multiple_of((place[1] * PAIR + place[0]) * part, part)
@@ -206,19 +229,19 @@
         send[:, column * stride : (column + 1) * stride] = rows_scratch[:, pl.ds(other, stride)].astype(BF16)
 
 
-def condition(place, parts, mix_weight, answers, done, spread):
+def condition(place, parts, mix_weight, answers, spread):
     model_width = mix_weight.shape[1]
-    shape = jax.ShapeDtypeStruct((parts.shape[1], model_width // PAIR), BF16)
+    shape = jax.ShapeDtypeStruct((parts[0].shape[0], model_width // PAIR), BF16)
     whole = pl.BlockSpec(memory_space=pltpu.VMEM)
     return pl.pallas_call(
         functools.partial(condition_kernel, spread=spread),
-        in_specs=[SCALARS, whole, whole, whole, whole],
+        in_specs=[SCALARS] + [whole] * (2 + len(parts)),
         out_specs=[whole, whole],
         out_shape=[shape, shape],
-        scratch_shapes=[pltpu.VMEM((parts.shape[1], model_width), F32)],
+        scratch_shapes=[pltpu.VMEM((parts[0].shape[0], model_width), F32)],
         compiler_params=grant(),
         name="condition",
-    )(place, parts, mix_weight, answers, done)
+    )(place, mix_weight, answers, *parts)
 
 
 def project_kernel(place, states, *refs):
@@ -286,7 +309,7 @@
     tokens = values[0].shape[3]
     head_at = lax.broadcasted_iota(jnp.int32, query.shape, 0) // head_width
     spaced = jnp.concatenate([jnp.where(head_at == head, query, jnp.zeros_like(query)) for head in range(count)], 1)
-    entry = z * inner + lax.bitwise_xor(place[2], offset)
+    entry = relative * inner + offset
     bundle = min(HEAD_BUNDLE, count)
     shelves = []
     for shelf in range(PAIR):
@@ -512,13 +535,16 @@
     *by_column, place_own = merge_pair(place, keep, swap(send, "pa", 1), spread)
     parts = [by_column[0]] + [swap(by_column[at], "pa", at * PAIR) for at in range(1, spread)]
     own_key, own_value, own_done = project(place_own, states, key_weight, value_weight, spread, tokens)
-    by_group, place_pair = merge_columns(place, note, own_done, parts)
-    mine = lax.all_to_all(by_group, "pb", split_axis=0, concat_axis=0, tiled=True)
+    *by_group, place_pair = merge_columns(place, note, own_done, parts, inner)
+    parts = [by_group[0]] + [swap(by_group[at], "pb", at) for at in range(1, inner)]
     pair_key, pair_value, pair_done = project(place_pair, pair_states, key_weight, value_weight, spread, tokens)
+    own_part, *by_reader = merge_near(place, pair_done, parts)
+    mine = [own_part] + [swap(part, "pb", (at + 1) * inner) for at, part in enumerate(by_reader)]
     keys, values = (own_key, pair_key), (own_value, pair_value)
-    kept, sent = condition(place, mine, mix_weight, answer_queries, pair_done, spread)
-
-    digits = mine[:, 0, queries.shape[1] + NOTE_AT :][:, : digits.shape[0]].astype(jnp.int32)
+    kept, sent = condition(place, mine, mix_weight, answer_queries, spread)
+
+    first = queries.shape[1] + NOTE_AT
+    digits = jnp.concatenate([part[:inner, first : first + digits.shape[0]] for part in mine]).astype(jnp.int32)
     slot_ids = digits[:, : wanted.shape[0]] * LANES + digits[:, wanted.shape[0] :]
     slot_ids = slot_ids.reshape(readers, PAIR, -1)
     holder = (runner ^ jnp.arange(PAIR, dtype=jnp.int32)) * readers + group

time: 124 us -> 118 us (0.952)
  waiting for transfers between devices: 30.9 us -> 25.4 us
  starting transfers between devices: 23.6 us -> 21.8 us
    all_to_all x1 -> x0, waiting for transfers between devices: 12.8 us -> none  [local(): lax.all_to_all(by_group, 'pb', split_axis=0, concat_axis=0, tiled=True)]
    ppermute x13 -> x17, waiting for transfers between devices: 16.8 us -> 23.5 us  [swap(): return lax.ppermute(value, axis, [(at, at ^ bits) for at in range(size)])]
    all_to_all x1 -> x0, starting transfers between devices: 6.08 us -> none  [local(): lax.all_to_all(by_group, 'pb', split_axis=0, concat_axis=0, tiled=True)]
    ppermute x13 -> x17, starting transfers between devices: 13.8 us -> 17.8 us  [swap(): return lax.ppermute(value, axis, [(at, at ^ bits) for at in range(size)])]
    pallas_call x1 -> x2, Pallas kernels: 1.88 us -> 2.94 us  [the longest x1 1.69 us: merge_columns(): pl.pallas_call(functools.partial(column_kernel, inner=inner), in_specs=[S...]
    unnamed x31 -> x34, local copies, waits for them, and re-layouts: 11.4 us -> 11.1 us
  transfers between devices with their start and end apart: 17 -> 20, of which waited for: 10 -> 12; matrix products, arithmetic and copies ran while one was open for 2% -> 3% of each run, Pallas kernels for 34% -> 43%
where the time goes in v9:
time: 118 us; the launch traced here: 117 us
  Pallas kernels  55.2 us (47%)
  waiting for transfers between devices  25.4 us (22%)
  starting transfers between devices  21.8 us (18%)
  local copies, waits for them, and re-layouts  12.6 us (11%)
  other arithmetic  1.59 us (1%)
    ppermute x17, waiting for transfers between devices, swap(): return lax.ppermute(value, axis, [(at, at ^ bits) for at in range(size)])  23.5 us
    pallas_call x4, Pallas kernels, attend(): pl.pallas_call(functools.partial(attend_kernel, offset=offset, column=col...  19.7 us
    pallas_call x2, Pallas kernels, project(): pl.pallas_call(project_kernel, grid_spec=pltpu.PrefetchScalarGridSpec(num...  18.5 us
    ppermute x17, starting transfers between devices, swap(): return lax.ppermute(value, axis, [(at, at ^ bits) for at in range(size)])  17.8 us
    unnamed x34, local copies, waits for them, and re-layouts  11.1 us
    pallas_call x1, Pallas kernels, retrieve(): pl.pallas_call(functools.partial(retrieval_kernel, spread=spread), grid_s...  7.41 us
    ppermute x3, starting transfers between devices, local(): lax.ppermute(lot, ('pa', 'pb'), [(at, at ^ bits) for at in range(runners...  3.96 us
  transfers between devices with their start and end apart: 20, of which 12 were waited for; matrix products, arithmetic and copies ran while one was open for 3% of the time, Pallas kernels for 43%

profile of v9, /device:TPU:0, one launch (start us, length us, event | category | flops | bytes accessed | tf_op | source)
XLA Modules:
  0.0 116.8 jit_solution(9612461882574057309)
XLA Ops:
  1.1 7.4 %retrieve.1 = (bf16[2,8,32,896]{3,2,1,0:T(8,128)(2,1)}, bf16[2,8,32,896]{3,2,1,0:T(8,128)(2,1)}) custom-call(s32[4]{0:T(128)} %pad_add_fusion.1.place, bf16[1024,768]{1,0:T(8,128)(2,1)} %queries.1, bf16[512,768]{1,0:T(8,128)(2,1)} %passages.1, bf16[1024,512]{1,0:T(8,128)(2,1)} %noise.1), custom_call_target="tpu_custom_call" | custom-call | flops 1610612736 | bytes 4980736 | tf_op jit(solution)/shard_map/retrieve/pallas_call | solution.py:102
  9.8 1.4 %collective-permute-done.1.recv = bf16[2,8,32,896]{3,2,1,0:T(8,128)(2,1)S(1)} collective-permute-done((bf16[2,8,32,896]{3,2,1,0:T(8,128)(2,1)}, bf16[2,8,32,896]{3,2,1,0:T(8,128)(2,1)S(1)}, u32[]{:S(2)}, u32[]{:S(2)}) %collective-permute-start.1) | collective-permute-done | bytes 917536 | tf_op jit(solution)/shard_map/ppermute | solution.py:525
  11.2 1.2 %copy-done.7 = bf16[2,8,32,896]{3,2,1,0:T(8,128)(2,1)S(1)} copy-done((bf16[2,8,32,896]{3,2,1,0:T(8,128)(2,1)S(1)}, bf16[2,8,32,896]{3,2,1,0:T(8,128)(2,1)}, u32[]{:S(2)}) %copy-start.7) | copy-done | bytes 917528
  12.4 2.1 %merge_pair.1 = (bf16[8,32,896]{2,1,0:T(8,128)(2,1)S(1)}, bf16[8,32,896]{2,1,0:T(8,128)(2,1)S(1)}, s32[4]{0:T(128)S(1)}) custom-call(s32[4]{0:T(128)S(1)} %copy-done.11, bf16[2,8,32,896]{3,2,1,0:T(8,128)(2,1)S(1)} %copy-done.7, bf16[2,8,32,896]{3,2,1,0:T(8,128)(2,1)S(1)} %collective-permute-done.1.recv), custom_call_target="tpu_custom_call" | custom-call | tf_op jit(solution)/shard_map/merge_pair/pallas_call | solution.py:152
  15.0 2.6 %collective-permute-start.2 = (bf16[8,32,896]{2,1,0:T(8,128)(2,1)S(1)}, bf16[8,32,896]{2,1,0:T(8,128)(2,1)S(1)}, u32[]{:S(2)}, u32[]{:S(2)}) collective-permute-start(bf16[8,32,896]{2,1,0:T(8,128)(2,1)S(1)} %get-tuple-element.34), channel_id=1, source_target_pairs={{0,16},{8,24},{16,0},{24,8},{1,17},{9,25},{17,1},{25,9},{2,18},{10... | collective-permute-start | bytes 1376264 | tf_op jit(solution)/shard_map/ppermute | solution.py:525
  17.9 9.2 %project.2 = (bf16[2,2048,256]{2,1,0:T(8,128)(2,1)}, bf16[2,8,256,256]{3,2,1,0:T(8,128)(2,1)}, f32[8,128]{1,0:T(8,128)}) custom-call(s32[4]{0:T(128)} %copy-done.14, bf16[2048,1024]{1,0:T(8,128)(2,1)} %bitcast.24, bf16[1024,1024]{1,0:T(8,128)(2,1)} %refs_1_.3, bf16[1024,1024]{1,0:T(8,128)(2,1)} %refs_1_.3, bf16[1024,1024]{1,0:T(8,128)(2,1)} %refs_3_.3, ...), custom_call_target="tpu_custom_call" | custom-call | flops 268435456 | bytes 655360 | tf_op jit(solution)/shard_map/project/pallas_call | solution.py:269
  27.1 1.6 %collective-permute-done.2.refs_1_ = bf16[8,32,896]{2,1,0:T(8,128)(2,1)S(1)} collective-permute-done((bf16[8,32,896]{2,1,0:T(8,128)(2,1)S(1)}, bf16[8,32,896]{2,1,0:T(8,128)(2,1)S(1)}, u32[]{:S(2)}, u32[]{:S(2)}) %collective-permute-start.2) | collective-permute-done | bytes 458784 | tf_op jit(solution)/shard_map/ppermute | solution.py:525
  29.4 1.7 %merge_columns.1 = (bf16[4,32,896]{2,1,0:T(8,128)(2,1)S(1)}, bf16[4,32,896]{2,1,0:T(8,128)(2,1)}, s32[4]{0:T(128)S(1)}) custom-call(s32[4]{0:T(128)S(1)} %copy-done.11, f32[1,128]{1,0:T(1,128)S(1)} %pad.4.note, f32[8,128]{1,0:T(8,128)S(1)} %copy-done.13, bf16[8,32,896]{2,1,0:T(8,128)(2,1)S(1)} %get-tuple-element.33.refs_0_, ...), custom_call_target="tpu_custom_call" | custom-call | tf_op jit(solution)/shard_map/merge_columns/pallas_call | solution.py:179
  31.8 1.8 %collective-permute-start.4 = (bf16[4,32,896]{2,1,0:T(8,128)(2,1)}, bf16[4,32,896]{2,1,0:T(8,128)(2,1)}, u32[]{:S(2)}, u32[]{:S(2)}) collective-permute-start(bf16[4,32,896]{2,1,0:T(8,128)(2,1)} %get-tuple-element.38), channel_id=1, source_target_pairs={{0,1},{1,0},{2,3},{3,2},{4,5},{5,4},{6,7},{7,6},{8,9},{9,8},{10,11... | collective-permute-start | bytes 688136 | tf_op jit(solution)/shard_map/ppermute | solution.py:525
  33.5 9.3 %project.3 = (bf16[2,2048,256]{2,1,0:T(8,128)(2,1)}, bf16[2,8,256,256]{3,2,1,0:T(8,128)(2,1)}, f32[8,128]{1,0:T(8,128)}) custom-call(s32[4]{0:T(128)} %copy-done.15, bf16[2048,1024]{1,0:T(8,128)(2,1)} %collective-permute-done.3.states, bf16[1024,1024]{1,0:T(8,128)(2,1)} %refs_1_.3, bf16[1024,1024]{1,0:T(8,128)(2,1)} %refs_1_.3, bf16[1024,1024]{1,0:T(8,128)(2,1)} %refs_3_.3, ...), custom_call_target="tpu_custom_call" | custom-call | flops 268435456 | bytes 655360 | tf_op jit(solution)/shard_map/project/pallas_call | solution.py:269
  44.5 1.2 %merge_near.1 = (bf16[32,896]{1,0:T(8,128)(2,1)S(1)}, bf16[32,896]{1,0:T(8,128)(2,1)S(1)}, bf16[32,896]{1,0:T(8,128)(2,1)S(1)}, bf16[32,896]{1,0:T(8,128)(2,1)S(1)}) custom-call(s32[4]{0:T(128)S(1)} %copy-done.11, f32[8,128]{1,0:T(8,128)S(1)} %copy-done.12, bf16[4,32,896]{2,1,0:T(8,128)(2,1)S(1)} %copy-done.10, ...), custom_call_target="tpu_custom_call" | custom-call | tf_op jit(solution)/shard_map/merge_near/pallas_call | solution.py:206
  45.8 1.6 %collective-permute-start.5 = (bf16[32,896]{1,0:T(8,128)(2,1)S(1)}, bf16[32,896]{1,0:T(8,128)(2,1)S(1)}, u32[]{:S(2)}, u32[]{:S(2)}) collective-permute-start(bf16[32,896]{1,0:T(8,128)(2,1)S(1)} %get-tuple-element.40), channel_id=1, source_target_pairs={{0,2},{1,3},{2,0},{3,1},{4,6},{5,7},{6,4},{7,5},{8,10},{9,11},{10,... | collective-permute-start | bytes 172040 | tf_op jit(solution)/shard_map/ppermute | solution.py:525
  47.4 2.6 %collective-permute-start.6 = (bf16[32,896]{1,0:T(8,128)(2,1)S(1)}, bf16[32,896]{1,0:T(8,128)(2,1)S(1)}, u32[]{:S(2)}, u32[]{:S(2)}) collective-permute-start(bf16[32,896]{1,0:T(8,128)(2,1)S(1)} %get-tuple-element.41), channel_id=1, source_target_pairs={{0,4},{1,5},{2,6},{3,7},{4,0},{5,1},{6,2},{7,3},{8,12},{9,13},{10,... | collective-permute-start | bytes 172040 | tf_op jit(solution)/shard_map/ppermute | solution.py:525
  50.6 2.5 %collective-permute-done.6.refs_2_ = bf16[32,896]{1,0:T(8,128)(2,1)S(1)} collective-permute-done((bf16[32,896]{1,0:T(8,128)(2,1)S(1)}, bf16[32,896]{1,0:T(8,128)(2,1)S(1)}, u32[]{:S(2)}, u32[]{:S(2)}) %collective-permute-start.6) | collective-permute-done | bytes 57376 | tf_op jit(solution)/shard_map/ppermute | solution.py:525
  53.1 2.9 %collective-permute-done.7.refs_3_ = bf16[32,896]{1,0:T(8,128)(2,1)S(1)} collective-permute-done((bf16[32,896]{1,0:T(8,128)(2,1)S(1)}, bf16[32,896]{1,0:T(8,128)(2,1)S(1)}, u32[]{:S(2)}, u32[]{:S(2)}) %collective-permute-start.7) | collective-permute-done | bytes 57376 | tf_op jit(solution)/shard_map/ppermute | solution.py:525
  58.6 4.1 %collective-permute-done.9 = bf16[1,2,32,512]{3,2,1,0:T(8,128)(2,1)S(1)} collective-permute-done((bf16[1,2,32,512]{3,2,1,0:T(8,128)(2,1)S(1)}, bf16[1,2,32,512]{3,2,1,0:T(8,128)(2,1)S(1)}, u32[]{:S(2)}, u32[]{:S(2)}) %collective-permute-start.9) | collective-permute-done | bytes 65568 | tf_op jit(solution)/shard_map/ppermute | solution.py:525
  64.3 1.6 %copy-done.1 = bf16[2,2048,256]{2,1,0:T(8,128)(2,1)S(1)} copy-done((bf16[2,2048,256]{2,1,0:T(8,128)(2,1)S(1)}, bf16[2,2048,256]{2,1,0:T(8,128)(2,1)}, u32[]{:S(2)}) %copy-start.1) | copy-done | bytes 2097176
  65.9 1.6 %copy-done.3 = bf16[2,8,256,256]{3,2,1,0:T(8,128)(2,1)S(1)} copy-done((bf16[2,8,256,256]{3,2,1,0:T(8,128)(2,1)S(1)}, bf16[2,8,256,256]{3,2,1,0:T(8,128)(2,1)}, u32[]{:S(2)}) %copy-start.3) | copy-done | bytes 2097176
  67.5 1.6 %copy-done.4 = bf16[2,2048,256]{2,1,0:T(8,128)(2,1)S(1)} copy-done((bf16[2,2048,256]{2,1,0:T(8,128)(2,1)S(1)}, bf16[2,2048,256]{2,1,0:T(8,128)(2,1)}, u32[]{:S(2)}) %copy-start.4) | copy-done | bytes 2097176
  69.1 1.6 %copy-done.5 = bf16[2,8,256,256]{3,2,1,0:T(8,128)(2,1)S(1)} copy-done((bf16[2,8,256,256]{3,2,1,0:T(8,128)(2,1)S(1)}, bf16[2,8,256,256]{3,2,1,0:T(8,128)(2,1)}, u32[]{:S(2)}) %copy-start.5) | copy-done | bytes 2097176
  72.4 1.6 %collective-permute-start.11 = (bf16[4,2,32,512]{3,2,1,0:T(8,128)(2,1)S(1)}, bf16[4,2,32,512]{3,2,1,0:T(8,128)(2,1)S(1)}, u32[]{:S(2)}, u32[]{:S(2)}) collective-permute-start(bf16[4,2,32,512]{3,2,1,0:T(8,128)(2,1)S(1)} %join.1.refs_0_), channel_id=1, source_target_pairs={{0,16},{8,24},{16,0},{24,8},{1,17},{9,25},{17,1},{25,9},{2,18},{10... | collective-permute-start | bytes 786440 | tf_op jit(solution)/shard_map/ppermute | solution.py:525
  74.7 4.8 %collective-permute-done.11.refs_1_ = bf16[4,2,32,512]{3,2,1,0:T(8,128)(2,1)S(1)} collective-permute-done((bf16[4,2,32,512]{3,2,1,0:T(8,128)(2,1)S(1)}, bf16[4,2,32,512]{3,2,1,0:T(8,128)(2,1)S(1)}, u32[]{:S(2)}, u32[]{:S(2)}) %collective-permute-start.11) | collective-permute-done | bytes 262176 | tf_op jit(solution)/shard_map/ppermute | solution.py:525
  80.1 4.9 %attend.4 = bf16[4,288,128]{2,1,0:T(8,128)(2,1)S(1)} custom-call(s32[4]{0:T(128)S(1)} %copy-done.11, s32[48]{0:T(128)S(1)} %stage.1.ready.table, bf16[2,2048,256]{2,1,0:T(8,128)(2,1)S(1)} %copy-done.2, bf16[2,2048,256]{2,1,0:T(8,128)(2,1)S(1)} %copy-done.4, bf16[2,8,256,256]{3,2,1,0:T(8,128)(2,1)S(1)} %copy-done.3, bf16[2,8,256,256]{3,2,1,0:T(8,128)(2,1)S(1)} %copy-done.5, ...), custom_call_target="tpu_custom_call" | custom-call | flops 2147483648 | bytes 294912 | tf_op jit(solution)/shard_map/attend/pallas_call | solution.py:373
  85.0 1.6 %collective-permute-start.12 = (bf16[4,288,128]{2,1,0:T(8,128)(2,1)S(1)}, bf16[4,288,128]{2,1,0:T(8,128)(2,1)S(1)}, u32[]{:S(2)}, u32[]{:S(2)}) collective-permute-start(bf16[4,288,128]{2,1,0:T(8,128)(2,1)S(1)} %attend.4), channel_id=1, source_target_pairs={{0,16},{1,17},{2,18},{3,19},{4,20},{5,21},{6,22},{7,23},{8,24},{9,... | collective-permute-start | bytes 884744 | tf_op jit(solution)/shard_map/ppermute | solution.py:578
  86.6 4.9 %attend.5 = bf16[4,288,128]{2,1,0:T(8,128)(2,1)S(1)} custom-call(s32[4]{0:T(128)S(1)} %copy-done.11, s32[48]{0:T(128)S(1)} %stage.1.ready.table, bf16[2,2048,256]{2,1,0:T(8,128)(2,1)S(1)} %copy-done.2, bf16[2,2048,256]{2,1,0:T(8,128)(2,1)S(1)} %copy-done.4, bf16[2,8,256,256]{3,2,1,0:T(8,128)(2,1)S(1)} %copy-done.3, bf16[2,8,256,256]{3,2,1,0:T(8,128)(2,1)S(1)} %copy-done.5, ...), custom_call_target="tpu_custom_call" | custom-call | flops 2147483648 | bytes 294912 | tf_op jit(solution)/shard_map/attend/pallas_call | solution.py:373
  91.4 1.5 %collective-permute-start.15 = (bf16[4,288,128]{2,1,0:T(8,128)(2,1)S(1)}, bf16[4,288,128]{2,1,0:T(8,128)(2,1)S(1)}, u32[]{:S(2)}, u32[]{:S(2)}) collective-permute-start(bf16[4,288,128]{2,1,0:T(8,128)(2,1)S(1)} %attend.5), channel_id=1, source_target_pairs={{0,1},{1,0},{2,3},{3,2},{4,5},{5,4},{6,7},{7,6},{8,9},{9,8},{10,11... | collective-permute-start | bytes 884744 | tf_op jit(solution)/shard_map/ppermute | solution.py:578
  92.9 5.1 %attend.6 = bf16[4,288,128]{2,1,0:T(8,128)(2,1)S(1)} custom-call(s32[4]{0:T(128)S(1)} %copy-done.11, s32[48]{0:T(128)S(1)} %stage.1.ready.table, bf16[2,2048,256]{2,1,0:T(8,128)(2,1)S(1)} %copy-done.2, bf16[2,2048,256]{2,1,0:T(8,128)(2,1)S(1)} %copy-done.4, bf16[2,8,256,256]{3,2,1,0:T(8,128)(2,1)S(1)} %copy-done.3, bf16[2,8,256,256]{3,2,1,0:T(8,128)(2,1)S(1)} %copy-done.5, ...), custom_call_target="tpu_custom_call" | custom-call | flops 2147483648 | bytes 294912 | tf_op jit(solution)/shard_map/attend/pallas_call | solution.py:373
  98.9 4.9 %attend.7.refs_3_ = bf16[4,288,128]{2,1,0:T(8,128)(2,1)S(1)} custom-call(s32[4]{0:T(128)S(1)} %copy-done.11, s32[48]{0:T(128)S(1)} %stage.1.ready.table, bf16[2,2048,256]{2,1,0:T(8,128)(2,1)S(1)} %copy-done.2, bf16[2,2048,256]{2,1,0:T(8,128)(2,1)S(1)} %copy-done.4, bf16[2,8,256,256]{3,2,1,0:T(8,128)(2,1)S(1)} %copy-done.3, ...), custom_call_target="tpu_custom_call" | custom-call | flops 2147483648 | bytes 294912 | tf_op jit(solution)/shard_map/attend/pallas_call | solution.py:373
  103.8 1.9 %collective-permute-done.16.refs_2_ = bf16[4,288,128]{2,1,0:T(8,128)(2,1)S(1)} collective-permute-done((bf16[4,288,128]{2,1,0:T(8,128)(2,1)S(1)}, bf16[4,288,128]{2,1,0:T(8,128)(2,1)S(1)}, u32[]{:S(2)}, u32[]{:S(2)}) %collective-permute-start.16) | collective-permute-done | bytes 294944 | tf_op jit(solution)/shard_map/ppermute | solution.py:578
  107.5 2.4 %collective-permute-start.18 = (bf16[288,128]{1,0:T(8,128)(2,1)S(1)}, bf16[288,128]{1,0:T(8,128)(2,1)S(1)}, u32[]{:S(2)}, u32[]{:S(2)}) collective-permute-start(bf16[288,128]{1,0:T(8,128)(2,1)S(1)} %get-tuple-element.51), channel_id=1, source_target_pairs={{0,4},{1,5},{2,6},{3,7},{4,0},{5,1},{6,2},{7,3},{8,12},{9,13},{10,... | collective-permute-start | bytes 221192 | tf_op jit(solution)/shard_map/ppermute | solution.py:525
  109.9 1.2 %collective-permute-start.19 = (bf16[288,128]{1,0:T(8,128)(2,1)S(1)}, bf16[288,128]{1,0:T(8,128)(2,1)S(1)}, u32[]{:S(2)}, u32[]{:S(2)}) collective-permute-start(bf16[288,128]{1,0:T(8,128)(2,1)S(1)} %get-tuple-element.52), channel_id=1, source_target_pairs={{0,6},{1,7},{2,4},{3,5},{4,2},{5,3},{6,0},{7,1},{8,14},{9,15},{10,... | collective-permute-start | bytes 221192 | tf_op jit(solution)/shard_map/ppermute | solution.py:525
  112.7 3.3 %collective-permute-done.19.refs_3_ = bf16[288,128]{1,0:T(8,128)(2,1)S(1)} collective-permute-done((bf16[288,128]{1,0:T(8,128)(2,1)S(1)}, bf16[288,128]{1,0:T(8,128)(2,1)S(1)}, u32[]{:S(2)}, u32[]{:S(2)}) %collective-permute-start.19) | collective-permute-done | bytes 73760 | tf_op jit(solution)/shard_map/ppermute | solution.py:525
  (85 shorter events, 19.0 us)
Async XLA Ops:
  0.0 8.6 %copy-start = (s32[256]{0:T(256)S(1)}, s32[256]{0:T(256)}, u32[]{:S(2)}) copy-start(s32[256]{0:T(256)} %param.18) | copy-start | bytes 3076
  0.0 33.5 %collective-permute-start.3 = (bf16[2048,1024]{1,0:T(8,128)(2,1)}, bf16[2048,1024]{1,0:T(8,128)(2,1)}, u32[]{:S(2)}, u32[]{:S(2)}) collective-permute-start(bf16[2048,1024]{1,0:T(8,128)(2,1)} %bitcast.23), channel_id=1, source_target_pairs={{0,8},{8,0},{16,24},{24,16},{1,9},{9,1},{17,25},{25,17},{2,10},{10... | collective-permute-start | bytes 12582920 | tf_op jit(solution)/shard_map/ppermute | solution.py:525
  1.1 7.5 %copy-start.16 = (s32[1,16]{1,0:T(1,128)S(1)}, s32[1,16]{1,0:T(1,128)}, u32[]{:S(2)}) copy-start(s32[1,16]{1,0:T(1,128)} %param.19) | copy-start | bytes 196
  1.1 10.1 %copy-start.11 = (s32[4]{0:T(128)S(1)}, s32[4]{0:T(128)}, u32[]{:S(2)}) copy-start(s32[4]{0:T(128)} %pad_add_fusion.1.place) | copy-start | bytes 52
  8.5 2.7 %collective-permute-start.1 = (bf16[2,8,32,896]{3,2,1,0:T(8,128)(2,1)}, bf16[2,8,32,896]{3,2,1,0:T(8,128)(2,1)S(1)}, u32[]{:S(2)}, u32[]{:S(2)}) collective-permute-start(bf16[2,8,32,896]{3,2,1,0:T(8,128)(2,1)} %get-tuple-element.30), channel_id=1, source_target_pairs={{0,8},{8,0},{16,24},{24,16},{1,9},{9,1},{17,25},{25,17},{2,10},{10... | collective-permute-start | bytes 2752520 | tf_op jit(solution)/shard_map/ppermute | solution.py:525
  9.3 8.3 %collective-permute-start = (s32[16]{0:T(128)S(1)}, s32[16]{0:T(128)S(1)}, u32[]{:S(2)}, u32[]{:S(2)}) collective-permute-start(s32[16]{0:T(128)S(1)} %and_select_fusion.4), channel_id=1, source_target_pairs={{0,8},{8,0},{16,24},{24,16},{1,9},{9,1},{17,25},{25,17},{2,10},{10... | collective-permute-start | bytes 200 | tf_op jit(solution)/shard_map/ppermute | solution.py:525
  11.2 1.2 %copy-start.7 = (bf16[2,8,32,896]{3,2,1,0:T(8,128)(2,1)S(1)}, bf16[2,8,32,896]{3,2,1,0:T(8,128)(2,1)}, u32[]{:S(2)}) copy-start(bf16[2,8,32,896]{3,2,1,0:T(8,128)(2,1)} %get-tuple-element.29.keep) | copy-start | bytes 2752516
  15.0 13.7 %collective-permute-start.2 = (bf16[8,32,896]{2,1,0:T(8,128)(2,1)S(1)}, bf16[8,32,896]{2,1,0:T(8,128)(2,1)S(1)}, u32[]{:S(2)}, u32[]{:S(2)}) collective-permute-start(bf16[8,32,896]{2,1,0:T(8,128)(2,1)S(1)} %get-tuple-element.34), channel_id=1, source_target_pairs={{0,16},{8,24},{16,0},{24,8},{1,17},{9,25},{17,1},{25,9},{2,18},{10... | collective-permute-start | bytes 1376264 | tf_op jit(solution)/shard_map/ppermute | solution.py:525
  31.8 1.8 %copy-start.15 = (s32[4]{0:T(128)}, s32[4]{0:T(128)S(1)}, u32[]{:S(2)}) copy-start(s32[4]{0:T(128)S(1)} %get-tuple-element.35.place) | copy-start | bytes 52
  31.8 11.1 %collective-permute-start.4 = (bf16[4,32,896]{2,1,0:T(8,128)(2,1)}, bf16[4,32,896]{2,1,0:T(8,128)(2,1)}, u32[]{:S(2)}, u32[]{:S(2)}) collective-permute-start(bf16[4,32,896]{2,1,0:T(8,128)(2,1)} %get-tuple-element.38), channel_id=1, source_target_pairs={{0,1},{1,0},{2,3},{3,2},{4,5},{5,4},{6,7},{7,6},{8,9},{9,8},{10,11... | collective-permute-start | bytes 688136 | tf_op jit(solution)/shard_map/ppermute | solution.py:525
  33.5 22.5 %copy-start.6 = (bf16[768,1024]{1,0:T(8,128)(2,1)S(1)}, bf16[768,1024]{1,0:T(8,128)(2,1)}, u32[]{:S(2)}) copy-start(bf16[768,1024]{1,0:T(8,128)(2,1)} %mix_weight.1) | copy-start | bytes 4718596
  33.5 22.5 %copy-start.8 = (bf16[128,1024]{1,0:T(8,128)(2,1)S(1)}, bf16[128,1024]{1,0:T(8,128)(2,1)}, u32[]{:S(2)}) copy-start(bf16[128,1024]{1,0:T(8,128)(2,1)} %answers.1) | copy-start | bytes 786436
  45.8 4.8 %collective-permute-start.5 = (bf16[32,896]{1,0:T(8,128)(2,1)S(1)}, bf16[32,896]{1,0:T(8,128)(2,1)S(1)}, u32[]{:S(2)}, u32[]{:S(2)}) collective-permute-start(bf16[32,896]{1,0:T(8,128)(2,1)S(1)} %get-tuple-element.40), channel_id=1, source_target_pairs={{0,2},{1,3},{2,0},{3,1},{4,6},{5,7},{6,4},{7,5},{8,10},{9,11},{10,... | collective-permute-start | bytes 172040 | tf_op jit(solution)/shard_map/ppermute | solution.py:525
  47.4 5.7 %collective-permute-start.6 = (bf16[32,896]{1,0:T(8,128)(2,1)S(1)}, bf16[32,896]{1,0:T(8,128)(2,1)S(1)}, u32[]{:S(2)}, u32[]{:S(2)}) collective-permute-start(bf16[32,896]{1,0:T(8,128)(2,1)S(1)} %get-tuple-element.41), channel_id=1, source_target_pairs={{0,4},{1,5},{2,6},{3,7},{4,0},{5,1},{6,2},{7,3},{8,12},{9,13},{10,... | collective-permute-start | bytes 172040 | tf_op jit(solution)/shard_map/ppermute | solution.py:525
  50.0 6.0 %collective-permute-start.7 = (bf16[32,896]{1,0:T(8,128)(2,1)S(1)}, bf16[32,896]{1,0:T(8,128)(2,1)S(1)}, u32[]{:S(2)}, u32[]{:S(2)}) collective-permute-start(bf16[32,896]{1,0:T(8,128)(2,1)S(1)} %get-tuple-element.42), channel_id=1, source_target_pairs={{0,6},{1,7},{2,4},{3,5},{4,2},{5,3},{6,0},{7,1},{8,14},{9,15},{10,... | collective-permute-start | bytes 172040 | tf_op jit(solution)/shard_map/ppermute | solution.py:525
  57.1 1.3 %collective-permute-start.8 = (bf16[32,512]{1,0:T(8,128)(2,1)S(1)}, bf16[32,512]{1,0:T(8,128)(2,1)S(1)}, u32[]{:S(2)}, u32[]{:S(2)}) collective-permute-start(bf16[32,512]{1,0:T(8,128)(2,1)S(1)} %get-tuple-element.48), channel_id=1, source_target_pairs={{0,8},{8,0},{16,24},{24,16},{1,9},{9,1},{17,25},{25,17},{2,10},{10... | collective-permute-start | bytes 98312 | tf_op jit(solution)/shard_map/ppermute | solution.py:525
  58.4 4.3 %collective-permute-start.9 = (bf16[1,2,32,512]{3,2,1,0:T(8,128)(2,1)S(1)}, bf16[1,2,32,512]{3,2,1,0:T(8,128)(2,1)S(1)}, u32[]{:S(2)}, u32[]{:S(2)}) collective-permute-start(bf16[1,2,32,512]{3,2,1,0:T(8,128)(2,1)S(1)} %maximum_bitcast_fusion), channel_id=1, source_target_pairs={{0,2},{1,3},{2,0},{3,1},{4,6},{5,7},{6,4},{7,5},{8,10},{9,11},{10,... | collective-permute-start | bytes 196616 | tf_op jit(solution)/shard_map/ppermute | solution.py:525
  62.7 9.1 %collective-permute-start.10 = (bf16[2,2,32,512]{3,2,1,0:T(8,128)(2,1)S(1)}, bf16[2,2,32,512]{3,2,1,0:T(8,128)(2,1)S(1)}, u32[]{:S(2)}, u32[]{:S(2)}) collective-permute-start(bf16[2,2,32,512]{3,2,1,0:T(8,128)(2,1)S(1)} %pad_maximum_fusion.queries.first), channel_id=1, source_target_pairs={{0,4},{1,5},{2,6},{3,7},{4,0},{5,1},{6,2},{7,3},{8,12},{9,13},{10,... | collective-permute-start | bytes 393224 | tf_op jit(solution)/shard_map/ppermute | solution.py:525
  64.3 1.6 %copy-start.1 = (bf16[2,2048,256]{2,1,0:T(8,128)(2,1)S(1)}, bf16[2,2048,256]{2,1,0:T(8,128)(2,1)}, u32[]{:S(2)}) copy-start(bf16[2,2048,256]{2,1,0:T(8,128)(2,1)} %get-tuple-element.43.key_own) | copy-start | bytes 6291460
  65.9 1.6 %copy-start.3 = (bf16[2,8,256,256]{3,2,1,0:T(8,128)(2,1)S(1)}, bf16[2,8,256,256]{3,2,1,0:T(8,128)(2,1)}, u32[]{:S(2)}) copy-start(bf16[2,8,256,256]{3,2,1,0:T(8,128)(2,1)} %get-tuple-element.45.value_own) | copy-start | bytes 6291460
  67.5 1.6 %copy-start.4 = (bf16[2,2048,256]{2,1,0:T(8,128)(2,1)S(1)}, bf16[2,2048,256]{2,1,0:T(8,128)(2,1)}, u32[]{:S(2)}) copy-start(bf16[2,2048,256]{2,1,0:T(8,128)(2,1)} %get-tuple-element.44.key_pair) | copy-start | bytes 6291460
  69.1 1.6 %copy-start.5 = (bf16[2,8,256,256]{3,2,1,0:T(8,128)(2,1)S(1)}, bf16[2,8,256,256]{3,2,1,0:T(8,128)(2,1)}, u32[]{:S(2)}) copy-start(bf16[2,8,256,256]{3,2,1,0:T(8,128)(2,1)} %get-tuple-element.46.value_pair) | copy-start | bytes 6291460
  70.7 9.4 %copy-start.2 = (bf16[2,2048,256]{2,1,0:T(8,128)(2,1)S(1)}, bf16[2,2048,256]{2,1,0:T(8,128)(2,1)}, u32[]{:S(2)}) copy-start(bf16[2,2048,256]{2,1,0:T(8,128)(2,1)} %get-tuple-element.43.key_own) | copy-start | bytes 6291460
  72.4 7.1 %collective-permute-start.11 = (bf16[4,2,32,512]{3,2,1,0:T(8,128)(2,1)S(1)}, bf16[4,2,32,512]{3,2,1,0:T(8,128)(2,1)S(1)}, u32[]{:S(2)}, u32[]{:S(2)}) collective-permute-start(bf16[4,2,32,512]{3,2,1,0:T(8,128)(2,1)S(1)} %join.1.refs_0_), channel_id=1, source_target_pairs={{0,16},{8,24},{16,0},{24,8},{1,17},{9,25},{17,1},{25,9},{2,18},{10... | collective-permute-start | bytes 786440 | tf_op jit(solution)/shard_map/ppermute | solution.py:525
  74.0 12.6 %collective-permute-start.13 = (bf16[4,2,32,512]{3,2,1,0:T(8,128)(2,1)S(1)}, bf16[4,2,32,512]{3,2,1,0:T(8,128)(2,1)S(1)}, u32[]{:S(2)}, u32[]{:S(2)}) collective-permute-start(bf16[4,2,32,512]{3,2,1,0:T(8,128)(2,1)S(1)} %join.1.refs_0_), channel_id=1, source_target_pairs={{0,1},{1,0},{2,3},{3,2},{4,5},{5,4},{6,7},{7,6},{8,9},{9,8},{10,11... | collective-permute-start | bytes 786440 | tf_op jit(solution)/shard_map/ppermute | solution.py:525
  79.5 7.0 %collective-permute-start.14 = (bf16[4,2,32,512]{3,2,1,0:T(8,128)(2,1)S(1)}, bf16[4,2,32,512]{3,2,1,0:T(8,128)(2,1)S(1)}, u32[]{:S(2)}, u32[]{:S(2)}) collective-permute-start(bf16[4,2,32,512]{3,2,1,0:T(8,128)(2,1)S(1)} %collective-permute-done.11.refs_1_), channel_id=1, source_target_pairs={{0,1},{1,0},{2,3},{3,2},{4,5},{5,4},{6,7},{7,6},{8,9},{9,8},{10,11... | collective-permute-start | bytes 786440 | tf_op jit(solution)/shard_map/ppermute | solution.py:525
  85.0 18.8 %collective-permute-start.12 = (bf16[4,288,128]{2,1,0:T(8,128)(2,1)S(1)}, bf16[4,288,128]{2,1,0:T(8,128)(2,1)S(1)}, u32[]{:S(2)}, u32[]{:S(2)}) collective-permute-start(bf16[4,288,128]{2,1,0:T(8,128)(2,1)S(1)} %attend.4), channel_id=1, source_target_pairs={{0,16},{1,17},{2,18},{3,19},{4,20},{5,21},{6,22},{7,23},{8,24},{9,... | collective-permute-start | bytes 884744 | tf_op jit(solution)/shard_map/ppermute | solution.py:578
  91.4 12.4 %collective-permute-start.15 = (bf16[4,288,128]{2,1,0:T(8,128)(2,1)S(1)}, bf16[4,288,128]{2,1,0:T(8,128)(2,1)S(1)}, u32[]{:S(2)}, u32[]{:S(2)}) collective-permute-start(bf16[4,288,128]{2,1,0:T(8,128)(2,1)S(1)} %attend.5), channel_id=1, source_target_pairs={{0,1},{1,0},{2,3},{3,2},{4,5},{5,4},{6,7},{7,6},{8,9},{9,8},{10,11... | collective-permute-start | bytes 884744 | tf_op jit(solution)/shard_map/ppermute | solution.py:578
  98.0 7.7 %collective-permute-start.16 = (bf16[4,288,128]{2,1,0:T(8,128)(2,1)S(1)}, bf16[4,288,128]{2,1,0:T(8,128)(2,1)S(1)}, u32[]{:S(2)}, u32[]{:S(2)}) collective-permute-start(bf16[4,288,128]{2,1,0:T(8,128)(2,1)S(1)} %attend.6), channel_id=1, source_target_pairs={{0,17},{1,16},{2,19},{3,18},{4,21},{5,20},{6,23},{7,22},{8,25},{9,... | collective-permute-start | bytes 884744 | tf_op jit(solution)/shard_map/ppermute | solution.py:578
  106.7 5.0 %collective-permute-start.17 = (bf16[288,128]{1,0:T(8,128)(2,1)S(1)}, bf16[288,128]{1,0:T(8,128)(2,1)S(1)}, u32[]{:S(2)}, u32[]{:S(2)}) collective-permute-start(bf16[288,128]{1,0:T(8,128)(2,1)S(1)} %get-tuple-element.50), channel_id=1, source_target_pairs={{0,2},{1,3},{2,0},{3,1},{4,6},{5,7},{6,4},{7,5},{8,10},{9,11},{10,... | collective-permute-start | bytes 221192 | tf_op jit(solution)/shard_map/ppermute | solution.py:525
  107.5 5.3 %collective-permute-start.18 = (bf16[288,128]{1,0:T(8,128)(2,1)S(1)}, bf16[288,128]{1,0:T(8,128)(2,1)S(1)}, u32[]{:S(2)}, u32[]{:S(2)}) collective-permute-start(bf16[288,128]{1,0:T(8,128)(2,1)S(1)} %get-tuple-element.51), channel_id=1, source_target_pairs={{0,4},{1,5},{2,6},{3,7},{4,0},{5,1},{6,2},{7,3},{8,12},{9,13},{10,... | collective-permute-start | bytes 221192 | tf_op jit(solution)/shard_map/ppermute | solution.py:525
  109.9 6.2 %collective-permute-start.19 = (bf16[288,128]{1,0:T(8,128)(2,1)S(1)}, bf16[288,128]{1,0:T(8,128)(2,1)S(1)}, u32[]{:S(2)}, u32[]{:S(2)}) collective-permute-start(bf16[288,128]{1,0:T(8,128)(2,1)S(1)} %get-tuple-element.52), channel_id=1, source_target_pairs={{0,6},{1,7},{2,4},{3,5},{4,2},{5,3},{6,0},{7,1},{8,14},{9,15},{10,... | collective-permute-start | bytes 221192 | tf_op jit(solution)/shard_map/ppermute | solution.py:525
  (5 other events, 3.5 us)

commit v10 on v9

--- a/solution.py
+++ b/solution.py
@@ -25,6 +25,7 @@
 BF16 = jnp.bfloat16
 NT = (((1,), (1,)), ((), ()))
 SCALARS = pl.BlockSpec(memory_space=pltpu.SMEM)
+UNREAD = pl.BlockSpec(memory_space=pl.ANY)
 
 
 def grant():
@@ -138,8 +139,6 @@
 
 
 def pair_kernel(place, keep, recv, *outs):
-    *outs, later = outs
-    hand_on(place, later)
     for offset, out in enumerate(outs):
         column = lax.bitwise_xor(place[1], offset)
         store_rows(out, *merge_rows([flat(keep[column]), flat(recv[column])]))
@@ -152,21 +151,18 @@
     return pl.pallas_call(
         pair_kernel,
         grid_spec=pltpu.PrefetchScalarGridSpec(
-            num_scalar_prefetch=1, grid=(2,), in_specs=[spec, spec], out_specs=[out] * spread + [SCALARS]
+            num_scalar_prefetch=1, grid=(2,), in_specs=[spec, spec], out_specs=[out] * spread
         ),
-        out_shape=[jax.ShapeDtypeStruct(keep.shape[1:], BF16)] * spread
-        + [jax.ShapeDtypeStruct(place.shape, place.dtype)],
+        out_shape=[jax.ShapeDtypeStruct(keep.shape[1:], BF16)] * spread,
         compiler_params=grant(),
         name="merge_pair",
     )(place, keep, recv)
 
 
 def column_kernel(place, note, done, *refs, inner):
-    *refs, later = refs
     parts, outs = refs[:-inner], refs[-inner:]
-    hand_on(place, later)
     row = lax.broadcasted_iota(jnp.int32, (outs[0].shape[1], LANES), 0)
-    first = jnp.where(row == 0, note[...] + done[0:1, :], 0.0)
+    first = jnp.where(row == 0, note[...], 0.0)
     for offset, out in enumerate(outs):
         for z in range(out.shape[0]):
             at = z * inner + lax.bitwise_xor(place[2], offset)
@@ -178,10 +174,9 @@
     whole = pl.BlockSpec(memory_space=pltpu.VMEM)
     return pl.pallas_call(
         functools.partial(column_kernel, inner=inner),
-        in_specs=[SCALARS] + [whole] * (2 + len(parts)),
-        out_specs=[whole] * inner + [SCALARS],
-        out_shape=[jax.ShapeDtypeStruct((readers // inner, part, width), BF16)] * inner
-        + [jax.ShapeDtypeStruct(place.shape, place.dtype)],
+        in_specs=[SCALARS, whole, UNREAD] + [whole] * len(parts),
+        out_specs=[whole] * inner,
+        out_shape=[jax.ShapeDtypeStruct((readers // inner, part, width), BF16)] * inner,
         compiler_params=grant(),
         name="merge_columns",
     )(place, note, done, *parts)
@@ -193,7 +188,7 @@
     row, lane = (lax.broadcasted_iota(jnp.int32, shape, at) for at in range(2))
     for step, out in enumerate(outs):
         taken = [part[lax.bitwise_xor(place[3], step)] for part in parts]
-        notes = jnp.zeros(shape, F32) + done[0:1, :]
+        notes = jnp.zeros(shape, F32)
         for offset, part in enumerate(taken):
             carried = part[0:1, part.shape[1] - LANES :].astype(F32)
             notes = jnp.where((row == offset) & (lane >= NOTE_AT), carried, notes)
@@ -205,7 +200,7 @@
     whole = pl.BlockSpec(memory_space=pltpu.VMEM)
     return pl.pallas_call(
         functools.partial(near_kernel, outer=outer),
-        in_specs=[SCALARS] + [whole] * (1 + len(parts)),
+        in_specs=[SCALARS, UNREAD] + [whole] * len(parts),
         out_specs=[whole] * outer,
         out_shape=[jax.ShapeDtypeStruct((part, width), BF16)] * outer,
         compiler_params=grant(),
@@ -245,7 +240,7 @@
 
 
 def project_kernel(place, states, *refs):
-    spread = (len(refs) - 3) // 2
+    spread = (len(refs) - 4) // 2
     keys, values, done = refs[-3:]
     done[...] = jnp.zeros_like(done)
     tokens = values.shape[3]
@@ -256,7 +251,7 @@
             values[column, block] = value[block * tokens : (block + 1) * tokens].T
 
 
-def project(place, states, key_weight, value_weight, spread, tokens):
+def project(place, states, key_weight, value_weight, after, spread, tokens):
     rows, model_width = states.shape
     width = model_width // (PAIR * spread)
     chunk = rows // PROJECT_STEPS
@@ -271,7 +266,7 @@
         grid_spec=pltpu.PrefetchScalarGridSpec(
             num_scalar_prefetch=1,
             grid=(PROJECT_STEPS,),
-            in_specs=[pl.BlockSpec((chunk, model_width), lambda t, place: (t, 0))] + specs + specs,
+            in_specs=[pl.BlockSpec((chunk, model_width), lambda t, place: (t, 0))] + specs + specs + [UNREAD],
             out_specs=[
                 pl.BlockSpec((spread, chunk, width), lambda t, place: (0, t, 0)),
                 pl.BlockSpec((spread, blocks, width, tokens), lambda t, place: (0, t, 0, 0)),
@@ -290,7 +285,7 @@
             transcendentals=0,
         ),
         name="project",
-    )(place, states, *([key_weight] * spread), *([value_weight] * spread))
+    )(place, states, *([key_weight] * spread), *([value_weight] * spread), after)
 
 
 def attend_group(z, place, table, pieces, keys, values, out, rows_scratch, offset, column, inner, head_width):
@@ -532,12 +527,14 @@
     digits = jnp.concatenate([wanted // LANES, wanted % LANES]).astype(F32)
     note = jnp.pad(digits[None], ((0, 0), (NOTE_AT, LANES - NOTE_AT - digits.shape[0])))
     keep, send = retrieve(place, queries, passages, noise, readers, spread)
-    *by_column, place_own = merge_pair(place, keep, swap(send, "pa", 1), spread)
+    by_column = merge_pair(place, keep, swap(send, "pa", 1), spread)
     parts = [by_column[0]] + [swap(by_column[at], "pa", at * PAIR) for at in range(1, spread)]
-    own_key, own_value, own_done = project(place_own, states, key_weight, value_weight, spread, tokens)
-    *by_group, place_pair = merge_columns(place, note, own_done, parts, inner)
+    own_key, own_value, own_done = project(place, states, key_weight, value_weight, by_column[0], spread, tokens)
+    by_group = merge_columns(place, note, own_done, parts, inner)
     parts = [by_group[0]] + [swap(by_group[at], "pb", at) for at in range(1, inner)]
-    pair_key, pair_value, pair_done = project(place_pair, pair_states, key_weight, value_weight, spread, tokens)
+    pair_key, pair_value, pair_done = project(
+        place, pair_states, key_weight, value_weight, by_group[0], spread, tokens
+    )
     own_part, *by_reader = merge_near(place, pair_done, parts)
     mine = [own_part] + [swap(part, "pb", (at + 1) * inner) for at, part in enumerate(by_reader)]
     keys, values = (own_key, pair_key), (own_value, pair_value)

time: 118 us -> 117 us (level)
    unnamed x34 -> x38, local copies, waits for them, and re-layouts: 11.1 us -> 11.4 us
where the time goes in v10:
time: 117 us
  Pallas kernels  54.9 us (47%)
  waiting for transfers between devices  25.5 us (22%)
  starting transfers between devices  21.6 us (18%)
  local copies, waits for them, and re-layouts  12.9 us (11%)
  other arithmetic  1.6 us (1%)
    ppermute x17, waiting for transfers between devices, swap(): return lax.ppermute(value, axis, [(at, at ^ bits) for at in range(size)])  23.6 us
    pallas_call x4, Pallas kernels, attend(): pl.pallas_call(functools.partial(attend_kernel, offset=offset, column=col...  19.7 us
    pallas_call x2, Pallas kernels, project(): pl.pallas_call(project_kernel, grid_spec=pltpu.PrefetchScalarGridSpec(num...  18.7 us
    ppermute x17, starting transfers between devices, swap(): return lax.ppermute(value, axis, [(at, at ^ bits) for at in range(size)])  17.5 us
    unnamed x38, local copies, waits for them, and re-layouts  11.4 us
    pallas_call x1, Pallas kernels, retrieve(): pl.pallas_call(functools.partial(retrieval_kernel, spread=spread), grid_s...  7.42 us
    ppermute x3, starting transfers between devices, local(): lax.ppermute(lot, ('pa', 'pb'), [(at, at ^ bits) for at in range(runners...  4.06 us
  transfers between devices with their start and end apart: 20, of which 12 were waited for; matrix products, arithmetic and copies ran while one was open for 3% of the time, Pallas kernels for 43%

profile of v10, /device:TPU:0, one launch (start us, length us, event | category | flops | bytes accessed | tf_op | source)
XLA Modules:
  0.0 116.7 jit_solution(1273236661375883949)
XLA Ops:
  1.1 7.4 %retrieve.1 = (bf16[2,8,32,896]{3,2,1,0:T(8,128)(2,1)}, bf16[2,8,32,896]{3,2,1,0:T(8,128)(2,1)}) custom-call(s32[4]{0:T(128)} %pad_add_fusion.1.place, bf16[1024,768]{1,0:T(8,128)(2,1)} %queries.1, bf16[512,768]{1,0:T(8,128)(2,1)} %passages.1, bf16[1024,512]{1,0:T(8,128)(2,1)} %noise.1), custom_call_target="tpu_custom_call" | custom-call | flops 1610612736 | bytes 4980736 | tf_op jit(solution)/shard_map/retrieve/pallas_call | solution.py:103
  9.8 1.4 %collective-permute-done.2.recv = bf16[2,8,32,896]{3,2,1,0:T(8,128)(2,1)S(1)} collective-permute-done((bf16[2,8,32,896]{3,2,1,0:T(8,128)(2,1)}, bf16[2,8,32,896]{3,2,1,0:T(8,128)(2,1)S(1)}, u32[]{:S(2)}, u32[]{:S(2)}) %collective-permute-start.2) | collective-permute-done | bytes 917536 | tf_op jit(solution)/shard_map/ppermute | solution.py:520
  11.2 1.2 %copy-done.9 = bf16[2,8,32,896]{3,2,1,0:T(8,128)(2,1)S(1)} copy-done((bf16[2,8,32,896]{3,2,1,0:T(8,128)(2,1)S(1)}, bf16[2,8,32,896]{3,2,1,0:T(8,128)(2,1)}, u32[]{:S(2)}) %copy-start.9) | copy-done | bytes 917528
  12.4 1.6 %merge_pair.1 = (bf16[8,32,896]{2,1,0:T(8,128)(2,1)S(1)}, bf16[8,32,896]{2,1,0:T(8,128)(2,1)S(1)}) custom-call(s32[4]{0:T(128)S(1)} %copy-done.13, bf16[2,8,32,896]{3,2,1,0:T(8,128)(2,1)S(1)} %copy-done.9, bf16[2,8,32,896]{3,2,1,0:T(8,128)(2,1)S(1)} %collective-permute-done.2.recv), custom_call_target="tpu_custom_call" | custom-call | tf_op jit(solution)/shard_map/merge_pair/pallas_call | solution.py:151
  14.8 2.6 %collective-permute-start.3 = (bf16[8,32,896]{2,1,0:T(8,128)(2,1)S(1)}, bf16[8,32,896]{2,1,0:T(8,128)(2,1)S(1)}, u32[]{:S(2)}, u32[]{:S(2)}) collective-permute-start(bf16[8,32,896]{2,1,0:T(8,128)(2,1)S(1)} %get-tuple-element.31), channel_id=1, source_target_pairs={{0,16},{8,24},{16,0},{24,8},{1,17},{9,25},{17,1},{25,9},{2,18},{10... | collective-permute-start | bytes 1376264 | tf_op jit(solution)/shard_map/ppermute | solution.py:520
  17.7 9.3 %project.2 = (bf16[2,2048,256]{2,1,0:T(8,128)(2,1)}, bf16[2,8,256,256]{3,2,1,0:T(8,128)(2,1)}, f32[8,128]{1,0:T(8,128)}) custom-call(s32[4]{0:T(128)} %pad_add_fusion.1.place, bf16[2048,1024]{1,0:T(8,128)(2,1)} %bitcast.24, bf16[1024,1024]{1,0:T(8,128)(2,1)} %refs_1_.3, bf16[1024,1024]{1,0:T(8,128)(2,1)} %refs_1_.3, bf16[1024,1024]{1,0:T(8,128)(2,1)} %refs_3_.3, ...), custom_call_target="tpu_custom_call" | custom-call | flops 268435456 | bytes 655360 | tf_op jit(solution)/shard_map/project/pallas_call | solution.py:264
  27.0 1.5 %collective-permute-done.3.refs_1_ = bf16[8,32,896]{2,1,0:T(8,128)(2,1)S(1)} collective-permute-done((bf16[8,32,896]{2,1,0:T(8,128)(2,1)S(1)}, bf16[8,32,896]{2,1,0:T(8,128)(2,1)S(1)}, u32[]{:S(2)}, u32[]{:S(2)}) %collective-permute-start.3) | collective-permute-done | bytes 458784 | tf_op jit(solution)/shard_map/ppermute | solution.py:520
  29.2 1.7 %merge_columns.1 = (bf16[4,32,896]{2,1,0:T(8,128)(2,1)S(1)}, bf16[4,32,896]{2,1,0:T(8,128)(2,1)}) custom-call(s32[4]{0:T(128)S(1)} %copy-done.14, f32[1,128]{1,0:T(1,128)S(1)} %pad.4.note, f32[8,128]{1,0:T(8,128)S(1)} %copy-done.17, bf16[8,32,896]{2,1,0:T(8,128)(2,1)S(1)} %copy-done.7, bf16[8,32,896]{2,1,0:T(8,128)(2,1)S(1)} %collective-permute-done.3.refs_1_), custom_call_target="tpu_custom_call" | custom-call | tf_op jit(solution)/shard_map/merge_columns/pallas_call | solution.py:175
  31.6 1.8 %collective-permute-start.4 = (bf16[4,32,896]{2,1,0:T(8,128)(2,1)}, bf16[4,32,896]{2,1,0:T(8,128)(2,1)}, u32[]{:S(2)}, u32[]{:S(2)}) collective-permute-start(bf16[4,32,896]{2,1,0:T(8,128)(2,1)} %get-tuple-element.34), channel_id=1, source_target_pairs={{0,1},{1,0},{2,3},{3,2},{4,5},{5,4},{6,7},{7,6},{8,9},{9,8},{10,11... | collective-permute-start | bytes 688136 | tf_op jit(solution)/shard_map/ppermute | solution.py:520
  33.4 9.4 %project.3 = (bf16[2,2048,256]{2,1,0:T(8,128)(2,1)}, bf16[2,8,256,256]{3,2,1,0:T(8,128)(2,1)}, f32[8,128]{1,0:T(8,128)}) custom-call(s32[4]{0:T(128)} %pad_add_fusion.1.place, bf16[2048,1024]{1,0:T(8,128)(2,1)} %collective-permute-done.states, bf16[1024,1024]{1,0:T(8,128)(2,1)} %refs_1_.3, bf16[1024,1024]{1,0:T(8,128)(2,1)} %refs_1_.3, ...), custom_call_target="tpu_custom_call" | custom-call | flops 268435456 | bytes 655360 | tf_op jit(solution)/shard_map/project/pallas_call | solution.py:264
  43.5 1.2 %merge_near.1 = (bf16[32,896]{1,0:T(8,128)(2,1)S(1)}, bf16[32,896]{1,0:T(8,128)(2,1)S(1)}, bf16[32,896]{1,0:T(8,128)(2,1)S(1)}, bf16[32,896]{1,0:T(8,128)(2,1)S(1)}) custom-call(s32[4]{0:T(128)S(1)} %copy-done.15, f32[8,128]{1,0:T(8,128)S(1)} %copy-done.16, bf16[4,32,896]{2,1,0:T(8,128)(2,1)S(1)} %copy-done.11, ...), custom_call_target="tpu_custom_call" | custom-call | tf_op jit(solution)/shard_map/merge_near/pallas_call | solution.py:201
  44.7 1.6 %collective-permute-start.5 = (bf16[32,896]{1,0:T(8,128)(2,1)S(1)}, bf16[32,896]{1,0:T(8,128)(2,1)S(1)}, u32[]{:S(2)}, u32[]{:S(2)}) collective-permute-start(bf16[32,896]{1,0:T(8,128)(2,1)S(1)} %get-tuple-element.36), channel_id=1, source_target_pairs={{0,2},{1,3},{2,0},{3,1},{4,6},{5,7},{6,4},{7,5},{8,10},{9,11},{10,... | collective-permute-start | bytes 172040 | tf_op jit(solution)/shard_map/ppermute | solution.py:520
  46.4 2.6 %collective-permute-start.6 = (bf16[32,896]{1,0:T(8,128)(2,1)S(1)}, bf16[32,896]{1,0:T(8,128)(2,1)S(1)}, u32[]{:S(2)}, u32[]{:S(2)}) collective-permute-start(bf16[32,896]{1,0:T(8,128)(2,1)S(1)} %get-tuple-element.37), channel_id=1, source_target_pairs={{0,4},{1,5},{2,6},{3,7},{4,0},{5,1},{6,2},{7,3},{8,12},{9,13},{10,... | collective-permute-start | bytes 172040 | tf_op jit(solution)/shard_map/ppermute | solution.py:520
  49.5 2.5 %collective-permute-done.6.refs_2_ = bf16[32,896]{1,0:T(8,128)(2,1)S(1)} collective-permute-done((bf16[32,896]{1,0:T(8,128)(2,1)S(1)}, bf16[32,896]{1,0:T(8,128)(2,1)S(1)}, u32[]{:S(2)}, u32[]{:S(2)}) %collective-permute-start.6) | collective-permute-done | bytes 57376 | tf_op jit(solution)/shard_map/ppermute | solution.py:520
  52.1 2.9 %collective-permute-done.7.refs_3_ = bf16[32,896]{1,0:T(8,128)(2,1)S(1)} collective-permute-done((bf16[32,896]{1,0:T(8,128)(2,1)S(1)}, bf16[32,896]{1,0:T(8,128)(2,1)S(1)}, u32[]{:S(2)}, u32[]{:S(2)}) %collective-permute-start.7) | collective-permute-done | bytes 57376 | tf_op jit(solution)/shard_map/ppermute | solution.py:520
  58.5 4.1 %collective-permute-done.9 = bf16[1,2,32,512]{3,2,1,0:T(8,128)(2,1)S(1)} collective-permute-done((bf16[1,2,32,512]{3,2,1,0:T(8,128)(2,1)S(1)}, bf16[1,2,32,512]{3,2,1,0:T(8,128)(2,1)S(1)}, u32[]{:S(2)}, u32[]{:S(2)}) %collective-permute-start.9) | collective-permute-done | bytes 65568 | tf_op jit(solution)/shard_map/ppermute | solution.py:520
  64.2 1.6 %copy-done.1 = bf16[2,2048,256]{2,1,0:T(8,128)(2,1)S(1)} copy-done((bf16[2,2048,256]{2,1,0:T(8,128)(2,1)S(1)}, bf16[2,2048,256]{2,1,0:T(8,128)(2,1)}, u32[]{:S(2)}) %copy-start.1) | copy-done | bytes 2097176
  65.8 1.6 %copy-done.3 = bf16[2,8,256,256]{3,2,1,0:T(8,128)(2,1)S(1)} copy-done((bf16[2,8,256,256]{3,2,1,0:T(8,128)(2,1)S(1)}, bf16[2,8,256,256]{3,2,1,0:T(8,128)(2,1)}, u32[]{:S(2)}) %copy-start.3) | copy-done | bytes 2097176
  67.4 1.6 %copy-done.4 = bf16[2,2048,256]{2,1,0:T(8,128)(2,1)S(1)} copy-done((bf16[2,2048,256]{2,1,0:T(8,128)(2,1)S(1)}, bf16[2,2048,256]{2,1,0:T(8,128)(2,1)}, u32[]{:S(2)}) %copy-start.4) | copy-done | bytes 2097176
  69.0 1.6 %copy-done.5 = bf16[2,8,256,256]{3,2,1,0:T(8,128)(2,1)S(1)} copy-done((bf16[2,8,256,256]{3,2,1,0:T(8,128)(2,1)S(1)}, bf16[2,8,256,256]{3,2,1,0:T(8,128)(2,1)}, u32[]{:S(2)}) %copy-start.5) | copy-done | bytes 2097176
  72.3 1.6 %collective-permute-start.11 = (bf16[4,2,32,512]{3,2,1,0:T(8,128)(2,1)S(1)}, bf16[4,2,32,512]{3,2,1,0:T(8,128)(2,1)S(1)}, u32[]{:S(2)}, u32[]{:S(2)}) collective-permute-start(bf16[4,2,32,512]{3,2,1,0:T(8,128)(2,1)S(1)} %join.1.refs_0_), channel_id=1, source_target_pairs={{0,16},{8,24},{16,0},{24,8},{1,17},{9,25},{17,1},{25,9},{2,18},{10... | collective-permute-start | bytes 786440 | tf_op jit(solution)/shard_map/ppermute | solution.py:520
  74.4 5.0 %collective-permute-done.11.refs_1_ = bf16[4,2,32,512]{3,2,1,0:T(8,128)(2,1)S(1)} collective-permute-done((bf16[4,2,32,512]{3,2,1,0:T(8,128)(2,1)S(1)}, bf16[4,2,32,512]{3,2,1,0:T(8,128)(2,1)S(1)}, u32[]{:S(2)}, u32[]{:S(2)}) %collective-permute-start.11) | collective-permute-done | bytes 262176 | tf_op jit(solution)/shard_map/ppermute | solution.py:520
  79.9 4.9 %attend.4 = bf16[4,288,128]{2,1,0:T(8,128)(2,1)S(1)} custom-call(s32[4]{0:T(128)S(1)} %copy-done.15, s32[48]{0:T(128)S(1)} %stage.1.ready.table, bf16[2,2048,256]{2,1,0:T(8,128)(2,1)S(1)} %copy-done.2, bf16[2,2048,256]{2,1,0:T(8,128)(2,1)S(1)} %copy-done.4, bf16[2,8,256,256]{3,2,1,0:T(8,128)(2,1)S(1)} %copy-done.3, bf16[2,8,256,256]{3,2,1,0:T(8,128)(2,1)S(1)} %copy-done.5, ...), custom_call_target="tpu_custom_call" | custom-call | flops 2147483648 | bytes 294912 | tf_op jit(solution)/shard_map/attend/pallas_call | solution.py:368
  84.8 1.6 %collective-permute-start.12 = (bf16[4,288,128]{2,1,0:T(8,128)(2,1)S(1)}, bf16[4,288,128]{2,1,0:T(8,128)(2,1)S(1)}, u32[]{:S(2)}, u32[]{:S(2)}) collective-permute-start(bf16[4,288,128]{2,1,0:T(8,128)(2,1)S(1)} %attend.4), channel_id=1, source_target_pairs={{0,16},{1,17},{2,18},{3,19},{4,20},{5,21},{6,22},{7,23},{8,24},{9,... | collective-permute-start | bytes 884744 | tf_op jit(solution)/shard_map/ppermute | solution.py:575
  86.4 4.9 %attend.5 = bf16[4,288,128]{2,1,0:T(8,128)(2,1)S(1)} custom-call(s32[4]{0:T(128)S(1)} %copy-done.15, s32[48]{0:T(128)S(1)} %stage.1.ready.table, bf16[2,2048,256]{2,1,0:T(8,128)(2,1)S(1)} %copy-done.2, bf16[2,2048,256]{2,1,0:T(8,128)(2,1)S(1)} %copy-done.4, bf16[2,8,256,256]{3,2,1,0:T(8,128)(2,1)S(1)} %copy-done.3, bf16[2,8,256,256]{3,2,1,0:T(8,128)(2,1)S(1)} %copy-done.5, ...), custom_call_target="tpu_custom_call" | custom-call | flops 2147483648 | bytes 294912 | tf_op jit(solution)/shard_map/attend/pallas_call | solution.py:368
  91.2 1.6 %collective-permute-start.15 = (bf16[4,288,128]{2,1,0:T(8,128)(2,1)S(1)}, bf16[4,288,128]{2,1,0:T(8,128)(2,1)S(1)}, u32[]{:S(2)}, u32[]{:S(2)}) collective-permute-start(bf16[4,288,128]{2,1,0:T(8,128)(2,1)S(1)} %attend.5), channel_id=1, source_target_pairs={{0,1},{1,0},{2,3},{3,2},{4,5},{5,4},{6,7},{7,6},{8,9},{9,8},{10,11... | collective-permute-start | bytes 884744 | tf_op jit(solution)/shard_map/ppermute | solution.py:575
  92.8 5.1 %attend.6 = bf16[4,288,128]{2,1,0:T(8,128)(2,1)S(1)} custom-call(s32[4]{0:T(128)S(1)} %copy-done.15, s32[48]{0:T(128)S(1)} %stage.1.ready.table, bf16[2,2048,256]{2,1,0:T(8,128)(2,1)S(1)} %copy-done.2, bf16[2,2048,256]{2,1,0:T(8,128)(2,1)S(1)} %copy-done.4, bf16[2,8,256,256]{3,2,1,0:T(8,128)(2,1)S(1)} %copy-done.3, bf16[2,8,256,256]{3,2,1,0:T(8,128)(2,1)S(1)} %copy-done.5, ...), custom_call_target="tpu_custom_call" | custom-call | flops 2147483648 | bytes 294912 | tf_op jit(solution)/shard_map/attend/pallas_call | solution.py:368
  98.8 4.9 %attend.7.refs_3_ = bf16[4,288,128]{2,1,0:T(8,128)(2,1)S(1)} custom-call(s32[4]{0:T(128)S(1)} %copy-done.15, s32[48]{0:T(128)S(1)} %stage.1.ready.table, bf16[2,2048,256]{2,1,0:T(8,128)(2,1)S(1)} %copy-done.2, bf16[2,2048,256]{2,1,0:T(8,128)(2,1)S(1)} %copy-done.4, bf16[2,8,256,256]{3,2,1,0:T(8,128)(2,1)S(1)} %copy-done.3, ...), custom_call_target="tpu_custom_call" | custom-call | flops 2147483648 | bytes 294912 | tf_op jit(solution)/shard_map/attend/pallas_call | solution.py:368
  103.7 1.9 %collective-permute-done.16.refs_2_ = bf16[4,288,128]{2,1,0:T(8,128)(2,1)S(1)} collective-permute-done((bf16[4,288,128]{2,1,0:T(8,128)(2,1)S(1)}, bf16[4,288,128]{2,1,0:T(8,128)(2,1)S(1)}, u32[]{:S(2)}, u32[]{:S(2)}) %collective-permute-start.16) | collective-permute-done | bytes 294944 | tf_op jit(solution)/shard_map/ppermute | solution.py:575
  107.4 2.4 %collective-permute-start.18 = (bf16[288,128]{1,0:T(8,128)(2,1)S(1)}, bf16[288,128]{1,0:T(8,128)(2,1)S(1)}, u32[]{:S(2)}, u32[]{:S(2)}) collective-permute-start(bf16[288,128]{1,0:T(8,128)(2,1)S(1)} %get-tuple-element.47), channel_id=1, source_target_pairs={{0,4},{1,5},{2,6},{3,7},{4,0},{5,1},{6,2},{7,3},{8,12},{9,13},{10,... | collective-permute-start | bytes 221192 | tf_op jit(solution)/shard_map/ppermute | solution.py:520
  109.8 1.2 %collective-permute-start.19 = (bf16[288,128]{1,0:T(8,128)(2,1)S(1)}, bf16[288,128]{1,0:T(8,128)(2,1)S(1)}, u32[]{:S(2)}, u32[]{:S(2)}) collective-permute-start(bf16[288,128]{1,0:T(8,128)(2,1)S(1)} %get-tuple-element.48), channel_id=1, source_target_pairs={{0,6},{1,7},{2,4},{3,5},{4,2},{5,3},{6,0},{7,1},{8,14},{9,15},{10,... | collective-permute-start | bytes 221192 | tf_op jit(solution)/shard_map/ppermute | solution.py:520
  112.6 3.3 %collective-permute-done.19.refs_3_ = bf16[288,128]{1,0:T(8,128)(2,1)S(1)} collective-permute-done((bf16[288,128]{1,0:T(8,128)(2,1)S(1)}, bf16[288,128]{1,0:T(8,128)(2,1)S(1)}, u32[]{:S(2)}, u32[]{:S(2)}) %collective-permute-start.19) | collective-permute-done | bytes 73760 | tf_op jit(solution)/shard_map/ppermute | solution.py:520
  (89 shorter events, 19.0 us)
Async XLA Ops:
  0.0 8.6 %copy-start = (s32[256]{0:T(256)S(1)}, s32[256]{0:T(256)}, u32[]{:S(2)}) copy-start(s32[256]{0:T(256)} %param.18) | copy-start | bytes 3076
  0.0 33.4 %collective-permute-start = (bf16[2048,1024]{1,0:T(8,128)(2,1)}, bf16[2048,1024]{1,0:T(8,128)(2,1)}, u32[]{:S(2)}, u32[]{:S(2)}) collective-permute-start(bf16[2048,1024]{1,0:T(8,128)(2,1)} %bitcast.23), channel_id=1, source_target_pairs={{0,8},{8,0},{16,24},{24,16},{1,9},{9,1},{17,25},{25,17},{2,10},{10... | collective-permute-start | bytes 12582920 | tf_op jit(solution)/shard_map/ppermute | solution.py:520
  1.1 7.5 %copy-start.18 = (s32[1,16]{1,0:T(1,128)S(1)}, s32[1,16]{1,0:T(1,128)}, u32[]{:S(2)}) copy-start(s32[1,16]{1,0:T(1,128)} %param.19) | copy-start | bytes 196
  1.1 10.1 %copy-start.13 = (s32[4]{0:T(128)S(1)}, s32[4]{0:T(128)}, u32[]{:S(2)}) copy-start(s32[4]{0:T(128)} %pad_add_fusion.1.place) | copy-start | bytes 52
  8.5 2.7 %collective-permute-start.2 = (bf16[2,8,32,896]{3,2,1,0:T(8,128)(2,1)}, bf16[2,8,32,896]{3,2,1,0:T(8,128)(2,1)S(1)}, u32[]{:S(2)}, u32[]{:S(2)}) collective-permute-start(bf16[2,8,32,896]{3,2,1,0:T(8,128)(2,1)} %get-tuple-element.28), channel_id=1, source_target_pairs={{0,8},{8,0},{16,24},{24,16},{1,9},{9,1},{17,25},{25,17},{2,10},{10... | collective-permute-start | bytes 2752520 | tf_op jit(solution)/shard_map/ppermute | solution.py:520
  9.3 8.2 %collective-permute-start.1 = (s32[16]{0:T(128)S(1)}, s32[16]{0:T(128)S(1)}, u32[]{:S(2)}, u32[]{:S(2)}) collective-permute-start(s32[16]{0:T(128)S(1)} %and_select_fusion.4), channel_id=1, source_target_pairs={{0,8},{8,0},{16,24},{24,16},{1,9},{9,1},{17,25},{25,17},{2,10},{10... | collective-permute-start | bytes 200 | tf_op jit(solution)/shard_map/ppermute | solution.py:520
  14.8 13.7 %collective-permute-start.3 = (bf16[8,32,896]{2,1,0:T(8,128)(2,1)S(1)}, bf16[8,32,896]{2,1,0:T(8,128)(2,1)S(1)}, u32[]{:S(2)}, u32[]{:S(2)}) collective-permute-start(bf16[8,32,896]{2,1,0:T(8,128)(2,1)S(1)} %get-tuple-element.31), channel_id=1, source_target_pairs={{0,16},{8,24},{16,0},{24,8},{1,17},{9,25},{17,1},{25,9},{2,18},{10... | collective-permute-start | bytes 1376264 | tf_op jit(solution)/shard_map/ppermute | solution.py:520
  17.7 10.8 %copy-start.7 = (bf16[8,32,896]{2,1,0:T(8,128)(2,1)S(1)}, bf16[8,32,896]{2,1,0:T(8,128)(2,1)}, u32[]{:S(2)}) copy-start(bf16[8,32,896]{2,1,0:T(8,128)(2,1)} %copy-done.6) | copy-start | bytes 1376260
  17.7 10.8 %copy-start.14 = (s32[4]{0:T(128)S(1)}, s32[4]{0:T(128)}, u32[]{:S(2)}) copy-start(s32[4]{0:T(128)} %pad_add_fusion.1.place) | copy-start | bytes 52
  31.6 11.2 %collective-permute-start.4 = (bf16[4,32,896]{2,1,0:T(8,128)(2,1)}, bf16[4,32,896]{2,1,0:T(8,128)(2,1)}, u32[]{:S(2)}, u32[]{:S(2)}) collective-permute-start(bf16[4,32,896]{2,1,0:T(8,128)(2,1)} %get-tuple-element.34), channel_id=1, source_target_pairs={{0,1},{1,0},{2,3},{3,2},{4,5},{5,4},{6,7},{7,6},{8,9},{9,8},{10,11... | collective-permute-start | bytes 688136 | tf_op jit(solution)/shard_map/ppermute | solution.py:520
  33.4 9.4 %copy-start.11 = (bf16[4,32,896]{2,1,0:T(8,128)(2,1)S(1)}, bf16[4,32,896]{2,1,0:T(8,128)(2,1)}, u32[]{:S(2)}) copy-start(bf16[4,32,896]{2,1,0:T(8,128)(2,1)} %copy-done.10) | copy-start | bytes 688132
  33.4 9.4 %copy-start.15 = (s32[4]{0:T(128)S(1)}, s32[4]{0:T(128)}, u32[]{:S(2)}) copy-start(s32[4]{0:T(128)} %pad_add_fusion.1.place) | copy-start | bytes 52
  33.4 21.5 %copy-start.8 = (bf16[768,1024]{1,0:T(8,128)(2,1)S(1)}, bf16[768,1024]{1,0:T(8,128)(2,1)}, u32[]{:S(2)}) copy-start(bf16[768,1024]{1,0:T(8,128)(2,1)} %mix_weight.1) | copy-start | bytes 4718596
  44.7 4.8 %collective-permute-start.5 = (bf16[32,896]{1,0:T(8,128)(2,1)S(1)}, bf16[32,896]{1,0:T(8,128)(2,1)S(1)}, u32[]{:S(2)}, u32[]{:S(2)}) collective-permute-start(bf16[32,896]{1,0:T(8,128)(2,1)S(1)} %get-tuple-element.36), channel_id=1, source_target_pairs={{0,2},{1,3},{2,0},{3,1},{4,6},{5,7},{6,4},{7,5},{8,10},{9,11},{10,... | collective-permute-start | bytes 172040 | tf_op jit(solution)/shard_map/ppermute | solution.py:520
  46.4 5.7 %collective-permute-start.6 = (bf16[32,896]{1,0:T(8,128)(2,1)S(1)}, bf16[32,896]{1,0:T(8,128)(2,1)S(1)}, u32[]{:S(2)}, u32[]{:S(2)}) collective-permute-start(bf16[32,896]{1,0:T(8,128)(2,1)S(1)} %get-tuple-element.37), channel_id=1, source_target_pairs={{0,4},{1,5},{2,6},{3,7},{4,0},{5,1},{6,2},{7,3},{8,12},{9,13},{10,... | collective-permute-start | bytes 172040 | tf_op jit(solution)/shard_map/ppermute | solution.py:520
  49.0 6.0 %collective-permute-start.7 = (bf16[32,896]{1,0:T(8,128)(2,1)S(1)}, bf16[32,896]{1,0:T(8,128)(2,1)S(1)}, u32[]{:S(2)}, u32[]{:S(2)}) collective-permute-start(bf16[32,896]{1,0:T(8,128)(2,1)S(1)} %get-tuple-element.38), channel_id=1, source_target_pairs={{0,6},{1,7},{2,4},{3,5},{4,2},{5,3},{6,0},{7,1},{8,14},{9,15},{10,... | collective-permute-start | bytes 172040 | tf_op jit(solution)/shard_map/ppermute | solution.py:520
  57.0 1.3 %collective-permute-start.8 = (bf16[32,512]{1,0:T(8,128)(2,1)S(1)}, bf16[32,512]{1,0:T(8,128)(2,1)S(1)}, u32[]{:S(2)}, u32[]{:S(2)}) collective-permute-start(bf16[32,512]{1,0:T(8,128)(2,1)S(1)} %get-tuple-element.44), channel_id=1, source_target_pairs={{0,8},{8,0},{16,24},{24,16},{1,9},{9,1},{17,25},{25,17},{2,10},{10... | collective-permute-start | bytes 98312 | tf_op jit(solution)/shard_map/ppermute | solution.py:520
  58.3 4.3 %collective-permute-start.9 = (bf16[1,2,32,512]{3,2,1,0:T(8,128)(2,1)S(1)}, bf16[1,2,32,512]{3,2,1,0:T(8,128)(2,1)S(1)}, u32[]{:S(2)}, u32[]{:S(2)}) collective-permute-start(bf16[1,2,32,512]{3,2,1,0:T(8,128)(2,1)S(1)} %maximum_bitcast_fusion), channel_id=1, source_target_pairs={{0,2},{1,3},{2,0},{3,1},{4,6},{5,7},{6,4},{7,5},{8,10},{9,11},{10,... | collective-permute-start | bytes 196616 | tf_op jit(solution)/shard_map/ppermute | solution.py:520
  62.6 9.1 %collective-permute-start.10 = (bf16[2,2,32,512]{3,2,1,0:T(8,128)(2,1)S(1)}, bf16[2,2,32,512]{3,2,1,0:T(8,128)(2,1)S(1)}, u32[]{:S(2)}, u32[]{:S(2)}) collective-permute-start(bf16[2,2,32,512]{3,2,1,0:T(8,128)(2,1)S(1)} %pad_maximum_fusion.queries.first), channel_id=1, source_target_pairs={{0,4},{1,5},{2,6},{3,7},{4,0},{5,1},{6,2},{7,3},{8,12},{9,13},{10,... | collective-permute-start | bytes 393224 | tf_op jit(solution)/shard_map/ppermute | solution.py:520
  64.2 1.6 %copy-start.1 = (bf16[2,2048,256]{2,1,0:T(8,128)(2,1)S(1)}, bf16[2,2048,256]{2,1,0:T(8,128)(2,1)}, u32[]{:S(2)}) copy-start(bf16[2,2048,256]{2,1,0:T(8,128)(2,1)} %get-tuple-element.39.key_own) | copy-start | bytes 6291460
  65.8 1.6 %copy-start.3 = (bf16[2,8,256,256]{3,2,1,0:T(8,128)(2,1)S(1)}, bf16[2,8,256,256]{3,2,1,0:T(8,128)(2,1)}, u32[]{:S(2)}) copy-start(bf16[2,8,256,256]{3,2,1,0:T(8,128)(2,1)} %get-tuple-element.41.value_own) | copy-start | bytes 6291460
  67.4 1.6 %copy-start.4 = (bf16[2,2048,256]{2,1,0:T(8,128)(2,1)S(1)}, bf16[2,2048,256]{2,1,0:T(8,128)(2,1)}, u32[]{:S(2)}) copy-start(bf16[2,2048,256]{2,1,0:T(8,128)(2,1)} %get-tuple-element.40.key_pair) | copy-start | bytes 6291460
  70.6 9.4 %copy-start.2 = (bf16[2,2048,256]{2,1,0:T(8,128)(2,1)S(1)}, bf16[2,2048,256]{2,1,0:T(8,128)(2,1)}, u32[]{:S(2)}) copy-start(bf16[2,2048,256]{2,1,0:T(8,128)(2,1)} %get-tuple-element.39.key_own) | copy-start | bytes 6291460
  72.3 7.1 %collective-permute-start.11 = (bf16[4,2,32,512]{3,2,1,0:T(8,128)(2,1)S(1)}, bf16[4,2,32,512]{3,2,1,0:T(8,128)(2,1)S(1)}, u32[]{:S(2)}, u32[]{:S(2)}) collective-permute-start(bf16[4,2,32,512]{3,2,1,0:T(8,128)(2,1)S(1)} %join.1.refs_0_), channel_id=1, source_target_pairs={{0,16},{8,24},{16,0},{24,8},{1,17},{9,25},{17,1},{25,9},{2,18},{10... | collective-permute-start | bytes 786440 | tf_op jit(solution)/shard_map/ppermute | solution.py:520
  73.9 12.5 %collective-permute-start.13 = (bf16[4,2,32,512]{3,2,1,0:T(8,128)(2,1)S(1)}, bf16[4,2,32,512]{3,2,1,0:T(8,128)(2,1)S(1)}, u32[]{:S(2)}, u32[]{:S(2)}) collective-permute-start(bf16[4,2,32,512]{3,2,1,0:T(8,128)(2,1)S(1)} %join.1.refs_0_), channel_id=1, source_target_pairs={{0,1},{1,0},{2,3},{3,2},{4,5},{5,4},{6,7},{7,6},{8,9},{9,8},{10,11... | collective-permute-start | bytes 786440 | tf_op jit(solution)/shard_map/ppermute | solution.py:520
  79.4 7.0 %collective-permute-start.14 = (bf16[4,2,32,512]{3,2,1,0:T(8,128)(2,1)S(1)}, bf16[4,2,32,512]{3,2,1,0:T(8,128)(2,1)S(1)}, u32[]{:S(2)}, u32[]{:S(2)}) collective-permute-start(bf16[4,2,32,512]{3,2,1,0:T(8,128)(2,1)S(1)} %collective-permute-done.11.refs_1_), channel_id=1, source_target_pairs={{0,1},{1,0},{2,3},{3,2},{4,5},{5,4},{6,7},{7,6},{8,9},{9,8},{10,11... | collective-permute-start | bytes 786440 | tf_op jit(solution)/shard_map/ppermute | solution.py:520
  84.8 18.9 %collective-permute-start.12 = (bf16[4,288,128]{2,1,0:T(8,128)(2,1)S(1)}, bf16[4,288,128]{2,1,0:T(8,128)(2,1)S(1)}, u32[]{:S(2)}, u32[]{:S(2)}) collective-permute-start(bf16[4,288,128]{2,1,0:T(8,128)(2,1)S(1)} %attend.4), channel_id=1, source_target_pairs={{0,16},{1,17},{2,18},{3,19},{4,20},{5,21},{6,22},{7,23},{8,24},{9,... | collective-permute-start | bytes 884744 | tf_op jit(solution)/shard_map/ppermute | solution.py:575
  91.2 12.5 %collective-permute-start.15 = (bf16[4,288,128]{2,1,0:T(8,128)(2,1)S(1)}, bf16[4,288,128]{2,1,0:T(8,128)(2,1)S(1)}, u32[]{:S(2)}, u32[]{:S(2)}) collective-permute-start(bf16[4,288,128]{2,1,0:T(8,128)(2,1)S(1)} %attend.5), channel_id=1, source_target_pairs={{0,1},{1,0},{2,3},{3,2},{4,5},{5,4},{6,7},{7,6},{8,9},{9,8},{10,11... | collective-permute-start | bytes 884744 | tf_op jit(solution)/shard_map/ppermute | solution.py:575
  97.9 7.7 %collective-permute-start.16 = (bf16[4,288,128]{2,1,0:T(8,128)(2,1)S(1)}, bf16[4,288,128]{2,1,0:T(8,128)(2,1)S(1)}, u32[]{:S(2)}, u32[]{:S(2)}) collective-permute-start(bf16[4,288,128]{2,1,0:T(8,128)(2,1)S(1)} %attend.6), channel_id=1, source_target_pairs={{0,17},{1,16},{2,19},{3,18},{4,21},{5,20},{6,23},{7,22},{8,25},{9,... | collective-permute-start | bytes 884744 | tf_op jit(solution)/shard_map/ppermute | solution.py:575
  106.6 5.0 %collective-permute-start.17 = (bf16[288,128]{1,0:T(8,128)(2,1)S(1)}, bf16[288,128]{1,0:T(8,128)(2,1)S(1)}, u32[]{:S(2)}, u32[]{:S(2)}) collective-permute-start(bf16[288,128]{1,0:T(8,128)(2,1)S(1)} %get-tuple-element.46), channel_id=1, source_target_pairs={{0,2},{1,3},{2,0},{3,1},{4,6},{5,7},{6,4},{7,5},{8,10},{9,11},{10,... | collective-permute-start | bytes 221192 | tf_op jit(solution)/shard_map/ppermute | solution.py:520
  107.4 5.3 %collective-permute-start.18 = (bf16[288,128]{1,0:T(8,128)(2,1)S(1)}, bf16[288,128]{1,0:T(8,128)(2,1)S(1)}, u32[]{:S(2)}, u32[]{:S(2)}) collective-permute-start(bf16[288,128]{1,0:T(8,128)(2,1)S(1)} %get-tuple-element.47), channel_id=1, source_target_pairs={{0,4},{1,5},{2,6},{3,7},{4,0},{5,1},{6,2},{7,3},{8,12},{9,13},{10,... | collective-permute-start | bytes 221192 | tf_op jit(solution)/shard_map/ppermute | solution.py:520
  109.8 6.2 %collective-permute-start.19 = (bf16[288,128]{1,0:T(8,128)(2,1)S(1)}, bf16[288,128]{1,0:T(8,128)(2,1)S(1)}, u32[]{:S(2)}, u32[]{:S(2)}) collective-permute-start(bf16[288,128]{1,0:T(8,128)(2,1)S(1)} %get-tuple-element.48), channel_id=1, source_target_pairs={{0,6},{1,7},{2,4},{3,5},{4,2},{5,3},{6,0},{7,1},{8,14},{9,15},{10,... | collective-permute-start | bytes 221192 | tf_op jit(solution)/shard_map/ppermute | solution.py:520
  (7 other events, 6.6 us)
